TPU v7x, 32 devices: a whole 2x2x4 slice. The times are simulated.
32 devices in a mesh: pb: 4 (over y, x), ka: 8 (over z, core).
Axes of the slice: x: 2, y: 2, z: 4, core: 2. Of those that a mesh axis runs over, the one named last changes fastest.
Arguments:
- envelopes: bfloat16 [256, 36864], P('ka'), may hold values from -6 to 6
- coupling: bfloat16 [8, 9, 32, 2304], P('pb', None, None, 'ka'), may hold values from -3 to 3
- kq_map: int32 [8, 2304], P('pb', 'ka'), may hold values from 0 to 2303, as said below
Outputs:
- exciton_coupling: float32 [8, 9, 256, 256], P('pb', None, 'ka')
Inputs may be any that keep to these rules, and one draw needn't show every extreme that they name: `kq_map`: each row q is a lattice translation: k = kx * 96 + ky goes to ((kx + a_q) mod 24) * 96 + (ky + b_q) mod 96, with -3 <= a_q <= 3; a_q = 3 and a_q = -3 both occur.
All inputs are finite; a program needn't handle non-finite values.
Results may differ from a plain program's by a relative error of at most 0.0029.
Values may be sent and summed in bfloat16 or wider, within the bound.
No kernel may reach another device: no remote copies, remote signals or barrier semaphores. Data moves between devices by JAX's collectives and lax.ppermute only.
A program may use at most 64 MiB of HBM per device.

v0:
```python
import math

import jax
import jax.numpy as jnp
from jax import lax
from jax.sharding import PartitionSpec as P

NU = 9
KY = 96


def extended(cells, sides, width):
    for axis, dim in sides:
        count = lax.axis_size(axis)
        head = lax.slice_in_dim(cells, 0, width, axis=dim)
        tail = lax.slice_in_dim(cells, cells.shape[dim] - width, cells.shape[dim], axis=dim)
        cells = jnp.concatenate(
            [
                lax.ppermute(tail, axis, [(i, (i + 1) % count) for i in range(count)]),
                cells,
                lax.ppermute(head, axis, [((i + 1) % count, i) for i in range(count)]),
            ],
            axis=dim,
        )
    return cells


def shards(envelopes, coupling, kq_map):
    n_ka = lax.axis_size("ka")
    s_loc, width = envelopes.shape
    states = s_loc * n_ka
    total_k = width // 16
    lines = total_k // (n_ka * KY)
    lines_all = lines * n_ka
    local_k = lines * KY
    blocks = envelopes.reshape(s_loc, n_ka, local_k * 16)
    mine = lax.all_to_all(blocks, "ka", split_axis=1, concat_axis=0, tiled=True)
    mine = mine.reshape(states, lines, KY * 16)
    padded = extended(mine, (("ka", 1),), lines)
    padded = padded.reshape(states, 3 * local_k, 16)
    own = padded[:, local_k : 2 * local_k].reshape(states, local_k, 4, 4)
    first_line = lax.axis_index("ka") * lines
    line_x = kq_map // KY
    line_y = kq_map % KY
    padded_row = (line_x - first_line + lines) % lines_all
    local_index = padded_row * KY + line_y
    n_q = kq_map.shape[0]
    shifted_all = jnp.stack(
        [
            jnp.take(padded, local_index[qidx], axis=1).reshape(states, local_k * 16)
            for qidx in range(n_q)
        ],
        axis=1,
    )
    factor = 1.0 / math.sqrt(16.0 * lines_all * KY)

    def make_diff(qidx, mode):
        table = coupling[qidx, mode]
        g_cond = table[:16].reshape(4, 4, local_k)
        g_val = table[16:].reshape(4, 4, local_k)
        elec = jnp.einsum("dck,skvc->skvd", g_cond, own, preferred_element_type=jnp.float32)
        hole = jnp.einsum("vwk,skvc->skwc", g_val, own, preferred_element_type=jnp.float32)
        return (elec - hole).astype(jnp.bfloat16).reshape(states, local_k * 16)

    pieces = []
    for qidx in range(n_q):
        left_rows = shifted_all[:, qidx]

        def per_mode(mode):
            diff = make_diff(qidx, mode)
            return jnp.einsum("ap,bp->ab", left_rows, diff, preferred_element_type=jnp.float32)

        partial_sum = lax.map(per_mode, jnp.arange(NU, dtype=jnp.int32))
        pieces.append(lax.psum_scatter(partial_sum, "ka", scatter_dimension=1, tiled=True))
    result = jnp.stack(pieces, axis=0)
    return result * factor


def solution(mesh):
    return jax.shard_map(
        shards,
        mesh=mesh,
        in_specs=(P("ka", None), P("pb", None, None, "ka"), P("pb", "ka")),
        out_specs=P("pb", None, "ka", None),
        check_vma=False,
    )
```

profile of v0, /device:TPU:0, one launch (start us, length us, event | category | flops | bytes accessed | tf_op | source)
XLA Modules:
  0.0 656.5 jit_solution(14212025625330809154)
XLA Ops:
  8.4 60.9 %all_to_all.15 = bf16[32,8,4608]{2,0,1:T(8,128)(2,1)} all-to-all(bf16[32,8,4608]{2,0,1:T(8,128)(2,1)S(1)} %bitcast.119), channel_id=1, replica_groups=mesh['pb'=4,'ka'=8] {'ka'}, dimensions={1} | all-to-all | bytes 4718592 | tf_op jit(solution)/shard_map/all_to_all | solution.py:37
  69.3 6.5 reshape.45
  78.3 3.5 collective-permute-start.1
  82.0 51.5 %collective-permute-done = bf16[256,3,1536]{2,0,1:T(8,128)(2,1)} collective-permute-done((bf16[256,3,1536]{2,0,1:T(8,128)(2,1)S(1)}, bf16[256,3,1536]{2,0,1:T(8,128)(2,1)}, u32[]{:S(2)}, u32[]{:S(2)}) %collective-permute-start) | collective-permute-done | bytes 2359328 | tf_op jit(solution)/shard_map/ppermute | solution.py:19
  133.5 3.7 copy.40
  137.2 3.8 copy.41
  141.1 9.8 %pad_maximum_fusion = bf16[256,9,1536]{2,1,0:T(8,128)(2,1)} fusion(bf16[256,3,1536]{2,1,0:T(4,128)(2,1)S(1)} %copy.41, bf16[256,3,1536]{2,1,0:T(4,128)(2,1)S(1)} %copy-done, bf16[256,3,1536]{2,1,0:T(4,128)(2,1)S(1)} %copy.40), kind=kLoop, calls=%fused_computation.18 | loop fusion | flops 21233664 | bytes 14155776 | tf_op jit(solution)/shard_map/concatenate | solution.py:17
  150.8 16.1 %copy.42 = bf16[256,9,1536]{0,2,1:T(8,128)(2,1)} copy(bf16[256,9,1536]{2,1,0:T(8,128)(2,1)} %pad_maximum_fusion) | data formatting | bytes 14155776 | tf_op jit(solution)/shard_map/concatenate | solution.py:17
  170.1 4.1 gather_fusion
  176.3 4.5 copy.45
  185.1 206.4 %while.20 = (s32[]{:T(128)}, f32[9,256,256]{2,1,0:T(8,128)}, s32[9]{0:T(128)S(1)}, bf16[2,9,32,288]{3,2,1,0:T(8,128)(2,1)}, bf16[256,288,4,4]{0,2,3,1:T(4,128)(2...) while((s32[]{:T(128)}, f32[9,256,256]{2,1,0:T(8,128)}, ...), condition=%wide.region_1.3_spmd, body=%wide.region_0.2_spmd.sunk | while | flops 625213440 | bytes 27392680 | solution.py:73
  192.6 6.4 fusion.47
  199.0 5.0 reshape.84
  211.8 3.5 fusion.46
  215.5 6.4 fusion.47
  221.9 5.0 reshape.84
  234.7 3.5 fusion.46
  238.4 6.4 fusion.47
  244.8 5.0 reshape.84
  257.6 3.5 fusion.46
  261.3 6.4 fusion.47
  267.7 5.0 reshape.84
  280.5 3.5 fusion.46
  284.3 6.4 fusion.47
  290.7 5.0 reshape.84
  303.5 3.5 fusion.46
  307.2 6.4 fusion.47
  313.6 5.0 reshape.84
  326.4 3.5 fusion.46
  330.2 6.4 fusion.47
  336.6 5.0 reshape.84
  353.1 6.4 fusion.47
  359.5 5.0 reshape.84
  372.3 3.5 fusion.46
  376.1 6.4 fusion.47
  382.5 5.0 reshape.84
  391.8 5.6 gather_fusion.1
  400.7 4.4 copy.48
  406.8 206.4 %while.21 = (s32[]{:T(128)}, f32[9,256,256]{2,1,0:T(8,128)}, s32[9]{0:T(128)S(1)}, bf16[2,9,32,288]{3,2,1,0:T(8,128)(2,1)}, bf16[256,288,4,4]{0,2,3,1:T(4,128)(2...) while((s32[]{:T(128)}, f32[9,256,256]{2,1,0:T(8,128)}, ...), condition=%wide.region_4.6_spmd, body=%wide.region_3.5_spmd.sunk | while | flops 625213440 | bytes 27392680 | solution.py:73
  414.2 6.4 fusion.55
  420.6 5.0 reshape.87
  433.4 3.5 fusion.54
  437.2 6.4 fusion.55
  443.6 5.0 reshape.87
  456.3 3.5 fusion.54
  460.1 6.4 fusion.55
  466.5 5.0 reshape.87
  483.0 6.4 fusion.55
  489.4 5.0 reshape.87
  502.2 3.5 fusion.54
  506.0 6.4 fusion.55
  512.4 5.0 reshape.87
  528.9 6.4 fusion.55
  535.3 5.0 reshape.87
  548.1 3.5 fusion.54
  551.9 6.4 fusion.55
  558.3 5.0 reshape.87
  571.0 3.5 fusion.54
  574.8 6.4 fusion.55
  581.2 5.0 reshape.87
  594.0 3.5 fusion.54
  597.7 6.4 fusion.55
  604.1 5.0 reshape.87
  613.2 34.6 %reduce-scatter.5.cloned.1.call-done = f32[9,32,256]{2,1,0:T(8,128)} async-done(((f32[9,256,256]{2,1,0:T(8,128)}), f32[9,32,256]{2,1,0:T(8,128)}) %reduce-scatter.5.cloned.1.call-update) | async-done | bytes 294928 | tf_op jit(solution)/shard_map/reduce_scatter | solution.py:74
  (198 shorter events, 146.0 us)
Async XLA Ops:
  6.5 606.7 %reduce-scatter.3.cloned.1.call-start = ((), (), s32[]{:S(2)}) async-start(), calls=%async_computation.3 | async-start | bytes 2654208 | tf_op jit(solution)/shard_map/reduce_scatter | solution.py:74
  75.8 6.0 copy-start.2
  78.3 55.3 %collective-permute-start = (bf16[256,3,1536]{2,0,1:T(8,128)(2,1)S(1)}, bf16[256,3,1536]{2,0,1:T(8,128)(2,1)}, u32[]{:S(2)}, u32[]{:S(2)}) collective-permute-start(bf16[256,3,1536]{2,0,1:T(8,128)(2,1)S(1)} %copy.38), channel_id=1, source_target_pairs={{0,1},{1,2},{2,3},{3,4},{4,5},{5,6},{6,7},{7,0},{8,9},{9,10},{10,1... | collective-permute-start | bytes 7077896 | tf_op jit(solution)/shard_map/ppermute | solution.py:19
  78.3 58.9 %collective-permute-start.1 = (bf16[256,3,1536]{2,0,1:T(8,128)(2,1)S(1)}, bf16[256,3,1536]{2,0,1:T(8,128)(2,1)}, u32[]{:S(2)}, u32[]{:S(2)}) collective-permute-start(bf16[256,3,1536]{2,0,1:T(8,128)(2,1)S(1)} %copy.38), channel_id=1, source_target_pairs={{1,0},{2,1},{3,2},{4,3},{5,4},{6,5},{7,6},{0,7},{9,8},{10,9},{11,1... | collective-permute-start | bytes 7077896 | tf_op jit(solution)/shard_map/ppermute | solution.py:21
  137.2 3.9 copy-start
  176.3 4.5 copy-start.1
  391.6 256.2 %reduce-scatter.5.cloned.1.call-start = ((), (), s32[]{:S(2)}) async-start(), calls=%async_computation.4 | async-start | bytes 2654208 | tf_op jit(solution)/shard_map/reduce_scatter | solution.py:74
Sparse Core Ops, SparseCore 0:
  391.7 34.6 reduce-scatter.2
  613.3 34.4 reduce-scatter.4
where the time goes:
time: 661 us; the launch traced here: 657 us
  matrix products  236 us (36%)
  local copies, waits for them, and re-layouts  202 us (31%)
  waiting for transfers between devices  86.2 us (13%)
  blocking collectives  60.9 us (9%)
  loops' own time  37.9 us (6%)
  other arithmetic  17.1 us (3%)
  between operations  13.5 us (2%)
    dot_general x18, matrix products, make_diff(): jnp.einsum('dck,skvc->skvd', g_cond, own, preferred_element_type=jnp.floa...  115 us
    reshape x18, local copies, waits for them, and re-layouts, make_diff(): return (elec - hole).astype(jnp.bfloat16).reshape(states, local_k * 16)  89.6 us
    dot_general x18, matrix products, make_diff(): jnp.einsum('vwk,skvc->skwc', g_val, own, preferred_element_type=jnp.float32)  62.9 us
    all_to_all x1, blocking collectives, shards(): mine = lax.all_to_all(blocks, 'ka', split_axis=1, concat_axis=0, tiled=True)  60.9 us
    dot_general x18, matrix products, per_mode(): jnp.einsum('ap,bp->ab', left_rows, diff, preferred_element_type=jnp.float32)  57.5 us
    ppermute x1, waiting for transfers between devices, extended(): lax.ppermute(tail, axis, [(i, (i + 1) % count) for i in range(count)])  51.5 us
    another operation x2, loops' own time, shards(): partial_sum = lax.map(per_mode, jnp.arange(NU, dtype=jnp.int32))  37.9 us
    reduce_scatter x2, waiting for transfers between devices, shards(): lax.psum_scatter(partial_sum, 'ka', scatter_dimension=1, tiled=True)  34.6 us
  transfers between devices with their start and end apart: 4, of which 2 were waited for; matrix products, arithmetic and copies ran while one was open for 31% of the time, Pallas kernels for 0%

commit v1 on v0

v1 whole, which is shorter than its diff:
```python
import functools
import math

import jax
import jax.numpy as jnp
from jax import lax
from jax.experimental import pallas as pl
from jax.experimental.pallas import tpu as pltpu
from jax.sharding import PartitionSpec as P

KY = 96
BANDS = 16
LINE = KY * BANDS
GROUPS = 3
F32 = jnp.float32
BF16 = jnp.bfloat16


def contract(a, b, dim_a, dim_b):
    return lax.dot_general(a, b, (((dim_a,), (dim_b,)), ((), ())), preferred_element_type=F32)


def prep_kernel(pieces, block, lines, scalars, *refs):
    ins, (own_ref, shift_ref, window, sems) = refs[: 2 * pieces], refs[2 * pieces :]
    start_line, roll, core, pb = scalars[0], scalars[1], scalars[2], scalars[3]
    rows = ins[0].shape[0]
    copies = []
    for half in range(2):
        for index in range(pieces):
            src = ins[half * pieces + index]
            size = src.shape[1]
            offset = 0
            if pieces > 1:
                turn = core if half == 0 else 1 - core
                rel = (0, 1 + turn, 2 - turn, 3)[index]
                offset = pl.multiple_of((pb ^ rel) * block, 128)
            copy = pltpu.make_async_copy(src, window.at[half, :, pl.ds(offset, size)], sems.at[half, index])
            copy.start()
            copies.append(copy)
    for copy in copies:
        copy.wait()
    first = core == 0

    def both(lane):
        mine = window[0, :, pl.ds(pl.multiple_of(lane, 128), LINE)].astype(F32)
        other = window[1, :, pl.ds(pl.multiple_of(lane, 128), LINE)].astype(F32)
        return jnp.concatenate([jnp.where(first, mine, other), jnp.where(first, other, mine)], axis=0)

    for line in range(lines):
        to = slice(line * LINE, (line + 1) * LINE)
        own_ref[:, to] = both((lines // 2 + line) * LINE).astype(BF16)
        shifted = both((start_line + line) * LINE)
        shift_ref[:, to] = pltpu.roll(shifted, roll, 1).astype(BF16)


def prepare(scalars, mine, other, block, lines):
    rows = mine[0].shape[0]
    pieces = len(mine)
    out = jax.ShapeDtypeStruct((2 * rows, lines * LINE), BF16)
    return pl.pallas_call(
        functools.partial(prep_kernel, pieces, block, lines),
        in_specs=[pl.BlockSpec(memory_space=pltpu.SMEM)] + [pl.BlockSpec(memory_space=pl.ANY)] * (2 * pieces),
        out_specs=[pl.BlockSpec(memory_space=pltpu.VMEM)] * 2,
        out_shape=[out, out],
        scratch_shapes=[
            pltpu.VMEM((2, rows, 2 * lines * LINE), BF16),
            pltpu.SemaphoreType.DMA((2, pieces)),
        ],
        compiler_params=pltpu.CompilerParams(vmem_limit_bytes=24 << 20),
        name="prepare",
    )(scalars, *mine, *other)


def main_kernel(n_z, factor, scalars, x_ref, mask_ref, *refs):
    owns, shifts = refs[:n_z], refs[n_z : 2 * n_z]
    mine_ref, sends, total = refs[2 * n_z], refs[2 * n_z + 1 : -1], refs[-1]
    step = pl.program_id(0)
    branches = x_ref.shape[0]

    @pl.when(step == 0)
    def _():
        total[...] = jnp.zeros_like(total)

    for branch in range(branches):
        parts = []
        for tile in range(LINE // 256):
            lanes = slice(tile * 256, (tile + 1) * 256)
            matrix = jnp.concatenate([x_ref[branch, :, lanes]] * 16, axis=0) * mask_ref[...]
            amps = jnp.concatenate([ref[:, lanes] for ref in owns], axis=0)
            parts.append(contract(amps, matrix, 1, 0).astype(BF16))
        diff = jnp.concatenate(parts, axis=1)
        shifted = jnp.concatenate([ref[...] for ref in shifts], axis=0)
        total[branch] += contract(shifted, diff, 1, 1)

    @pl.when(step == pl.num_programs(0) - 1)
    def _():
        core, roll = scalars[0], scalars[1]
        rows = mine_ref.shape[1]
        index = 0
        for chip in range(n_z):
            for flip in range(2):
                at = pl.multiple_of(chip * 2 * rows + rows * (core ^ flip), rows)
                for branch in range(branches):
                    piece = pltpu.roll(total[branch, pl.ds(at, rows), :] * factor, roll, 1)
                    if chip == 0 and flip == 0:
                        mine_ref[branch] = piece
                    else:
                        sends[index][branch] = piece.astype(BF16)
                if chip or flip:
                    index += 1


def products(scalars, x, mask, owns, shifts, rows, factor):
    n_z = len(owns)
    branches = x.shape[0]
    states = 2 * n_z * rows
    lines = x.shape[2] // LINE
    by_line = pl.BlockSpec((2 * rows, LINE), lambda i: (0, i))
    piece = pl.BlockSpec((branches, rows, states), lambda i: (0, 0, 0))
    sends = 2 * n_z - 1
    return pl.pallas_call(
        functools.partial(main_kernel, n_z, factor),
        grid=(lines,),
        in_specs=[
            pl.BlockSpec(memory_space=pltpu.SMEM),
            pl.BlockSpec((branches, BANDS, LINE), lambda i: (0, 0, i)),
            pl.BlockSpec((256, 256), lambda i: (0, 0)),
        ]
        + [by_line] * (2 * n_z),
        out_specs=[piece] * (1 + sends),
        out_shape=[jax.ShapeDtypeStruct((branches, rows, states), F32)]
        + [jax.ShapeDtypeStruct((branches, rows, states), BF16)] * sends,
        scratch_shapes=[pltpu.VMEM((branches, states, states), F32)],
        compiler_params=pltpu.CompilerParams(vmem_limit_bytes=40 << 20),
        cost_estimate=pl.CostEstimate(
            flops=4 * branches * states * states * lines * LINE,
            bytes_accessed=4 * states * lines * LINE,
            transcendentals=0,
        ),
        name="products",
    )(scalars, x, mask, *owns, *shifts)


def band_matrices(table):
    branches, _, count = table.shape
    table = table.astype(F32)
    cond = table[:, :16].reshape(branches, 4, 4, count)
    val = table[:, 16:].reshape(branches, 4, 4, count)
    eye = jnp.eye(4, dtype=F32)
    cond = jnp.swapaxes(cond, 1, 2)[:, None, :, None] * eye[None, :, None, :, None, None]
    val = val[:, :, None, :, None] * eye[None, None, :, None, :, None]
    x = (cond - val).astype(BF16).reshape(branches, 16, 16, count)
    return jnp.swapaxes(x, 2, 3).reshape(branches, 16, count * 16)


def shards(envelopes, coupling, kq_map):
    n_pb, n_ka = lax.axis_size("pb"), lax.axis_size("ka")
    assert n_pb == 4 and n_ka % 2 == 0 and coupling.shape[0] == 2
    n_z = n_ka // 2
    rows, width = envelopes.shape
    block = width // n_ka
    block_lines = block // LINE
    lines = 2 * block_lines
    pb, ka = lax.axis_index("pb"), lax.axis_index("ka")
    z, core = ka // 2, ka % 2

    def permute(x, to):
        pairs = []
        for p in range(n_pb):
            for k in range(n_ka):
                tp, tz, tc = to(p, k // 2, k % 2)
                pairs.append((p * n_ka + k, tp * n_ka + (tz % n_z) * 2 + tc))
        return lax.ppermute(x, ("pb", "ka"), pairs)

    def sibling(x):
        return permute(x, lambda p, zz, c: (p, zz, 1 - c))

    def own_block(index):
        return lax.dynamic_slice_in_dim(envelopes, (index % n_ka) * block, block, axis=1)

    window = jnp.concatenate([own_block(2 * z - 1 + w + n_ka) for w in range(4)], axis=1)
    window_other = sibling(window)
    arrived = []
    for e in range(1, n_z):
        piece = own_block(2 * (z - e) - 1 + pb + 2 * n_ka)
        arrived.append(permute(piece, lambda p, zz, c: (p, zz - e, c)))

    first = jnp.where(core == 0, 1, 2)
    table = lax.dynamic_index_in_dim(coupling, core, 0, keepdims=False)
    table_other = sibling(lax.dynamic_index_in_dim(coupling, 1 - core, 0, keepdims=False))
    table = jnp.where(
        core == 0,
        jnp.concatenate([table, table_other], axis=2),
        jnp.concatenate([table_other, table], axis=2),
    )
    x = band_matrices(table)

    origin = lax.dynamic_slice(kq_map, (core, 0), (1, 1))[0, 0]
    lines_all = width // LINE
    start_line = (origin // KY - ka * block_lines + block_lines + lines_all) % lines_all
    roll = (LINE - (origin % KY) * BANDS) % LINE
    scalars = jnp.stack([start_line, roll, core, pb]).astype(jnp.int32)

    chunks = [([window], [window_other])]
    for piece in arrived:
        one = permute(piece, lambda p, zz, c: (p ^ (1 + c), zz, c))
        two = permute(piece, lambda p, zz, c: (p ^ (2 - c), zz, c))
        three = permute(one, lambda p, zz, c: (p ^ (2 - c), zz, c))
        mine = [piece, one, two, three]
        chunks.append((mine, [sibling(m) for m in mine]))
    owns, shifts = [], []
    for mine, other in chunks:
        own, shift = prepare(scalars, mine, other, block, lines)
        owns.append(own)
        shifts.append(shift)

    index = jnp.arange(256, dtype=jnp.int32) // BANDS
    mask = (index[:, None] == index[None, :]).astype(BF16)
    factor = 1.0 / math.sqrt(float(width))
    out_scalars = jnp.stack([core, z * (2 * rows)]).astype(jnp.int32)
    branches = coupling.shape[1]
    results = []
    for group in range(GROUPS):
        lo, hi = group * branches // GROUPS, (group + 1) * branches // GROUPS
        mine, *sends = products(out_scalars, x[lo:hi], mask, owns, shifts, rows, factor)
        same, cross = mine, 0.0
        for number, piece in enumerate(sends, 1):
            e, flip = number // 2, number % 2
            got = permute(piece, lambda p, zz, c: (p, zz + e, c ^ flip)).astype(F32)
            if flip:
                cross = cross + got
            else:
                same = same + got
        results.append(
            jnp.where(core == 0, jnp.stack([same, cross]), jnp.stack([cross, same]))
        )
    return jnp.concatenate(results, axis=1)


def solution(mesh):
    return jax.shard_map(
        shards,
        mesh=mesh,
        in_specs=(P("ka", None), P("pb", None, None, "ka"), P("pb", "ka")),
        out_specs=P("pb", None, "ka", None),
        check_vma=False,
    )
```

time: 661 us -> 230 us (0.35)
  matrix products: 236 us -> 0 us
  local copies, waits for them, and re-layouts: 202 us -> 98.3 us
  blocking collectives: 60.9 us -> 0 us
  waiting for transfers between devices: 86.2 us -> 26.6 us
  Pallas kernels: 0 us -> 44.8 us
  starting transfers between devices: 3.85 us -> 44 us
  loops' own time: 37.9 us -> 0 us
  between operations: 13.5 us -> 4.42 us
    dot_general x54 -> x0, matrix products: 236 us -> none  [the longest x18 115 us: make_diff(): jnp.einsum('dck,skvc->skvd', g_cond, own, preferred_element_type=jnp.floa...]
    reshape x93 -> x1, local copies, waits for them, and re-layouts: 110 us -> 1.09 us  [band_matrices(): cond = table[:, :16].reshape(branches, 4, 4, count)]
    all_to_all x1 -> x0, blocking collectives: 60.9 us -> none  [shards(): mine = lax.all_to_all(blocks, 'ka', split_axis=1, concat_axis=0, tiled=True)]
    slice x21 -> x8, local copies, waits for them, and re-layouts: 17.3 us -> 62.5 us  [the longest x7 61.5 us: shards(): x[lo:hi]]
    pallas_call x0 -> x7, Pallas kernels: none -> 44.8 us  [the longest x3 33.4 us: products(): pl.pallas_call(functools.partial(main_kernel, n_z, factor), grid=(lines,)...]
    ppermute x2 -> x47, starting transfers between devices: 3.59 us -> 44 us  [permute(): return lax.ppermute(x, ('pb', 'ka'), pairs)]
    another operation x2 -> x0, loops' own time: 37.9 us -> none  [shards(): partial_sum = lax.map(per_mode, jnp.arange(NU, dtype=jnp.int32))]
    reduce_scatter x2 -> x0, waiting for transfers between devices: 34.6 us -> none  [shards(): lax.psum_scatter(partial_sum, 'ka', scatter_dimension=1, tiled=True)]
  transfers between devices with their start and end apart: 4 -> 47, of which waited for: 2 -> 10; matrix products, arithmetic and copies ran while one was open for 31% -> 45% of each run, Pallas kernels for 0% -> 13%
where the time goes in v1:
time: 230 us; the launch traced here: 229 us
  local copies, waits for them, and re-layouts  98.3 us (43%)
  Pallas kernels  44.8 us (19%)
  starting transfers between devices  44 us (19%)
  waiting for transfers between devices  26.6 us (12%)
  other arithmetic  10.6 us (5%)
  between operations  4.42 us (2%)
    slice x7, local copies, waits for them, and re-layouts, shards(): x[lo:hi]  61.5 us
    ppermute x47, starting transfers between devices, permute(): return lax.ppermute(x, ('pb', 'ka'), pairs)  44 us
    pallas_call x3, Pallas kernels, products(): pl.pallas_call(functools.partial(main_kernel, n_z, factor), grid=(lines,)...  33.4 us
    ppermute x47, waiting for transfers between devices, permute(): return lax.ppermute(x, ('pb', 'ka'), pairs)  26.6 us
    mul x5, local copies, waits for them, and re-layouts, band_matrices(): val = val[:, :, None, :, None] * eye[None, None, :, None, :, None]  15.5 us
    mul x4, local copies, waits for them, and re-layouts, band_matrices(): jnp.swapaxes(cond, 1, 2)[:, None, :, None]  13.3 us
    pallas_call x4, Pallas kernels, prepare(): pl.pallas_call(functools.partial(prep_kernel, pieces, block, lines), in_s...  11.3 us
    transpose x1, other arithmetic, band_matrices(): return jnp.swapaxes(x, 2, 3).reshape(branches, 16, count * 16)  5.72 us
  transfers between devices with their start and end apart: 47, of which 10 were waited for; matrix products, arithmetic and copies ran while one was open for 45% of the time, Pallas kernels for 13%

profile of v1, /device:TPU:0, one launch (start us, length us, event | category | flops | bytes accessed | tf_op | source)
XLA Modules:
  0.0 228.6 jit_solution(3274431203954481236)
XLA Ops:
  0.0 1.8 dynamic-slice_bitcast_fusion.1
  2.2 1.6 constant_dynamic-slice_fusion
  3.9 4.7 %collective-permute-start.2 = (bf16[32,4608]{1,0:T(8,128)(2,1)S(1)}, bf16[32,4608]{1,0:T(8,128)(2,1)S(1)}, u32[]{:S(2)}, u32[]{:S(2)}) collective-permute-start(bf16[32,4608]{1,0:T(8,128)(2,1)S(1)} %get-tuple-element.73), channel_id=1, source_target_pairs={{0,6},{1,7},{2,0},{3,1},{4,2},{5,3},{6,4},{7,5},{8,14},{9,15},{10,... | collective-permute-start | bytes 884744 | tf_op jit(solution)/shard_map/ppermute | solution.py:173
  8.5 1.0 collective-permute-start.18
  9.6 1.3 fusion.5
  14.8 1.2 collective-permute-done.2.refs_0_
  15.9 1.5 collective-permute-start.3
  17.4 1.5 collective-permute-start.4
  19.0 0.6 mul.97
  19.6 0.8 mul.98
  20.4 0.7 mul.90
  21.1 1.4 mul.91
  22.5 11.8 %collective-permute-done.10.refs_0_ = bf16[32,4608]{1,0:T(8,128)(2,1)S(1)} collective-permute-done((bf16[32,4608]{1,0:T(8,128)(2,1)S(1)}, bf16[32,4608]{1,0:T(8,128)(2,1)S(1)}, u32[]{:S(2)}, u32[]{:S(2)}) %collective-permute-start.10) | collective-permute-done | bytes 294944 | tf_op jit(solution)/shard_map/ppermute | solution.py:173
  34.3 1.5 collective-permute-start.11
  35.9 1.5 collective-permute-start.12
  38.1 0.7 copy-done.10
  39.4 4.9 %collective-permute-done.11.refs_1_ = bf16[32,4608]{1,0:T(8,128)(2,1)} collective-permute-done((bf16[32,4608]{1,0:T(8,128)(2,1)S(1)}, bf16[32,4608]{1,0:T(8,128)(2,1)}, u32[]{:S(2)}, u32[]{:S(2)}) %collective-permute-start.11) | collective-permute-done | bytes 294944 | tf_op jit(solution)/shard_map/ppermute | solution.py:173
  44.2 0.8 compare_convert_fusion.mask_ref
  45.4 2.0 collective-permute-start.5
  47.4 0.7 copy-done.15
  48.1 2.4 %collective-permute-done.19.refs_1_ = bf16[32,4608]{1,0:T(8,128)(2,1)} collective-permute-done((bf16[32,4608]{1,0:T(8,128)(2,1)S(1)}, bf16[32,4608]{1,0:T(8,128)(2,1)}, u32[]{:S(2)}, u32[]{:S(2)}) %collective-permute-start.19) | collective-permute-done | bytes 294944 | tf_op jit(solution)/shard_map/ppermute | solution.py:173
  50.6 1.7 collective-permute-start.13
  52.2 1.5 fusion.1
  53.7 0.9 fusion.4
  54.6 1.8 mul.94
  56.5 4.4 %mul.95 = f32[9,4,4,4,4,576]{5,4,3,2,1,0:T(4,128)} broadcast(f32[9,4,4,576]{3,2,1,0:T(4,128)} %mul.94), dimensions={0,1,3,5} | broadcast | bytes 5640192 | tf_op jit(solution)/shard_map/mul | solution.py:151
  60.9 7.8 %mul.96 = f32[9,16,16,576]{3,2,1,0:T(8,128)} reshape(f32[9,4,4,4,4,576]{5,4,3,2,1,0:T(4,128)} %mul.95) | data formatting | bytes 10616832 | tf_op jit(solution)/shard_map/mul | solution.py:151
  68.7 1.1 reshape.63
  69.9 3.5 %mul.88 = f32[9,4,4,4,4,576]{5,4,3,2,1,0:T(4,128)} broadcast(f32[9,4,4,576]{3,2,1,0:T(4,128)S(1)} %copy.4), dimensions={0,2,4,5} | broadcast | bytes 5640192 | tf_op jit(solution)/shard_map/mul | solution.py:150
  73.4 7.6 %mul.89 = f32[9,16,16,576]{3,2,1,0:T(8,128)} reshape(f32[9,4,4,4,4,576]{5,4,3,2,1,0:T(4,128)} %mul.88) | data formatting | bytes 10616832 | tf_op jit(solution)/shard_map/mul | solution.py:150
  81.6 1.2 collective-permute-start.21
  82.9 5.7 %fusion = bf16[9,16,576,16]{2,3,1,0:T(8,128)(2,1)S(1)} fusion(f32[9,16,16,576]{3,2,1,0:T(8,128)} %mul.96, f32[9,16,16,576]{3,2,1,0:T(8,128)} %mul.89, f32[16,16]{1,0:T(8,128)S(1)} %mul.98, f32[16,16]{1,0:T(8,128)} %mul.91), kind=kLoop, calls=%fused_computation.1 | loop fusion | flops 5308416 | bytes 13273088 | tf_op jit(solution)/shard_map/transpose | solution.py:153
  90.2 1.8 fusion.3
  91.9 6.4 %copy.7 = bf16[3,16,576,16]{3,2,1,0:T(8,128)(2,1)} copy(bf16[3,16,576,16]{2,3,1,0:T(8,128)(2,1)} %get-tuple-element.70) | data formatting | bytes 1769472 | tf_op jit(solution)/shard_map/slice | solution.py:225
  98.3 13.8 %slice.31.x_ref = bf16[3,16,9216]{2,1,0:T(8,128)(2,1)} reshape(bf16[3,16,576,16]{3,2,1,0:T(8,128)(2,1)} %copy.7) | data formatting | bytes 1769472 | tf_op jit(solution)/shard_map/slice | solution.py:225
  112.1 6.3 %copy.6 = bf16[3,16,576,16]{3,2,1,0:T(8,128)(2,1)} copy(bf16[3,16,576,16]{2,3,1,0:T(8,128)(2,1)} %get-tuple-element.71) | data formatting | bytes 1769472 | tf_op jit(solution)/shard_map/slice | solution.py:225
  118.4 13.8 %slice.29.x_ref = bf16[3,16,9216]{2,1,0:T(8,128)(2,1)} reshape(bf16[3,16,576,16]{3,2,1,0:T(8,128)(2,1)} %copy.6) | data formatting | bytes 1769472 | tf_op jit(solution)/shard_map/slice | solution.py:225
  132.2 6.3 %copy.5 = bf16[3,16,576,16]{3,2,1,0:T(8,128)(2,1)} copy(bf16[3,16,576,16]{2,3,1,0:T(8,128)(2,1)} %get-tuple-element.69) | data formatting | bytes 1769472 | tf_op jit(solution)/shard_map/slice | solution.py:225
  138.6 13.1 %slice.27.x_ref = bf16[3,16,9216]{2,1,0:T(8,128)(2,1)S(1)} reshape(bf16[3,16,576,16]{3,2,1,0:T(8,128)(2,1)} %copy.5) | data formatting | bytes 1769472 | tf_op jit(solution)/shard_map/slice | solution.py:225
  151.8 2.3 %prepare.4 = (bf16[64,9216]{1,0:T(8,128)(2,1)S(1)}, bf16[64,9216]{1,0:T(8,128)(2,1)S(1)}) custom-call(s32[4]{0:T(128)S(1)} %pad_add_fusion.1.scalars, bf16[32,18432]{1,0:T(8,128)(2,1)S(1)} %pad_maximum_fusion.refs_0_, bf16[32,18432]{1,0:T(8,128)(2,1)S(1)} %collective-permute-done.1.refs_1_), custom_call_target="tpu_custom_call" | custom-call | tf_op jit(solution)/shard_map/prepare/pallas_call | solution.py:60
  154.2 1.0 copy-done.22
  155.1 2.9 %prepare.5 = (bf16[64,9216]{1,0:T(8,128)(2,1)S(1)}, bf16[64,9216]{1,0:T(8,128)(2,1)S(1)}) custom-call(s32[4]{0:T(128)S(1)} %pad_add_fusion.1.scalars, bf16[32,4608]{1,0:T(8,128)(2,1)S(1)} %copy-done.5, bf16[32,4608]{1,0:T(8,128)(2,1)S(1)} %copy-done.7, bf16[32,4608]{1,0:T(8,128)(2,1)S(1)} %copy-done.9, bf16[32,4608]{1,0:T(8,128)(2,1)} %collective-permute-done.5.refs_3_, ...), custom_call_target="tpu_custom_call" | custom-call | tf_op jit(solution)/shard_map/prepare/pallas_call | solution.py:60
  158.1 2.9 %prepare.6 = (bf16[64,9216]{1,0:T(8,128)(2,1)S(1)}, bf16[64,9216]{1,0:T(8,128)(2,1)S(1)}) custom-call(s32[4]{0:T(128)S(1)} %pad_add_fusion.1.scalars, bf16[32,4608]{1,0:T(8,128)(2,1)S(1)} %copy-done.3, bf16[32,4608]{1,0:T(8,128)(2,1)} %collective-permute-done.11.refs_1_, bf16[32,4608]{1,0:T(8,128)(2,1)S(1)} %copy-done.14, ...), custom_call_target="tpu_custom_call" | custom-call | tf_op jit(solution)/shard_map/prepare/pallas_call | solution.py:60
  161.1 3.2 %prepare.7 = (bf16[64,9216]{1,0:T(8,128)(2,1)S(1)}, bf16[64,9216]{1,0:T(8,128)(2,1)S(1)}) custom-call(s32[4]{0:T(128)S(1)} %pad_add_fusion.1.scalars, bf16[32,4608]{1,0:T(8,128)(2,1)S(1)} %collective-permute-done.18.refs_0_, bf16[32,4608]{1,0:T(8,128)(2,1)} %collective-permute-done.19.refs_1_, bf16[32,4608]{1,0:T(8,128)(2,1)} %collective-permute-done.20.refs_2_, ...), custom_call_target="tpu_custom_call" | custom-call | tf_op jit(solution)/shard_map/prepare/pallas_call | solution.py:60
  164.3 11.2 %products.5 = (f32[3,32,256]{2,1,0:T(8,128)S(1)}, bf16[3,32,256]{2,1,0:T(8,128)(2,1)S(1)}, bf16[3,32,256]{2,1,0:T(8,128)(2,1)S(1)}, bf16[3,32,256]{2,1,0:T(8,128...) custom-call(s32[2]{0:T(128)S(1)} %pad_add_fusion.scalars, ...), custom_call_target="tpu_custom_call" | custom-call | flops 7247757312 | bytes 9437184 | tf_op jit(solution)/shard_map/products/pallas_call | solution.py:121
  175.6 4.0 %collective-permute-start.42 = (bf16[3,32,256]{2,1,0:T(8,128)(2,1)S(1)}, bf16[3,32,256]{2,1,0:T(8,128)(2,1)S(1)}, u32[]{:S(2)}, u32[]{:S(2)}) collective-permute-start(bf16[3,32,256]{2,1,0:T(8,128)(2,1)S(1)} %get-tuple-element.64), channel_id=1, source_target_pairs={{0,6},{1,7},{2,0},{3,1},{4,2},{5,3},{6,4},{7,5},{8,14},{9,15},{10,... | collective-permute-start | bytes 147464 | tf_op jit(solution)/shard_map/ppermute | solution.py:173
  180.3 11.1 %products.4 = (f32[3,32,256]{2,1,0:T(8,128)S(1)}, bf16[3,32,256]{2,1,0:T(8,128)(2,1)S(1)}, bf16[3,32,256]{2,1,0:T(8,128)(2,1)S(1)}, bf16[3,32,256]{2,1,0:T(8,128...) custom-call(s32[2]{0:T(128)S(1)} %pad_add_fusion.scalars, ...), custom_call_target="tpu_custom_call" | custom-call | flops 7247757312 | bytes 9437184 | tf_op jit(solution)/shard_map/products/pallas_call | solution.py:121
  191.4 11.2 %products.3 = (f32[3,32,256]{2,1,0:T(8,128)S(1)}, bf16[3,32,256]{2,1,0:T(8,128)(2,1)S(1)}, bf16[3,32,256]{2,1,0:T(8,128)(2,1)S(1)}, bf16[3,32,256]{2,1,0:T(8,128...) custom-call(s32[2]{0:T(128)S(1)} %pad_add_fusion.scalars, ...), custom_call_target="tpu_custom_call" | custom-call | flops 7247757312 | bytes 9437184 | tf_op jit(solution)/shard_map/products/pallas_call | solution.py:121
  202.6 1.8 collective-permute-start.44
  204.4 1.3 collective-permute-start.43
  205.6 0.6 collective-permute-start.39
  206.3 0.7 collective-permute-start.38
  207.0 1.1 collective-permute-start.37
  208.5 2.4 %collective-permute-start.35 = (bf16[3,32,256]{2,1,0:T(8,128)(2,1)S(1)}, bf16[3,32,256]{2,1,0:T(8,128)(2,1)S(1)}, u32[]{:S(2)}, u32[]{:S(2)}) collective-permute-start(bf16[3,32,256]{2,1,0:T(8,128)(2,1)S(1)} %get-tuple-element.56), channel_id=1, source_target_pairs={{0,6},{1,7},{2,0},{3,1},{4,2},{5,3},{6,4},{7,5},{8,14},{9,15},{10,... | collective-permute-start | bytes 147464 | tf_op jit(solution)/shard_map/ppermute | solution.py:173
  210.9 0.6 collective-permute-start.34
  211.6 1.2 collective-permute-start.33
  212.8 4.0 %collective-permute-start.32 = (bf16[3,32,256]{2,1,0:T(8,128)(2,1)S(1)}, bf16[3,32,256]{2,1,0:T(8,128)(2,1)S(1)}, u32[]{:S(2)}, u32[]{:S(2)}) collective-permute-start(bf16[3,32,256]{2,1,0:T(8,128)(2,1)S(1)} %get-tuple-element.52), channel_id=1, source_target_pairs={{0,7},{1,6},{2,1},{3,0},{4,3},{5,2},{6,5},{7,4},{8,15},{9,14},{10,... | collective-permute-start | bytes 147464 | tf_op jit(solution)/shard_map/ppermute | solution.py:173
  216.9 0.7 collective-permute-start.29
  217.7 3.2 %collective-permute-start.28 = (bf16[3,32,256]{2,1,0:T(8,128)(2,1)S(1)}, bf16[3,32,256]{2,1,0:T(8,128)(2,1)S(1)}, u32[]{:S(2)}, u32[]{:S(2)}) collective-permute-start(bf16[3,32,256]{2,1,0:T(8,128)(2,1)S(1)} %get-tuple-element.48), channel_id=1, source_target_pairs={{0,6},{1,7},{2,0},{3,1},{4,2},{5,3},{6,4},{7,5},{8,14},{9,15},{10,... | collective-permute-start | bytes 147464 | tf_op jit(solution)/shard_map/ppermute | solution.py:173
  220.9 0.8 collective-permute-start.27
  222.4 0.9 collective-permute-done.28
  223.3 2.7 %collective-permute-done.27 = bf16[3,32,256]{2,1,0:T(8,128)(2,1)S(1)} collective-permute-done((bf16[3,32,256]{2,1,0:T(8,128)(2,1)S(1)}, bf16[3,32,256]{2,1,0:T(8,128)(2,1)S(1)}, u32[]{:S(2)}, u32[]{:S(2)}) %collective-permute-start.27) | collective-permute-done | bytes 49184 | tf_op jit(solution)/shard_map/ppermute | solution.py:173
  226.0 1.7 collective-permute-done.26
  227.7 0.9 pad_maximum_fusion.1
  (125 shorter events, 6.6 us)
Async XLA Ops:
  1.8 17.2 %collective-permute-start = (bf16[9,32,288]{2,1,0:T(8,128)(2,1)S(1)}, bf16[9,32,288]{2,1,0:T(8,128)(2,1)}, u32[]{:S(2)}, u32[]{:S(2)}) collective-permute-start(bf16[9,32,288]{2,1,0:T(8,128)(2,1)S(1)} %get-tuple-element.82), channel_id=1, source_target_pairs={{0,1},{1,0},{2,3},{3,2},{4,5},{5,4},{6,7},{7,6},{8,9},{9,8},{10,11... | collective-permute-start | bytes 497672 | tf_op jit(solution)/shard_map/ppermute | solution.py:173
  3.9 12.1 %collective-permute-start.2 = (bf16[32,4608]{1,0:T(8,128)(2,1)S(1)}, bf16[32,4608]{1,0:T(8,128)(2,1)S(1)}, u32[]{:S(2)}, u32[]{:S(2)}) collective-permute-start(bf16[32,4608]{1,0:T(8,128)(2,1)S(1)} %get-tuple-element.73), channel_id=1, source_target_pairs={{0,6},{1,7},{2,0},{3,1},{4,2},{5,3},{6,4},{7,5},{8,14},{9,15},{10,... | collective-permute-start | bytes 884744 | tf_op jit(solution)/shard_map/ppermute | solution.py:173
  8.5 25.8 %collective-permute-start.10 = (bf16[32,4608]{1,0:T(8,128)(2,1)S(1)}, bf16[32,4608]{1,0:T(8,128)(2,1)S(1)}, u32[]{:S(2)}, u32[]{:S(2)}) collective-permute-start(bf16[32,4608]{1,0:T(8,128)(2,1)S(1)} %get-tuple-element.78), channel_id=1, source_target_pairs={{0,4},{1,5},{2,6},{3,7},{4,0},{5,1},{6,2},{7,3},{8,12},{9,13},{10,... | collective-permute-start | bytes 884744 | tf_op jit(solution)/shard_map/ppermute | solution.py:173
  8.5 27.4 %collective-permute-start.18 = (bf16[32,4608]{1,0:T(8,128)(2,1)S(1)}, bf16[32,4608]{1,0:T(8,128)(2,1)S(1)}, u32[]{:S(2)}, u32[]{:S(2)}) collective-permute-start(bf16[32,4608]{1,0:T(8,128)(2,1)S(1)} %get-tuple-element.72), channel_id=1, source_target_pairs={{0,2},{1,3},{2,4},{3,5},{4,6},{5,7},{6,0},{7,1},{8,10},{9,11},{10,... | collective-permute-start | bytes 884744 | tf_op jit(solution)/shard_map/ppermute | solution.py:173
  15.9 45.0 %copy-start.4 = (bf16[32,4608]{1,0:T(8,128)(2,1)}, bf16[32,4608]{1,0:T(8,128)(2,1)S(1)}, u32[]{:S(2)}) copy-start(bf16[32,4608]{1,0:T(8,128)(2,1)S(1)} %collective-permute-done.2.refs_0_) | copy-start | bytes 884740
  15.9 21.5 %collective-permute-start.3 = (bf16[32,4608]{1,0:T(8,128)(2,1)S(1)}, bf16[32,4608]{1,0:T(8,128)(2,1)S(1)}, u32[]{:S(2)}, u32[]{:S(2)}) collective-permute-start(bf16[32,4608]{1,0:T(8,128)(2,1)S(1)} %collective-permute-done.2.refs_0_), channel_id=1, source_target_pairs={{0,8},{1,17},{2,10},{3,19},{4,12},{5,21},{6,14},{7,23},{8,0},{9,25... | collective-permute-start | bytes 884744 | tf_op jit(solution)/shard_map/ppermute | solution.py:173
  17.4 20.0 %collective-permute-start.4 = (bf16[32,4608]{1,0:T(8,128)(2,1)S(1)}, bf16[32,4608]{1,0:T(8,128)(2,1)S(1)}, u32[]{:S(2)}, u32[]{:S(2)}) collective-permute-start(bf16[32,4608]{1,0:T(8,128)(2,1)S(1)} %collective-permute-done.2.refs_0_), channel_id=1, source_target_pairs={{0,16},{1,9},{2,18},{3,11},{4,20},{5,13},{6,22},{7,15},{8,24},{9,1... | collective-permute-start | bytes 884744 | tf_op jit(solution)/shard_map/ppermute | solution.py:173
  19.0 19.1 %collective-permute-start.6 = (bf16[32,4608]{1,0:T(8,128)(2,1)S(1)}, bf16[32,4608]{1,0:T(8,128)(2,1)S(1)}, u32[]{:S(2)}, u32[]{:S(2)}) collective-permute-start(bf16[32,4608]{1,0:T(8,128)(2,1)S(1)} %collective-permute-done.2.refs_0_), channel_id=1, source_target_pairs={{0,1},{1,0},{2,3},{3,2},{4,5},{5,4},{6,7},{7,6},{8,9},{9,8},{10,11... | collective-permute-start | bytes 884744 | tf_op jit(solution)/shard_map/ppermute | solution.py:173
  34.3 26.6 %copy-start.2 = (bf16[32,4608]{1,0:T(8,128)(2,1)}, bf16[32,4608]{1,0:T(8,128)(2,1)S(1)}, u32[]{:S(2)}) copy-start(bf16[32,4608]{1,0:T(8,128)(2,1)S(1)} %collective-permute-done.10.refs_0_) | copy-start | bytes 884740
  34.3 9.9 %collective-permute-start.11 = (bf16[32,4608]{1,0:T(8,128)(2,1)S(1)}, bf16[32,4608]{1,0:T(8,128)(2,1)}, u32[]{:S(2)}, u32[]{:S(2)}) collective-permute-start(bf16[32,4608]{1,0:T(8,128)(2,1)S(1)} %collective-permute-done.10.refs_0_), channel_id=1, source_target_pairs={{0,8},{1,17},{2,10},{3,19},{4,12},{5,21},{6,14},{7,23},{8,0},{9,25... | collective-permute-start | bytes 884744 | tf_op jit(solution)/shard_map/ppermute | solution.py:173
  35.9 9.5 %collective-permute-start.12 = (bf16[32,4608]{1,0:T(8,128)(2,1)S(1)}, bf16[32,4608]{1,0:T(8,128)(2,1)S(1)}, u32[]{:S(2)}, u32[]{:S(2)}) collective-permute-start(bf16[32,4608]{1,0:T(8,128)(2,1)S(1)} %collective-permute-done.10.refs_0_), channel_id=1, source_target_pairs={{0,16},{1,9},{2,18},{3,11},{4,20},{5,13},{6,22},{7,15},{8,24},{9,1... | collective-permute-start | bytes 884744 | tf_op jit(solution)/shard_map/ppermute | solution.py:173
  37.4 23.5 %copy-start.6 = (bf16[32,4608]{1,0:T(8,128)(2,1)}, bf16[32,4608]{1,0:T(8,128)(2,1)S(1)}, u32[]{:S(2)}) copy-start(bf16[32,4608]{1,0:T(8,128)(2,1)S(1)} %collective-permute-done.3.refs_1_) | copy-start | bytes 884740
  37.4 9.9 %collective-permute-start.14 = (bf16[32,4608]{1,0:T(8,128)(2,1)S(1)}, bf16[32,4608]{1,0:T(8,128)(2,1)S(1)}, u32[]{:S(2)}, u32[]{:S(2)}) collective-permute-start(bf16[32,4608]{1,0:T(8,128)(2,1)S(1)} %collective-permute-done.10.refs_0_), channel_id=1, source_target_pairs={{0,1},{1,0},{2,3},{3,2},{4,5},{5,4},{6,7},{7,6},{8,9},{9,8},{10,11... | collective-permute-start | bytes 884744 | tf_op jit(solution)/shard_map/ppermute | solution.py:173
  37.5 13.1 %collective-permute-start.19 = (bf16[32,4608]{1,0:T(8,128)(2,1)S(1)}, bf16[32,4608]{1,0:T(8,128)(2,1)}, u32[]{:S(2)}, u32[]{:S(2)}) collective-permute-start(bf16[32,4608]{1,0:T(8,128)(2,1)S(1)} %collective-permute-done.18.refs_0_), channel_id=1, source_target_pairs={{0,8},{1,17},{2,10},{3,19},{4,12},{5,21},{6,14},{7,23},{8,0},{9,25... | collective-permute-start | bytes 884744 | tf_op jit(solution)/shard_map/ppermute | solution.py:173
  38.8 11.8 %collective-permute-start.20 = (bf16[32,4608]{1,0:T(8,128)(2,1)S(1)}, bf16[32,4608]{1,0:T(8,128)(2,1)}, u32[]{:S(2)}, u32[]{:S(2)}) collective-permute-start(bf16[32,4608]{1,0:T(8,128)(2,1)S(1)} %collective-permute-done.18.refs_0_), channel_id=1, source_target_pairs={{0,16},{1,9},{2,18},{3,11},{4,20},{5,13},{6,22},{7,15},{8,24},{9,1... | collective-permute-start | bytes 884744 | tf_op jit(solution)/shard_map/ppermute | solution.py:173
  44.2 45.4 %collective-permute-start.1 = (bf16[32,18432]{1,0:T(8,128)(2,1)S(1)}, bf16[32,18432]{1,0:T(8,128)(2,1)S(1)}, u32[]{:S(2)}, u32[]{:S(2)}) collective-permute-start(bf16[32,18432]{1,0:T(8,128)(2,1)S(1)} %pad_maximum_fusion.refs_0_), channel_id=1, source_target_pairs={{0,1},{1,0},{2,3},{3,2},{4,5},{5,4},{6,7},{7,6},{8,9},{9,8},{10,11... | collective-permute-start | bytes 3538952 | tf_op jit(solution)/shard_map/ppermute | solution.py:173
  45.4 5.2 %copy-start.12 = (bf16[32,4608]{1,0:T(8,128)(2,1)}, bf16[32,4608]{1,0:T(8,128)(2,1)S(1)}, u32[]{:S(2)}) copy-start(bf16[32,4608]{1,0:T(8,128)(2,1)S(1)} %collective-permute-done.12.refs_2_) | copy-start | bytes 884740
  45.4 35.7 %collective-permute-start.5 = (bf16[32,4608]{1,0:T(8,128)(2,1)S(1)}, bf16[32,4608]{1,0:T(8,128)(2,1)}, u32[]{:S(2)}, u32[]{:S(2)}) collective-permute-start(bf16[32,4608]{1,0:T(8,128)(2,1)S(1)} %collective-permute-done.3.refs_1_), channel_id=1, source_target_pairs={{0,16},{1,9},{2,18},{3,11},{4,20},{5,13},{6,22},{7,15},{8,24},{9,1... | collective-permute-start | bytes 884744 | tf_op jit(solution)/shard_map/ppermute | solution.py:173
  48.1 33.0 %collective-permute-start.7 = (bf16[32,4608]{1,0:T(8,128)(2,1)S(1)}, bf16[32,4608]{1,0:T(8,128)(2,1)}, u32[]{:S(2)}, u32[]{:S(2)}) collective-permute-start(bf16[32,4608]{1,0:T(8,128)(2,1)S(1)} %collective-permute-done.3.refs_1_), channel_id=1, source_target_pairs={{0,1},{1,0},{2,3},{3,2},{4,5},{5,4},{6,7},{7,6},{8,9},{9,8},{10,11... | collective-permute-start | bytes 884744 | tf_op jit(solution)/shard_map/ppermute | solution.py:173
  50.5 31.0 %collective-permute-start.8 = (bf16[32,4608]{1,0:T(8,128)(2,1)}, bf16[32,4608]{1,0:T(8,128)(2,1)}, u32[]{:S(2)}, u32[]{:S(2)}) collective-permute-start(bf16[32,4608]{1,0:T(8,128)(2,1)} %copy-done.8), channel_id=1, source_target_pairs={{0,1},{1,0},{2,3},{3,2},{4,5},{5,4},{6,7},{7,6},{8,9},{9,8},{10,11... | collective-permute-start | bytes 884744 | tf_op jit(solution)/shard_map/ppermute | solution.py:173
  50.6 32.2 %collective-permute-start.13 = (bf16[32,4608]{1,0:T(8,128)(2,1)}, bf16[32,4608]{1,0:T(8,128)(2,1)}, u32[]{:S(2)}, u32[]{:S(2)}) collective-permute-start(bf16[32,4608]{1,0:T(8,128)(2,1)} %collective-permute-done.11.refs_1_), channel_id=1, source_target_pairs={{0,16},{1,9},{2,18},{3,11},{4,20},{5,13},{6,22},{7,15},{8,24},{9,1... | collective-permute-start | bytes 884744 | tf_op jit(solution)/shard_map/ppermute | solution.py:173
  73.4 7.7 %copy-start.13 = (bf16[32,4608]{1,0:T(8,128)(2,1)S(1)}, bf16[32,4608]{1,0:T(8,128)(2,1)}, u32[]{:S(2)}) copy-start(bf16[32,4608]{1,0:T(8,128)(2,1)} %copy-done.12) | copy-start | bytes 884740
  81.0 7.5 %collective-permute-start.15 = (bf16[32,4608]{1,0:T(8,128)(2,1)}, bf16[32,4608]{1,0:T(8,128)(2,1)S(1)}, u32[]{:S(2)}, u32[]{:S(2)}) collective-permute-start(bf16[32,4608]{1,0:T(8,128)(2,1)} %collective-permute-done.11.refs_1_), channel_id=1, source_target_pairs={{0,1},{1,0},{2,3},{3,2},{4,5},{5,4},{6,7},{7,6},{8,9},{9,8},{10,11... | collective-permute-start | bytes 884744 | tf_op jit(solution)/shard_map/ppermute | solution.py:173
  81.1 8.0 %collective-permute-start.16 = (bf16[32,4608]{1,0:T(8,128)(2,1)S(1)}, bf16[32,4608]{1,0:T(8,128)(2,1)S(1)}, u32[]{:S(2)}, u32[]{:S(2)}) collective-permute-start(bf16[32,4608]{1,0:T(8,128)(2,1)S(1)} %copy-done.13), channel_id=1, source_target_pairs={{0,1},{1,0},{2,3},{3,2},{4,5},{5,4},{6,7},{7,6},{8,9},{9,8},{10,11... | collective-permute-start | bytes 884744 | tf_op jit(solution)/shard_map/ppermute | solution.py:173
  81.6 7.7 %collective-permute-start.21 = (bf16[32,4608]{1,0:T(8,128)(2,1)}, bf16[32,4608]{1,0:T(8,128)(2,1)}, u32[]{:S(2)}, u32[]{:S(2)}) collective-permute-start(bf16[32,4608]{1,0:T(8,128)(2,1)} %collective-permute-done.19.refs_1_), channel_id=1, source_target_pairs={{0,16},{1,9},{2,18},{3,11},{4,20},{5,13},{6,22},{7,15},{8,24},{9,1... | collective-permute-start | bytes 884744 | tf_op jit(solution)/shard_map/ppermute | solution.py:173
  82.8 6.9 %collective-permute-start.9 = (bf16[32,4608]{1,0:T(8,128)(2,1)}, bf16[32,4608]{1,0:T(8,128)(2,1)S(1)}, u32[]{:S(2)}, u32[]{:S(2)}) collective-permute-start(bf16[32,4608]{1,0:T(8,128)(2,1)} %collective-permute-done.5.refs_3_), channel_id=1, source_target_pairs={{0,1},{1,0},{2,3},{3,2},{4,5},{5,4},{6,7},{7,6},{8,9},{9,8},{10,11... | collective-permute-start | bytes 884744 | tf_op jit(solution)/shard_map/ppermute | solution.py:173
  88.6 3.3 %copy-start.17 = (bf16[32,4608]{1,0:T(8,128)(2,1)}, bf16[32,4608]{1,0:T(8,128)(2,1)S(1)}, u32[]{:S(2)}) copy-start(bf16[32,4608]{1,0:T(8,128)(2,1)S(1)} %collective-permute-done.15.refs_5_) | copy-start | bytes 884740
  88.6 72.4 %collective-permute-start.22 = (bf16[32,4608]{1,0:T(8,128)(2,1)S(1)}, bf16[32,4608]{1,0:T(8,128)(2,1)}, u32[]{:S(2)}, u32[]{:S(2)}) collective-permute-start(bf16[32,4608]{1,0:T(8,128)(2,1)S(1)} %collective-permute-done.18.refs_0_), channel_id=1, source_target_pairs={{0,1},{1,0},{2,3},{3,2},{4,5},{5,4},{6,7},{7,6},{8,9},{9,8},{10,11... | collective-permute-start | bytes 884744 | tf_op jit(solution)/shard_map/ppermute | solution.py:173
  89.1 2.8 %copy-start.19 = (bf16[32,4608]{1,0:T(8,128)(2,1)}, bf16[32,4608]{1,0:T(8,128)(2,1)S(1)}, u32[]{:S(2)}) copy-start(bf16[32,4608]{1,0:T(8,128)(2,1)S(1)} %collective-permute-done.16.refs_6_) | copy-start | bytes 884740
  89.1 71.9 %collective-permute-start.23 = (bf16[32,4608]{1,0:T(8,128)(2,1)}, bf16[32,4608]{1,0:T(8,128)(2,1)}, u32[]{:S(2)}, u32[]{:S(2)}) collective-permute-start(bf16[32,4608]{1,0:T(8,128)(2,1)} %collective-permute-done.19.refs_1_), channel_id=1, source_target_pairs={{0,1},{1,0},{2,3},{3,2},{4,5},{5,4},{6,7},{7,6},{8,9},{9,8},{10,11... | collective-permute-start | bytes 884744 | tf_op jit(solution)/shard_map/ppermute | solution.py:173
  89.2 71.8 %collective-permute-start.24 = (bf16[32,4608]{1,0:T(8,128)(2,1)}, bf16[32,4608]{1,0:T(8,128)(2,1)}, u32[]{:S(2)}, u32[]{:S(2)}) collective-permute-start(bf16[32,4608]{1,0:T(8,128)(2,1)} %collective-permute-done.20.refs_2_), channel_id=1, source_target_pairs={{0,1},{1,0},{2,3},{3,2},{4,5},{5,4},{6,7},{7,6},{8,9},{9,8},{10,11... | collective-permute-start | bytes 884744 | tf_op jit(solution)/shard_map/ppermute | solution.py:173
  89.6 68.4 %collective-permute-start.17 = (bf16[32,4608]{1,0:T(8,128)(2,1)}, bf16[32,4608]{1,0:T(8,128)(2,1)}, u32[]{:S(2)}, u32[]{:S(2)}) collective-permute-start(bf16[32,4608]{1,0:T(8,128)(2,1)} %collective-permute-done.13.refs_3_), channel_id=1, source_target_pairs={{0,1},{1,0},{2,3},{3,2},{4,5},{5,4},{6,7},{7,6},{8,9},{9,8},{10,11... | collective-permute-start | bytes 884744 | tf_op jit(solution)/shard_map/ppermute | solution.py:173
  89.7 71.3 %collective-permute-start.25 = (bf16[32,4608]{1,0:T(8,128)(2,1)}, bf16[32,4608]{1,0:T(8,128)(2,1)}, u32[]{:S(2)}, u32[]{:S(2)}) collective-permute-start(bf16[32,4608]{1,0:T(8,128)(2,1)} %collective-permute-done.21.refs_3_), channel_id=1, source_target_pairs={{0,1},{1,0},{2,3},{3,2},{4,5},{5,4},{6,7},{7,6},{8,9},{9,8},{10,11... | collective-permute-start | bytes 884744 | tf_op jit(solution)/shard_map/ppermute | solution.py:173
  151.7 2.4 %copy-start.5 = (bf16[32,4608]{1,0:T(8,128)(2,1)S(1)}, bf16[32,4608]{1,0:T(8,128)(2,1)}, u32[]{:S(2)}) copy-start(bf16[32,4608]{1,0:T(8,128)(2,1)} %copy-done.4) | copy-start | bytes 884740
  151.7 2.4 %copy-start.7 = (bf16[32,4608]{1,0:T(8,128)(2,1)S(1)}, bf16[32,4608]{1,0:T(8,128)(2,1)}, u32[]{:S(2)}) copy-start(bf16[32,4608]{1,0:T(8,128)(2,1)} %copy-done.6) | copy-start | bytes 884740
  151.7 6.3 %copy-start.3 = (bf16[32,4608]{1,0:T(8,128)(2,1)S(1)}, bf16[32,4608]{1,0:T(8,128)(2,1)}, u32[]{:S(2)}) copy-start(bf16[32,4608]{1,0:T(8,128)(2,1)} %copy-done.2) | copy-start | bytes 884740
  151.8 6.3 %copy-start.14 = (bf16[32,4608]{1,0:T(8,128)(2,1)S(1)}, bf16[32,4608]{1,0:T(8,128)(2,1)}, u32[]{:S(2)}) copy-start(bf16[32,4608]{1,0:T(8,128)(2,1)} %copy-done.12) | copy-start | bytes 884740
  151.8 6.3 %copy-start.16 = (bf16[32,4608]{1,0:T(8,128)(2,1)S(1)}, bf16[32,4608]{1,0:T(8,128)(2,1)}, u32[]{:S(2)}) copy-start(bf16[32,4608]{1,0:T(8,128)(2,1)} %copy-done.15) | copy-start | bytes 884740
  151.8 6.3 %copy-start.18 = (bf16[32,4608]{1,0:T(8,128)(2,1)S(1)}, bf16[32,4608]{1,0:T(8,128)(2,1)}, u32[]{:S(2)}) copy-start(bf16[32,4608]{1,0:T(8,128)(2,1)} %copy-done.17) | copy-start | bytes 884740
  151.8 6.3 %copy-start.20 = (bf16[32,4608]{1,0:T(8,128)(2,1)S(1)}, bf16[32,4608]{1,0:T(8,128)(2,1)}, u32[]{:S(2)}) copy-start(bf16[32,4608]{1,0:T(8,128)(2,1)} %copy-done.19) | copy-start | bytes 884740
  158.1 6.2 %copy-start.1 = (bf16[3,16,9216]{2,1,0:T(8,128)(2,1)S(1)}, bf16[3,16,9216]{2,1,0:T(8,128)(2,1)}, u32[]{:S(2)}) copy-start(bf16[3,16,9216]{2,1,0:T(8,128)(2,1)} %slice.31.x_ref) | copy-start | bytes 2654212
  158.1 6.2 %copy-start.23 = (bf16[256,256]{1,0:T(8,128)(2,1)S(1)}, bf16[256,256]{1,0:T(8,128)(2,1)}, u32[]{:S(2)}) copy-start(bf16[256,256]{1,0:T(8,128)(2,1)} %compare_convert_fusion.mask_ref) | copy-start | bytes 393220
  164.3 16.0 %copy-start = (bf16[3,16,9216]{2,1,0:T(8,128)(2,1)S(1)}, bf16[3,16,9216]{2,1,0:T(8,128)(2,1)}, u32[]{:S(2)}) copy-start(bf16[3,16,9216]{2,1,0:T(8,128)(2,1)} %slice.29.x_ref) | copy-start | bytes 2654212
  175.5 30.8 %collective-permute-start.46 = (bf16[3,32,256]{2,1,0:T(8,128)(2,1)S(1)}, bf16[3,32,256]{2,1,0:T(8,128)(2,1)S(1)}, u32[]{:S(2)}, u32[]{:S(2)}) collective-permute-start(bf16[3,32,256]{2,1,0:T(8,128)(2,1)S(1)} %get-tuple-element.68), channel_id=1, source_target_pairs={{0,7},{1,6},{2,1},{3,0},{4,3},{5,2},{6,5},{7,4},{8,15},{9,14},{10,... | collective-permute-start | bytes 147464 | tf_op jit(solution)/shard_map/ppermute | solution.py:173
  175.5 31.4 %collective-permute-start.45 = (bf16[3,32,256]{2,1,0:T(8,128)(2,1)S(1)}, bf16[3,32,256]{2,1,0:T(8,128)(2,1)S(1)}, u32[]{:S(2)}, u32[]{:S(2)}) collective-permute-start(bf16[3,32,256]{2,1,0:T(8,128)(2,1)S(1)} %get-tuple-element.67), channel_id=1, source_target_pairs={{0,5},{1,4},{2,7},{3,6},{4,1},{5,0},{6,3},{7,2},{8,13},{9,12},{10,... | collective-permute-start | bytes 147464 | tf_op jit(solution)/shard_map/ppermute | solution.py:173
  175.6 27.0 %collective-permute-start.42 = (bf16[3,32,256]{2,1,0:T(8,128)(2,1)S(1)}, bf16[3,32,256]{2,1,0:T(8,128)(2,1)S(1)}, u32[]{:S(2)}, u32[]{:S(2)}) collective-permute-start(bf16[3,32,256]{2,1,0:T(8,128)(2,1)S(1)} %get-tuple-element.64), channel_id=1, source_target_pairs={{0,6},{1,7},{2,0},{3,1},{4,2},{5,3},{6,4},{7,5},{8,14},{9,15},{10,... | collective-permute-start | bytes 147464 | tf_op jit(solution)/shard_map/ppermute | solution.py:173
  179.6 24.7 %collective-permute-start.41 = (bf16[3,32,256]{2,1,0:T(8,128)(2,1)S(1)}, bf16[3,32,256]{2,1,0:T(8,128)(2,1)S(1)}, u32[]{:S(2)}, u32[]{:S(2)}) collective-permute-start(bf16[3,32,256]{2,1,0:T(8,128)(2,1)S(1)} %get-tuple-element.63), channel_id=1, source_target_pairs={{0,4},{1,5},{2,6},{3,7},{4,0},{5,1},{6,2},{7,3},{8,12},{9,13},{10,... | collective-permute-start | bytes 147464 | tf_op jit(solution)/shard_map/ppermute | solution.py:173
  179.6 26.0 %collective-permute-start.40 = (bf16[3,32,256]{2,1,0:T(8,128)(2,1)S(1)}, bf16[3,32,256]{2,1,0:T(8,128)(2,1)S(1)}, u32[]{:S(2)}, u32[]{:S(2)}) collective-permute-start(bf16[3,32,256]{2,1,0:T(8,128)(2,1)S(1)} %get-tuple-element.62), channel_id=1, source_target_pairs={{0,2},{1,3},{2,4},{3,5},{4,6},{5,7},{6,0},{7,1},{8,10},{9,11},{10,... | collective-permute-start | bytes 147464 | tf_op jit(solution)/shard_map/ppermute | solution.py:173
  202.6 5.9 %collective-permute-start.44 = (bf16[3,32,256]{2,1,0:T(8,128)(2,1)S(1)}, bf16[3,32,256]{2,1,0:T(8,128)(2,1)S(1)}, u32[]{:S(2)}, u32[]{:S(2)}) collective-permute-start(bf16[3,32,256]{2,1,0:T(8,128)(2,1)S(1)} %get-tuple-element.66), channel_id=1, source_target_pairs={{0,3},{1,2},{2,5},{3,4},{4,7},{5,6},{6,1},{7,0},{8,11},{9,10},{10,... | collective-permute-start | bytes 147464 | tf_op jit(solution)/shard_map/ppermute | solution.py:173
  204.4 4.2 %collective-permute-start.43 = (bf16[3,32,256]{2,1,0:T(8,128)(2,1)S(1)}, bf16[3,32,256]{2,1,0:T(8,128)(2,1)S(1)}, u32[]{:S(2)}, u32[]{:S(2)}) collective-permute-start(bf16[3,32,256]{2,1,0:T(8,128)(2,1)S(1)} %get-tuple-element.65), channel_id=1, source_target_pairs={{0,1},{1,0},{2,3},{3,2},{4,5},{5,4},{6,7},{7,6},{8,9},{9,8},{10,11... | collective-permute-start | bytes 147464 | tf_op jit(solution)/shard_map/ppermute | solution.py:173
  205.6 5.3 %collective-permute-start.39 = (bf16[3,32,256]{2,1,0:T(8,128)(2,1)S(1)}, bf16[3,32,256]{2,1,0:T(8,128)(2,1)S(1)}, u32[]{:S(2)}, u32[]{:S(2)}) collective-permute-start(bf16[3,32,256]{2,1,0:T(8,128)(2,1)S(1)} %get-tuple-element.60), channel_id=1, source_target_pairs={{0,7},{1,6},{2,1},{3,0},{4,3},{5,2},{6,5},{7,4},{8,15},{9,14},{10,... | collective-permute-start | bytes 147464 | tf_op jit(solution)/shard_map/ppermute | solution.py:173
  206.3 5.3 %collective-permute-start.38 = (bf16[3,32,256]{2,1,0:T(8,128)(2,1)S(1)}, bf16[3,32,256]{2,1,0:T(8,128)(2,1)S(1)}, u32[]{:S(2)}, u32[]{:S(2)}) collective-permute-start(bf16[3,32,256]{2,1,0:T(8,128)(2,1)S(1)} %get-tuple-element.59), channel_id=1, source_target_pairs={{0,5},{1,4},{2,7},{3,6},{4,1},{5,0},{6,3},{7,2},{8,13},{9,12},{10,... | collective-permute-start | bytes 147464 | tf_op jit(solution)/shard_map/ppermute | solution.py:173
  207.0 5.8 %collective-permute-start.37 = (bf16[3,32,256]{2,1,0:T(8,128)(2,1)S(1)}, bf16[3,32,256]{2,1,0:T(8,128)(2,1)S(1)}, u32[]{:S(2)}, u32[]{:S(2)}) collective-permute-start(bf16[3,32,256]{2,1,0:T(8,128)(2,1)S(1)} %get-tuple-element.58), channel_id=1, source_target_pairs={{0,3},{1,2},{2,5},{3,4},{4,7},{5,6},{6,1},{7,0},{8,11},{9,10},{10,... | collective-permute-start | bytes 147464 | tf_op jit(solution)/shard_map/ppermute | solution.py:173
  208.5 8.3 %collective-permute-start.36 = (bf16[3,32,256]{2,1,0:T(8,128)(2,1)S(1)}, bf16[3,32,256]{2,1,0:T(8,128)(2,1)S(1)}, u32[]{:S(2)}, u32[]{:S(2)}) collective-permute-start(bf16[3,32,256]{2,1,0:T(8,128)(2,1)S(1)} %get-tuple-element.57), channel_id=1, source_target_pairs={{0,1},{1,0},{2,3},{3,2},{4,5},{5,4},{6,7},{7,6},{8,9},{9,8},{10,11... | collective-permute-start | bytes 147464 | tf_op jit(solution)/shard_map/ppermute | solution.py:173
  208.5 8.3 %collective-permute-start.35 = (bf16[3,32,256]{2,1,0:T(8,128)(2,1)S(1)}, bf16[3,32,256]{2,1,0:T(8,128)(2,1)S(1)}, u32[]{:S(2)}, u32[]{:S(2)}) collective-permute-start(bf16[3,32,256]{2,1,0:T(8,128)(2,1)S(1)} %get-tuple-element.56), channel_id=1, source_target_pairs={{0,6},{1,7},{2,0},{3,1},{4,2},{5,3},{6,4},{7,5},{8,14},{9,15},{10,... | collective-permute-start | bytes 147464 | tf_op jit(solution)/shard_map/ppermute | solution.py:173
  210.9 6.0 %collective-permute-start.34 = (bf16[3,32,256]{2,1,0:T(8,128)(2,1)S(1)}, bf16[3,32,256]{2,1,0:T(8,128)(2,1)S(1)}, u32[]{:S(2)}, u32[]{:S(2)}) collective-permute-start(bf16[3,32,256]{2,1,0:T(8,128)(2,1)S(1)} %get-tuple-element.55), channel_id=1, source_target_pairs={{0,4},{1,5},{2,6},{3,7},{4,0},{5,1},{6,2},{7,3},{8,12},{9,13},{10,... | collective-permute-start | bytes 147464 | tf_op jit(solution)/shard_map/ppermute | solution.py:173
  211.6 6.1 %collective-permute-start.33 = (bf16[3,32,256]{2,1,0:T(8,128)(2,1)S(1)}, bf16[3,32,256]{2,1,0:T(8,128)(2,1)S(1)}, u32[]{:S(2)}, u32[]{:S(2)}) collective-permute-start(bf16[3,32,256]{2,1,0:T(8,128)(2,1)S(1)} %get-tuple-element.54), channel_id=1, source_target_pairs={{0,2},{1,3},{2,4},{3,5},{4,6},{5,7},{6,0},{7,1},{8,10},{9,11},{10,... | collective-permute-start | bytes 147464 | tf_op jit(solution)/shard_map/ppermute | solution.py:173
  212.8 8.1 %collective-permute-start.32 = (bf16[3,32,256]{2,1,0:T(8,128)(2,1)S(1)}, bf16[3,32,256]{2,1,0:T(8,128)(2,1)S(1)}, u32[]{:S(2)}, u32[]{:S(2)}) collective-permute-start(bf16[3,32,256]{2,1,0:T(8,128)(2,1)S(1)} %get-tuple-element.52), channel_id=1, source_target_pairs={{0,7},{1,6},{2,1},{3,0},{4,3},{5,2},{6,5},{7,4},{8,15},{9,14},{10,... | collective-permute-start | bytes 147464 | tf_op jit(solution)/shard_map/ppermute | solution.py:173
  216.8 5.0 %collective-permute-start.31 = (bf16[3,32,256]{2,1,0:T(8,128)(2,1)S(1)}, bf16[3,32,256]{2,1,0:T(8,128)(2,1)S(1)}, u32[]{:S(2)}, u32[]{:S(2)}) collective-permute-start(bf16[3,32,256]{2,1,0:T(8,128)(2,1)S(1)} %get-tuple-element.51), channel_id=1, source_target_pairs={{0,5},{1,4},{2,7},{3,6},{4,1},{5,0},{6,3},{7,2},{8,13},{9,12},{10,... | collective-permute-start | bytes 147464 | tf_op jit(solution)/shard_map/ppermute | solution.py:173
  216.9 5.4 %collective-permute-start.30 = (bf16[3,32,256]{2,1,0:T(8,128)(2,1)S(1)}, bf16[3,32,256]{2,1,0:T(8,128)(2,1)S(1)}, u32[]{:S(2)}, u32[]{:S(2)}) collective-permute-start(bf16[3,32,256]{2,1,0:T(8,128)(2,1)S(1)} %get-tuple-element.50), channel_id=1, source_target_pairs={{0,3},{1,2},{2,5},{3,4},{4,7},{5,6},{6,1},{7,0},{8,11},{9,10},{10,... | collective-permute-start | bytes 147464 | tf_op jit(solution)/shard_map/ppermute | solution.py:173
  216.9 5.4 %collective-permute-start.29 = (bf16[3,32,256]{2,1,0:T(8,128)(2,1)S(1)}, bf16[3,32,256]{2,1,0:T(8,128)(2,1)S(1)}, u32[]{:S(2)}, u32[]{:S(2)}) collective-permute-start(bf16[3,32,256]{2,1,0:T(8,128)(2,1)S(1)} %get-tuple-element.49), channel_id=1, source_target_pairs={{0,1},{1,0},{2,3},{3,2},{4,5},{5,4},{6,7},{7,6},{8,9},{9,8},{10,11... | collective-permute-start | bytes 147464 | tf_op jit(solution)/shard_map/ppermute | solution.py:173
  217.7 5.6 %collective-permute-start.28 = (bf16[3,32,256]{2,1,0:T(8,128)(2,1)S(1)}, bf16[3,32,256]{2,1,0:T(8,128)(2,1)S(1)}, u32[]{:S(2)}, u32[]{:S(2)}) collective-permute-start(bf16[3,32,256]{2,1,0:T(8,128)(2,1)S(1)} %get-tuple-element.48), channel_id=1, source_target_pairs={{0,6},{1,7},{2,0},{3,1},{4,2},{5,3},{6,4},{7,5},{8,14},{9,15},{10,... | collective-permute-start | bytes 147464 | tf_op jit(solution)/shard_map/ppermute | solution.py:173
  220.9 5.1 %collective-permute-start.27 = (bf16[3,32,256]{2,1,0:T(8,128)(2,1)S(1)}, bf16[3,32,256]{2,1,0:T(8,128)(2,1)S(1)}, u32[]{:S(2)}, u32[]{:S(2)}) collective-permute-start(bf16[3,32,256]{2,1,0:T(8,128)(2,1)S(1)} %get-tuple-element.47), channel_id=1, source_target_pairs={{0,4},{1,5},{2,6},{3,7},{4,0},{5,1},{6,2},{7,3},{8,12},{9,13},{10,... | collective-permute-start | bytes 147464 | tf_op jit(solution)/shard_map/ppermute | solution.py:173
  221.8 5.9 %collective-permute-start.26 = (bf16[3,32,256]{2,1,0:T(8,128)(2,1)S(1)}, bf16[3,32,256]{2,1,0:T(8,128)(2,1)S(1)}, u32[]{:S(2)}, u32[]{:S(2)}) collective-permute-start(bf16[3,32,256]{2,1,0:T(8,128)(2,1)S(1)} %get-tuple-element.46), channel_id=1, source_target_pairs={{0,2},{1,3},{2,4},{3,5},{4,6},{5,7},{6,0},{7,1},{8,10},{9,11},{10,... | collective-permute-start | bytes 147464 | tf_op jit(solution)/shard_map/ppermute | solution.py:173
  (7 other events, 11.4 us)

commit v2 on v1

v2 whole, which is shorter than its diff:
```python
import functools
import math

import jax
import jax.numpy as jnp
from jax import lax
from jax.experimental import pallas as pl
from jax.experimental.pallas import tpu as pltpu
from jax.sharding import PartitionSpec as P

KY = 96
BANDS = 16
LINE = KY * BANDS
GROUPS = 3
F32 = jnp.float32
BF16 = jnp.bfloat16


def contract(a, b, dim_a, dim_b):
    return lax.dot_general(a, b, (((dim_a,), (dim_b,)), ((), ())), preferred_element_type=F32)


def cut_kernel(block, scalars, env_ref, coupling_ref, *refs):
    pieces, (window, give, sems) = refs[:-3], refs[-3:]
    n_z = len(pieces) + 1
    core, pb, z = scalars[2], scalars[3], scalars[4]

    def lanes(index):
        return pl.ds(pl.multiple_of(lax.rem(index + 2 * n_z, 2 * n_z) * block, 128), block)

    jobs = []
    for e in range(1, n_z):
        to = lax.rem(z - e + n_z, n_z)
        jobs.append((env_ref.at[:, lanes(2 * to - 1 + pb)], pieces[e - 1]))
    for w in range(4):
        jobs.append((env_ref.at[:, lanes(2 * z - 1 + w)], window.at[:, w * block : (w + 1) * block]))
    jobs.append((coupling_ref.at[1 - core], give))
    copies = [pltpu.make_async_copy(src, dst, sems.at[i]) for i, (src, dst) in enumerate(jobs)]
    for copy in copies:
        copy.start()
    for copy in copies:
        copy.wait()


def cut(scalars, envelopes, coupling, n_z, block):
    rows = envelopes.shape[0]
    shape = functools.partial(jax.ShapeDtypeStruct, dtype=BF16)
    outs = [shape((rows, block))] * (n_z - 1) + [shape((rows, 4 * block)), shape(coupling.shape[1:])]
    *pieces, window, give = pl.pallas_call(
        functools.partial(cut_kernel, block),
        in_specs=[pl.BlockSpec(memory_space=pltpu.SMEM)] + [pl.BlockSpec(memory_space=pl.ANY)] * 2,
        out_specs=[pl.BlockSpec(memory_space=pl.ANY)] * len(outs),
        out_shape=outs,
        scratch_shapes=[pltpu.SemaphoreType.DMA((n_z + 4,))],
        name="cut",
    )(scalars, envelopes, coupling)
    return pieces, window, give


def prep_kernel(pieces, block, lines, scalars, *refs):
    ins, (keep_ref, give_ref, window, sems) = refs[:pieces], refs[pieces:]
    core, pb = scalars[2], scalars[3]
    copies = []
    for index, src in enumerate(ins):
        offset = 0
        if pieces > 1:
            rel = (0, 1 + core, 2 - core, 3)[index]
            offset = pl.multiple_of((pb ^ rel) * block, 128)
        copy = pltpu.make_async_copy(src, window.at[:, pl.ds(offset, src.shape[1])], sems.at[index])
        copy.start()
        copies.append(copy)
    for copy in copies:
        copy.wait()
    for line in range(lines):
        to = slice(line * LINE, (line + 1) * LINE)
        own = window[:, (lines // 2 + line) * LINE : (lines // 2 + line + 1) * LINE]
        for out_ref, q in ((keep_ref, core), (give_ref, 1 - core)):
            out_ref[0, :, to] = own
            start_line, roll = scalars[5 + 2 * q], scalars[6 + 2 * q]
            lane = pl.multiple_of((start_line + line) * LINE, 128)
            shifted = window[:, pl.ds(lane, LINE)].astype(F32)
            out_ref[1, :, to] = pltpu.roll(shifted, roll, 1).astype(BF16)


def prepare(scalars, ins, block, lines):
    rows = ins[0].shape[0]
    pieces = len(ins)
    out = jax.ShapeDtypeStruct((2, rows, lines * LINE), BF16)
    return pl.pallas_call(
        functools.partial(prep_kernel, pieces, block, lines),
        in_specs=[pl.BlockSpec(memory_space=pltpu.SMEM)] + [pl.BlockSpec(memory_space=pl.ANY)] * pieces,
        out_specs=[pl.BlockSpec(memory_space=pltpu.VMEM)] * 2,
        out_shape=[out, out],
        scratch_shapes=[
            pltpu.VMEM((rows, 2 * lines * LINE), BF16),
            pltpu.SemaphoreType.DMA((pieces,)),
        ],
        compiler_params=pltpu.CompilerParams(vmem_limit_bytes=24 << 20),
        name="prepare",
    )(scalars, *ins)


def main_kernel(first, branches, factor, scalars, x_ref, mask_ref, *refs):
    sources = len(refs) // 2
    amps, (mine_ref, *sends, total) = refs[:sources], refs[sources:]
    step = pl.program_id(0)

    @pl.when(step == 0)
    def _():
        total[...] = jnp.zeros_like(total)

    for branch in range(branches):
        parts = []
        for tile in range(LINE // 256):
            lanes = slice(tile * 256, (tile + 1) * 256)
            matrix = jnp.concatenate([x_ref[first + branch, :, lanes]] * 16, axis=0) * mask_ref[...]
            own = jnp.concatenate([ref[0, :, lanes] for ref in amps], axis=0)
            parts.append(contract(own, matrix, 1, 0).astype(BF16))
        diff = jnp.concatenate(parts, axis=1)
        shifted = jnp.concatenate([ref[1] for ref in amps], axis=0)
        total[branch] += contract(shifted, diff, 1, 1)

    @pl.when(step == pl.num_programs(0) - 1)
    def _():
        core, z = scalars[2], scalars[4]
        rows = mine_ref.shape[1]
        states = total.shape[2]
        low = lax.broadcasted_iota(jnp.int32, (rows, states), 1) // rows % 2 == 0
        for branch in range(branches):
            for source in range(sources):
                piece = pltpu.roll(total[branch, source * rows : (source + 1) * rows] * factor, z * (2 * rows), 1)
                swapped = jnp.where(low, pltpu.roll(piece, states - rows, 1), pltpu.roll(piece, rows, 1))
                piece = jnp.where(core == 0, piece, swapped)
                if source == 0:
                    mine_ref[branch] = piece
                else:
                    sends[source - 1][branch] = piece.astype(BF16)


def products(scalars, x, mask, amps, first, branches, factor):
    sources, rows = len(amps), amps[0].shape[1]
    states = sources * rows
    lines = x.shape[2] // LINE
    piece = pl.BlockSpec((branches, rows, states), lambda i: (0, 0, 0))
    return pl.pallas_call(
        functools.partial(main_kernel, first, branches, factor),
        grid=(lines,),
        in_specs=[
            pl.BlockSpec(memory_space=pltpu.SMEM),
            pl.BlockSpec((x.shape[0], BANDS, LINE), lambda i: (0, 0, i)),
            pl.BlockSpec((256, 256), lambda i: (0, 0)),
        ]
        + [pl.BlockSpec((2, rows, LINE), lambda i: (0, 0, i))] * sources,
        out_specs=[piece] * sources,
        out_shape=[jax.ShapeDtypeStruct((branches, rows, states), F32 if i == 0 else BF16) for i in range(sources)],
        scratch_shapes=[pltpu.VMEM((branches, states, states), F32)],
        compiler_params=pltpu.CompilerParams(vmem_limit_bytes=40 << 20),
        cost_estimate=pl.CostEstimate(
            flops=4 * branches * states * states * lines * LINE,
            bytes_accessed=4 * states * lines * LINE,
            transcendentals=0,
        ),
        name="products",
    )(scalars, x, mask, *amps)


def band_kernel(scalars, coupling_ref, other_ref, x_ref):
    branches, _, count = other_ref.shape
    half = BANDS // 4
    size = min(count, 128)

    def iota(shape, dim):
        return lax.broadcasted_iota(jnp.int32, shape, dim)

    shape = (8 * BANDS, 32)
    row, col = iota(shape, 0), iota(shape, 1)
    term, v, c = row // BANDS, row % BANDS // half, row % half
    choice = jnp.where(term < 4, 4 * term + c, 16 + 4 * v + (term - 4))
    pick = (choice == col).astype(F32).astype(BF16)
    spread = []
    for by_a in (False, True):
        shape = (4 * size, size * BANDS)
        row, lane = iota(shape, 0), iota(shape, 1)
        band = lane % BANDS
        index = band // half if by_a else band % half
        hit = (row % size == lane // BANDS) & (row // size == index)
        spread.append(hit.astype(F32).astype(BF16))
    shape = (branches * BANDS, size * BANDS)
    row, lane = iota(shape, 0) % BANDS, iota(shape, 1) % BANDS
    keep_cond = (row // half == lane // half).astype(F32)
    keep_val = (row % half == lane % half).astype(F32)
    core = scalars[2]
    for mine in (True, False):
        tables = [coupling_ref[core, branch] if mine else other_ref[branch] for branch in range(branches)]
        terms = [contract(pick, table, 1, 0).astype(BF16) for table in tables]
        base = (core if mine else 1 - core) * (count * BANDS)
        for start in range(0, count, size):
            width = min(size, count - start)
            lanes = width * BANDS
            values = []
            for kind in range(2):
                rows = []
                for term in terms:
                    slabs = []
                    for index in range(4):
                        at = (4 * kind + index) * BANDS
                        slab = term[at : at + BANDS, start : start + width]
                        if width < size:
                            slab = jnp.concatenate([slab, jnp.zeros((BANDS, size - width), BF16)], axis=1)
                        slabs.append(slab)
                    rows.append(jnp.concatenate(slabs, axis=1))
                values.append(contract(jnp.concatenate(rows, axis=0), spread[kind][:, :lanes], 1, 0))
            total = (values[0] * keep_cond[:, :lanes] - values[1] * keep_val[:, :lanes]).astype(BF16)
            at = pl.multiple_of(base + start * BANDS, 128)
            for branch in range(branches):
                x_ref[branch, :, pl.ds(at, lanes)] = total[branch * BANDS : (branch + 1) * BANDS]


def band_matrices(scalars, coupling, other):
    branches, _, count = other.shape
    return pl.pallas_call(
        band_kernel,
        in_specs=[pl.BlockSpec(memory_space=pltpu.SMEM)] + [pl.BlockSpec(memory_space=pltpu.VMEM)] * 2,
        out_specs=pl.BlockSpec(memory_space=pltpu.VMEM),
        out_shape=jax.ShapeDtypeStruct((branches, BANDS, 2 * count * BANDS), BF16),
        compiler_params=pltpu.CompilerParams(vmem_limit_bytes=40 << 20),
        cost_estimate=pl.CostEstimate(flops=10**10, bytes_accessed=10**6, transcendentals=0),
        name="band_matrices",
    )(scalars, coupling, other)


def shards(envelopes, coupling, kq_map):
    n_pb, n_ka = lax.axis_size("pb"), lax.axis_size("ka")
    assert n_pb == 4 and n_ka % 2 == 0 and coupling.shape[0] == 2
    n_z = n_ka // 2
    rows, width = envelopes.shape
    block = width // n_ka
    block_lines = block // LINE
    lines = 2 * block_lines
    pb, ka = lax.axis_index("pb"), lax.axis_index("ka")
    z, core = ka // 2, ka % 2

    def permute(x, to):
        pairs = []
        for p in range(n_pb):
            for k in range(n_ka):
                tp, tz, tc = to(p, k // 2, k % 2)
                pairs.append((p * n_ka + k, tp * n_ka + (tz % n_z) * 2 + tc))
        return lax.ppermute(x, ("pb", "ka"), pairs)

    def sibling(x):
        return permute(x, lambda p, zz, c: (p, zz, 1 - c))

    origin = kq_map[:, 0]
    lines_all = width // LINE
    start_line = (origin // KY - ka * block_lines + block_lines + lines_all) % lines_all
    roll = (LINE - (origin % KY) * BANDS) % LINE
    turns = jnp.stack([start_line, roll], axis=1).reshape(-1)
    scalars = jnp.concatenate([jnp.stack([ka, ka, core, pb, z]), turns]).astype(jnp.int32)

    pieces, window, give = cut(scalars, envelopes, coupling, n_z, block)
    arrived = []
    for e in range(1, n_z):
        arrived.append(permute(pieces[e - 1], lambda p, zz, c: (p, zz - e, c)))
    x = band_matrices(scalars, coupling, sibling(give))

    amps = []
    keep, pass_on = prepare(scalars, [window], block, lines)
    amps += [keep, sibling(pass_on)]
    for piece in arrived:
        one = permute(piece, lambda p, zz, c: (p ^ (1 + c), zz, c))
        two = permute(piece, lambda p, zz, c: (p ^ (2 - c), zz, c))
        three = permute(one, lambda p, zz, c: (p ^ (2 - c), zz, c))
        keep, pass_on = prepare(scalars, [piece, one, two, three], block, lines)
        amps += [keep, sibling(pass_on)]

    index = jnp.arange(256, dtype=jnp.int32) // BANDS
    mask = (index[:, None] == index[None, :]).astype(BF16)
    factor = 1.0 / math.sqrt(float(width))
    branches = coupling.shape[1]
    results = []
    for group in range(GROUPS):
        lo, hi = group * branches // GROUPS, (group + 1) * branches // GROUPS
        mine, *sends = products(scalars, x, mask, amps, lo, hi - lo, factor)
        same, cross = mine, 0.0
        for number, piece in enumerate(sends, 1):
            e, flip = number // 2, number % 2
            got = permute(piece, lambda p, zz, c: (p, zz + e, c ^ flip)).astype(F32)
            if flip:
                cross = cross + got
            else:
                same = same + got
        results.append(
            jnp.where(core == 0, jnp.stack([same, cross]), jnp.stack([cross, same]))
        )
    return jnp.concatenate(results, axis=1)


def solution(mesh):
    return jax.shard_map(
        shards,
        mesh=mesh,
        in_specs=(P("ka", None), P("pb", None, None, "ka"), P("pb", "ka")),
        out_specs=P("pb", None, "ka", None),
        check_vma=False,
    )
```

time: 230 us -> 214 us (0.930)
  local copies, waits for them, and re-layouts: 98.3 us -> 4.17 us
  Pallas kernels: 44.8 us -> 125 us
  waiting for transfers between devices: 26.6 us -> 40 us
  other arithmetic: 10.6 us -> 1.95 us
  between operations: 4.42 us -> 0.37 us
    pallas_call x3 -> x5, Pallas kernels: 33.4 us -> 115 us  [the longest x1 71.2 us: cut(): pl.pallas_call(functools.partial(cut_kernel, block), in_specs=[pl.BlockSp...]
    slice x8 -> x0, local copies, waits for them, and re-layouts: 62.5 us -> none  [the longest x7 61.5 us: shards(): x[lo:hi]]
    mul x9 -> x0, local copies, waits for them, and re-layouts: 28.8 us -> none  [the longest x5 15.5 us: band_matrices(): val = val[:, :, None, :, None] * eye[None, None, :, None, :, None]]
    ppermute x47 -> x38, waiting for transfers between devices: 26.6 us -> 40 us  [permute(): return lax.ppermute(x, ('pb', 'ka'), pairs)]
    transpose x1 -> x0, other arithmetic: 5.72 us -> none  [band_matrices(): return jnp.swapaxes(x, 2, 3).reshape(branches, 16, count * 16)]
    ppermute x47 -> x38, starting transfers between devices: 44 us -> 42.5 us  [permute(): return lax.ppermute(x, ('pb', 'ka'), pairs)]
  transfers between devices with their start and end apart: 47 -> 38, of which waited for: 10 -> 12; matrix products, arithmetic and copies ran while one was open for 45% -> 0% of each run, Pallas kernels for 13% -> 19%
where the time goes in v2:
time: 214 us
  Pallas kernels  125 us (58%)
  starting transfers between devices  42.5 us (20%)
  waiting for transfers between devices  40 us (19%)
  local copies, waits for them, and re-layouts  4.17 us (2%)
    pallas_call x1, Pallas kernels, cut(): pl.pallas_call(functools.partial(cut_kernel, block), in_specs=[pl.BlockSp...  71.2 us
    ppermute x38, starting transfers between devices, permute(): return lax.ppermute(x, ('pb', 'ka'), pairs)  42.5 us
    ppermute x38, waiting for transfers between devices, permute(): return lax.ppermute(x, ('pb', 'ka'), pairs)  40 us
    pallas_call x3, Pallas kernels, products(): pl.pallas_call(functools.partial(main_kernel, first, branches, factor), g...  39.1 us
    pallas_call x4, Pallas kernels, prepare(): pl.pallas_call(functools.partial(prep_kernel, pieces, block, lines), in_s...  10 us
    pallas_call x1, Pallas kernels, band_matrices(): pl.pallas_call(band_kernel, in_specs=[pl.BlockSpec(memory_space=pltpu.SME...  4.29 us
  transfers between devices with their start and end apart: 38, of which 12 were waited for; matrix products, arithmetic and copies ran while one was open for 0% of the time, Pallas kernels for 19%

profile of v2, /device:TPU:0, one launch (start us, length us, event | category | flops | bytes accessed | tf_op | source)
XLA Modules:
  0.0 213.6 jit_solution(14501983048330690529)
XLA Ops:
  0.0 0.7 and_select_fusion.3
  0.7 0.1 pad_add_fusion
  0.8 0.1 reshape.29
  0.9 0.7 concatenate.6.scalars
  1.6 71.2 %cut.1 = (bf16[32,4608]{1,0:T(8,128)(2,1)}, bf16[32,4608]{1,0:T(8,128)(2,1)}, bf16[32,4608]{1,0:T(8,128)(2,1)}, bf16[32,18432]{1,0:T(8,128)(2,1)}, bf16[9,32,288]{2,1,0:T(8,128)(2,1)}) custom-call(s32[9]{0:T(128)} %concatenate.6.scalars, bf16[32,36864]{1,0:T(8,128)(2,1)} %env_ref.1, bf16[2,9,32,288]{3,2,1,0:T(8,128)(2,1)} %coupling_ref.3), custom_call_target="tpu_custom_call" | custom-call | tf_op jit(solution)/shard_map/cut/pallas_call | solution.py:49
  72.8 4.1 %collective-permute-start.7 = (bf16[32,4608]{1,0:T(8,128)(2,1)}, bf16[32,4608]{1,0:T(8,128)(2,1)S(1)}, u32[]{:S(2)}, u32[]{:S(2)}) collective-permute-start(bf16[32,4608]{1,0:T(8,128)(2,1)} %get-tuple-element.49), channel_id=1, source_target_pairs={{0,4},{1,5},{2,6},{3,7},{4,0},{5,1},{6,2},{7,3},{8,12},{9,13},{10,... | collective-permute-start | bytes 884744 | tf_op jit(solution)/shard_map/ppermute | solution.py:249
  76.9 1.6 collective-permute-start.12
  78.5 2.2 %collective-permute-start.2 = (bf16[32,4608]{1,0:T(8,128)(2,1)}, bf16[32,4608]{1,0:T(8,128)(2,1)S(1)}, u32[]{:S(2)}, u32[]{:S(2)}) collective-permute-start(bf16[32,4608]{1,0:T(8,128)(2,1)} %get-tuple-element.46), channel_id=1, source_target_pairs={{0,6},{1,7},{2,0},{3,1},{4,2},{5,3},{6,4},{7,5},{8,14},{9,15},{10,... | collective-permute-start | bytes 884744 | tf_op jit(solution)/shard_map/ppermute | solution.py:249
  80.7 16.9 %collective-permute-done.7.refs_0_ = bf16[32,4608]{1,0:T(8,128)(2,1)S(1)} collective-permute-done((bf16[32,4608]{1,0:T(8,128)(2,1)}, bf16[32,4608]{1,0:T(8,128)(2,1)S(1)}, u32[]{:S(2)}, u32[]{:S(2)}) %collective-permute-start.7) | collective-permute-done | bytes 294944 | tf_op jit(solution)/shard_map/ppermute | solution.py:249
  97.6 1.8 collective-permute-start.8
  99.5 0.2 collective-permute-start.13
  99.6 1.9 collective-permute-start.9
  101.5 1.5 collective-permute-start.3
  103.0 4.5 %collective-permute-done.8.refs_1_ = bf16[32,4608]{1,0:T(8,128)(2,1)S(1)} collective-permute-done((bf16[32,4608]{1,0:T(8,128)(2,1)S(1)}, bf16[32,4608]{1,0:T(8,128)(2,1)S(1)}, u32[]{:S(2)}, u32[]{:S(2)}) %collective-permute-start.8) | collective-permute-done | bytes 294944 | tf_op jit(solution)/shard_map/ppermute | solution.py:249
  107.5 1.9 collective-permute-start.10
  109.4 0.1 collective-permute-start.14
  109.5 4.3 %collective-permute-done.13.refs_1_ = bf16[32,4608]{1,0:T(8,128)(2,1)S(1)} collective-permute-done((bf16[32,4608]{1,0:T(8,128)(2,1)S(1)}, bf16[32,4608]{1,0:T(8,128)(2,1)S(1)}, u32[]{:S(2)}, u32[]{:S(2)}) %collective-permute-start.13) | collective-permute-done | bytes 294944 | tf_op jit(solution)/shard_map/ppermute | solution.py:249
  113.8 1.9 collective-permute-start.15
  115.7 0.1 collective-permute-start.4
  115.8 4.3 %collective-permute-done.3.refs_1_ = bf16[32,4608]{1,0:T(8,128)(2,1)S(1)} collective-permute-done((bf16[32,4608]{1,0:T(8,128)(2,1)S(1)}, bf16[32,4608]{1,0:T(8,128)(2,1)S(1)}, u32[]{:S(2)}, u32[]{:S(2)}) %collective-permute-start.3) | collective-permute-done | bytes 294944 | tf_op jit(solution)/shard_map/ppermute | solution.py:249
  120.1 1.9 collective-permute-start.5
  122.1 1.3 copy-done
  123.3 2.6 %prepare.4 = (bf16[2,32,9216]{2,1,0:T(8,128)(2,1)S(1)}, bf16[2,32,9216]{2,1,0:T(8,128)(2,1)}) custom-call(s32[9]{0:T(128)S(1)} %copy-done.2, bf16[32,18432]{1,0:T(8,128)(2,1)S(1)} %copy-done), custom_call_target="tpu_custom_call" | custom-call | tf_op jit(solution)/shard_map/prepare/pallas_call | solution.py:89
  125.9 0.1 collective-permute-start.1
  126.0 2.5 %prepare.6 = (bf16[2,32,9216]{2,1,0:T(8,128)(2,1)S(1)}, bf16[2,32,9216]{2,1,0:T(8,128)(2,1)}) custom-call(s32[9]{0:T(128)S(1)} %copy-done.2, bf16[32,4608]{1,0:T(8,128)(2,1)S(1)} %collective-permute-done.7.refs_0_, bf16[32,4608]{1,0:T(8,128)(2,1)S(1)} %collective-permute-done.8.refs_1_, bf16[32,4608]{1,0:T(8,128)(2,1)S(1)} %collective-permute-done.9.refs_2_, ...), custom_call_target="tpu_custom_call" | custom-call | tf_op jit(solution)/shard_map/prepare/pallas_call | solution.py:89
  128.6 0.6 collective-permute-start
  129.1 0.1 collective-permute-start.11
  129.2 2.5 %prepare.7 = (bf16[2,32,9216]{2,1,0:T(8,128)(2,1)S(1)}, bf16[2,32,9216]{2,1,0:T(8,128)(2,1)}) custom-call(s32[9]{0:T(128)S(1)} %copy-done.2, bf16[32,4608]{1,0:T(8,128)(2,1)S(1)} %collective-permute-done.12.refs_0_, bf16[32,4608]{1,0:T(8,128)(2,1)S(1)} %collective-permute-done.13.refs_1_, bf16[32,4608]{1,0:T(8,128)(2,1)S(1)} %collective-permute-done.14.refs_2_, ...), custom_call_target="tpu_custom_call" | custom-call | tf_op jit(solution)/shard_map/prepare/pallas_call | solution.py:89
  131.7 1.1 copy-done.5
  132.8 0.4 collective-permute-start.16
  133.2 2.5 %prepare.5 = (bf16[2,32,9216]{2,1,0:T(8,128)(2,1)S(1)}, bf16[2,32,9216]{2,1,0:T(8,128)(2,1)}) custom-call(s32[9]{0:T(128)S(1)} %copy-done.2, bf16[32,4608]{1,0:T(8,128)(2,1)S(1)} %collective-permute-done.2.refs_0_, bf16[32,4608]{1,0:T(8,128)(2,1)S(1)} %collective-permute-done.3.refs_1_, bf16[32,4608]{1,0:T(8,128)(2,1)S(1)} %collective-permute-done.4.refs_2_, ...), custom_call_target="tpu_custom_call" | custom-call | tf_op jit(solution)/shard_map/prepare/pallas_call | solution.py:89
  135.8 1.0 copy-done.7
  136.8 0.1 collective-permute-start.6
  136.9 0.1 compare_convert_fusion.mask_ref
  137.0 4.3 %band_matrices.1.x_ref = bf16[9,16,9216]{2,1,0:T(8,128)(2,1)S(1)} custom-call(s32[9]{0:T(128)S(1)} %copy-done.2, bf16[2,9,32,288]{3,2,1,0:T(8,128)(2,1)S(1)} %copy-done.1, bf16[9,32,288]{2,1,0:T(8,128)(2,1)S(1)} %collective-permute-done.other_ref), custom_call_target="tpu_custom_call" | custom-call | flops 10000000000 | bytes 1000000 | tf_op jit(solution)/shard_map/band_matrices/pallas_call | solution.py:221
  141.4 13.0 %products.3 = (f32[3,32,256]{2,1,0:T(8,128)S(1)}, bf16[3,32,256]{2,1,0:T(8,128)(2,1)S(1)}, bf16[3,32,256]{2,1,0:T(8,128)(2,1)S(1)}, bf16[3,32,256]{2,1,0:T(8,128...) custom-call(s32[9]{0:T(128)S(1)} %copy-done.2, ...), custom_call_target="tpu_custom_call" | custom-call | flops 7247757312 | bytes 9437184 | tf_op jit(solution)/shard_map/products/pallas_call | solution.py:145
  154.4 0.1 collective-permute-start.17
  154.5 1.4 collective-permute-start.18
  155.9 2.8 %collective-permute-start.19 = (bf16[3,32,256]{2,1,0:T(8,128)(2,1)S(1)}, bf16[3,32,256]{2,1,0:T(8,128)(2,1)S(1)}, u32[]{:S(2)}, u32[]{:S(2)}) collective-permute-start(bf16[3,32,256]{2,1,0:T(8,128)(2,1)S(1)} %get-tuple-element.58), channel_id=1, source_target_pairs={{0,6},{1,7},{2,0},{3,1},{4,2},{5,3},{6,4},{7,5},{8,14},{9,15},{10,... | collective-permute-start | bytes 147464 | tf_op jit(solution)/shard_map/ppermute | solution.py:249
  158.7 0.3 collective-permute-start.21
  159.0 13.0 %products.4 = (f32[3,32,256]{2,1,0:T(8,128)S(1)}, bf16[3,32,256]{2,1,0:T(8,128)(2,1)S(1)}, bf16[3,32,256]{2,1,0:T(8,128)(2,1)S(1)}, bf16[3,32,256]{2,1,0:T(8,128...) custom-call(s32[9]{0:T(128)S(1)} %copy-done.2, ...), custom_call_target="tpu_custom_call" | custom-call | flops 7247757312 | bytes 9437184 | tf_op jit(solution)/shard_map/products/pallas_call | solution.py:145
  172.0 13.0 %products.5 = (f32[3,32,256]{2,1,0:T(8,128)S(1)}, bf16[3,32,256]{2,1,0:T(8,128)(2,1)S(1)}, bf16[3,32,256]{2,1,0:T(8,128)(2,1)S(1)}, bf16[3,32,256]{2,1,0:T(8,128...) custom-call(s32[9]{0:T(128)S(1)} %copy-done.2, ...), custom_call_target="tpu_custom_call" | custom-call | flops 7247757312 | bytes 9437184 | tf_op jit(solution)/shard_map/products/pallas_call | solution.py:145
  185.1 2.1 collective-permute-start.24
  187.1 2.2 %collective-permute-start.25 = (bf16[3,32,256]{2,1,0:T(8,128)(2,1)S(1)}, bf16[3,32,256]{2,1,0:T(8,128)(2,1)S(1)}, u32[]{:S(2)}, u32[]{:S(2)}) collective-permute-start(bf16[3,32,256]{2,1,0:T(8,128)(2,1)S(1)} %get-tuple-element.65), channel_id=1, source_target_pairs={{0,4},{1,5},{2,6},{3,7},{4,0},{5,1},{6,2},{7,3},{8,12},{9,13},{10,... | collective-permute-start | bytes 147464 | tf_op jit(solution)/shard_map/ppermute | solution.py:249
  189.4 0.2 collective-permute-start.26
  189.6 1.8 collective-permute-done.24
  191.4 1.6 collective-permute-done.25
  193.0 0.6 collective-permute-start.23
  193.6 2.6 %collective-permute-start.27 = (bf16[3,32,256]{2,1,0:T(8,128)(2,1)S(1)}, bf16[3,32,256]{2,1,0:T(8,128)(2,1)S(1)}, u32[]{:S(2)}, u32[]{:S(2)}) collective-permute-start(bf16[3,32,256]{2,1,0:T(8,128)(2,1)S(1)} %get-tuple-element.67), channel_id=1, source_target_pairs={{0,1},{1,0},{2,3},{3,2},{4,5},{5,4},{6,7},{7,6},{8,9},{9,8},{10,11... | collective-permute-start | bytes 147464 | tf_op jit(solution)/shard_map/ppermute | solution.py:249
  196.2 0.1 collective-permute-start.28
  196.3 0.2 collective-permute-start.29
  196.4 3.4 %collective-permute-start.30 = (bf16[3,32,256]{2,1,0:T(8,128)(2,1)S(1)}, bf16[3,32,256]{2,1,0:T(8,128)(2,1)S(1)}, u32[]{:S(2)}, u32[]{:S(2)}) collective-permute-start(bf16[3,32,256]{2,1,0:T(8,128)(2,1)S(1)} %get-tuple-element.70), channel_id=1, source_target_pairs={{0,7},{1,6},{2,1},{3,0},{4,3},{5,2},{6,5},{7,4},{8,15},{9,14},{10,... | collective-permute-start | bytes 147464 | tf_op jit(solution)/shard_map/ppermute | solution.py:249
  199.9 0.6 collective-permute-start.31
  200.5 1.6 collective-permute-start.32
  202.0 0.1 collective-permute-done.28
  202.1 2.4 %collective-permute-start.33 = (bf16[3,32,256]{2,1,0:T(8,128)(2,1)S(1)}, bf16[3,32,256]{2,1,0:T(8,128)(2,1)S(1)}, u32[]{:S(2)}, u32[]{:S(2)}) collective-permute-start(bf16[3,32,256]{2,1,0:T(8,128)(2,1)S(1)} %get-tuple-element.74), channel_id=1, source_target_pairs={{0,6},{1,7},{2,0},{3,1},{4,2},{5,3},{6,4},{7,5},{8,14},{9,15},{10,... | collective-permute-start | bytes 147464 | tf_op jit(solution)/shard_map/ppermute | solution.py:249
  204.5 0.5 collective-permute-start.35
  205.1 1.1 collective-permute-done.31
  206.2 1.4 collective-permute-done.32
  207.7 1.0 collective-permute-start.37
  208.8 1.2 collective-permute-done.35
  210.0 2.6 %collective-permute-done.36 = bf16[3,32,256]{2,1,0:T(8,128)(2,1)S(1)} collective-permute-done((bf16[3,32,256]{2,1,0:T(8,128)(2,1)S(1)}, bf16[3,32,256]{2,1,0:T(8,128)(2,1)S(1)}, u32[]{:S(2)}, u32[]{:S(2)}) %collective-permute-start.36) | collective-permute-done | bytes 49184 | tf_op jit(solution)/shard_map/ppermute | solution.py:249
  212.6 0.1 collective-permute-done.37
  212.7 0.9 pad_maximum_fusion
  (57 shorter events, 0.3 us)
Async XLA Ops:
  1.5 120.5 %copy-start.2 = (s32[9]{0:T(128)S(1)}, s32[9]{0:T(128)}, u32[]{:S(2)}) copy-start(s32[9]{0:T(128)} %concatenate.6.scalars) | copy-start | bytes 112
  72.8 24.8 %collective-permute-start.7 = (bf16[32,4608]{1,0:T(8,128)(2,1)}, bf16[32,4608]{1,0:T(8,128)(2,1)S(1)}, u32[]{:S(2)}, u32[]{:S(2)}) collective-permute-start(bf16[32,4608]{1,0:T(8,128)(2,1)} %get-tuple-element.49), channel_id=1, source_target_pairs={{0,4},{1,5},{2,6},{3,7},{4,0},{5,1},{6,2},{7,3},{8,12},{9,13},{10,... | collective-permute-start | bytes 884744 | tf_op jit(solution)/shard_map/ppermute | solution.py:249
  76.9 22.6 %collective-permute-start.12 = (bf16[32,4608]{1,0:T(8,128)(2,1)}, bf16[32,4608]{1,0:T(8,128)(2,1)S(1)}, u32[]{:S(2)}, u32[]{:S(2)}) collective-permute-start(bf16[32,4608]{1,0:T(8,128)(2,1)} %get-tuple-element.52), channel_id=1, source_target_pairs={{0,2},{1,3},{2,4},{3,5},{4,6},{5,7},{6,0},{7,1},{8,10},{9,11},{10,... | collective-permute-start | bytes 884744 | tf_op jit(solution)/shard_map/ppermute | solution.py:249
  78.5 23.1 %collective-permute-start.2 = (bf16[32,4608]{1,0:T(8,128)(2,1)}, bf16[32,4608]{1,0:T(8,128)(2,1)S(1)}, u32[]{:S(2)}, u32[]{:S(2)}) collective-permute-start(bf16[32,4608]{1,0:T(8,128)(2,1)} %get-tuple-element.46), channel_id=1, source_target_pairs={{0,6},{1,7},{2,0},{3,1},{4,2},{5,3},{6,4},{7,5},{8,14},{9,15},{10,... | collective-permute-start | bytes 884744 | tf_op jit(solution)/shard_map/ppermute | solution.py:249
  97.6 9.9 %collective-permute-start.8 = (bf16[32,4608]{1,0:T(8,128)(2,1)S(1)}, bf16[32,4608]{1,0:T(8,128)(2,1)S(1)}, u32[]{:S(2)}, u32[]{:S(2)}) collective-permute-start(bf16[32,4608]{1,0:T(8,128)(2,1)S(1)} %collective-permute-done.7.refs_0_), channel_id=1, source_target_pairs={{0,8},{1,17},{2,10},{3,19},{4,12},{5,21},{6,14},{7,23},{8,0},{9,25... | collective-permute-start | bytes 884744 | tf_op jit(solution)/shard_map/ppermute | solution.py:249
  99.5 14.4 %collective-permute-start.13 = (bf16[32,4608]{1,0:T(8,128)(2,1)S(1)}, bf16[32,4608]{1,0:T(8,128)(2,1)S(1)}, u32[]{:S(2)}, u32[]{:S(2)}) collective-permute-start(bf16[32,4608]{1,0:T(8,128)(2,1)S(1)} %collective-permute-done.12.refs_0_), channel_id=1, source_target_pairs={{0,8},{1,17},{2,10},{3,19},{4,12},{5,21},{6,14},{7,23},{8,0},{9,25... | collective-permute-start | bytes 884744 | tf_op jit(solution)/shard_map/ppermute | solution.py:249
  99.6 16.1 %collective-permute-start.9 = (bf16[32,4608]{1,0:T(8,128)(2,1)S(1)}, bf16[32,4608]{1,0:T(8,128)(2,1)S(1)}, u32[]{:S(2)}, u32[]{:S(2)}) collective-permute-start(bf16[32,4608]{1,0:T(8,128)(2,1)S(1)} %collective-permute-done.7.refs_0_), channel_id=1, source_target_pairs={{0,16},{1,9},{2,18},{3,11},{4,20},{5,13},{6,22},{7,15},{8,24},{9,1... | collective-permute-start | bytes 884744 | tf_op jit(solution)/shard_map/ppermute | solution.py:249
  101.5 18.6 %collective-permute-start.3 = (bf16[32,4608]{1,0:T(8,128)(2,1)S(1)}, bf16[32,4608]{1,0:T(8,128)(2,1)S(1)}, u32[]{:S(2)}, u32[]{:S(2)}) collective-permute-start(bf16[32,4608]{1,0:T(8,128)(2,1)S(1)} %collective-permute-done.2.refs_0_), channel_id=1, source_target_pairs={{0,8},{1,17},{2,10},{3,19},{4,12},{5,21},{6,14},{7,23},{8,0},{9,25... | collective-permute-start | bytes 884744 | tf_op jit(solution)/shard_map/ppermute | solution.py:249
  107.5 18.4 %collective-permute-start.10 = (bf16[32,4608]{1,0:T(8,128)(2,1)S(1)}, bf16[32,4608]{1,0:T(8,128)(2,1)S(1)}, u32[]{:S(2)}, u32[]{:S(2)}) collective-permute-start(bf16[32,4608]{1,0:T(8,128)(2,1)S(1)} %collective-permute-done.8.refs_1_), channel_id=1, source_target_pairs={{0,16},{1,9},{2,18},{3,11},{4,20},{5,13},{6,22},{7,15},{8,24},{9,1... | collective-permute-start | bytes 884744 | tf_op jit(solution)/shard_map/ppermute | solution.py:249
  109.4 19.1 %collective-permute-start.14 = (bf16[32,4608]{1,0:T(8,128)(2,1)S(1)}, bf16[32,4608]{1,0:T(8,128)(2,1)S(1)}, u32[]{:S(2)}, u32[]{:S(2)}) collective-permute-start(bf16[32,4608]{1,0:T(8,128)(2,1)S(1)} %collective-permute-done.12.refs_0_), channel_id=1, source_target_pairs={{0,16},{1,9},{2,18},{3,11},{4,20},{5,13},{6,22},{7,15},{8,24},{9,1... | collective-permute-start | bytes 884744 | tf_op jit(solution)/shard_map/ppermute | solution.py:249
  113.8 15.3 %collective-permute-start.15 = (bf16[32,4608]{1,0:T(8,128)(2,1)S(1)}, bf16[32,4608]{1,0:T(8,128)(2,1)S(1)}, u32[]{:S(2)}, u32[]{:S(2)}) collective-permute-start(bf16[32,4608]{1,0:T(8,128)(2,1)S(1)} %collective-permute-done.13.refs_1_), channel_id=1, source_target_pairs={{0,16},{1,9},{2,18},{3,11},{4,20},{5,13},{6,22},{7,15},{8,24},{9,1... | collective-permute-start | bytes 884744 | tf_op jit(solution)/shard_map/ppermute | solution.py:249
  115.7 17.1 %collective-permute-start.4 = (bf16[32,4608]{1,0:T(8,128)(2,1)S(1)}, bf16[32,4608]{1,0:T(8,128)(2,1)S(1)}, u32[]{:S(2)}, u32[]{:S(2)}) collective-permute-start(bf16[32,4608]{1,0:T(8,128)(2,1)S(1)} %collective-permute-done.2.refs_0_), channel_id=1, source_target_pairs={{0,16},{1,9},{2,18},{3,11},{4,20},{5,13},{6,22},{7,15},{8,24},{9,1... | collective-permute-start | bytes 884744 | tf_op jit(solution)/shard_map/ppermute | solution.py:249
  120.1 13.1 %collective-permute-start.5 = (bf16[32,4608]{1,0:T(8,128)(2,1)S(1)}, bf16[32,4608]{1,0:T(8,128)(2,1)S(1)}, u32[]{:S(2)}, u32[]{:S(2)}) collective-permute-start(bf16[32,4608]{1,0:T(8,128)(2,1)S(1)} %collective-permute-done.3.refs_1_), channel_id=1, source_target_pairs={{0,16},{1,9},{2,18},{3,11},{4,20},{5,13},{6,22},{7,15},{8,24},{9,1... | collective-permute-start | bytes 884744 | tf_op jit(solution)/shard_map/ppermute | solution.py:249
  122.1 1.3 copy-start
  123.3 5.2 %copy-start.9 = (bf16[9,32,288]{2,1,0:T(8,128)(2,1)S(1)}, bf16[9,32,288]{2,1,0:T(8,128)(2,1)}, u32[]{:S(2)}) copy-start(bf16[9,32,288]{2,1,0:T(8,128)(2,1)} %get-tuple-element.42) | copy-start | bytes 497668
  125.9 15.4 %collective-permute-start.1 = (bf16[2,32,9216]{2,1,0:T(8,128)(2,1)}, bf16[2,32,9216]{2,1,0:T(8,128)(2,1)S(1)}, u32[]{:S(2)}, u32[]{:S(2)}) collective-permute-start(bf16[2,32,9216]{2,1,0:T(8,128)(2,1)} %get-tuple-element.45), channel_id=1, source_target_pairs={{0,1},{1,0},{2,3},{3,2},{4,5},{5,4},{6,7},{7,6},{8,9},{9,8},{10,11... | collective-permute-start | bytes 3538952 | tf_op jit(solution)/shard_map/ppermute | solution.py:249
  128.5 7.2 %copy-start.3 = (bf16[2,32,9216]{2,1,0:T(8,128)(2,1)}, bf16[2,32,9216]{2,1,0:T(8,128)(2,1)S(1)}, u32[]{:S(2)}) copy-start(bf16[2,32,9216]{2,1,0:T(8,128)(2,1)S(1)} %get-tuple-element.50.refs_4_) | copy-start | bytes 3538948
  128.6 8.4 %collective-permute-start = (bf16[9,32,288]{2,1,0:T(8,128)(2,1)S(1)}, bf16[9,32,288]{2,1,0:T(8,128)(2,1)S(1)}, u32[]{:S(2)}, u32[]{:S(2)}) collective-permute-start(bf16[9,32,288]{2,1,0:T(8,128)(2,1)S(1)} %copy-done.9), channel_id=1, source_target_pairs={{0,1},{1,0},{2,3},{3,2},{4,5},{5,4},{6,7},{7,6},{8,9},{9,8},{10,11... | collective-permute-start | bytes 497672 | tf_op jit(solution)/shard_map/ppermute | solution.py:249
  129.1 7.9 %copy-start.1 = (bf16[2,9,32,288]{3,2,1,0:T(8,128)(2,1)S(1)}, bf16[2,9,32,288]{3,2,1,0:T(8,128)(2,1)}, u32[]{:S(2)}) copy-start(bf16[2,9,32,288]{3,2,1,0:T(8,128)(2,1)} %coupling_ref.3) | copy-start | bytes 995332
  129.1 12.2 %collective-permute-start.11 = (bf16[2,32,9216]{2,1,0:T(8,128)(2,1)}, bf16[2,32,9216]{2,1,0:T(8,128)(2,1)}, u32[]{:S(2)}, u32[]{:S(2)}) collective-permute-start(bf16[2,32,9216]{2,1,0:T(8,128)(2,1)} %get-tuple-element.51), channel_id=1, source_target_pairs={{0,1},{1,0},{2,3},{3,2},{4,5},{5,4},{6,7},{7,6},{8,9},{9,8},{10,11... | collective-permute-start | bytes 3538952 | tf_op jit(solution)/shard_map/ppermute | solution.py:249
  131.7 1.1 copy-start.5
  132.8 8.5 %collective-permute-start.16 = (bf16[2,32,9216]{2,1,0:T(8,128)(2,1)}, bf16[2,32,9216]{2,1,0:T(8,128)(2,1)}, u32[]{:S(2)}, u32[]{:S(2)}) collective-permute-start(bf16[2,32,9216]{2,1,0:T(8,128)(2,1)} %get-tuple-element.54), channel_id=1, source_target_pairs={{0,1},{1,0},{2,3},{3,2},{4,5},{5,4},{6,7},{7,6},{8,9},{9,8},{10,11... | collective-permute-start | bytes 3538952 | tf_op jit(solution)/shard_map/ppermute | solution.py:249
  135.7 1.0 copy-start.7
  136.8 4.6 %collective-permute-start.6 = (bf16[2,32,9216]{2,1,0:T(8,128)(2,1)}, bf16[2,32,9216]{2,1,0:T(8,128)(2,1)}, u32[]{:S(2)}, u32[]{:S(2)}) collective-permute-start(bf16[2,32,9216]{2,1,0:T(8,128)(2,1)} %get-tuple-element.48), channel_id=1, source_target_pairs={{0,1},{1,0},{2,3},{3,2},{4,5},{5,4},{6,7},{7,6},{8,9},{9,8},{10,11... | collective-permute-start | bytes 3538952 | tf_op jit(solution)/shard_map/ppermute | solution.py:249
  137.0 4.4 %copy-start.4 = (bf16[2,32,9216]{2,1,0:T(8,128)(2,1)S(1)}, bf16[2,32,9216]{2,1,0:T(8,128)(2,1)}, u32[]{:S(2)}) copy-start(bf16[2,32,9216]{2,1,0:T(8,128)(2,1)} %copy-done.3) | copy-start | bytes 3538948
  137.0 4.4 %copy-start.6 = (bf16[2,32,9216]{2,1,0:T(8,128)(2,1)S(1)}, bf16[2,32,9216]{2,1,0:T(8,128)(2,1)}, u32[]{:S(2)}) copy-start(bf16[2,32,9216]{2,1,0:T(8,128)(2,1)} %copy-done.5) | copy-start | bytes 3538948
  137.0 4.4 %copy-start.8 = (bf16[2,32,9216]{2,1,0:T(8,128)(2,1)S(1)}, bf16[2,32,9216]{2,1,0:T(8,128)(2,1)}, u32[]{:S(2)}) copy-start(bf16[2,32,9216]{2,1,0:T(8,128)(2,1)} %copy-done.7) | copy-start | bytes 3538948
  154.4 30.6 %collective-permute-start.17 = (bf16[3,32,256]{2,1,0:T(8,128)(2,1)S(1)}, bf16[3,32,256]{2,1,0:T(8,128)(2,1)S(1)}, u32[]{:S(2)}, u32[]{:S(2)}) collective-permute-start(bf16[3,32,256]{2,1,0:T(8,128)(2,1)S(1)} %get-tuple-element.56), channel_id=1, source_target_pairs={{0,2},{1,3},{2,4},{3,5},{4,6},{5,7},{6,0},{7,1},{8,10},{9,11},{10,... | collective-permute-start | bytes 147464 | tf_op jit(solution)/shard_map/ppermute | solution.py:249
  154.5 32.6 %collective-permute-start.18 = (bf16[3,32,256]{2,1,0:T(8,128)(2,1)S(1)}, bf16[3,32,256]{2,1,0:T(8,128)(2,1)S(1)}, u32[]{:S(2)}, u32[]{:S(2)}) collective-permute-start(bf16[3,32,256]{2,1,0:T(8,128)(2,1)S(1)} %get-tuple-element.57), channel_id=1, source_target_pairs={{0,4},{1,5},{2,6},{3,7},{4,0},{5,1},{6,2},{7,3},{8,12},{9,13},{10,... | collective-permute-start | bytes 147464 | tf_op jit(solution)/shard_map/ppermute | solution.py:249
  155.9 33.5 %collective-permute-start.19 = (bf16[3,32,256]{2,1,0:T(8,128)(2,1)S(1)}, bf16[3,32,256]{2,1,0:T(8,128)(2,1)S(1)}, u32[]{:S(2)}, u32[]{:S(2)}) collective-permute-start(bf16[3,32,256]{2,1,0:T(8,128)(2,1)S(1)} %get-tuple-element.58), channel_id=1, source_target_pairs={{0,6},{1,7},{2,0},{3,1},{4,2},{5,3},{6,4},{7,5},{8,14},{9,15},{10,... | collective-permute-start | bytes 147464 | tf_op jit(solution)/shard_map/ppermute | solution.py:249
  158.7 37.5 %collective-permute-start.20 = (bf16[3,32,256]{2,1,0:T(8,128)(2,1)S(1)}, bf16[3,32,256]{2,1,0:T(8,128)(2,1)S(1)}, u32[]{:S(2)}, u32[]{:S(2)}) collective-permute-start(bf16[3,32,256]{2,1,0:T(8,128)(2,1)S(1)} %get-tuple-element.59), channel_id=1, source_target_pairs={{0,1},{1,0},{2,3},{3,2},{4,5},{5,4},{6,7},{7,6},{8,9},{9,8},{10,11... | collective-permute-start | bytes 147464 | tf_op jit(solution)/shard_map/ppermute | solution.py:249
  158.7 37.5 %collective-permute-start.21 = (bf16[3,32,256]{2,1,0:T(8,128)(2,1)S(1)}, bf16[3,32,256]{2,1,0:T(8,128)(2,1)S(1)}, u32[]{:S(2)}, u32[]{:S(2)}) collective-permute-start(bf16[3,32,256]{2,1,0:T(8,128)(2,1)S(1)} %get-tuple-element.60), channel_id=1, source_target_pairs={{0,3},{1,2},{2,5},{3,4},{4,7},{5,6},{6,1},{7,0},{8,11},{9,10},{10,... | collective-permute-start | bytes 147464 | tf_op jit(solution)/shard_map/ppermute | solution.py:249
  185.1 6.4 %collective-permute-start.24 = (bf16[3,32,256]{2,1,0:T(8,128)(2,1)S(1)}, bf16[3,32,256]{2,1,0:T(8,128)(2,1)S(1)}, u32[]{:S(2)}, u32[]{:S(2)}) collective-permute-start(bf16[3,32,256]{2,1,0:T(8,128)(2,1)S(1)} %get-tuple-element.64), channel_id=1, source_target_pairs={{0,2},{1,3},{2,4},{3,5},{4,6},{5,7},{6,0},{7,1},{8,10},{9,11},{10,... | collective-permute-start | bytes 147464 | tf_op jit(solution)/shard_map/ppermute | solution.py:249
  187.1 5.9 %collective-permute-start.25 = (bf16[3,32,256]{2,1,0:T(8,128)(2,1)S(1)}, bf16[3,32,256]{2,1,0:T(8,128)(2,1)S(1)}, u32[]{:S(2)}, u32[]{:S(2)}) collective-permute-start(bf16[3,32,256]{2,1,0:T(8,128)(2,1)S(1)} %get-tuple-element.65), channel_id=1, source_target_pairs={{0,4},{1,5},{2,6},{3,7},{4,0},{5,1},{6,2},{7,3},{8,12},{9,13},{10,... | collective-permute-start | bytes 147464 | tf_op jit(solution)/shard_map/ppermute | solution.py:249
  189.4 4.2 %collective-permute-start.26 = (bf16[3,32,256]{2,1,0:T(8,128)(2,1)S(1)}, bf16[3,32,256]{2,1,0:T(8,128)(2,1)S(1)}, u32[]{:S(2)}, u32[]{:S(2)}) collective-permute-start(bf16[3,32,256]{2,1,0:T(8,128)(2,1)S(1)} %get-tuple-element.66), channel_id=1, source_target_pairs={{0,6},{1,7},{2,0},{3,1},{4,2},{5,3},{6,4},{7,5},{8,14},{9,15},{10,... | collective-permute-start | bytes 147464 | tf_op jit(solution)/shard_map/ppermute | solution.py:249
  191.4 5.0 %collective-permute-start.22 = (bf16[3,32,256]{2,1,0:T(8,128)(2,1)S(1)}, bf16[3,32,256]{2,1,0:T(8,128)(2,1)S(1)}, u32[]{:S(2)}, u32[]{:S(2)}) collective-permute-start(bf16[3,32,256]{2,1,0:T(8,128)(2,1)S(1)} %get-tuple-element.61), channel_id=1, source_target_pairs={{0,5},{1,4},{2,7},{3,6},{4,1},{5,0},{6,3},{7,2},{8,13},{9,12},{10,... | collective-permute-start | bytes 147464 | tf_op jit(solution)/shard_map/ppermute | solution.py:249
  193.0 6.9 %collective-permute-start.23 = (bf16[3,32,256]{2,1,0:T(8,128)(2,1)S(1)}, bf16[3,32,256]{2,1,0:T(8,128)(2,1)S(1)}, u32[]{:S(2)}, u32[]{:S(2)}) collective-permute-start(bf16[3,32,256]{2,1,0:T(8,128)(2,1)S(1)} %get-tuple-element.62), channel_id=1, source_target_pairs={{0,7},{1,6},{2,1},{3,0},{4,3},{5,2},{6,5},{7,4},{8,15},{9,14},{10,... | collective-permute-start | bytes 147464 | tf_op jit(solution)/shard_map/ppermute | solution.py:249
  193.6 6.9 %collective-permute-start.27 = (bf16[3,32,256]{2,1,0:T(8,128)(2,1)S(1)}, bf16[3,32,256]{2,1,0:T(8,128)(2,1)S(1)}, u32[]{:S(2)}, u32[]{:S(2)}) collective-permute-start(bf16[3,32,256]{2,1,0:T(8,128)(2,1)S(1)} %get-tuple-element.67), channel_id=1, source_target_pairs={{0,1},{1,0},{2,3},{3,2},{4,5},{5,4},{6,7},{7,6},{8,9},{9,8},{10,11... | collective-permute-start | bytes 147464 | tf_op jit(solution)/shard_map/ppermute | solution.py:249
  196.2 5.9 %collective-permute-start.28 = (bf16[3,32,256]{2,1,0:T(8,128)(2,1)S(1)}, bf16[3,32,256]{2,1,0:T(8,128)(2,1)S(1)}, u32[]{:S(2)}, u32[]{:S(2)}) collective-permute-start(bf16[3,32,256]{2,1,0:T(8,128)(2,1)S(1)} %get-tuple-element.68), channel_id=1, source_target_pairs={{0,3},{1,2},{2,5},{3,4},{4,7},{5,6},{6,1},{7,0},{8,11},{9,10},{10,... | collective-permute-start | bytes 147464 | tf_op jit(solution)/shard_map/ppermute | solution.py:249
  196.3 8.2 %collective-permute-start.29 = (bf16[3,32,256]{2,1,0:T(8,128)(2,1)S(1)}, bf16[3,32,256]{2,1,0:T(8,128)(2,1)S(1)}, u32[]{:S(2)}, u32[]{:S(2)}) collective-permute-start(bf16[3,32,256]{2,1,0:T(8,128)(2,1)S(1)} %get-tuple-element.69), channel_id=1, source_target_pairs={{0,5},{1,4},{2,7},{3,6},{4,1},{5,0},{6,3},{7,2},{8,13},{9,12},{10,... | collective-permute-start | bytes 147464 | tf_op jit(solution)/shard_map/ppermute | solution.py:249
  196.4 8.0 %collective-permute-start.30 = (bf16[3,32,256]{2,1,0:T(8,128)(2,1)S(1)}, bf16[3,32,256]{2,1,0:T(8,128)(2,1)S(1)}, u32[]{:S(2)}, u32[]{:S(2)}) collective-permute-start(bf16[3,32,256]{2,1,0:T(8,128)(2,1)S(1)} %get-tuple-element.70), channel_id=1, source_target_pairs={{0,7},{1,6},{2,1},{3,0},{4,3},{5,2},{6,5},{7,4},{8,15},{9,14},{10,... | collective-permute-start | bytes 147464 | tf_op jit(solution)/shard_map/ppermute | solution.py:249
  199.9 6.4 %collective-permute-start.31 = (bf16[3,32,256]{2,1,0:T(8,128)(2,1)S(1)}, bf16[3,32,256]{2,1,0:T(8,128)(2,1)S(1)}, u32[]{:S(2)}, u32[]{:S(2)}) collective-permute-start(bf16[3,32,256]{2,1,0:T(8,128)(2,1)S(1)} %get-tuple-element.72), channel_id=1, source_target_pairs={{0,2},{1,3},{2,4},{3,5},{4,6},{5,7},{6,0},{7,1},{8,10},{9,11},{10,... | collective-permute-start | bytes 147464 | tf_op jit(solution)/shard_map/ppermute | solution.py:249
  200.5 7.2 %collective-permute-start.32 = (bf16[3,32,256]{2,1,0:T(8,128)(2,1)S(1)}, bf16[3,32,256]{2,1,0:T(8,128)(2,1)S(1)}, u32[]{:S(2)}, u32[]{:S(2)}) collective-permute-start(bf16[3,32,256]{2,1,0:T(8,128)(2,1)S(1)} %get-tuple-element.73), channel_id=1, source_target_pairs={{0,4},{1,5},{2,6},{3,7},{4,0},{5,1},{6,2},{7,3},{8,12},{9,13},{10,... | collective-permute-start | bytes 147464 | tf_op jit(solution)/shard_map/ppermute | solution.py:249
  202.1 6.6 %collective-permute-start.33 = (bf16[3,32,256]{2,1,0:T(8,128)(2,1)S(1)}, bf16[3,32,256]{2,1,0:T(8,128)(2,1)S(1)}, u32[]{:S(2)}, u32[]{:S(2)}) collective-permute-start(bf16[3,32,256]{2,1,0:T(8,128)(2,1)S(1)} %get-tuple-element.74), channel_id=1, source_target_pairs={{0,6},{1,7},{2,0},{3,1},{4,2},{5,3},{6,4},{7,5},{8,14},{9,15},{10,... | collective-permute-start | bytes 147464 | tf_op jit(solution)/shard_map/ppermute | solution.py:249
  204.5 4.3 %collective-permute-start.34 = (bf16[3,32,256]{2,1,0:T(8,128)(2,1)S(1)}, bf16[3,32,256]{2,1,0:T(8,128)(2,1)S(1)}, u32[]{:S(2)}, u32[]{:S(2)}) collective-permute-start(bf16[3,32,256]{2,1,0:T(8,128)(2,1)S(1)} %get-tuple-element.75), channel_id=1, source_target_pairs={{0,1},{1,0},{2,3},{3,2},{4,5},{5,4},{6,7},{7,6},{8,9},{9,8},{10,11... | collective-permute-start | bytes 147464 | tf_op jit(solution)/shard_map/ppermute | solution.py:249
  204.5 5.5 %collective-permute-start.35 = (bf16[3,32,256]{2,1,0:T(8,128)(2,1)S(1)}, bf16[3,32,256]{2,1,0:T(8,128)(2,1)S(1)}, u32[]{:S(2)}, u32[]{:S(2)}) collective-permute-start(bf16[3,32,256]{2,1,0:T(8,128)(2,1)S(1)} %get-tuple-element.76), channel_id=1, source_target_pairs={{0,3},{1,2},{2,5},{3,4},{4,7},{5,6},{6,1},{7,0},{8,11},{9,10},{10,... | collective-permute-start | bytes 147464 | tf_op jit(solution)/shard_map/ppermute | solution.py:249
  206.2 6.4 %collective-permute-start.36 = (bf16[3,32,256]{2,1,0:T(8,128)(2,1)S(1)}, bf16[3,32,256]{2,1,0:T(8,128)(2,1)S(1)}, u32[]{:S(2)}, u32[]{:S(2)}) collective-permute-start(bf16[3,32,256]{2,1,0:T(8,128)(2,1)S(1)} %get-tuple-element.77), channel_id=1, source_target_pairs={{0,5},{1,4},{2,7},{3,6},{4,1},{5,0},{6,3},{7,2},{8,13},{9,12},{10,... | collective-permute-start | bytes 147464 | tf_op jit(solution)/shard_map/ppermute | solution.py:249
  207.7 5.0 %collective-permute-start.37 = (bf16[3,32,256]{2,1,0:T(8,128)(2,1)S(1)}, bf16[3,32,256]{2,1,0:T(8,128)(2,1)S(1)}, u32[]{:S(2)}, u32[]{:S(2)}) collective-permute-start(bf16[3,32,256]{2,1,0:T(8,128)(2,1)S(1)} %get-tuple-element.78), channel_id=1, source_target_pairs={{0,7},{1,6},{2,1},{3,0},{4,3},{5,2},{6,5},{7,4},{8,15},{9,14},{10,... | collective-permute-start | bytes 147464 | tf_op jit(solution)/shard_map/ppermute | solution.py:249

commit v3 on v2

v3 whole, which is shorter than its diff:
```python
import functools
import math

import jax
import jax.numpy as jnp
from jax import lax
from jax.experimental import pallas as pl
from jax.experimental.pallas import tpu as pltpu
from jax.sharding import PartitionSpec as P

KY = 96
BANDS = 16
LINE = KY * BANDS
GROUPS = (5, 8)
F32 = jnp.float32
BF16 = jnp.bfloat16


def contract(a, b, dim_a, dim_b):
    return lax.dot_general(a, b, (((dim_a,), (dim_b,)), ((), ())), preferred_element_type=F32)


def place():
    ka = lax.axis_index("ka")
    return lax.axis_index("pb"), ka // 2, ka % 2


def cut_kernel(block, env_ref, coupling_ref, *refs):
    pieces, (window, give, sems) = refs[:-3], refs[-3:]
    n_z = len(pieces) + 1
    pb, z, core = place()

    def lanes(index):
        return pl.ds(pl.multiple_of(lax.rem(index + 2 * n_z, 2 * n_z) * block, 128), block)

    jobs = []
    for e in range(1, n_z):
        to = lax.rem(z - e + n_z, n_z)
        jobs.append((env_ref.at[:, lanes(2 * to - 1 + pb)], pieces[e - 1]))
    for w in range(4):
        jobs.append((env_ref.at[:, lanes(2 * z - 1 + w)], window.at[:, w * block : (w + 1) * block]))
    jobs.append((coupling_ref.at[1 - core], give))
    copies = [pltpu.make_async_copy(src, dst, sems.at[i]) for i, (src, dst) in enumerate(jobs)]
    for copy in copies:
        copy.start()
    for copy in copies:
        copy.wait()


def cut(envelopes, coupling, n_z, block):
    rows = envelopes.shape[0]
    shape = functools.partial(jax.ShapeDtypeStruct, dtype=BF16)
    outs = [shape((rows, block))] * (n_z - 1) + [shape((rows, 4 * block)), shape(coupling.shape[1:])]
    *pieces, window, give = pl.pallas_call(
        functools.partial(cut_kernel, block),
        in_specs=[pl.BlockSpec(memory_space=pl.ANY)] * 2,
        out_specs=[pl.BlockSpec(memory_space=pltpu.VMEM)] * len(outs),
        out_shape=outs,
        scratch_shapes=[pltpu.SemaphoreType.DMA((n_z + 4,))],
        name="cut",
    )(envelopes, coupling)
    return pieces, window, give


def prep_kernel(block, lines, lines_all, kq_ref, *refs):
    ins, (keep_ref, give_ref, window, sems) = refs[:-4], refs[-4:]
    pb, z, core = place()
    copies = []
    for index, src in enumerate(ins):
        offset = 0
        if len(ins) > 1:
            rel = (0, 1 + core, 2 - core, 3)[index]
            offset = pl.multiple_of((pb ^ rel) * block, 128)
        copy = pltpu.make_async_copy(src, window.at[:, pl.ds(offset, src.shape[1])], sems.at[index])
        copy.start()
        copies.append(copy)
    for copy in copies:
        copy.wait()
    half = lines // 2
    turns = []
    for q in (core, 1 - core):
        origin = kq_ref[q, 0]
        start_line = lax.rem(origin // KY - (2 * z + core) * half + half + lines_all, lines_all)
        turns.append((start_line, lax.rem(LINE - lax.rem(origin, KY) * BANDS, LINE)))
    for line in range(lines):
        to = slice(line * LINE, (line + 1) * LINE)
        own = window[:, (half + line) * LINE : (half + line + 1) * LINE]
        for out_ref, (start_line, turn) in zip((keep_ref, give_ref), turns):
            out_ref[0, :, to] = own
            lane = pl.multiple_of((start_line + line) * LINE, 128)
            shifted = window[:, pl.ds(lane, LINE)].astype(F32)
            out_ref[1, :, to] = pltpu.roll(shifted, turn, 1).astype(BF16)


def prepare(kq_map, ins, block, lines, lines_all):
    rows = ins[0].shape[0]
    out = jax.ShapeDtypeStruct((2, rows, lines * LINE), BF16)
    return pl.pallas_call(
        functools.partial(prep_kernel, block, lines, lines_all),
        in_specs=[pl.BlockSpec(memory_space=pltpu.SMEM)] + [pl.BlockSpec(memory_space=pl.ANY)] * len(ins),
        out_specs=[pl.BlockSpec(memory_space=pltpu.VMEM)] * 2,
        out_shape=[out, out],
        scratch_shapes=[
            pltpu.VMEM((rows, 2 * lines * LINE), BF16),
            pltpu.SemaphoreType.DMA((len(ins),)),
        ],
        compiler_params=pltpu.CompilerParams(vmem_limit_bytes=24 << 20),
        name="prepare",
    )(kq_map, *ins)


def main_kernel(sources, first, branches, factor, x_ref, mask_ref, *refs):
    amps, (mine_ref, *sends, total) = refs[:sources], refs[sources:]
    step = pl.program_id(0)

    @pl.when(step == 0)
    def _():
        total[...] = jnp.zeros_like(total)

    for branch in range(branches):
        parts = []
        for tile in range(LINE // 256):
            lanes = slice(tile * 256, (tile + 1) * 256)
            matrix = jnp.concatenate([x_ref[first + branch, :, lanes]] * 16, axis=0) * mask_ref[...]
            own = jnp.concatenate([ref[0, :, lanes] for ref in amps], axis=0)
            parts.append(contract(own, matrix, 1, 0).astype(BF16))
        diff = jnp.concatenate(parts, axis=1)
        shifted = jnp.concatenate([ref[1] for ref in amps], axis=0)
        total[branch] += contract(shifted, diff, 1, 1)

    @pl.when(step == pl.num_programs(0) - 1)
    def _():
        _, z, core = place()
        states = total.shape[2]
        rows = states // sources
        col = lax.broadcasted_iota(jnp.int32, (states, states), 0)
        target = lax.broadcasted_iota(jnp.int32, (states, states), 1)
        source = lax.rem(col // rows + 2 * z, sources)
        home = (source // 2 * 2 + (source % 2 ^ core)) * rows + col % rows
        to_home = (home == target).astype(F32).astype(BF16)
        for branch in range(branches):
            value = total[branch] * factor
            high = value.astype(BF16)
            moved = contract(high, to_home, 1, 0)
            rest = value[: 2 * rows] - high[: 2 * rows].astype(F32)
            middle = rest.astype(BF16)
            low = (rest - middle.astype(F32)).astype(BF16)
            mine_ref[branch] = moved[: 2 * rows] + contract(middle, to_home, 1, 0) + contract(low, to_home, 1, 0)
            for chip, send in enumerate(sends, 1):
                send[branch] = moved[chip * 2 * rows : (chip + 1) * 2 * rows].astype(BF16)


def products(x, mask, amps, first, branches, factor):
    sources, rows = len(amps), amps[0].shape[1]
    states = sources * rows
    lines = x.shape[2] // LINE
    piece = pl.BlockSpec((branches, 2 * rows, states), lambda i: (0, 0, 0))
    shape = (branches, 2 * rows, states)
    return pl.pallas_call(
        functools.partial(main_kernel, sources, first, branches, factor),
        grid=(lines,),
        in_specs=[
            pl.BlockSpec((x.shape[0], BANDS, LINE), lambda i: (0, 0, i)),
            pl.BlockSpec((256, 256), lambda i: (0, 0)),
        ]
        + [pl.BlockSpec((2, rows, LINE), lambda i: (0, 0, i))] * sources,
        out_specs=[piece] * (sources // 2),
        out_shape=[jax.ShapeDtypeStruct(shape, F32 if i == 0 else BF16) for i in range(sources // 2)],
        scratch_shapes=[pltpu.VMEM((branches, states, states), F32)],
        compiler_params=pltpu.CompilerParams(vmem_limit_bytes=40 << 20),
        cost_estimate=pl.CostEstimate(
            flops=4 * branches * states * states * lines * LINE,
            bytes_accessed=4 * states * lines * LINE,
            transcendentals=0,
        ),
        name="products",
    )(x, mask, *amps)


def band_kernel(coupling_ref, other_ref, x_ref):
    branches, _, count = other_ref.shape
    half = BANDS // 4
    size = min(count, 128)

    def iota(shape, dim):
        return lax.broadcasted_iota(jnp.int32, shape, dim)

    shape = (8 * BANDS, 32)
    row, col = iota(shape, 0), iota(shape, 1)
    term, v, c = row // BANDS, row % BANDS // half, row % half
    choice = jnp.where(term < 4, 4 * term + c, 16 + 4 * v + (term - 4))
    pick = (choice == col).astype(F32).astype(BF16)
    spread = []
    for by_a in (False, True):
        shape = (4 * size, size * BANDS)
        row, lane = iota(shape, 0), iota(shape, 1)
        band = lane % BANDS
        index = band // half if by_a else band % half
        hit = (row % size == lane // BANDS) & (row // size == index)
        spread.append(hit.astype(F32).astype(BF16))
    shape = (branches * BANDS, size * BANDS)
    row, lane = iota(shape, 0) % BANDS, iota(shape, 1) % BANDS
    keep_cond = (row // half == lane // half).astype(F32)
    keep_val = (row % half == lane % half).astype(F32)
    _, _, core = place()
    for mine in (True, False):
        tables = [coupling_ref[core, branch] if mine else other_ref[branch] for branch in range(branches)]
        terms = [contract(pick, table, 1, 0).astype(BF16) for table in tables]
        base = (core if mine else 1 - core) * (count * BANDS)
        for start in range(0, count, size):
            width = min(size, count - start)
            lanes = width * BANDS
            values = []
            for kind in range(2):
                rows = []
                for term in terms:
                    slabs = []
                    for index in range(4):
                        at = (4 * kind + index) * BANDS
                        slab = term[at : at + BANDS, start : start + width]
                        if width < size:
                            slab = jnp.concatenate([slab, jnp.zeros((BANDS, size - width), BF16)], axis=1)
                        slabs.append(slab)
                    rows.append(jnp.concatenate(slabs, axis=1))
                values.append(contract(jnp.concatenate(rows, axis=0), spread[kind][:, :lanes], 1, 0))
            total = (values[0] * keep_cond[:, :lanes] - values[1] * keep_val[:, :lanes]).astype(BF16)
            at = pl.multiple_of(base + start * BANDS, 128)
            for branch in range(branches):
                x_ref[branch, :, pl.ds(at, lanes)] = total[branch * BANDS : (branch + 1) * BANDS]


def band_matrices(coupling, other):
    branches, _, count = other.shape
    return pl.pallas_call(
        band_kernel,
        in_specs=[pl.BlockSpec(memory_space=pltpu.VMEM)] * 2,
        out_specs=pl.BlockSpec(memory_space=pltpu.VMEM),
        out_shape=jax.ShapeDtypeStruct((branches, BANDS, 2 * count * BANDS), BF16),
        compiler_params=pltpu.CompilerParams(vmem_limit_bytes=40 << 20),
        cost_estimate=pl.CostEstimate(flops=10**10, bytes_accessed=10**6, transcendentals=0),
        name="band_matrices",
    )(coupling, other)


def shards(envelopes, coupling, kq_map):
    n_pb, n_ka = lax.axis_size("pb"), lax.axis_size("ka")
    assert n_pb == 4 and n_ka % 2 == 0 and coupling.shape[0] == 2
    n_z = n_ka // 2
    rows, width = envelopes.shape
    block = width // n_ka
    lines, lines_all = 2 * block // LINE, width // LINE
    branches = coupling.shape[1]
    core = lax.axis_index("ka") % 2

    def permute(x, to):
        pairs = []
        for p in range(n_pb):
            for k in range(n_ka):
                tp, tz, tc = to(p, k // 2, k % 2)
                pairs.append((p * n_ka + k, tp * n_ka + (tz % n_z) * 2 + tc))
        return lax.ppermute(x, ("pb", "ka"), pairs)

    def sibling(x):
        return permute(x, lambda p, zz, c: (p, zz, 1 - c))

    pieces, window, give = cut(envelopes, coupling, n_z, block)
    arrived = []
    for e in range(1, n_z):
        arrived.append(permute(pieces[e - 1], lambda p, zz, c: (p, zz - e, c)))
    keep, pass_on = prepare(kq_map, [window], block, lines, lines_all)
    amps = [keep, sibling(pass_on)]
    x = band_matrices(coupling, sibling(give))
    arrived[0], x, amps[0] = lax.optimization_barrier((arrived[0], x, amps[0]))

    for piece in arrived:
        one = permute(piece, lambda p, zz, c: (p ^ (1 + c), zz, c))
        two = permute(piece, lambda p, zz, c: (p ^ (2 - c), zz, c))
        three = permute(one, lambda p, zz, c: (p ^ (2 - c), zz, c))
        keep, pass_on = prepare(kq_map, [piece, one, two, three], block, lines, lines_all)
        amps += [keep, sibling(pass_on)]

    index = jnp.arange(256, dtype=jnp.int32) // BANDS
    mask = (index[:, None] == index[None, :]).astype(BF16)
    factor = 1.0 / math.sqrt(float(width))
    edges = [0] + [edge * branches // 9 for edge in GROUPS] + [branches]
    received, mine, other = [], [], []
    for lo, hi in zip(edges[:-1], edges[1:]):
        if len(received) >= 2:
            received[-2], x = lax.optimization_barrier((received[-2], x))
        own, *sends = products(x, mask, amps, lo, hi - lo, factor)
        received.append([own] + [permute(p, lambda p, zz, c: (p, zz + e, c)) for e, p in enumerate(sends, 1)])
    for parts in received:
        total = parts[0]
        for part in parts[1:]:
            total = total + part.astype(F32)
        mine.append(total[:, :rows])
        other.append(sibling(total[:, rows:]))
    mine, other = jnp.concatenate(mine, axis=0), jnp.concatenate(other, axis=0)
    return jnp.where(core == 0, jnp.stack([mine, other]), jnp.stack([other, mine]))


def solution(mesh):
    return jax.shard_map(
        shards,
        mesh=mesh,
        in_specs=(P("ka", None), P("pb", None, None, "ka"), P("pb", "ka")),
        out_specs=P("pb", None, "ka", None),
        check_vma=False,
    )
```

time: 214 us -> 141 us (0.66)
  Pallas kernels: 125 us -> 53.1 us
  starting transfers between devices: 42.5 us -> 35.2 us
  local copies, waits for them, and re-layouts: 4.17 us -> 10.5 us
    pallas_call x1, Pallas kernels: 71.2 us -> 3.04 us  [cut(): pl.pallas_call(functools.partial(cut_kernel, block), in_specs=[pl.BlockSp...]
    ppermute x38 -> x29, starting transfers between devices: 42.5 us -> 35.2 us  [permute(): return lax.ppermute(x, ('pb', 'ka'), pairs)]
    unnamed x20 -> x22, local copies, waits for them, and re-layouts: 3.4 us -> 10.4 us
    pallas_call x8, Pallas kernels: 53.4 us -> 50.1 us  [the longest x3 36.1 us: products(): pl.pallas_call(functools.partial(main_kernel, sources, first, branches, f...]
    ppermute x38 -> x29, waiting for transfers between devices: 40 us -> 40 us  [permute(): return lax.ppermute(x, ('pb', 'ka'), pairs)]
  transfers between devices with their start and end apart: 38 -> 29, of which waited for: 12 -> 11; matrix products, arithmetic and copies ran while one was open for 0% -> 0% of each run, Pallas kernels for 19% -> 27%
where the time goes in v3:
time: 141 us; the launch traced here: 140 us
  Pallas kernels  53.1 us (38%)
  waiting for transfers between devices  40 us (28%)
  starting transfers between devices  35.2 us (25%)
  local copies, waits for them, and re-layouts  10.5 us (7%)
    ppermute x29, waiting for transfers between devices, permute(): return lax.ppermute(x, ('pb', 'ka'), pairs)  40 us
    pallas_call x3, Pallas kernels, products(): pl.pallas_call(functools.partial(main_kernel, sources, first, branches, f...  36.1 us
    ppermute x29, starting transfers between devices, permute(): return lax.ppermute(x, ('pb', 'ka'), pairs)  35.2 us
    unnamed x22, local copies, waits for them, and re-layouts  10.4 us
    pallas_call x4, Pallas kernels, prepare(): pl.pallas_call(functools.partial(prep_kernel, block, lines, lines_all), i...  10.2 us
    pallas_call x1, Pallas kernels, band_matrices(): pl.pallas_call(band_kernel, in_specs=[pl.BlockSpec(memory_space=pltpu.VME...  3.73 us
    pallas_call x1, Pallas kernels, cut(): pl.pallas_call(functools.partial(cut_kernel, block), in_specs=[pl.BlockSp...  3.04 us
  transfers between devices with their start and end apart: 29, of which 11 were waited for; matrix products, arithmetic and copies ran while one was open for 0% of the time, Pallas kernels for 27%

profile of v3, /device:TPU:0, one launch (start us, length us, event | category | flops | bytes accessed | tf_op | source)
XLA Modules:
  0.0 140.2 jit_solution(945705530849122246)
XLA Ops:
  0.0 3.0 %cut.1 = (bf16[32,4608]{1,0:T(8,128)(2,1)}, bf16[32,4608]{1,0:T(8,128)(2,1)}, bf16[32,4608]{1,0:T(8,128)(2,1)}, bf16[32,18432]{1,0:T(8,128)(2,1)}, bf16[9,32,288]{2,1,0:T(8,128)(2,1)}) custom-call(bf16[32,36864]{1,0:T(8,128)(2,1)} %env_ref.1, bf16[2,9,32,288]{3,2,1,0:T(8,128)(2,1)} %coupling_ref.3), custom_call_target="tpu_custom_call" | custom-call | tf_op jit(solution)/shard_map/cut/pallas_call | solution.py:54
  3.1 0.5 collective-permute-start.1
  3.6 4.7 %collective-permute-start = (bf16[32,4608]{1,0:T(8,128)(2,1)}, bf16[32,4608]{1,0:T(8,128)(2,1)S(1)}, u32[]{:S(2)}, u32[]{:S(2)}) collective-permute-start(bf16[32,4608]{1,0:T(8,128)(2,1)} %get-tuple-element.38), channel_id=1, source_target_pairs={{0,6},{1,7},{2,0},{3,1},{4,2},{5,3},{6,4},{7,5},{8,14},{9,15},{10,... | collective-permute-start | bytes 884744 | tf_op jit(solution)/shard_map/ppermute | solution.py:261
  8.3 1.0 collective-permute-start.12
  9.3 1.3 copy-done.8
  10.5 2.6 %prepare.4 = (bf16[2,32,9216]{2,1,0:T(8,128)(2,1)S(1)}, bf16[2,32,9216]{2,1,0:T(8,128)(2,1)}) custom-call(s32[2,288]{1,0:T(2,128)S(1)} %copy-done.10, bf16[32,18432]{1,0:T(8,128)(2,1)S(1)} %copy-done.8), custom_call_target="tpu_custom_call" | custom-call | tf_op jit(solution)/shard_map/prepare/pallas_call | solution.py:98
  13.2 1.1 copy-done
  14.2 3.7 %band_matrices.1.x_ref = bf16[9,16,9216]{2,1,0:T(8,128)(2,1)S(1)} custom-call(bf16[2,9,32,288]{3,2,1,0:T(8,128)(2,1)S(1)} %copy-done.9, bf16[9,32,288]{2,1,0:T(8,128)(2,1)S(1)} %collective-permute-done.1.other_ref), custom_call_target="tpu_custom_call" | custom-call | flops 10000000000 | bytes 1000000 | tf_op jit(solution)/shard_map/band_matrices/pallas_call | solution.py:234
  18.0 1.6 %collective-permute-start.3 = (bf16[32,4608]{1,0:T(8,128)(2,1)S(1)}, bf16[32,4608]{1,0:T(8,128)(2,1)S(1)}, u32[]{:S(2)}, u32[]{:S(2)}) collective-permute-start(bf16[32,4608]{1,0:T(8,128)(2,1)S(1)} %collective-permute-done.refs_0_), channel_id=1, source_target_pairs={{0,8},{1,17},{2,10},{3,19},{4,12},{5,21},{6,14},{7,23},{8,0},{9,25... | collective-permute-start | bytes 884744 | tf_op jit(solution)/shard_map/ppermute | solution.py:261
  19.5 14.7 %collective-permute-done.7.refs_0_ = bf16[32,4608]{1,0:T(8,128)(2,1)S(1)} collective-permute-done((bf16[32,4608]{1,0:T(8,128)(2,1)}, bf16[32,4608]{1,0:T(8,128)(2,1)S(1)}, u32[]{:S(2)}, u32[]{:S(2)}) %collective-permute-start.7) | collective-permute-done | bytes 294944 | tf_op jit(solution)/shard_map/ppermute | solution.py:261
  34.2 1.5 %collective-permute-start.8 = (bf16[32,4608]{1,0:T(8,128)(2,1)S(1)}, bf16[32,4608]{1,0:T(8,128)(2,1)S(1)}, u32[]{:S(2)}, u32[]{:S(2)}) collective-permute-start(bf16[32,4608]{1,0:T(8,128)(2,1)S(1)} %collective-permute-done.7.refs_0_), channel_id=1, source_target_pairs={{0,8},{1,17},{2,10},{3,19},{4,12},{5,21},{6,14},{7,23},{8,0},{9,25... | collective-permute-start | bytes 884744 | tf_op jit(solution)/shard_map/ppermute | solution.py:261
  35.7 1.5 %collective-permute-start.4 = (bf16[32,4608]{1,0:T(8,128)(2,1)S(1)}, bf16[32,4608]{1,0:T(8,128)(2,1)S(1)}, u32[]{:S(2)}, u32[]{:S(2)}) collective-permute-start(bf16[32,4608]{1,0:T(8,128)(2,1)S(1)} %collective-permute-done.refs_0_), channel_id=1, source_target_pairs={{0,16},{1,9},{2,18},{3,11},{4,20},{5,13},{6,22},{7,15},{8,24},{9,1... | collective-permute-start | bytes 884744 | tf_op jit(solution)/shard_map/ppermute | solution.py:261
  37.2 0.5 collective-permute-start.13
  37.7 0.5 collective-permute-start.5
  38.3 1.5 %collective-permute-start.9 = (bf16[32,4608]{1,0:T(8,128)(2,1)S(1)}, bf16[32,4608]{1,0:T(8,128)(2,1)S(1)}, u32[]{:S(2)}, u32[]{:S(2)}) collective-permute-start(bf16[32,4608]{1,0:T(8,128)(2,1)S(1)} %collective-permute-done.7.refs_0_), channel_id=1, source_target_pairs={{0,16},{1,9},{2,18},{3,11},{4,20},{5,13},{6,22},{7,15},{8,24},{9,1... | collective-permute-start | bytes 884744 | tf_op jit(solution)/shard_map/ppermute | solution.py:261
  39.8 4.3 %collective-permute-done.8.refs_1_ = bf16[32,4608]{1,0:T(8,128)(2,1)S(1)} collective-permute-done((bf16[32,4608]{1,0:T(8,128)(2,1)S(1)}, bf16[32,4608]{1,0:T(8,128)(2,1)S(1)}, u32[]{:S(2)}, u32[]{:S(2)}) %collective-permute-start.8) | collective-permute-done | bytes 294944 | tf_op jit(solution)/shard_map/ppermute | solution.py:261
  44.1 1.5 %collective-permute-start.10 = (bf16[32,4608]{1,0:T(8,128)(2,1)S(1)}, bf16[32,4608]{1,0:T(8,128)(2,1)S(1)}, u32[]{:S(2)}, u32[]{:S(2)}) collective-permute-start(bf16[32,4608]{1,0:T(8,128)(2,1)S(1)} %collective-permute-done.8.refs_1_), channel_id=1, source_target_pairs={{0,16},{1,9},{2,18},{3,11},{4,20},{5,13},{6,22},{7,15},{8,24},{9,1... | collective-permute-start | bytes 884744 | tf_op jit(solution)/shard_map/ppermute | solution.py:261
  45.6 0.0 collective-permute-done.4.refs_2_
  45.6 1.5 %collective-permute-start.14 = (bf16[32,4608]{1,0:T(8,128)(2,1)S(1)}, bf16[32,4608]{1,0:T(8,128)(2,1)S(1)}, u32[]{:S(2)}, u32[]{:S(2)}) collective-permute-start(bf16[32,4608]{1,0:T(8,128)(2,1)S(1)} %collective-permute-done.12.refs_0_), channel_id=1, source_target_pairs={{0,16},{1,9},{2,18},{3,11},{4,20},{5,13},{6,22},{7,15},{8,24},{9,1... | collective-permute-start | bytes 884744 | tf_op jit(solution)/shard_map/ppermute | solution.py:261
  47.2 3.2 %collective-permute-done.13.refs_1_ = bf16[32,4608]{1,0:T(8,128)(2,1)S(1)} collective-permute-done((bf16[32,4608]{1,0:T(8,128)(2,1)S(1)}, bf16[32,4608]{1,0:T(8,128)(2,1)S(1)}, u32[]{:S(2)}, u32[]{:S(2)}) %collective-permute-start.13) | collective-permute-done | bytes 294944 | tf_op jit(solution)/shard_map/ppermute | solution.py:261
  50.4 1.5 %collective-permute-start.15 = (bf16[32,4608]{1,0:T(8,128)(2,1)S(1)}, bf16[32,4608]{1,0:T(8,128)(2,1)S(1)}, u32[]{:S(2)}, u32[]{:S(2)}) collective-permute-start(bf16[32,4608]{1,0:T(8,128)(2,1)S(1)} %collective-permute-done.13.refs_1_), channel_id=1, source_target_pairs={{0,16},{1,9},{2,18},{3,11},{4,20},{5,13},{6,22},{7,15},{8,24},{9,1... | collective-permute-start | bytes 884744 | tf_op jit(solution)/shard_map/ppermute | solution.py:261
  51.9 2.5 %prepare.5 = (bf16[2,32,9216]{2,1,0:T(8,128)(2,1)S(1)}, bf16[2,32,9216]{2,1,0:T(8,128)(2,1)}) custom-call(s32[2,288]{1,0:T(2,128)S(1)} %copy-done.10, bf16[32,4608]{1,0:T(8,128)(2,1)S(1)} %collective-permute-done.refs_0_, bf16[32,4608]{1,0:T(8,128)(2,1)S(1)} %collective-permute-done.3.refs_1_, bf16[32,4608]{1,0:T(8,128)(2,1)S(1)} %collective-permute-done.4.refs_2_, ...), custom_call_target="tpu_custom_call" | custom-call | tf_op jit(solution)/shard_map/prepare/pallas_call | solution.py:98
  54.5 1.0 copy-done.2
  55.5 0.5 collective-permute-start.6
  56.0 2.6 %prepare.6 = (bf16[2,32,9216]{2,1,0:T(8,128)(2,1)S(1)}, bf16[2,32,9216]{2,1,0:T(8,128)(2,1)}) custom-call(s32[2,288]{1,0:T(2,128)S(1)} %copy-done.10, bf16[32,4608]{1,0:T(8,128)(2,1)S(1)} %collective-permute-done.7.refs_0_, bf16[32,4608]{1,0:T(8,128)(2,1)S(1)} %collective-permute-done.8.refs_1_, bf16[32,4608]{1,0:T(8,128)(2,1)S(1)} %collective-permute-done.9.refs_2_, ...), custom_call_target="tpu_custom_call" | custom-call | tf_op jit(solution)/shard_map/prepare/pallas_call | solution.py:98
  58.6 1.0 copy-done.4
  59.6 0.8 collective-permute-start.11
  60.4 1.3 collective-permute-done.15.refs_3_
  61.7 2.5 %prepare.7 = (bf16[2,32,9216]{2,1,0:T(8,128)(2,1)S(1)}, bf16[2,32,9216]{2,1,0:T(8,128)(2,1)}) custom-call(s32[2,288]{1,0:T(2,128)S(1)} %copy-done.10, bf16[32,4608]{1,0:T(8,128)(2,1)S(1)} %collective-permute-done.12.refs_0_, bf16[32,4608]{1,0:T(8,128)(2,1)S(1)} %collective-permute-done.13.refs_1_, bf16[32,4608]{1,0:T(8,128)(2,1)S(1)} %collective-permute-done.14.refs_2_, ...), custom_call_target="tpu_custom_call" | custom-call | tf_op jit(solution)/shard_map/prepare/pallas_call | solution.py:98
  64.2 1.0 copy-done.6
  65.2 1.1 collective-permute-start.16
  66.3 0.1 compare_convert_fusion.mask_ref
  66.4 0.0 collective-permute-done.6.refs_3_
  66.4 0.0 collective-permute-done.11.refs_5_
  66.5 2.7 %collective-permute-done.16.refs_7_ = bf16[2,32,9216]{2,1,0:T(8,128)(2,1)} collective-permute-done((bf16[2,32,9216]{2,1,0:T(8,128)(2,1)}, bf16[2,32,9216]{2,1,0:T(8,128)(2,1)}, u32[]{:S(2)}, u32[]{:S(2)}) %collective-permute-start.16) | collective-permute-done | bytes 1179680 | tf_op jit(solution)/shard_map/ppermute | solution.py:261
  69.1 1.3 copy-done.1
  70.4 1.3 copy-done.3
  71.7 1.3 copy-done.5
  72.9 1.3 copy-done.7
  74.2 11.8 %products.4 = (f32[3,64,256]{2,1,0:T(8,128)S(1)}, bf16[3,64,256]{2,1,0:T(8,128)(2,1)S(1)}, bf16[3,64,256]{2,1,0:T(8,128)(2,1)S(1)}, bf16[3,64,256]{2,1,0:T(8,128)(2,1)S(1)}) custom-call(bf16[9,16,9216]{2,1,0:T(8,128)(2,1)S(1)} %band_matrices.1.x_ref, bf16[256,256]{1,0:T(8,128)(2,1)S(1)} %compare_convert_fusion.mask_ref, bf16[2,32,9216]{2,1,0:T(8,128)(2,1)S(1)} %copy-done.1, ...), custom_call_target="tpu_custom_call" | custom-call | flops 7247757312 | bytes 9437184 | tf_op jit(solution)/shard_map/products/pallas_call | solution.py:159
  86.0 0.1 collective-permute-start.20
  86.1 0.1 collective-permute-start.21
  86.2 3.7 %collective-permute-start.22 = (bf16[3,64,256]{2,1,0:T(8,128)(2,1)S(1)}, bf16[3,64,256]{2,1,0:T(8,128)(2,1)S(1)}, u32[]{:S(2)}, u32[]{:S(2)}) collective-permute-start(bf16[3,64,256]{2,1,0:T(8,128)(2,1)S(1)} %get-tuple-element.65), channel_id=1, source_target_pairs={{0,6},{1,7},{2,0},{3,1},{4,2},{5,3},{6,4},{7,5},{8,14},{9,15},{10,... | collective-permute-start | bytes 294920 | tf_op jit(solution)/shard_map/ppermute | solution.py:261
  89.9 16.9 %products.3 = (f32[5,64,256]{2,1,0:T(8,128)S(1)}, bf16[5,64,256]{2,1,0:T(8,128)(2,1)S(1)}, bf16[5,64,256]{2,1,0:T(8,128)(2,1)S(1)}, bf16[5,64,256]{2,1,0:T(8,128)(2,1)S(1)}) custom-call(bf16[9,16,9216]{2,1,0:T(8,128)(2,1)S(1)} %band_matrices.1.x_ref, bf16[256,256]{1,0:T(8,128)(2,1)S(1)} %compare_convert_fusion.mask_ref, bf16[2,32,9216]{2,1,0:T(8,128)(2,1)S(1)} %copy-done.1, ...), custom_call_target="tpu_custom_call" | custom-call | flops 12079595520 | bytes 9437184 | tf_op jit(solution)/shard_map/products/pallas_call | solution.py:159
  106.9 0.6 collective-permute-start.17
  107.5 1.5 %collective-permute-start.18 = (bf16[5,64,256]{2,1,0:T(8,128)(2,1)S(1)}, bf16[5,64,256]{2,1,0:T(8,128)(2,1)S(1)}, u32[]{:S(2)}, u32[]{:S(2)}) collective-permute-start(bf16[5,64,256]{2,1,0:T(8,128)(2,1)S(1)} %get-tuple-element.56), channel_id=1, source_target_pairs={{0,4},{1,5},{2,6},{3,7},{4,0},{5,1},{6,2},{7,3},{8,12},{9,13},{10,... | collective-permute-start | bytes 491528 | tf_op jit(solution)/shard_map/ppermute | solution.py:261
  109.0 0.0 collective-permute-done.20
  109.0 2.8 %collective-permute-start.19 = (bf16[5,64,256]{2,1,0:T(8,128)(2,1)S(1)}, bf16[5,64,256]{2,1,0:T(8,128)(2,1)S(1)}, u32[]{:S(2)}, u32[]{:S(2)}) collective-permute-start(bf16[5,64,256]{2,1,0:T(8,128)(2,1)S(1)} %get-tuple-element.57), channel_id=1, source_target_pairs={{0,6},{1,7},{2,0},{3,1},{4,2},{5,3},{6,4},{7,5},{8,14},{9,15},{10,... | collective-permute-start | bytes 491528 | tf_op jit(solution)/shard_map/ppermute | solution.py:261
  111.9 0.0 collective-permute-done.21
  112.0 0.1 collective-permute-start.27
  112.0 3.9 %collective-permute-done.17 = bf16[5,64,256]{2,1,0:T(8,128)(2,1)S(1)} collective-permute-done((bf16[5,64,256]{2,1,0:T(8,128)(2,1)S(1)}, bf16[5,64,256]{2,1,0:T(8,128)(2,1)S(1)}, u32[]{:S(2)}, u32[]{:S(2)}) %collective-permute-start.17) | collective-permute-done | bytes 163872 | tf_op jit(solution)/shard_map/ppermute | solution.py:261
  115.9 5.9 %collective-permute-done.18 = bf16[5,64,256]{2,1,0:T(8,128)(2,1)S(1)} collective-permute-done((bf16[5,64,256]{2,1,0:T(8,128)(2,1)S(1)}, bf16[5,64,256]{2,1,0:T(8,128)(2,1)S(1)}, u32[]{:S(2)}, u32[]{:S(2)}) %collective-permute-start.18) | collective-permute-done | bytes 163872 | tf_op jit(solution)/shard_map/ppermute | solution.py:261
  121.9 7.4 %products.5 = (f32[1,64,256]{2,1,0:T(8,128)S(1)}, bf16[1,64,256]{2,1,0:T(8,128)(2,1)S(1)}, bf16[1,64,256]{2,1,0:T(8,128)(2,1)S(1)}, bf16[1,64,256]{2,1,0:T(8,128)(2,1)S(1)}) custom-call(bf16[9,16,9216]{2,1,0:T(8,128)(2,1)S(1)} %band_matrices.1.x_ref, bf16[256,256]{1,0:T(8,128)(2,1)S(1)} %compare_convert_fusion.mask_ref, bf16[2,32,9216]{2,1,0:T(8,128)(2,1)S(1)} %copy-done.1, ...), custom_call_target="tpu_custom_call" | custom-call | flops 2415919104 | bytes 9437184 | tf_op jit(solution)/shard_map/products/pallas_call | solution.py:159
  129.2 3.3 %collective-permute-start.23 = (bf16[1,64,256]{2,1,0:T(8,128)(2,1)S(1)}, bf16[1,64,256]{2,1,0:T(8,128)(2,1)S(1)}, u32[]{:S(2)}, u32[]{:S(2)}) collective-permute-start(bf16[1,64,256]{2,1,0:T(8,128)(2,1)S(1)} %get-tuple-element.68), channel_id=1, source_target_pairs={{0,2},{1,3},{2,4},{3,5},{4,6},{5,7},{6,0},{7,1},{8,10},{9,11},{10,... | collective-permute-start | bytes 98312 | tf_op jit(solution)/shard_map/ppermute | solution.py:261
  132.6 1.4 %collective-permute-start.24 = (bf16[1,64,256]{2,1,0:T(8,128)(2,1)S(1)}, bf16[1,64,256]{2,1,0:T(8,128)(2,1)S(1)}, u32[]{:S(2)}, u32[]{:S(2)}) collective-permute-start(bf16[1,64,256]{2,1,0:T(8,128)(2,1)S(1)} %get-tuple-element.69), channel_id=1, source_target_pairs={{0,4},{1,5},{2,6},{3,7},{4,0},{5,1},{6,2},{7,3},{8,12},{9,13},{10,... | collective-permute-start | bytes 98312 | tf_op jit(solution)/shard_map/ppermute | solution.py:261
  134.0 1.0 collective-permute-start.25
  135.0 0.1 convert_add_fusion
  135.1 0.1 collective-permute-start.26
  135.2 0.5 collective-permute-done.23
  135.7 1.7 %collective-permute-done.24 = bf16[1,64,256]{2,1,0:T(8,128)(2,1)S(1)} collective-permute-done((bf16[1,64,256]{2,1,0:T(8,128)(2,1)S(1)}, bf16[1,64,256]{2,1,0:T(8,128)(2,1)S(1)}, u32[]{:S(2)}, u32[]{:S(2)}) %collective-permute-start.24) | collective-permute-done | bytes 32800 | tf_op jit(solution)/shard_map/ppermute | solution.py:261
  137.4 0.5 collective-permute-done.25
  138.0 0.1 collective-permute-start.28
  138.1 1.2 collective-permute-done.28
  139.3 0.9 maximum_select_fusion
  (36 shorter events, 0.2 us)
Async XLA Ops:
  0.0 9.3 %copy-start.10 = (s32[2,288]{1,0:T(2,128)S(1)}, s32[2,288]{1,0:T(2,128)}, u32[]{:S(2)}) copy-start(s32[2,288]{1,0:T(2,128)} %kq_ref.7) | copy-start | bytes 6916
  0.0 14.2 %copy-start.9 = (bf16[2,9,32,288]{3,2,1,0:T(8,128)(2,1)S(1)}, bf16[2,9,32,288]{3,2,1,0:T(8,128)(2,1)}, u32[]{:S(2)}) copy-start(bf16[2,9,32,288]{3,2,1,0:T(8,128)(2,1)} %coupling_ref.3) | copy-start | bytes 995332
  3.1 11.2 %collective-permute-start.1 = (bf16[9,32,288]{2,1,0:T(8,128)(2,1)}, bf16[9,32,288]{2,1,0:T(8,128)(2,1)S(1)}, u32[]{:S(2)}, u32[]{:S(2)}) collective-permute-start(bf16[9,32,288]{2,1,0:T(8,128)(2,1)} %get-tuple-element.39), channel_id=1, source_target_pairs={{0,1},{1,0},{2,3},{3,2},{4,5},{5,4},{6,7},{7,6},{8,9},{9,8},{10,11... | collective-permute-start | bytes 497672 | tf_op jit(solution)/shard_map/ppermute | solution.py:261
  3.6 14.4 %collective-permute-start = (bf16[32,4608]{1,0:T(8,128)(2,1)}, bf16[32,4608]{1,0:T(8,128)(2,1)S(1)}, u32[]{:S(2)}, u32[]{:S(2)}) collective-permute-start(bf16[32,4608]{1,0:T(8,128)(2,1)} %get-tuple-element.38), channel_id=1, source_target_pairs={{0,6},{1,7},{2,0},{3,1},{4,2},{5,3},{6,4},{7,5},{8,14},{9,15},{10,... | collective-permute-start | bytes 884744 | tf_op jit(solution)/shard_map/ppermute | solution.py:261
  8.3 25.9 %collective-permute-start.7 = (bf16[32,4608]{1,0:T(8,128)(2,1)}, bf16[32,4608]{1,0:T(8,128)(2,1)S(1)}, u32[]{:S(2)}, u32[]{:S(2)}) collective-permute-start(bf16[32,4608]{1,0:T(8,128)(2,1)} %get-tuple-element.48), channel_id=1, source_target_pairs={{0,4},{1,5},{2,6},{3,7},{4,0},{5,1},{6,2},{7,3},{8,12},{9,13},{10,... | collective-permute-start | bytes 884744 | tf_op jit(solution)/shard_map/ppermute | solution.py:261
  8.3 29.0 %collective-permute-start.12 = (bf16[32,4608]{1,0:T(8,128)(2,1)}, bf16[32,4608]{1,0:T(8,128)(2,1)S(1)}, u32[]{:S(2)}, u32[]{:S(2)}) collective-permute-start(bf16[32,4608]{1,0:T(8,128)(2,1)} %get-tuple-element.51), channel_id=1, source_target_pairs={{0,2},{1,3},{2,4},{3,5},{4,6},{5,7},{6,0},{7,1},{8,10},{9,11},{10,... | collective-permute-start | bytes 884744 | tf_op jit(solution)/shard_map/ppermute | solution.py:261
  9.3 1.3 copy-start.8
  13.1 1.1 copy-start
  18.0 19.8 %collective-permute-start.3 = (bf16[32,4608]{1,0:T(8,128)(2,1)S(1)}, bf16[32,4608]{1,0:T(8,128)(2,1)S(1)}, u32[]{:S(2)}, u32[]{:S(2)}) collective-permute-start(bf16[32,4608]{1,0:T(8,128)(2,1)S(1)} %collective-permute-done.refs_0_), channel_id=1, source_target_pairs={{0,8},{1,17},{2,10},{3,19},{4,12},{5,21},{6,14},{7,23},{8,0},{9,25... | collective-permute-start | bytes 884744 | tf_op jit(solution)/shard_map/ppermute | solution.py:261
  34.2 9.9 %collective-permute-start.8 = (bf16[32,4608]{1,0:T(8,128)(2,1)S(1)}, bf16[32,4608]{1,0:T(8,128)(2,1)S(1)}, u32[]{:S(2)}, u32[]{:S(2)}) collective-permute-start(bf16[32,4608]{1,0:T(8,128)(2,1)S(1)} %collective-permute-done.7.refs_0_), channel_id=1, source_target_pairs={{0,8},{1,17},{2,10},{3,19},{4,12},{5,21},{6,14},{7,23},{8,0},{9,25... | collective-permute-start | bytes 884744 | tf_op jit(solution)/shard_map/ppermute | solution.py:261
  35.7 9.9 %collective-permute-start.4 = (bf16[32,4608]{1,0:T(8,128)(2,1)S(1)}, bf16[32,4608]{1,0:T(8,128)(2,1)S(1)}, u32[]{:S(2)}, u32[]{:S(2)}) collective-permute-start(bf16[32,4608]{1,0:T(8,128)(2,1)S(1)} %collective-permute-done.refs_0_), channel_id=1, source_target_pairs={{0,16},{1,9},{2,18},{3,11},{4,20},{5,13},{6,22},{7,15},{8,24},{9,1... | collective-permute-start | bytes 884744 | tf_op jit(solution)/shard_map/ppermute | solution.py:261
  37.2 13.2 %collective-permute-start.13 = (bf16[32,4608]{1,0:T(8,128)(2,1)S(1)}, bf16[32,4608]{1,0:T(8,128)(2,1)S(1)}, u32[]{:S(2)}, u32[]{:S(2)}) collective-permute-start(bf16[32,4608]{1,0:T(8,128)(2,1)S(1)} %collective-permute-done.12.refs_0_), channel_id=1, source_target_pairs={{0,8},{1,17},{2,10},{3,19},{4,12},{5,21},{6,14},{7,23},{8,0},{9,25... | collective-permute-start | bytes 884744 | tf_op jit(solution)/shard_map/ppermute | solution.py:261
  37.7 14.2 %collective-permute-start.5 = (bf16[32,4608]{1,0:T(8,128)(2,1)S(1)}, bf16[32,4608]{1,0:T(8,128)(2,1)S(1)}, u32[]{:S(2)}, u32[]{:S(2)}) collective-permute-start(bf16[32,4608]{1,0:T(8,128)(2,1)S(1)} %collective-permute-done.3.refs_1_), channel_id=1, source_target_pairs={{0,16},{1,9},{2,18},{3,11},{4,20},{5,13},{6,22},{7,15},{8,24},{9,1... | collective-permute-start | bytes 884744 | tf_op jit(solution)/shard_map/ppermute | solution.py:261
  38.3 17.2 %collective-permute-start.9 = (bf16[32,4608]{1,0:T(8,128)(2,1)S(1)}, bf16[32,4608]{1,0:T(8,128)(2,1)S(1)}, u32[]{:S(2)}, u32[]{:S(2)}) collective-permute-start(bf16[32,4608]{1,0:T(8,128)(2,1)S(1)} %collective-permute-done.7.refs_0_), channel_id=1, source_target_pairs={{0,16},{1,9},{2,18},{3,11},{4,20},{5,13},{6,22},{7,15},{8,24},{9,1... | collective-permute-start | bytes 884744 | tf_op jit(solution)/shard_map/ppermute | solution.py:261
  44.1 11.9 %collective-permute-start.10 = (bf16[32,4608]{1,0:T(8,128)(2,1)S(1)}, bf16[32,4608]{1,0:T(8,128)(2,1)S(1)}, u32[]{:S(2)}, u32[]{:S(2)}) collective-permute-start(bf16[32,4608]{1,0:T(8,128)(2,1)S(1)} %collective-permute-done.8.refs_1_), channel_id=1, source_target_pairs={{0,16},{1,9},{2,18},{3,11},{4,20},{5,13},{6,22},{7,15},{8,24},{9,1... | collective-permute-start | bytes 884744 | tf_op jit(solution)/shard_map/ppermute | solution.py:261
  45.6 14.8 %collective-permute-start.14 = (bf16[32,4608]{1,0:T(8,128)(2,1)S(1)}, bf16[32,4608]{1,0:T(8,128)(2,1)S(1)}, u32[]{:S(2)}, u32[]{:S(2)}) collective-permute-start(bf16[32,4608]{1,0:T(8,128)(2,1)S(1)} %collective-permute-done.12.refs_0_), channel_id=1, source_target_pairs={{0,16},{1,9},{2,18},{3,11},{4,20},{5,13},{6,22},{7,15},{8,24},{9,1... | collective-permute-start | bytes 884744 | tf_op jit(solution)/shard_map/ppermute | solution.py:261
  50.4 11.3 %collective-permute-start.15 = (bf16[32,4608]{1,0:T(8,128)(2,1)S(1)}, bf16[32,4608]{1,0:T(8,128)(2,1)S(1)}, u32[]{:S(2)}, u32[]{:S(2)}) collective-permute-start(bf16[32,4608]{1,0:T(8,128)(2,1)S(1)} %collective-permute-done.13.refs_1_), channel_id=1, source_target_pairs={{0,16},{1,9},{2,18},{3,11},{4,20},{5,13},{6,22},{7,15},{8,24},{9,1... | collective-permute-start | bytes 884744 | tf_op jit(solution)/shard_map/ppermute | solution.py:261
  51.9 14.5 %collective-permute-start.2 = (bf16[2,32,9216]{2,1,0:T(8,128)(2,1)}, bf16[2,32,9216]{2,1,0:T(8,128)(2,1)}, u32[]{:S(2)}, u32[]{:S(2)}) collective-permute-start(bf16[2,32,9216]{2,1,0:T(8,128)(2,1)} %get-tuple-element.44), channel_id=1, source_target_pairs={{0,1},{1,0},{2,3},{3,2},{4,5},{5,4},{6,7},{7,6},{8,9},{9,8},{10,11... | collective-permute-start | bytes 3538952 | tf_op jit(solution)/shard_map/ppermute | solution.py:261
  54.5 1.0 copy-start.2
  55.5 11.0 %collective-permute-start.6 = (bf16[2,32,9216]{2,1,0:T(8,128)(2,1)}, bf16[2,32,9216]{2,1,0:T(8,128)(2,1)}, u32[]{:S(2)}, u32[]{:S(2)}) collective-permute-start(bf16[2,32,9216]{2,1,0:T(8,128)(2,1)} %get-tuple-element.47), channel_id=1, source_target_pairs={{0,1},{1,0},{2,3},{3,2},{4,5},{5,4},{6,7},{7,6},{8,9},{9,8},{10,11... | collective-permute-start | bytes 3538952 | tf_op jit(solution)/shard_map/ppermute | solution.py:261
  58.6 1.0 copy-start.4
  59.6 6.8 %collective-permute-start.11 = (bf16[2,32,9216]{2,1,0:T(8,128)(2,1)}, bf16[2,32,9216]{2,1,0:T(8,128)(2,1)}, u32[]{:S(2)}, u32[]{:S(2)}) collective-permute-start(bf16[2,32,9216]{2,1,0:T(8,128)(2,1)} %get-tuple-element.50), channel_id=1, source_target_pairs={{0,1},{1,0},{2,3},{3,2},{4,5},{5,4},{6,7},{7,6},{8,9},{9,8},{10,11... | collective-permute-start | bytes 3538952 | tf_op jit(solution)/shard_map/ppermute | solution.py:261
  64.2 1.0 copy-start.6
  65.2 3.9 %collective-permute-start.16 = (bf16[2,32,9216]{2,1,0:T(8,128)(2,1)}, bf16[2,32,9216]{2,1,0:T(8,128)(2,1)}, u32[]{:S(2)}, u32[]{:S(2)}) collective-permute-start(bf16[2,32,9216]{2,1,0:T(8,128)(2,1)} %get-tuple-element.53), channel_id=1, source_target_pairs={{0,1},{1,0},{2,3},{3,2},{4,5},{5,4},{6,7},{7,6},{8,9},{9,8},{10,11... | collective-permute-start | bytes 3538952 | tf_op jit(solution)/shard_map/ppermute | solution.py:261
  69.1 1.3 copy-start.1
  70.4 1.3 copy-start.3
  71.7 1.3 copy-start.5
  72.9 1.3 copy-start.7
  86.0 23.0 %collective-permute-start.20 = (bf16[3,64,256]{2,1,0:T(8,128)(2,1)S(1)}, bf16[3,64,256]{2,1,0:T(8,128)(2,1)S(1)}, u32[]{:S(2)}, u32[]{:S(2)}) collective-permute-start(bf16[3,64,256]{2,1,0:T(8,128)(2,1)S(1)} %get-tuple-element.63), channel_id=1, source_target_pairs={{0,2},{1,3},{2,4},{3,5},{4,6},{5,7},{6,0},{7,1},{8,10},{9,11},{10,... | collective-permute-start | bytes 294920 | tf_op jit(solution)/shard_map/ppermute | solution.py:261
  86.1 25.8 %collective-permute-start.21 = (bf16[3,64,256]{2,1,0:T(8,128)(2,1)S(1)}, bf16[3,64,256]{2,1,0:T(8,128)(2,1)S(1)}, u32[]{:S(2)}, u32[]{:S(2)}) collective-permute-start(bf16[3,64,256]{2,1,0:T(8,128)(2,1)S(1)} %get-tuple-element.64), channel_id=1, source_target_pairs={{0,4},{1,5},{2,6},{3,7},{4,0},{5,1},{6,2},{7,3},{8,12},{9,13},{10,... | collective-permute-start | bytes 294920 | tf_op jit(solution)/shard_map/ppermute | solution.py:261
  86.2 25.7 %collective-permute-start.22 = (bf16[3,64,256]{2,1,0:T(8,128)(2,1)S(1)}, bf16[3,64,256]{2,1,0:T(8,128)(2,1)S(1)}, u32[]{:S(2)}, u32[]{:S(2)}) collective-permute-start(bf16[3,64,256]{2,1,0:T(8,128)(2,1)S(1)} %get-tuple-element.65), channel_id=1, source_target_pairs={{0,6},{1,7},{2,0},{3,1},{4,2},{5,3},{6,4},{7,5},{8,14},{9,15},{10,... | collective-permute-start | bytes 294920 | tf_op jit(solution)/shard_map/ppermute | solution.py:261
  106.9 9.0 %collective-permute-start.17 = (bf16[5,64,256]{2,1,0:T(8,128)(2,1)S(1)}, bf16[5,64,256]{2,1,0:T(8,128)(2,1)S(1)}, u32[]{:S(2)}, u32[]{:S(2)}) collective-permute-start(bf16[5,64,256]{2,1,0:T(8,128)(2,1)S(1)} %get-tuple-element.55), channel_id=1, source_target_pairs={{0,2},{1,3},{2,4},{3,5},{4,6},{5,7},{6,0},{7,1},{8,10},{9,11},{10,... | collective-permute-start | bytes 491528 | tf_op jit(solution)/shard_map/ppermute | solution.py:261
  107.5 14.4 %collective-permute-start.18 = (bf16[5,64,256]{2,1,0:T(8,128)(2,1)S(1)}, bf16[5,64,256]{2,1,0:T(8,128)(2,1)S(1)}, u32[]{:S(2)}, u32[]{:S(2)}) collective-permute-start(bf16[5,64,256]{2,1,0:T(8,128)(2,1)S(1)} %get-tuple-element.56), channel_id=1, source_target_pairs={{0,4},{1,5},{2,6},{3,7},{4,0},{5,1},{6,2},{7,3},{8,12},{9,13},{10,... | collective-permute-start | bytes 491528 | tf_op jit(solution)/shard_map/ppermute | solution.py:261
  109.0 12.8 %collective-permute-start.19 = (bf16[5,64,256]{2,1,0:T(8,128)(2,1)S(1)}, bf16[5,64,256]{2,1,0:T(8,128)(2,1)S(1)}, u32[]{:S(2)}, u32[]{:S(2)}) collective-permute-start(bf16[5,64,256]{2,1,0:T(8,128)(2,1)S(1)} %get-tuple-element.57), channel_id=1, source_target_pairs={{0,6},{1,7},{2,0},{3,1},{4,2},{5,3},{6,4},{7,5},{8,14},{9,15},{10,... | collective-permute-start | bytes 491528 | tf_op jit(solution)/shard_map/ppermute | solution.py:261
  112.0 26.1 %collective-permute-start.27 = (f32[3,32,256]{2,1,0:T(8,128)S(1)}, f32[3,32,256]{2,1,0:T(8,128)S(1)}, u32[]{:S(2)}, u32[]{:S(2)}) collective-permute-start(f32[3,32,256]{2,1,0:T(8,128)S(1)} %get-tuple-element.74), channel_id=1, source_target_pairs={{0,1},{1,0},{2,3},{3,2},{4,5},{5,4},{6,7},{7,6},{8,9},{9,8},{10,11... | collective-permute-start | bytes 294920 | tf_op jit(solution)/shard_map/ppermute | solution.py:261
  129.2 6.4 %collective-permute-start.23 = (bf16[1,64,256]{2,1,0:T(8,128)(2,1)S(1)}, bf16[1,64,256]{2,1,0:T(8,128)(2,1)S(1)}, u32[]{:S(2)}, u32[]{:S(2)}) collective-permute-start(bf16[1,64,256]{2,1,0:T(8,128)(2,1)S(1)} %get-tuple-element.68), channel_id=1, source_target_pairs={{0,2},{1,3},{2,4},{3,5},{4,6},{5,7},{6,0},{7,1},{8,10},{9,11},{10,... | collective-permute-start | bytes 98312 | tf_op jit(solution)/shard_map/ppermute | solution.py:261
  132.6 4.8 %collective-permute-start.24 = (bf16[1,64,256]{2,1,0:T(8,128)(2,1)S(1)}, bf16[1,64,256]{2,1,0:T(8,128)(2,1)S(1)}, u32[]{:S(2)}, u32[]{:S(2)}) collective-permute-start(bf16[1,64,256]{2,1,0:T(8,128)(2,1)S(1)} %get-tuple-element.69), channel_id=1, source_target_pairs={{0,4},{1,5},{2,6},{3,7},{4,0},{5,1},{6,2},{7,3},{8,12},{9,13},{10,... | collective-permute-start | bytes 98312 | tf_op jit(solution)/shard_map/ppermute | solution.py:261
  134.0 3.9 %collective-permute-start.25 = (bf16[1,64,256]{2,1,0:T(8,128)(2,1)S(1)}, bf16[1,64,256]{2,1,0:T(8,128)(2,1)S(1)}, u32[]{:S(2)}, u32[]{:S(2)}) collective-permute-start(bf16[1,64,256]{2,1,0:T(8,128)(2,1)S(1)} %get-tuple-element.70), channel_id=1, source_target_pairs={{0,6},{1,7},{2,0},{3,1},{4,2},{5,3},{6,4},{7,5},{8,14},{9,15},{10,... | collective-permute-start | bytes 98312 | tf_op jit(solution)/shard_map/ppermute | solution.py:261
  135.1 4.1 %collective-permute-start.26 = (f32[5,32,256]{2,1,0:T(8,128)S(1)}, f32[5,32,256]{2,1,0:T(8,128)S(1)}, u32[]{:S(2)}, u32[]{:S(2)}) collective-permute-start(f32[5,32,256]{2,1,0:T(8,128)S(1)} %get-tuple-element.72), channel_id=1, source_target_pairs={{0,1},{1,0},{2,3},{3,2},{4,5},{5,4},{6,7},{7,6},{8,9},{9,8},{10,11... | collective-permute-start | bytes 491528 | tf_op jit(solution)/shard_map/ppermute | solution.py:261
  138.0 1.3 collective-permute-start.28

commit v4 on v3

--- a/solution.py
+++ b/solution.py
@@ -12,6 +12,7 @@
 BANDS = 16
 LINE = KY * BANDS
 GROUPS = (5, 8)
+VMEM_ALL = 56 << 20
 F32 = jnp.float32
 BF16 = jnp.bfloat16
 
@@ -23,22 +24,32 @@
 def place():
     ka = lax.axis_index("ka")
     return lax.axis_index("pb"), ka // 2, ka % 2
+
+
+def turns_of(kq_ref, q, block_lines, lines_all):
+    _, z, core = place()
+    origin = kq_ref[q, 0]
+    step = lax.rem(origin // KY - (2 * z + core) * block_lines + block_lines + lines_all, lines_all) - block_lines
+    base = jnp.where(step < 0, block_lines, 0)
+    return base, base + step, lax.rem(LINE - lax.rem(origin, KY) * BANDS, LINE)
 
 
 def cut_kernel(block, env_ref, coupling_ref, *refs):
     pieces, (window, give, sems) = refs[:-3], refs[-3:]
     n_z = len(pieces) + 1
     pb, z, core = place()
-
-    def lanes(index):
-        return pl.ds(pl.multiple_of(lax.rem(index + 2 * n_z, 2 * n_z) * block, 128), block)
+    part = block // 4
+
+    def lanes(chip, index):
+        return pl.ds(pl.multiple_of(lax.rem(8 * chip + index, 8 * n_z) * part, 128), part)
 
     jobs = []
     for e in range(1, n_z):
         to = lax.rem(z - e + n_z, n_z)
-        jobs.append((env_ref.at[:, lanes(2 * to - 1 + pb)], pieces[e - 1]))
-    for w in range(4):
-        jobs.append((env_ref.at[:, lanes(2 * z - 1 + w)], window.at[:, w * block : (w + 1) * block]))
+        for i in range(3):
+            jobs.append((env_ref.at[:, lanes(to, 3 * pb + i)], pieces[e - 1].at[:, i * part : (i + 1) * part]))
+    for i in range(12):
+        jobs.append((env_ref.at[:, lanes(z, i)], window.at[:, i * part : (i + 1) * part]))
     jobs.append((coupling_ref.at[1 - core], give))
     copies = [pltpu.make_async_copy(src, dst, sems.at[i]) for i, (src, dst) in enumerate(jobs)]
     for copy in copies:
@@ -50,61 +61,59 @@
 def cut(envelopes, coupling, n_z, block):
     rows = envelopes.shape[0]
     shape = functools.partial(jax.ShapeDtypeStruct, dtype=BF16)
-    outs = [shape((rows, block))] * (n_z - 1) + [shape((rows, 4 * block)), shape(coupling.shape[1:])]
+    outs = [shape((rows, 3 * block // 4))] * (n_z - 1) + [shape((rows, 3 * block)), shape(coupling.shape[1:])]
     *pieces, window, give = pl.pallas_call(
         functools.partial(cut_kernel, block),
         in_specs=[pl.BlockSpec(memory_space=pl.ANY)] * 2,
         out_specs=[pl.BlockSpec(memory_space=pltpu.VMEM)] * len(outs),
         out_shape=outs,
-        scratch_shapes=[pltpu.SemaphoreType.DMA((n_z + 4,))],
+        scratch_shapes=[pltpu.SemaphoreType.DMA((3 * n_z + 10,))],
         name="cut",
     )(envelopes, coupling)
     return pieces, window, give
 
 
-def prep_kernel(block, lines, lines_all, kq_ref, *refs):
+def prep_kernel(lines_all, kq_ref, *refs):
     ins, (keep_ref, give_ref, window, sems) = refs[:-4], refs[-4:]
-    pb, z, core = place()
-    copies = []
-    for index, src in enumerate(ins):
-        offset = 0
-        if len(ins) > 1:
-            rel = (0, 1 + core, 2 - core, 3)[index]
-            offset = pl.multiple_of((pb ^ rel) * block, 128)
-        copy = pltpu.make_async_copy(src, window.at[:, pl.ds(offset, src.shape[1])], sems.at[index])
-        copy.start()
-        copies.append(copy)
-    for copy in copies:
-        copy.wait()
-    half = lines // 2
-    turns = []
-    for q in (core, 1 - core):
-        origin = kq_ref[q, 0]
-        start_line = lax.rem(origin // KY - (2 * z + core) * half + half + lines_all, lines_all)
-        turns.append((start_line, lax.rem(LINE - lax.rem(origin, KY) * BANDS, LINE)))
-    for line in range(lines):
-        to = slice(line * LINE, (line + 1) * LINE)
-        own = window[:, (half + line) * LINE : (half + line + 1) * LINE]
-        for out_ref, (start_line, turn) in zip((keep_ref, give_ref), turns):
-            out_ref[0, :, to] = own
-            lane = pl.multiple_of((start_line + line) * LINE, 128)
-            shifted = window[:, pl.ds(lane, LINE)].astype(F32)
-            out_ref[1, :, to] = pltpu.roll(shifted, turn, 1).astype(BF16)
-
-
-def prepare(kq_map, ins, block, lines, lines_all):
-    rows = ins[0].shape[0]
+    pb, _, core = place()
+    line = pl.program_id(0)
+    block_lines = pl.num_programs(0) // 2
+
+    @pl.when(line == 0)
+    def _():
+        copies = []
+        for index, src in enumerate(ins):
+            offset, size = 0, src.shape[1]
+            if len(ins) > 1:
+                rel = (0, 1 + core, 2 - core, 3)[index]
+                offset = pl.multiple_of((pb ^ rel) * size, 128)
+            copy = pltpu.make_async_copy(src, window.at[:, pl.ds(offset, size)], sems.at[index])
+            copy.start()
+            copies.append(copy)
+        for copy in copies:
+            copy.wait()
+
+    for out_ref, q in ((keep_ref, core), (give_ref, 1 - core)):
+        base, image, turn = turns_of(kq_ref, q, block_lines, lines_all)
+        out_ref[0] = window[:, pl.ds(pl.multiple_of((base + line) * LINE, 128), LINE)]
+        shifted = window[:, pl.ds(pl.multiple_of((image + line) * LINE, 128), LINE)].astype(F32)
+        out_ref[1] = pltpu.roll(shifted, turn, 1).astype(BF16)
+
+
+def prepare(kq_map, ins, block, lines_all):
+    rows, lines = ins[0].shape[0], 2 * block // LINE
     out = jax.ShapeDtypeStruct((2, rows, lines * LINE), BF16)
     return pl.pallas_call(
-        functools.partial(prep_kernel, block, lines, lines_all),
+        functools.partial(prep_kernel, lines_all),
+        grid=(lines,),
         in_specs=[pl.BlockSpec(memory_space=pltpu.SMEM)] + [pl.BlockSpec(memory_space=pl.ANY)] * len(ins),
-        out_specs=[pl.BlockSpec(memory_space=pltpu.VMEM)] * 2,
+        out_specs=[pl.BlockSpec((2, rows, LINE), lambda i: (0, 0, i))] * 2,
         out_shape=[out, out],
         scratch_shapes=[
-            pltpu.VMEM((rows, 2 * lines * LINE), BF16),
+            pltpu.VMEM((rows, 3 * block), BF16),
             pltpu.SemaphoreType.DMA((len(ins),)),
         ],
-        compiler_params=pltpu.CompilerParams(vmem_limit_bytes=24 << 20),
+        compiler_params=pltpu.CompilerParams(vmem_limit_bytes=VMEM_ALL),
         name="prepare",
     )(kq_map, *ins)
 
@@ -167,7 +176,7 @@
         out_specs=[piece] * (sources // 2),
         out_shape=[jax.ShapeDtypeStruct(shape, F32 if i == 0 else BF16) for i in range(sources // 2)],
         scratch_shapes=[pltpu.VMEM((branches, states, states), F32)],
-        compiler_params=pltpu.CompilerParams(vmem_limit_bytes=40 << 20),
+        compiler_params=pltpu.CompilerParams(vmem_limit_bytes=VMEM_ALL),
         cost_estimate=pl.CostEstimate(
             flops=4 * branches * states * states * lines * LINE,
             bytes_accessed=4 * states * lines * LINE,
@@ -177,7 +186,7 @@
     )(x, mask, *amps)
 
 
-def band_kernel(coupling_ref, other_ref, x_ref):
+def band_kernel(block_lines, lines_all, kq_ref, coupling_ref, other_ref, next_ref, x_ref):
     branches, _, count = other_ref.shape
     half = BANDS // 4
     size = min(count, 128)
@@ -203,10 +212,15 @@
     keep_cond = (row // half == lane // half).astype(F32)
     keep_val = (row % half == lane % half).astype(F32)
     _, _, core = place()
-    for mine in (True, False):
-        tables = [coupling_ref[core, branch] if mine else other_ref[branch] for branch in range(branches)]
-        terms = [contract(pick, table, 1, 0).astype(BF16) for table in tables]
-        base = (core if mine else 1 - core) * (count * BANDS)
+    base, _, _ = turns_of(kq_ref, core, block_lines, lines_all)
+    late = jnp.where(base > 0, 1, 0)
+    for part in range(2):
+        block = part + late
+        terms = []
+        for branch in range(branches):
+            table = jnp.where(block == core, coupling_ref[core, branch], other_ref[branch])
+            table = jnp.where(block == 2, next_ref[branch], table)
+            terms.append(contract(pick, table, 1, 0).astype(BF16))
         for start in range(0, count, size):
             width = min(size, count - start)
             lanes = width * BANDS
@@ -224,22 +238,22 @@
                     rows.append(jnp.concatenate(slabs, axis=1))
                 values.append(contract(jnp.concatenate(rows, axis=0), spread[kind][:, :lanes], 1, 0))
             total = (values[0] * keep_cond[:, :lanes] - values[1] * keep_val[:, :lanes]).astype(BF16)
-            at = pl.multiple_of(base + start * BANDS, 128)
+            at = (part * count + start) * BANDS
             for branch in range(branches):
-                x_ref[branch, :, pl.ds(at, lanes)] = total[branch * BANDS : (branch + 1) * BANDS]
-
-
-def band_matrices(coupling, other):
+                x_ref[branch, :, at : at + lanes] = total[branch * BANDS : (branch + 1) * BANDS]
+
+
+def band_matrices(kq_map, coupling, other, following, lines_all):
     branches, _, count = other.shape
     return pl.pallas_call(
-        band_kernel,
-        in_specs=[pl.BlockSpec(memory_space=pltpu.VMEM)] * 2,
+        functools.partial(band_kernel, count // KY, lines_all),
+        in_specs=[pl.BlockSpec(memory_space=pltpu.SMEM)] + [pl.BlockSpec(memory_space=pltpu.VMEM)] * 3,
         out_specs=pl.BlockSpec(memory_space=pltpu.VMEM),
         out_shape=jax.ShapeDtypeStruct((branches, BANDS, 2 * count * BANDS), BF16),
         compiler_params=pltpu.CompilerParams(vmem_limit_bytes=40 << 20),
         cost_estimate=pl.CostEstimate(flops=10**10, bytes_accessed=10**6, transcendentals=0),
         name="band_matrices",
-    )(coupling, other)
+    )(kq_map, coupling, other, following)
 
 
 def shards(envelopes, coupling, kq_map):
@@ -248,7 +262,7 @@
     n_z = n_ka // 2
     rows, width = envelopes.shape
     block = width // n_ka
-    lines, lines_all = 2 * block // LINE, width // LINE
+    lines_all = width // LINE
     branches = coupling.shape[1]
     core = lax.axis_index("ka") % 2
 
@@ -263,21 +277,33 @@
     def sibling(x):
         return permute(x, lambda p, zz, c: (p, zz, 1 - c))
 
+    def passed_down(e):
+        return lambda x: permute(x, lambda p, zz, c: (p, zz - e, c))
+
     pieces, window, give = cut(envelopes, coupling, n_z, block)
-    arrived = []
-    for e in range(1, n_z):
-        arrived.append(permute(pieces[e - 1], lambda p, zz, c: (p, zz - e, c)))
-    keep, pass_on = prepare(kq_map, [window], block, lines, lines_all)
-    amps = [keep, sibling(pass_on)]
-    x = band_matrices(coupling, sibling(give))
-    arrived[0], x, amps[0] = lax.optimization_barrier((arrived[0], x, amps[0]))
-
-    for piece in arrived:
+    near = sorted({1, n_z - 1})
+    far = [e for e in range(2, n_z - 1)]
+    arrived = {e: passed_down(e)(pieces[e - 1]) for e in near}
+    other_table = sibling(give)
+    first_table = jnp.where(core == 0, lax.dynamic_index_in_dim(coupling, core, 0, keepdims=False), other_table)
+    next_table = passed_down(1)(first_table)
+    keep, pass_on = prepare(kq_map, [window], block, lines_all)
+    waiting = [pieces[e - 1] for e in far]
+    keep, pass_on, *waiting = lax.optimization_barrier((keep, pass_on, *waiting))
+    for e, piece in zip(far, waiting):
+        arrived[e] = passed_down(e)(piece)
+    amps = {0: (keep, sibling(pass_on))}
+    x = band_matrices(kq_map, coupling, other_table, next_table, lines_all)
+    arrived[1], x = lax.optimization_barrier((arrived[1], x))
+
+    for e in near + far:
+        piece = arrived[e]
         one = permute(piece, lambda p, zz, c: (p ^ (1 + c), zz, c))
         two = permute(piece, lambda p, zz, c: (p ^ (2 - c), zz, c))
         three = permute(one, lambda p, zz, c: (p ^ (2 - c), zz, c))
-        keep, pass_on = prepare(kq_map, [piece, one, two, three], block, lines, lines_all)
-        amps += [keep, sibling(pass_on)]
+        keep, pass_on = prepare(kq_map, [piece, one, two, three], block, lines_all)
+        amps[e] = (keep, sibling(pass_on))
+    amps = [half for e in range(n_z) for half in amps[e]]
 
     index = jnp.arange(256, dtype=jnp.int32) // BANDS
     mask = (index[:, None] == index[None, :]).astype(BF16)
@@ -288,6 +314,7 @@
         if len(received) >= 2:
             received[-2], x = lax.optimization_barrier((received[-2], x))
         own, *sends = products(x, mask, amps, lo, hi - lo, factor)
+        own, x = lax.optimization_barrier((own, x))
         received.append([own] + [permute(p, lambda p, zz, c: (p, zz + e, c)) for e, p in enumerate(sends, 1)])
     for parts in received:
         total = parts[0]

time: 141 us -> 150 us (1.064)
  Pallas kernels: 53.1 us -> 68.2 us
  waiting for transfers between devices: 40 us -> 29.4 us
  starting transfers between devices: 35.2 us -> 42.8 us
  local copies, waits for them, and re-layouts: 10.5 us -> 5.88 us
  other arithmetic: 1.15 us -> 2.76 us
    pallas_call x5, Pallas kernels: 13.9 us -> 24.7 us  [the longest x4 20.3 us: prepare(): pl.pallas_call(functools.partial(prep_kernel, lines_all), grid=(lines,),...]
    ppermute x29 -> x30, waiting for transfers between devices: 40 us -> 29.4 us  [permute(): return lax.ppermute(x, ('pb', 'ka'), pairs)]
    ppermute x29 -> x30, starting transfers between devices: 35.2 us -> 42.8 us  [permute(): return lax.ppermute(x, ('pb', 'ka'), pairs)]
    unnamed x22 -> x52, local copies, waits for them, and re-layouts: 10.4 us -> 5.84 us
    pallas_call x3, Pallas kernels: 36.1 us -> 40.6 us  [products(): pl.pallas_call(functools.partial(main_kernel, sources, first, branches, f...]
  transfers between devices with their start and end apart: 29 -> 30, of which waited for: 11 -> 8; matrix products, arithmetic and copies ran while one was open for 0% -> 1% of each run, Pallas kernels for 27% -> 23%
where the time goes in v4:
time: 150 us; the launch traced here: 149 us
  Pallas kernels  68.2 us (45%)
  starting transfers between devices  42.8 us (29%)
  waiting for transfers between devices  29.4 us (20%)
  local copies, waits for them, and re-layouts  5.88 us (4%)
  other arithmetic  2.76 us (2%)
    ppermute x30, starting transfers between devices, permute(): return lax.ppermute(x, ('pb', 'ka'), pairs)  42.8 us
    pallas_call x3, Pallas kernels, products(): pl.pallas_call(functools.partial(main_kernel, sources, first, branches, f...  40.6 us
    ppermute x30, waiting for transfers between devices, permute(): return lax.ppermute(x, ('pb', 'ka'), pairs)  29.4 us
    pallas_call x4, Pallas kernels, prepare(): pl.pallas_call(functools.partial(prep_kernel, lines_all), grid=(lines,),...  20.3 us
    unnamed x52, local copies, waits for them, and re-layouts  5.84 us
    pallas_call x1, Pallas kernels, band_matrices(): pl.pallas_call(functools.partial(band_kernel, count // KY, lines_all), in...  4.34 us
  transfers between devices with their start and end apart: 30, of which 8 were waited for; matrix products, arithmetic and copies ran while one was open for 1% of the time, Pallas kernels for 23%

profile of v4, /device:TPU:0, one launch (start us, length us, event | category | flops | bytes accessed | tf_op | source)
XLA Modules:
  0.0 149.4 jit_solution(3228035114517991166)
XLA Ops:
  0.0 3.0 %cut.1 = (bf16[32,3456]{1,0:T(8,128)(2,1)}, bf16[32,3456]{1,0:T(8,128)(2,1)}, bf16[32,3456]{1,0:T(8,128)(2,1)}, bf16[32,13824]{1,0:T(8,128)(2,1)}, bf16[9,32,288]{2,1,0:T(8,128)(2,1)}) custom-call(bf16[32,36864]{1,0:T(8,128)(2,1)} %env_ref.1, bf16[2,9,32,288]{3,2,1,0:T(8,128)(2,1)} %coupling_ref.3), custom_call_target="tpu_custom_call" | custom-call | tf_op jit(solution)/shard_map/cut/pallas_call | solution.py:65
  3.0 0.0 copy-start.22
  3.0 0.0 copy-start.2
  3.0 0.5 collective-permute-start.1
  3.5 2.6 %collective-permute-start.13 = (bf16[32,3456]{1,0:T(8,128)(2,1)}, bf16[32,3456]{1,0:T(8,128)(2,1)S(1)}, u32[]{:S(2)}, u32[]{:S(2)}) collective-permute-start(bf16[32,3456]{1,0:T(8,128)(2,1)} %get-tuple-element.60), channel_id=1, source_target_pairs={{0,2},{1,3},{2,4},{3,5},{4,6},{5,7},{6,0},{7,1},{8,10},{9,11},{10,... | collective-permute-start | bytes 663560 | tf_op jit(solution)/shard_map/ppermute | solution.py:275
  6.2 4.9 %prepare.4 = (bf16[2,32,9216]{2,1,0:T(8,128)(2,1)}, bf16[2,32,9216]{2,1,0:T(8,128)(2,1)}) custom-call(s32[2,288]{1,0:T(2,128)} %kq_ref.9, bf16[32,13824]{1,0:T(8,128)(2,1)} %get-tuple-element.48.refs_0_), custom_call_target="tpu_custom_call" | custom-call | tf_op jit(solution)/shard_map/prepare/pallas_call | solution.py:106
  11.1 2.7 %collective-permute-start.8 = (bf16[32,3456]{1,0:T(8,128)(2,1)}, bf16[32,3456]{1,0:T(8,128)(2,1)S(1)}, u32[]{:S(2)}, u32[]{:S(2)}) collective-permute-start(bf16[32,3456]{1,0:T(8,128)(2,1)} %get-tuple-element.57), channel_id=1, source_target_pairs={{0,4},{1,5},{2,6},{3,7},{4,0},{5,1},{6,2},{7,3},{8,12},{9,13},{10,... | collective-permute-start | bytes 663560 | tf_op jit(solution)/shard_map/ppermute | solution.py:275
  13.8 0.0 collective-permute-done.1.other_ref
  13.8 1.4 collective-permute-start.2
  15.2 0.4 collective-permute-start
  15.7 1.5 %collective-permute-start.15 = (bf16[32,3456]{1,0:T(8,128)(2,1)S(1)}, bf16[32,3456]{1,0:T(8,128)(2,1)S(1)}, u32[]{:S(2)}, u32[]{:S(2)}) collective-permute-start(bf16[32,3456]{1,0:T(8,128)(2,1)S(1)} %collective-permute-done.13.refs_0_), channel_id=1, source_target_pairs={{0,16},{1,9},{2,18},{3,11},{4,20},{5,13},{6,22},{7,15},{8,24},{9,1... | collective-permute-start | bytes 663560 | tf_op jit(solution)/shard_map/ppermute | solution.py:275
  17.2 1.5 collective-permute-start.14
  18.7 6.7 %collective-permute-done.8.refs_0_ = bf16[32,3456]{1,0:T(8,128)(2,1)S(1)} collective-permute-done((bf16[32,3456]{1,0:T(8,128)(2,1)}, bf16[32,3456]{1,0:T(8,128)(2,1)S(1)}, u32[]{:S(2)}, u32[]{:S(2)}) %collective-permute-start.8) | collective-permute-done | bytes 221216 | tf_op jit(solution)/shard_map/ppermute | solution.py:275
  25.3 1.5 collective-permute-start.9
  26.8 0.0 collective-permute-done.2.next_ref
  26.8 4.3 %band_matrices.1.x_ref = bf16[9,16,9216]{2,1,0:T(8,128)(2,1)S(1)} custom-call(s32[2,288]{1,0:T(2,128)S(1)} %copy-done.2, bf16[2,9,32,288]{3,2,1,0:T(8,128)(2,1)S(1)} %copy-done.1, bf16[9,32,288]{2,1,0:T(8,128)(2,1)S(1)} %collective-permute-done.1.other_ref, bf16[9,32,288]{2,1,0:T(8,128)(2,1)S(1)} %collective-permute-done.2.next_ref), custom_call_target="tpu_custom_call" | custom-call | flops 10000000000 | bytes 1000000 | tf_op jit(solution)/shard_map/band_matrices/pallas_call | solution.py:248
  31.2 1.5 copy-done
  32.7 0.0 collective-permute-done.refs_0_
  32.7 0.5 collective-permute-start.4
  33.2 0.0 collective-permute-done.14.refs_1_
  33.2 1.5 %collective-permute-start.16 = (bf16[32,3456]{1,0:T(8,128)(2,1)S(1)}, bf16[32,3456]{1,0:T(8,128)(2,1)S(1)}, u32[]{:S(2)}, u32[]{:S(2)}) collective-permute-start(bf16[32,3456]{1,0:T(8,128)(2,1)S(1)} %collective-permute-done.14.refs_1_), channel_id=1, source_target_pairs={{0,16},{1,9},{2,18},{3,11},{4,20},{5,13},{6,22},{7,15},{8,24},{9,1... | collective-permute-start | bytes 663560 | tf_op jit(solution)/shard_map/ppermute | solution.py:275
  34.7 0.5 collective-permute-start.10
  35.3 1.5 %collective-permute-start.11 = (bf16[32,3456]{1,0:T(8,128)(2,1)S(1)}, bf16[32,3456]{1,0:T(8,128)(2,1)S(1)}, u32[]{:S(2)}, u32[]{:S(2)}) collective-permute-start(bf16[32,3456]{1,0:T(8,128)(2,1)S(1)} %collective-permute-done.9.refs_1_), channel_id=1, source_target_pairs={{0,16},{1,9},{2,18},{3,11},{4,20},{5,13},{6,22},{7,15},{8,24},{9,1... | collective-permute-start | bytes 663560 | tf_op jit(solution)/shard_map/ppermute | solution.py:275
  36.8 0.5 collective-permute-start.5
  37.3 3.8 %collective-permute-done.4.refs_1_ = bf16[32,3456]{1,0:T(8,128)(2,1)S(1)} collective-permute-done((bf16[32,3456]{1,0:T(8,128)(2,1)S(1)}, bf16[32,3456]{1,0:T(8,128)(2,1)S(1)}, u32[]{:S(2)}, u32[]{:S(2)}) %collective-permute-start.4) | collective-permute-done | bytes 221216 | tf_op jit(solution)/shard_map/ppermute | solution.py:275
  41.0 1.5 %collective-permute-start.6 = (bf16[32,3456]{1,0:T(8,128)(2,1)S(1)}, bf16[32,3456]{1,0:T(8,128)(2,1)S(1)}, u32[]{:S(2)}, u32[]{:S(2)}) collective-permute-start(bf16[32,3456]{1,0:T(8,128)(2,1)S(1)} %collective-permute-done.4.refs_1_), channel_id=1, source_target_pairs={{0,16},{1,9},{2,18},{3,11},{4,20},{5,13},{6,22},{7,15},{8,24},{9,1... | collective-permute-start | bytes 663560 | tf_op jit(solution)/shard_map/ppermute | solution.py:275
  42.6 0.1 collective-permute-start.3
  42.7 0.6 copy-done.19
  43.3 5.1 %prepare.7 = (bf16[2,32,9216]{2,1,0:T(8,128)(2,1)}, bf16[2,32,9216]{2,1,0:T(8,128)(2,1)}) custom-call(s32[2,288]{1,0:T(2,128)} %kq_ref.9, bf16[32,3456]{1,0:T(8,128)(2,1)} %copy-done.9, bf16[32,3456]{1,0:T(8,128)(2,1)} %copy-done.14, bf16[32,3456]{1,0:T(8,128)(2,1)} %copy-done.13, bf16[32,3456]{1,0:T(8,128)(2,1)} %copy-done.19), custom_call_target="tpu_custom_call" | custom-call | tf_op jit(solution)/shard_map/prepare/pallas_call | solution.py:106
  48.4 0.1 collective-permute-start.17
  48.5 0.6 copy-done.16
  49.1 0.7 copy-done.18
  49.8 5.1 %prepare.6 = (bf16[2,32,9216]{2,1,0:T(8,128)(2,1)}, bf16[2,32,9216]{2,1,0:T(8,128)(2,1)}) custom-call(s32[2,288]{1,0:T(2,128)} %kq_ref.9, bf16[32,3456]{1,0:T(8,128)(2,1)} %copy-done.8, bf16[32,3456]{1,0:T(8,128)(2,1)} %copy-done.12, bf16[32,3456]{1,0:T(8,128)(2,1)} %copy-done.16, bf16[32,3456]{1,0:T(8,128)(2,1)} %copy-done.18), custom_call_target="tpu_custom_call" | custom-call | tf_op jit(solution)/shard_map/prepare/pallas_call | solution.py:106
  54.9 0.1 collective-permute-start.12
  55.0 0.7 copy-done.15
  55.7 0.7 copy-done.17
  56.4 5.2 %prepare.5 = (bf16[2,32,9216]{2,1,0:T(8,128)(2,1)}, bf16[2,32,9216]{2,1,0:T(8,128)(2,1)}) custom-call(s32[2,288]{1,0:T(2,128)} %kq_ref.9, bf16[32,3456]{1,0:T(8,128)(2,1)} %copy-done.10, bf16[32,3456]{1,0:T(8,128)(2,1)} %copy-done.11, bf16[32,3456]{1,0:T(8,128)(2,1)} %copy-done.15, bf16[32,3456]{1,0:T(8,128)(2,1)} %copy-done.17), custom_call_target="tpu_custom_call" | custom-call | tf_op jit(solution)/shard_map/prepare/pallas_call | solution.py:106
  61.6 0.6 collective-permute-start.7
  62.1 0.7 compare_convert_fusion.mask_ref
  62.9 1.9 %collective-permute-done.7.refs_3_ = bf16[2,32,9216]{2,1,0:T(8,128)(2,1)S(1)} collective-permute-done((bf16[2,32,9216]{2,1,0:T(8,128)(2,1)}, bf16[2,32,9216]{2,1,0:T(8,128)(2,1)S(1)}, u32[]{:S(2)}, u32[]{:S(2)}) %collective-permute-start.7) | collective-permute-done | bytes 1179680 | tf_op jit(solution)/shard_map/ppermute | solution.py:275
  64.8 1.0 copy-done.6
  65.9 18.2 %products.3 = (f32[5,64,256]{2,1,0:T(8,128)}, bf16[5,64,256]{2,1,0:T(8,128)(2,1)}, bf16[5,64,256]{2,1,0:T(8,128)(2,1)}, bf16[5,64,256]{2,1,0:T(8,128)(2,1)}) custom-call(bf16[9,16,9216]{2,1,0:T(8,128)(2,1)} %copy-done, bf16[256,256]{1,0:T(8,128)(2,1)} %compare_convert_fusion.mask_ref, bf16[2,32,9216]{2,1,0:T(8,128)(2,1)} %get-tuple-element.52.refs_0_, ...), custom_call_target="tpu_custom_call" | custom-call | flops 12079595520 | bytes 9437184 | tf_op jit(solution)/shard_map/products/pallas_call | solution.py:168
  84.1 13.0 %products.4 = (f32[3,64,256]{2,1,0:T(8,128)}, bf16[3,64,256]{2,1,0:T(8,128)(2,1)}, bf16[3,64,256]{2,1,0:T(8,128)(2,1)}, bf16[3,64,256]{2,1,0:T(8,128)(2,1)}) custom-call(bf16[9,16,9216]{2,1,0:T(8,128)(2,1)} %copy-done, bf16[256,256]{1,0:T(8,128)(2,1)} %compare_convert_fusion.mask_ref, bf16[2,32,9216]{2,1,0:T(8,128)(2,1)} %get-tuple-element.52.refs_0_, ...), custom_call_target="tpu_custom_call" | custom-call | flops 7247757312 | bytes 9437184 | tf_op jit(solution)/shard_map/products/pallas_call | solution.py:168
  97.1 8.3 %collective-permute-start.21 = (bf16[3,64,256]{2,1,0:T(8,128)(2,1)}, bf16[3,64,256]{2,1,0:T(8,128)(2,1)S(1)}, u32[]{:S(2)}, u32[]{:S(2)}) collective-permute-start(bf16[3,64,256]{2,1,0:T(8,128)(2,1)} %get-tuple-element.76), channel_id=1, source_target_pairs={{0,2},{1,3},{2,4},{3,5},{4,6},{5,7},{6,0},{7,1},{8,10},{9,11},{10,... | collective-permute-start | bytes 294920 | tf_op jit(solution)/shard_map/ppermute | solution.py:275
  105.4 3.3 %collective-permute-start.22 = (bf16[3,64,256]{2,1,0:T(8,128)(2,1)}, bf16[3,64,256]{2,1,0:T(8,128)(2,1)S(1)}, u32[]{:S(2)}, u32[]{:S(2)}) collective-permute-start(bf16[3,64,256]{2,1,0:T(8,128)(2,1)} %get-tuple-element.77), channel_id=1, source_target_pairs={{0,4},{1,5},{2,6},{3,7},{4,0},{5,1},{6,2},{7,3},{8,12},{9,13},{10,... | collective-permute-start | bytes 294920 | tf_op jit(solution)/shard_map/ppermute | solution.py:275
  108.7 2.0 %collective-permute-start.18 = (bf16[5,64,256]{2,1,0:T(8,128)(2,1)S(1)}, bf16[5,64,256]{2,1,0:T(8,128)(2,1)S(1)}, u32[]{:S(2)}, u32[]{:S(2)}) collective-permute-start(bf16[5,64,256]{2,1,0:T(8,128)(2,1)S(1)} %copy-done.25), channel_id=1, source_target_pairs={{0,2},{1,3},{2,4},{3,5},{4,6},{5,7},{6,0},{7,1},{8,10},{9,11},{10,... | collective-permute-start | bytes 491528 | tf_op jit(solution)/shard_map/ppermute | solution.py:275
  110.7 1.3 collective-permute-done.21
  112.1 3.4 %collective-permute-start.20 = (bf16[5,64,256]{2,1,0:T(8,128)(2,1)S(1)}, bf16[5,64,256]{2,1,0:T(8,128)(2,1)S(1)}, u32[]{:S(2)}, u32[]{:S(2)}) collective-permute-start(bf16[5,64,256]{2,1,0:T(8,128)(2,1)S(1)} %copy-done.23), channel_id=1, source_target_pairs={{0,6},{1,7},{2,0},{3,1},{4,2},{5,3},{6,4},{7,5},{8,14},{9,15},{10,... | collective-permute-start | bytes 491528 | tf_op jit(solution)/shard_map/ppermute | solution.py:275
  115.5 7.2 %collective-permute-done.22 = bf16[3,64,256]{2,1,0:T(8,128)(2,1)S(1)} collective-permute-done((bf16[3,64,256]{2,1,0:T(8,128)(2,1)}, bf16[3,64,256]{2,1,0:T(8,128)(2,1)S(1)}, u32[]{:S(2)}, u32[]{:S(2)}) %collective-permute-start.22) | collective-permute-done | bytes 98336 | tf_op jit(solution)/shard_map/ppermute | solution.py:275
  122.7 1.0 convert_add_fusion.1
  123.7 0.0 copy-start.7
  123.7 0.1 collective-permute-start.28
  123.8 4.8 %collective-permute-done.19 = bf16[5,64,256]{2,1,0:T(8,128)(2,1)S(1)} collective-permute-done((bf16[5,64,256]{2,1,0:T(8,128)(2,1)S(1)}, bf16[5,64,256]{2,1,0:T(8,128)(2,1)S(1)}, u32[]{:S(2)}, u32[]{:S(2)}) %collective-permute-start.19) | collective-permute-done | bytes 163872 | tf_op jit(solution)/shard_map/ppermute | solution.py:275
  128.6 9.4 %products.5 = (f32[1,64,256]{2,1,0:T(8,128)}, bf16[1,64,256]{2,1,0:T(8,128)(2,1)}, bf16[1,64,256]{2,1,0:T(8,128)(2,1)}, bf16[1,64,256]{2,1,0:T(8,128)(2,1)}) custom-call(bf16[9,16,9216]{2,1,0:T(8,128)(2,1)} %copy-done, bf16[256,256]{1,0:T(8,128)(2,1)} %compare_convert_fusion.mask_ref, bf16[2,32,9216]{2,1,0:T(8,128)(2,1)} %get-tuple-element.52.refs_0_, ...), custom_call_target="tpu_custom_call" | custom-call | flops 2415919104 | bytes 9437184 | tf_op jit(solution)/shard_map/products/pallas_call | solution.py:168
  138.0 4.1 %collective-permute-start.24 = (bf16[1,64,256]{2,1,0:T(8,128)(2,1)}, bf16[1,64,256]{2,1,0:T(8,128)(2,1)S(1)}, u32[]{:S(2)}, u32[]{:S(2)}) collective-permute-start(bf16[1,64,256]{2,1,0:T(8,128)(2,1)} %get-tuple-element.82), channel_id=1, source_target_pairs={{0,2},{1,3},{2,4},{3,5},{4,6},{5,7},{6,0},{7,1},{8,10},{9,11},{10,... | collective-permute-start | bytes 98312 | tf_op jit(solution)/shard_map/ppermute | solution.py:275
  142.1 0.7 collective-permute-start.25
  142.7 1.8 %collective-permute-start.26 = (bf16[1,64,256]{2,1,0:T(8,128)(2,1)}, bf16[1,64,256]{2,1,0:T(8,128)(2,1)S(1)}, u32[]{:S(2)}, u32[]{:S(2)}) collective-permute-start(bf16[1,64,256]{2,1,0:T(8,128)(2,1)} %get-tuple-element.84), channel_id=1, source_target_pairs={{0,6},{1,7},{2,0},{3,1},{4,2},{5,3},{6,4},{7,5},{8,14},{9,15},{10,... | collective-permute-start | bytes 98312 | tf_op jit(solution)/shard_map/ppermute | solution.py:275
  144.5 0.1 convert_add_fusion
  144.6 0.1 collective-permute-start.27
  144.7 2.5 %collective-permute-done.25 = bf16[1,64,256]{2,1,0:T(8,128)(2,1)S(1)} collective-permute-done((bf16[1,64,256]{2,1,0:T(8,128)(2,1)}, bf16[1,64,256]{2,1,0:T(8,128)(2,1)S(1)}, u32[]{:S(2)}, u32[]{:S(2)}) %collective-permute-start.25) | collective-permute-done | bytes 32800 | tf_op jit(solution)/shard_map/ppermute | solution.py:275
  147.2 0.0 collective-permute-done.26
  147.2 0.1 collective-permute-start.29
  147.4 1.2 collective-permute-done.29
  148.5 0.9 maximum_select_fusion
  (69 shorter events, 0.3 us)
Async XLA Ops:
  0.0 13.8 %copy-start.1 = (bf16[2,9,32,288]{3,2,1,0:T(8,128)(2,1)S(1)}, bf16[2,9,32,288]{3,2,1,0:T(8,128)(2,1)}, u32[]{:S(2)}) copy-start(bf16[2,9,32,288]{3,2,1,0:T(8,128)(2,1)} %coupling_ref.3) | copy-start | bytes 995332
  3.0 12.2 %copy-start.22 = (bf16[32,3456]{1,0:T(8,128)(2,1)S(1)}, bf16[32,3456]{1,0:T(8,128)(2,1)}, u32[]{:S(2)}) copy-start(bf16[32,3456]{1,0:T(8,128)(2,1)} %get-tuple-element.45) | copy-start | bytes 663556
  3.0 23.8 %copy-start.2 = (s32[2,288]{1,0:T(2,128)S(1)}, s32[2,288]{1,0:T(2,128)}, u32[]{:S(2)}) copy-start(s32[2,288]{1,0:T(2,128)} %kq_ref.9) | copy-start | bytes 6916
  3.0 10.8 %collective-permute-start.1 = (bf16[9,32,288]{2,1,0:T(8,128)(2,1)}, bf16[9,32,288]{2,1,0:T(8,128)(2,1)S(1)}, u32[]{:S(2)}, u32[]{:S(2)}) collective-permute-start(bf16[9,32,288]{2,1,0:T(8,128)(2,1)} %get-tuple-element.46), channel_id=1, source_target_pairs={{0,1},{1,0},{2,3},{3,2},{4,5},{5,4},{6,7},{7,6},{8,9},{9,8},{10,11... | collective-permute-start | bytes 497672 | tf_op jit(solution)/shard_map/ppermute | solution.py:275
  3.5 12.1 %collective-permute-start.13 = (bf16[32,3456]{1,0:T(8,128)(2,1)}, bf16[32,3456]{1,0:T(8,128)(2,1)S(1)}, u32[]{:S(2)}, u32[]{:S(2)}) collective-permute-start(bf16[32,3456]{1,0:T(8,128)(2,1)} %get-tuple-element.60), channel_id=1, source_target_pairs={{0,2},{1,3},{2,4},{3,5},{4,6},{5,7},{6,0},{7,1},{8,10},{9,11},{10,... | collective-permute-start | bytes 663560 | tf_op jit(solution)/shard_map/ppermute | solution.py:275
  11.1 14.2 %collective-permute-start.8 = (bf16[32,3456]{1,0:T(8,128)(2,1)}, bf16[32,3456]{1,0:T(8,128)(2,1)S(1)}, u32[]{:S(2)}, u32[]{:S(2)}) collective-permute-start(bf16[32,3456]{1,0:T(8,128)(2,1)} %get-tuple-element.57), channel_id=1, source_target_pairs={{0,4},{1,5},{2,6},{3,7},{4,0},{5,1},{6,2},{7,3},{8,12},{9,13},{10,... | collective-permute-start | bytes 663560 | tf_op jit(solution)/shard_map/ppermute | solution.py:275
  13.8 13.0 %collective-permute-start.2 = (bf16[9,32,288]{2,1,0:T(8,128)(2,1)S(1)}, bf16[9,32,288]{2,1,0:T(8,128)(2,1)S(1)}, u32[]{:S(2)}, u32[]{:S(2)}) collective-permute-start(bf16[9,32,288]{2,1,0:T(8,128)(2,1)S(1)} %bitcast_select_fusion), channel_id=1, source_target_pairs={{0,6},{1,7},{2,0},{3,1},{4,2},{5,3},{6,4},{7,5},{8,14},{9,15},{10,... | collective-permute-start | bytes 497672 | tf_op jit(solution)/shard_map/ppermute | solution.py:275
  15.2 27.4 %copy-start.21 = (bf16[2,32,9216]{2,1,0:T(8,128)(2,1)S(1)}, bf16[2,32,9216]{2,1,0:T(8,128)(2,1)}, u32[]{:S(2)}) copy-start(bf16[2,32,9216]{2,1,0:T(8,128)(2,1)} %get-tuple-element.53) | copy-start | bytes 3538948
  15.2 17.5 %collective-permute-start = (bf16[32,3456]{1,0:T(8,128)(2,1)S(1)}, bf16[32,3456]{1,0:T(8,128)(2,1)S(1)}, u32[]{:S(2)}, u32[]{:S(2)}) collective-permute-start(bf16[32,3456]{1,0:T(8,128)(2,1)S(1)} %copy-done.22), channel_id=1, source_target_pairs={{0,6},{1,7},{2,0},{3,1},{4,2},{5,3},{6,4},{7,5},{8,14},{9,15},{10,... | collective-permute-start | bytes 663560 | tf_op jit(solution)/shard_map/ppermute | solution.py:275
  15.7 15.5 %copy-start.9 = (bf16[32,3456]{1,0:T(8,128)(2,1)}, bf16[32,3456]{1,0:T(8,128)(2,1)S(1)}, u32[]{:S(2)}) copy-start(bf16[32,3456]{1,0:T(8,128)(2,1)S(1)} %collective-permute-done.13.refs_0_) | copy-start | bytes 663556
  15.7 21.1 %collective-permute-start.15 = (bf16[32,3456]{1,0:T(8,128)(2,1)S(1)}, bf16[32,3456]{1,0:T(8,128)(2,1)S(1)}, u32[]{:S(2)}, u32[]{:S(2)}) collective-permute-start(bf16[32,3456]{1,0:T(8,128)(2,1)S(1)} %collective-permute-done.13.refs_0_), channel_id=1, source_target_pairs={{0,16},{1,9},{2,18},{3,11},{4,20},{5,13},{6,22},{7,15},{8,24},{9,1... | collective-permute-start | bytes 663560 | tf_op jit(solution)/shard_map/ppermute | solution.py:275
  17.2 16.0 %collective-permute-start.14 = (bf16[32,3456]{1,0:T(8,128)(2,1)S(1)}, bf16[32,3456]{1,0:T(8,128)(2,1)S(1)}, u32[]{:S(2)}, u32[]{:S(2)}) collective-permute-start(bf16[32,3456]{1,0:T(8,128)(2,1)S(1)} %collective-permute-done.13.refs_0_), channel_id=1, source_target_pairs={{0,8},{1,17},{2,10},{3,19},{4,12},{5,21},{6,14},{7,23},{8,0},{9,25... | collective-permute-start | bytes 663560 | tf_op jit(solution)/shard_map/ppermute | solution.py:275
  25.3 9.4 %copy-start.8 = (bf16[32,3456]{1,0:T(8,128)(2,1)}, bf16[32,3456]{1,0:T(8,128)(2,1)S(1)}, u32[]{:S(2)}) copy-start(bf16[32,3456]{1,0:T(8,128)(2,1)S(1)} %collective-permute-done.8.refs_0_) | copy-start | bytes 663556
  25.3 9.9 %collective-permute-start.9 = (bf16[32,3456]{1,0:T(8,128)(2,1)S(1)}, bf16[32,3456]{1,0:T(8,128)(2,1)S(1)}, u32[]{:S(2)}, u32[]{:S(2)}) collective-permute-start(bf16[32,3456]{1,0:T(8,128)(2,1)S(1)} %collective-permute-done.8.refs_0_), channel_id=1, source_target_pairs={{0,8},{1,17},{2,10},{3,19},{4,12},{5,21},{6,14},{7,23},{8,0},{9,25... | collective-permute-start | bytes 663560 | tf_op jit(solution)/shard_map/ppermute | solution.py:275
  31.2 1.5 copy-start
  32.7 22.3 %copy-start.10 = (bf16[32,3456]{1,0:T(8,128)(2,1)}, bf16[32,3456]{1,0:T(8,128)(2,1)S(1)}, u32[]{:S(2)}) copy-start(bf16[32,3456]{1,0:T(8,128)(2,1)S(1)} %collective-permute-done.refs_0_) | copy-start | bytes 663556
  32.7 8.4 %collective-permute-start.4 = (bf16[32,3456]{1,0:T(8,128)(2,1)S(1)}, bf16[32,3456]{1,0:T(8,128)(2,1)S(1)}, u32[]{:S(2)}, u32[]{:S(2)}) collective-permute-start(bf16[32,3456]{1,0:T(8,128)(2,1)S(1)} %collective-permute-done.refs_0_), channel_id=1, source_target_pairs={{0,8},{1,17},{2,10},{3,19},{4,12},{5,21},{6,14},{7,23},{8,0},{9,25... | collective-permute-start | bytes 663560 | tf_op jit(solution)/shard_map/ppermute | solution.py:275
  33.2 9.4 %copy-start.14 = (bf16[32,3456]{1,0:T(8,128)(2,1)}, bf16[32,3456]{1,0:T(8,128)(2,1)S(1)}, u32[]{:S(2)}) copy-start(bf16[32,3456]{1,0:T(8,128)(2,1)S(1)} %collective-permute-done.14.refs_1_) | copy-start | bytes 663556
  33.2 9.3 %collective-permute-start.16 = (bf16[32,3456]{1,0:T(8,128)(2,1)S(1)}, bf16[32,3456]{1,0:T(8,128)(2,1)S(1)}, u32[]{:S(2)}, u32[]{:S(2)}) collective-permute-start(bf16[32,3456]{1,0:T(8,128)(2,1)S(1)} %collective-permute-done.14.refs_1_), channel_id=1, source_target_pairs={{0,16},{1,9},{2,18},{3,11},{4,20},{5,13},{6,22},{7,15},{8,24},{9,1... | collective-permute-start | bytes 663560 | tf_op jit(solution)/shard_map/ppermute | solution.py:275
  34.7 13.7 %collective-permute-start.10 = (bf16[32,3456]{1,0:T(8,128)(2,1)S(1)}, bf16[32,3456]{1,0:T(8,128)(2,1)S(1)}, u32[]{:S(2)}, u32[]{:S(2)}) collective-permute-start(bf16[32,3456]{1,0:T(8,128)(2,1)S(1)} %collective-permute-done.8.refs_0_), channel_id=1, source_target_pairs={{0,16},{1,9},{2,18},{3,11},{4,20},{5,13},{6,22},{7,15},{8,24},{9,1... | collective-permute-start | bytes 663560 | tf_op jit(solution)/shard_map/ppermute | solution.py:275
  35.2 13.3 %copy-start.12 = (bf16[32,3456]{1,0:T(8,128)(2,1)}, bf16[32,3456]{1,0:T(8,128)(2,1)S(1)}, u32[]{:S(2)}) copy-start(bf16[32,3456]{1,0:T(8,128)(2,1)S(1)} %collective-permute-done.9.refs_1_) | copy-start | bytes 663556
  35.3 13.2 %collective-permute-start.11 = (bf16[32,3456]{1,0:T(8,128)(2,1)S(1)}, bf16[32,3456]{1,0:T(8,128)(2,1)S(1)}, u32[]{:S(2)}, u32[]{:S(2)}) collective-permute-start(bf16[32,3456]{1,0:T(8,128)(2,1)S(1)} %collective-permute-done.9.refs_1_), channel_id=1, source_target_pairs={{0,16},{1,9},{2,18},{3,11},{4,20},{5,13},{6,22},{7,15},{8,24},{9,1... | collective-permute-start | bytes 663560 | tf_op jit(solution)/shard_map/ppermute | solution.py:275
  36.8 5.9 %copy-start.13 = (bf16[32,3456]{1,0:T(8,128)(2,1)}, bf16[32,3456]{1,0:T(8,128)(2,1)S(1)}, u32[]{:S(2)}) copy-start(bf16[32,3456]{1,0:T(8,128)(2,1)S(1)} %collective-permute-done.15.refs_2_) | copy-start | bytes 663556
  36.8 18.2 %collective-permute-start.5 = (bf16[32,3456]{1,0:T(8,128)(2,1)S(1)}, bf16[32,3456]{1,0:T(8,128)(2,1)S(1)}, u32[]{:S(2)}, u32[]{:S(2)}) collective-permute-start(bf16[32,3456]{1,0:T(8,128)(2,1)S(1)} %collective-permute-done.refs_0_), channel_id=1, source_target_pairs={{0,16},{1,9},{2,18},{3,11},{4,20},{5,13},{6,22},{7,15},{8,24},{9,1... | collective-permute-start | bytes 663560 | tf_op jit(solution)/shard_map/ppermute | solution.py:275
  41.0 14.0 %copy-start.11 = (bf16[32,3456]{1,0:T(8,128)(2,1)}, bf16[32,3456]{1,0:T(8,128)(2,1)S(1)}, u32[]{:S(2)}) copy-start(bf16[32,3456]{1,0:T(8,128)(2,1)S(1)} %collective-permute-done.4.refs_1_) | copy-start | bytes 663556
  41.0 13.9 %collective-permute-start.6 = (bf16[32,3456]{1,0:T(8,128)(2,1)S(1)}, bf16[32,3456]{1,0:T(8,128)(2,1)S(1)}, u32[]{:S(2)}, u32[]{:S(2)}) collective-permute-start(bf16[32,3456]{1,0:T(8,128)(2,1)S(1)} %collective-permute-done.4.refs_1_), channel_id=1, source_target_pairs={{0,16},{1,9},{2,18},{3,11},{4,20},{5,13},{6,22},{7,15},{8,24},{9,1... | collective-permute-start | bytes 663560 | tf_op jit(solution)/shard_map/ppermute | solution.py:275
  42.6 0.7 copy-start.19
  42.6 20.3 %collective-permute-start.3 = (bf16[2,32,9216]{2,1,0:T(8,128)(2,1)S(1)}, bf16[2,32,9216]{2,1,0:T(8,128)(2,1)S(1)}, u32[]{:S(2)}, u32[]{:S(2)}) collective-permute-start(bf16[2,32,9216]{2,1,0:T(8,128)(2,1)S(1)} %copy-done.21), channel_id=1, source_target_pairs={{0,1},{1,0},{2,3},{3,2},{4,5},{5,4},{6,7},{7,6},{8,9},{9,8},{10,11... | collective-permute-start | bytes 3538952 | tf_op jit(solution)/shard_map/ppermute | solution.py:275
  48.4 0.7 copy-start.16
  48.4 14.5 %collective-permute-start.17 = (bf16[2,32,9216]{2,1,0:T(8,128)(2,1)}, bf16[2,32,9216]{2,1,0:T(8,128)(2,1)S(1)}, u32[]{:S(2)}, u32[]{:S(2)}) collective-permute-start(bf16[2,32,9216]{2,1,0:T(8,128)(2,1)} %get-tuple-element.62), channel_id=1, source_target_pairs={{0,1},{1,0},{2,3},{3,2},{4,5},{5,4},{6,7},{7,6},{8,9},{9,8},{10,11... | collective-permute-start | bytes 3538952 | tf_op jit(solution)/shard_map/ppermute | solution.py:275
  49.1 0.7 copy-start.18
  54.9 8.0 %collective-permute-start.12 = (bf16[2,32,9216]{2,1,0:T(8,128)(2,1)}, bf16[2,32,9216]{2,1,0:T(8,128)(2,1)S(1)}, u32[]{:S(2)}, u32[]{:S(2)}) collective-permute-start(bf16[2,32,9216]{2,1,0:T(8,128)(2,1)} %get-tuple-element.59), channel_id=1, source_target_pairs={{0,1},{1,0},{2,3},{3,2},{4,5},{5,4},{6,7},{7,6},{8,9},{9,8},{10,11... | collective-permute-start | bytes 3538952 | tf_op jit(solution)/shard_map/ppermute | solution.py:275
  55.0 0.7 copy-start.15
  55.7 0.7 copy-start.17
  61.6 3.2 %collective-permute-start.7 = (bf16[2,32,9216]{2,1,0:T(8,128)(2,1)}, bf16[2,32,9216]{2,1,0:T(8,128)(2,1)S(1)}, u32[]{:S(2)}, u32[]{:S(2)}) collective-permute-start(bf16[2,32,9216]{2,1,0:T(8,128)(2,1)} %get-tuple-element.56), channel_id=1, source_target_pairs={{0,1},{1,0},{2,3},{3,2},{4,5},{5,4},{6,7},{7,6},{8,9},{9,8},{10,11... | collective-permute-start | bytes 3538952 | tf_op jit(solution)/shard_map/ppermute | solution.py:275
  62.9 1.9 %copy-start.3 = (bf16[2,32,9216]{2,1,0:T(8,128)(2,1)}, bf16[2,32,9216]{2,1,0:T(8,128)(2,1)S(1)}, u32[]{:S(2)}) copy-start(bf16[2,32,9216]{2,1,0:T(8,128)(2,1)S(1)} %collective-permute-done.3.refs_1_) | copy-start | bytes 3538948
  62.9 1.9 %copy-start.4 = (bf16[2,32,9216]{2,1,0:T(8,128)(2,1)}, bf16[2,32,9216]{2,1,0:T(8,128)(2,1)S(1)}, u32[]{:S(2)}) copy-start(bf16[2,32,9216]{2,1,0:T(8,128)(2,1)S(1)} %collective-permute-done.17.refs_7_) | copy-start | bytes 3538948
  62.9 1.9 %copy-start.5 = (bf16[2,32,9216]{2,1,0:T(8,128)(2,1)}, bf16[2,32,9216]{2,1,0:T(8,128)(2,1)S(1)}, u32[]{:S(2)}) copy-start(bf16[2,32,9216]{2,1,0:T(8,128)(2,1)S(1)} %collective-permute-done.12.refs_5_) | copy-start | bytes 3538948
  64.8 1.1 copy-start.6
  84.0 24.6 %copy-start.25 = (bf16[5,64,256]{2,1,0:T(8,128)(2,1)S(1)}, bf16[5,64,256]{2,1,0:T(8,128)(2,1)}, u32[]{:S(2)}) copy-start(bf16[5,64,256]{2,1,0:T(8,128)(2,1)} %get-tuple-element.65) | copy-start | bytes 491524
  84.1 26.7 %copy-start.24 = (bf16[5,64,256]{2,1,0:T(8,128)(2,1)S(1)}, bf16[5,64,256]{2,1,0:T(8,128)(2,1)}, u32[]{:S(2)}) copy-start(bf16[5,64,256]{2,1,0:T(8,128)(2,1)} %get-tuple-element.66) | copy-start | bytes 491524
  84.1 28.0 %copy-start.23 = (bf16[5,64,256]{2,1,0:T(8,128)(2,1)S(1)}, bf16[5,64,256]{2,1,0:T(8,128)(2,1)}, u32[]{:S(2)}) copy-start(bf16[5,64,256]{2,1,0:T(8,128)(2,1)} %get-tuple-element.67) | copy-start | bytes 491524
  97.1 15.0 %collective-permute-start.21 = (bf16[3,64,256]{2,1,0:T(8,128)(2,1)}, bf16[3,64,256]{2,1,0:T(8,128)(2,1)S(1)}, u32[]{:S(2)}, u32[]{:S(2)}) collective-permute-start(bf16[3,64,256]{2,1,0:T(8,128)(2,1)} %get-tuple-element.76), channel_id=1, source_target_pairs={{0,2},{1,3},{2,4},{3,5},{4,6},{5,7},{6,0},{7,1},{8,10},{9,11},{10,... | collective-permute-start | bytes 294920 | tf_op jit(solution)/shard_map/ppermute | solution.py:275
  105.4 17.3 %collective-permute-start.22 = (bf16[3,64,256]{2,1,0:T(8,128)(2,1)}, bf16[3,64,256]{2,1,0:T(8,128)(2,1)S(1)}, u32[]{:S(2)}, u32[]{:S(2)}) collective-permute-start(bf16[3,64,256]{2,1,0:T(8,128)(2,1)} %get-tuple-element.77), channel_id=1, source_target_pairs={{0,4},{1,5},{2,6},{3,7},{4,0},{5,1},{6,2},{7,3},{8,12},{9,13},{10,... | collective-permute-start | bytes 294920 | tf_op jit(solution)/shard_map/ppermute | solution.py:275
  108.7 14.0 %collective-permute-start.23 = (bf16[3,64,256]{2,1,0:T(8,128)(2,1)}, bf16[3,64,256]{2,1,0:T(8,128)(2,1)S(1)}, u32[]{:S(2)}, u32[]{:S(2)}) collective-permute-start(bf16[3,64,256]{2,1,0:T(8,128)(2,1)} %get-tuple-element.78), channel_id=1, source_target_pairs={{0,6},{1,7},{2,0},{3,1},{4,2},{5,3},{6,4},{7,5},{8,14},{9,15},{10,... | collective-permute-start | bytes 294920 | tf_op jit(solution)/shard_map/ppermute | solution.py:275
  108.7 15.1 %collective-permute-start.18 = (bf16[5,64,256]{2,1,0:T(8,128)(2,1)S(1)}, bf16[5,64,256]{2,1,0:T(8,128)(2,1)S(1)}, u32[]{:S(2)}, u32[]{:S(2)}) collective-permute-start(bf16[5,64,256]{2,1,0:T(8,128)(2,1)S(1)} %copy-done.25), channel_id=1, source_target_pairs={{0,2},{1,3},{2,4},{3,5},{4,6},{5,7},{6,0},{7,1},{8,10},{9,11},{10,... | collective-permute-start | bytes 491528 | tf_op jit(solution)/shard_map/ppermute | solution.py:275
  110.7 17.9 %collective-permute-start.19 = (bf16[5,64,256]{2,1,0:T(8,128)(2,1)S(1)}, bf16[5,64,256]{2,1,0:T(8,128)(2,1)S(1)}, u32[]{:S(2)}, u32[]{:S(2)}) collective-permute-start(bf16[5,64,256]{2,1,0:T(8,128)(2,1)S(1)} %copy-done.24), channel_id=1, source_target_pairs={{0,4},{1,5},{2,6},{3,7},{4,0},{5,1},{6,2},{7,3},{8,12},{9,13},{10,... | collective-permute-start | bytes 491528 | tf_op jit(solution)/shard_map/ppermute | solution.py:275
  112.1 16.5 %collective-permute-start.20 = (bf16[5,64,256]{2,1,0:T(8,128)(2,1)S(1)}, bf16[5,64,256]{2,1,0:T(8,128)(2,1)S(1)}, u32[]{:S(2)}, u32[]{:S(2)}) collective-permute-start(bf16[5,64,256]{2,1,0:T(8,128)(2,1)S(1)} %copy-done.23), channel_id=1, source_target_pairs={{0,6},{1,7},{2,0},{3,1},{4,2},{5,3},{6,4},{7,5},{8,14},{9,15},{10,... | collective-permute-start | bytes 491528 | tf_op jit(solution)/shard_map/ppermute | solution.py:275
  123.7 20.8 %copy-start.7 = (f32[5,64,256]{2,1,0:T(8,128)S(1)}, f32[5,64,256]{2,1,0:T(8,128)}, u32[]{:S(2)}) copy-start(f32[5,64,256]{2,1,0:T(8,128)} %get-tuple-element.71) | copy-start | bytes 983044
  123.7 23.6 %collective-permute-start.28 = (f32[3,32,256]{2,1,0:T(8,128)S(1)}, f32[3,32,256]{2,1,0:T(8,128)S(1)}, u32[]{:S(2)}, u32[]{:S(2)}) collective-permute-start(f32[3,32,256]{2,1,0:T(8,128)S(1)} %get-tuple-element.88), channel_id=1, source_target_pairs={{0,1},{1,0},{2,3},{3,2},{4,5},{5,4},{6,7},{7,6},{8,9},{9,8},{10,11... | collective-permute-start | bytes 294920 | tf_op jit(solution)/shard_map/ppermute | solution.py:275
  138.0 9.2 %copy-start.20 = (f32[1,64,256]{2,1,0:T(8,128)S(1)}, f32[1,64,256]{2,1,0:T(8,128)}, u32[]{:S(2)}) copy-start(f32[1,64,256]{2,1,0:T(8,128)} %get-tuple-element.81) | copy-start | bytes 196612
  138.0 6.7 %collective-permute-start.24 = (bf16[1,64,256]{2,1,0:T(8,128)(2,1)}, bf16[1,64,256]{2,1,0:T(8,128)(2,1)S(1)}, u32[]{:S(2)}, u32[]{:S(2)}) collective-permute-start(bf16[1,64,256]{2,1,0:T(8,128)(2,1)} %get-tuple-element.82), channel_id=1, source_target_pairs={{0,2},{1,3},{2,4},{3,5},{4,6},{5,7},{6,0},{7,1},{8,10},{9,11},{10,... | collective-permute-start | bytes 98312 | tf_op jit(solution)/shard_map/ppermute | solution.py:275
  142.1 5.1 %collective-permute-start.25 = (bf16[1,64,256]{2,1,0:T(8,128)(2,1)}, bf16[1,64,256]{2,1,0:T(8,128)(2,1)S(1)}, u32[]{:S(2)}, u32[]{:S(2)}) collective-permute-start(bf16[1,64,256]{2,1,0:T(8,128)(2,1)} %get-tuple-element.83), channel_id=1, source_target_pairs={{0,4},{1,5},{2,6},{3,7},{4,0},{5,1},{6,2},{7,3},{8,12},{9,13},{10,... | collective-permute-start | bytes 98312 | tf_op jit(solution)/shard_map/ppermute | solution.py:275
  142.7 4.5 %collective-permute-start.26 = (bf16[1,64,256]{2,1,0:T(8,128)(2,1)}, bf16[1,64,256]{2,1,0:T(8,128)(2,1)S(1)}, u32[]{:S(2)}, u32[]{:S(2)}) collective-permute-start(bf16[1,64,256]{2,1,0:T(8,128)(2,1)} %get-tuple-element.84), channel_id=1, source_target_pairs={{0,6},{1,7},{2,0},{3,1},{4,2},{5,3},{6,4},{7,5},{8,14},{9,15},{10,... | collective-permute-start | bytes 98312 | tf_op jit(solution)/shard_map/ppermute | solution.py:275
  144.6 3.9 %collective-permute-start.27 = (f32[5,32,256]{2,1,0:T(8,128)S(1)}, f32[5,32,256]{2,1,0:T(8,128)S(1)}, u32[]{:S(2)}, u32[]{:S(2)}) collective-permute-start(f32[5,32,256]{2,1,0:T(8,128)S(1)} %get-tuple-element.86), channel_id=1, source_target_pairs={{0,1},{1,0},{2,3},{3,2},{4,5},{5,4},{6,7},{7,6},{8,9},{9,8},{10,11... | collective-permute-start | bytes 491528 | tf_op jit(solution)/shard_map/ppermute | solution.py:275
  147.2 1.3 collective-permute-start.29

commit v5 on v4

--- a/solution.py
+++ b/solution.py
@@ -12,7 +12,6 @@
 BANDS = 16
 LINE = KY * BANDS
 GROUPS = (5, 8)
-VMEM_ALL = 56 << 20
 F32 = jnp.float32
 BF16 = jnp.bfloat16
 
@@ -73,117 +72,90 @@
     return pieces, window, give
 
 
-def prep_kernel(lines_all, kq_ref, *refs):
-    ins, (keep_ref, give_ref, window, sems) = refs[:-4], refs[-4:]
+def prep_kernel(block_lines, lines_all, for_other, kq_ref, *refs):
+    ins, (out_ref, window) = refs[:-2], refs[-2:]
     pb, _, core = place()
-    line = pl.program_id(0)
-    block_lines = pl.num_programs(0) // 2
-
-    @pl.when(line == 0)
-    def _():
-        copies = []
-        for index, src in enumerate(ins):
-            offset, size = 0, src.shape[1]
-            if len(ins) > 1:
-                rel = (0, 1 + core, 2 - core, 3)[index]
-                offset = pl.multiple_of((pb ^ rel) * size, 128)
-            copy = pltpu.make_async_copy(src, window.at[:, pl.ds(offset, size)], sems.at[index])
-            copy.start()
-            copies.append(copy)
-        for copy in copies:
-            copy.wait()
-
-    for out_ref, q in ((keep_ref, core), (give_ref, 1 - core)):
-        base, image, turn = turns_of(kq_ref, q, block_lines, lines_all)
-        out_ref[0] = window[:, pl.ds(pl.multiple_of((base + line) * LINE, 128), LINE)]
+    q = 1 - core if for_other else core
+    base, image, turn = turns_of(kq_ref, q, block_lines, lines_all)
+    if len(ins) == 1:
+        window = ins[0]
+    else:
+        for rel, src in zip((0, 1 + core, 2 - core, 3), ins):
+            size = src.shape[1]
+            window[:, pl.ds(pl.multiple_of((pb ^ rel) * size, 128), size)] = src[...]
+    for line in range(2 * block_lines):
+        to = slice(line * LINE, (line + 1) * LINE)
+        out_ref[0, :, to] = window[:, pl.ds(pl.multiple_of((base + line) * LINE, 128), LINE)]
         shifted = window[:, pl.ds(pl.multiple_of((image + line) * LINE, 128), LINE)].astype(F32)
-        out_ref[1] = pltpu.roll(shifted, turn, 1).astype(BF16)
-
-
-def prepare(kq_map, ins, block, lines_all):
-    rows, lines = ins[0].shape[0], 2 * block // LINE
-    out = jax.ShapeDtypeStruct((2, rows, lines * LINE), BF16)
+        out_ref[1, :, to] = pltpu.roll(shifted, turn, 1).astype(BF16)
+
+
+def prepare(kq_map, ins, block, lines_all, for_other):
+    rows = ins[0].shape[0]
     return pl.pallas_call(
-        functools.partial(prep_kernel, lines_all),
-        grid=(lines,),
-        in_specs=[pl.BlockSpec(memory_space=pltpu.SMEM)] + [pl.BlockSpec(memory_space=pl.ANY)] * len(ins),
-        out_specs=[pl.BlockSpec((2, rows, LINE), lambda i: (0, 0, i))] * 2,
-        out_shape=[out, out],
-        scratch_shapes=[
-            pltpu.VMEM((rows, 3 * block), BF16),
-            pltpu.SemaphoreType.DMA((len(ins),)),
-        ],
-        compiler_params=pltpu.CompilerParams(vmem_limit_bytes=VMEM_ALL),
-        name="prepare",
+        functools.partial(prep_kernel, block // LINE, lines_all, for_other),
+        in_specs=[pl.BlockSpec(memory_space=pltpu.SMEM)] + [pl.BlockSpec(memory_space=pltpu.VMEM)] * len(ins),
+        out_specs=pl.BlockSpec(memory_space=pltpu.VMEM),
+        out_shape=jax.ShapeDtypeStruct((2, rows, 2 * block), BF16),
+        scratch_shapes=[pltpu.VMEM((rows, 3 * block), BF16)],
+        compiler_params=pltpu.CompilerParams(vmem_limit_bytes=16 << 20),
+        name="prepare_other" if for_other else "prepare_own",
     )(kq_map, *ins)
 
 
-def main_kernel(sources, first, branches, factor, x_ref, mask_ref, *refs):
-    amps, (mine_ref, *sends, total) = refs[:sources], refs[sources:]
-    step = pl.program_id(0)
-
-    @pl.when(step == 0)
-    def _():
-        total[...] = jnp.zeros_like(total)
-
+def main_kernel(sources, first, branches, factor, x_ref, *refs):
+    amps, (mine_ref, *sends, total, mask) = refs[:sources], refs[sources:]
+    shape = mask.shape
+    same = lax.broadcasted_iota(jnp.int32, shape, 0) // BANDS == lax.broadcasted_iota(jnp.int32, shape, 1) // BANDS
+    mask[...] = same.astype(F32).astype(BF16)
+    for line in range(x_ref.shape[2] // LINE):
+        to = slice(line * LINE, (line + 1) * LINE)
+        for branch in range(branches):
+            parts = []
+            for tile in range(LINE // 256):
+                lanes = slice(line * LINE + tile * 256, line * LINE + (tile + 1) * 256)
+                matrix = jnp.concatenate([x_ref[first + branch, :, lanes]] * 16, axis=0) * mask[...]
+                own = jnp.concatenate([ref[0, :, lanes] for ref in amps], axis=0)
+                parts.append(contract(own, matrix, 1, 0).astype(BF16))
+            shifted = jnp.concatenate([ref[1, :, to] for ref in amps], axis=0)
+            part = contract(shifted, jnp.concatenate(parts, axis=1), 1, 1)
+            total[branch] = part if line == 0 else total[branch] + part
+    _, z, core = place()
+    states = total.shape[2]
+    rows = states // sources
+    col = lax.broadcasted_iota(jnp.int32, (states, states), 0)
+    target = lax.broadcasted_iota(jnp.int32, (states, states), 1)
+    source = lax.rem(col // rows + 2 * z, sources)
+    home = (source // 2 * 2 + (source % 2 ^ core)) * rows + col % rows
+    to_home = (home == target).astype(F32).astype(BF16)
     for branch in range(branches):
-        parts = []
-        for tile in range(LINE // 256):
-            lanes = slice(tile * 256, (tile + 1) * 256)
-            matrix = jnp.concatenate([x_ref[first + branch, :, lanes]] * 16, axis=0) * mask_ref[...]
-            own = jnp.concatenate([ref[0, :, lanes] for ref in amps], axis=0)
-            parts.append(contract(own, matrix, 1, 0).astype(BF16))
-        diff = jnp.concatenate(parts, axis=1)
-        shifted = jnp.concatenate([ref[1] for ref in amps], axis=0)
-        total[branch] += contract(shifted, diff, 1, 1)
-
-    @pl.when(step == pl.num_programs(0) - 1)
-    def _():
-        _, z, core = place()
-        states = total.shape[2]
-        rows = states // sources
-        col = lax.broadcasted_iota(jnp.int32, (states, states), 0)
-        target = lax.broadcasted_iota(jnp.int32, (states, states), 1)
-        source = lax.rem(col // rows + 2 * z, sources)
-        home = (source // 2 * 2 + (source % 2 ^ core)) * rows + col % rows
-        to_home = (home == target).astype(F32).astype(BF16)
-        for branch in range(branches):
-            value = total[branch] * factor
-            high = value.astype(BF16)
-            moved = contract(high, to_home, 1, 0)
-            rest = value[: 2 * rows] - high[: 2 * rows].astype(F32)
-            middle = rest.astype(BF16)
-            low = (rest - middle.astype(F32)).astype(BF16)
-            mine_ref[branch] = moved[: 2 * rows] + contract(middle, to_home, 1, 0) + contract(low, to_home, 1, 0)
-            for chip, send in enumerate(sends, 1):
-                send[branch] = moved[chip * 2 * rows : (chip + 1) * 2 * rows].astype(BF16)
-
-
-def products(x, mask, amps, first, branches, factor):
+        value = total[branch] * factor
+        high = value.astype(BF16)
+        moved = contract(high, to_home, 1, 0)
+        rest = value[: 2 * rows] - high[: 2 * rows].astype(F32)
+        middle = rest.astype(BF16)
+        low = (rest - middle.astype(F32)).astype(BF16)
+        mine_ref[branch] = moved[: 2 * rows] + contract(middle, to_home, 1, 0) + contract(low, to_home, 1, 0)
+        for chip, send in enumerate(sends, 1):
+            send[branch] = moved[chip * 2 * rows : (chip + 1) * 2 * rows].astype(BF16)
+
+
+def products(x, amps, first, branches, factor):
     sources, rows = len(amps), amps[0].shape[1]
-    states = sources * rows
-    lines = x.shape[2] // LINE
-    piece = pl.BlockSpec((branches, 2 * rows, states), lambda i: (0, 0, 0))
+    states, width = sources * rows, x.shape[2]
     shape = (branches, 2 * rows, states)
     return pl.pallas_call(
         functools.partial(main_kernel, sources, first, branches, factor),
-        grid=(lines,),
-        in_specs=[
-            pl.BlockSpec((x.shape[0], BANDS, LINE), lambda i: (0, 0, i)),
-            pl.BlockSpec((256, 256), lambda i: (0, 0)),
-        ]
-        + [pl.BlockSpec((2, rows, LINE), lambda i: (0, 0, i))] * sources,
-        out_specs=[piece] * (sources // 2),
+        in_specs=[pl.BlockSpec(memory_space=pltpu.VMEM)] * (1 + sources),
+        out_specs=[pl.BlockSpec(memory_space=pltpu.VMEM)] * (sources // 2),
         out_shape=[jax.ShapeDtypeStruct(shape, F32 if i == 0 else BF16) for i in range(sources // 2)],
-        scratch_shapes=[pltpu.VMEM((branches, states, states), F32)],
-        compiler_params=pltpu.CompilerParams(vmem_limit_bytes=VMEM_ALL),
+        scratch_shapes=[pltpu.VMEM((branches, states, states), F32), pltpu.VMEM((256, 256), BF16)],
+        compiler_params=pltpu.CompilerParams(vmem_limit_bytes=32 << 20),
         cost_estimate=pl.CostEstimate(
-            flops=4 * branches * states * states * lines * LINE,
-            bytes_accessed=4 * states * lines * LINE,
-            transcendentals=0,
+            flops=4 * branches * states * states * width, bytes_accessed=4 * states * width, transcendentals=0
         ),
         name="products",
-    )(x, mask, *amps)
+    )(x, *amps)
 
 
 def band_kernel(block_lines, lines_all, kq_ref, coupling_ref, other_ref, next_ref, x_ref):
@@ -280,41 +252,52 @@
     def passed_down(e):
         return lambda x: permute(x, lambda p, zz, c: (p, zz - e, c))
 
+    def passed_down(x, e):
+        return permute(x, lambda p, zz, c: (p, zz - e, c))
+
+    def prepared(ins, for_other):
+        return prepare(kq_map, ins, block, lines_all, for_other)
+
+    def after(x, *others):
+        return lax.optimization_barrier((x, *others))[0]
+
     pieces, window, give = cut(envelopes, coupling, n_z, block)
     near = sorted({1, n_z - 1})
     far = [e for e in range(2, n_z - 1)]
-    arrived = {e: passed_down(e)(pieces[e - 1]) for e in near}
+    arrived = {1: passed_down(pieces[0], 1)}
+    pass_on = prepared([window], True)
+    if len(near) > 1:
+        arrived[n_z - 1] = passed_down(after(pieces[n_z - 2], pass_on), n_z - 1)
+    keep = prepared([after(window, pass_on)], False)
+    for e in far:
+        arrived[e] = passed_down(after(pieces[e - 1], keep), e)
+    amps = {0: (keep, sibling(pass_on))}
     other_table = sibling(give)
     first_table = jnp.where(core == 0, lax.dynamic_index_in_dim(coupling, core, 0, keepdims=False), other_table)
-    next_table = passed_down(1)(first_table)
-    keep, pass_on = prepare(kq_map, [window], block, lines_all)
-    waiting = [pieces[e - 1] for e in far]
-    keep, pass_on, *waiting = lax.optimization_barrier((keep, pass_on, *waiting))
-    for e, piece in zip(far, waiting):
-        arrived[e] = passed_down(e)(piece)
-    amps = {0: (keep, sibling(pass_on))}
+    next_table = passed_down(first_table, 1)
     x = band_matrices(kq_map, coupling, other_table, next_table, lines_all)
-    arrived[1], x = lax.optimization_barrier((arrived[1], x))
+    arrived[1] = after(arrived[1], x)
 
     for e in near + far:
         piece = arrived[e]
         one = permute(piece, lambda p, zz, c: (p ^ (1 + c), zz, c))
         two = permute(piece, lambda p, zz, c: (p ^ (2 - c), zz, c))
         three = permute(one, lambda p, zz, c: (p ^ (2 - c), zz, c))
-        keep, pass_on = prepare(kq_map, [piece, one, two, three], block, lines_all)
+        pass_on = prepared([piece, one, two, three], True)
+        keep = prepared([after(piece, pass_on), one, two, three], False)
         amps[e] = (keep, sibling(pass_on))
     amps = [half for e in range(n_z) for half in amps[e]]
 
-    index = jnp.arange(256, dtype=jnp.int32) // BANDS
-    mask = (index[:, None] == index[None, :]).astype(BF16)
     factor = 1.0 / math.sqrt(float(width))
     edges = [0] + [edge * branches // 9 for edge in GROUPS] + [branches]
     received, mine, other = [], [], []
     for lo, hi in zip(edges[:-1], edges[1:]):
         if len(received) >= 2:
-            received[-2], x = lax.optimization_barrier((received[-2], x))
-        own, *sends = products(x, mask, amps, lo, hi - lo, factor)
-        own, x = lax.optimization_barrier((own, x))
+            x, received[-2] = lax.optimization_barrier((x, received[-2]))
+        own, *sends = products(x, amps, lo, hi - lo, factor)
+        x, own = lax.optimization_barrier((x, own))
+        if received:
+            own, received[-1] = lax.optimization_barrier((own, received[-1]))
         received.append([own] + [permute(p, lambda p, zz, c: (p, zz + e, c)) for e, p in enumerate(sends, 1)])
     for parts in received:
         total = parts[0]

time: 150 us -> 108 us (0.72)
  Pallas kernels: 68.2 us -> 39.9 us
  waiting for transfers between devices: 29.4 us -> 19.5 us
  local copies, waits for them, and re-layouts: 5.88 us -> 1.22 us
  starting transfers between devices: 42.8 us -> 45.6 us
  other arithmetic: 2.76 us -> 1.1 us
    pallas_call x3, Pallas kernels: 40.6 us -> 24.2 us  [products(): pl.pallas_call(functools.partial(main_kernel, sources, first, branches, f...]
    pallas_call x4 -> x8, Pallas kernels: 20.3 us -> 8.32 us  [prepare(): pl.pallas_call(functools.partial(prep_kernel, block // LINE, lines_all, f...]
    ppermute x30, waiting for transfers between devices: 29.4 us -> 19.5 us  [permute(): return lax.ppermute(x, ('pb', 'ka'), pairs)]
    unnamed x52 -> x6, local copies, waits for them, and re-layouts: 5.84 us -> 1.18 us
    ppermute x30, starting transfers between devices: 42.8 us -> 45.6 us  [permute(): return lax.ppermute(x, ('pb', 'ka'), pairs)]
  transfers between devices with their start and end apart: 30 -> 30, of which waited for: 8 -> 8; matrix products, arithmetic and copies ran while one was open for 1% -> 0% of each run, Pallas kernels for 23% -> 22%
where the time goes in v5:
time: 108 us
  starting transfers between devices  45.6 us (42%)
  Pallas kernels  39.9 us (37%)
  waiting for transfers between devices  19.5 us (18%)
  local copies, waits for them, and re-layouts  1.22 us (1%)
  other arithmetic  1.1 us (1%)
    ppermute x30, starting transfers between devices, permute(): return lax.ppermute(x, ('pb', 'ka'), pairs)  45.6 us
    pallas_call x3, Pallas kernels, products(): pl.pallas_call(functools.partial(main_kernel, sources, first, branches, f...  24.2 us
    ppermute x30, waiting for transfers between devices, permute(): return lax.ppermute(x, ('pb', 'ka'), pairs)  19.5 us
    pallas_call x8, Pallas kernels, prepare(): pl.pallas_call(functools.partial(prep_kernel, block // LINE, lines_all, f...  8.32 us
    pallas_call x1, Pallas kernels, band_matrices(): pl.pallas_call(functools.partial(band_kernel, count // KY, lines_all), in...  4.37 us
    pallas_call x1, Pallas kernels, cut(): pl.pallas_call(functools.partial(cut_kernel, block), in_specs=[pl.BlockSp...  2.94 us
  transfers between devices with their start and end apart: 30, of which 8 were waited for; matrix products, arithmetic and copies ran while one was open for 0% of the time, Pallas kernels for 22%

profile of v5, /device:TPU:0, one launch (start us, length us, event | category | flops | bytes accessed | tf_op | source)
XLA Modules:
  0.0 107.6 jit_solution(221634250631262230)
XLA Ops:
  0.0 2.9 %cut.1 = (bf16[32,3456]{1,0:T(8,128)(2,1)}, bf16[32,3456]{1,0:T(8,128)(2,1)}, bf16[32,3456]{1,0:T(8,128)(2,1)}, bf16[32,13824]{1,0:T(8,128)(2,1)}, bf16[9,32,288]{2,1,0:T(8,128)(2,1)}) custom-call(bf16[32,36864]{1,0:T(8,128)(2,1)} %env_ref.1, bf16[2,9,32,288]{3,2,1,0:T(8,128)(2,1)} %coupling_ref.3), custom_call_target="tpu_custom_call" | custom-call | tf_op jit(solution)/shard_map/cut/pallas_call | solution.py:64
  2.9 0.5 collective-permute-start
  3.5 1.2 %copy-done = bf16[32,13824]{1,0:T(8,128)(2,1)S(1)} copy-done((bf16[32,13824]{1,0:T(8,128)(2,1)S(1)}, bf16[32,13824]{1,0:T(8,128)(2,1)}, u32[]{:S(2)}) %copy-start) | copy-done | bytes 884760
  4.6 1.0 prepare_other.4
  5.6 0.0 copy-start.1
  5.7 2.6 %collective-permute-start.13 = (bf16[32,3456]{1,0:T(8,128)(2,1)}, bf16[32,3456]{1,0:T(8,128)(2,1)S(1)}, u32[]{:S(2)}, u32[]{:S(2)}) collective-permute-start(bf16[32,3456]{1,0:T(8,128)(2,1)} %get-tuple-element.59), channel_id=1, source_target_pairs={{0,2},{1,3},{2,4},{3,5},{4,6},{5,7},{6,0},{7,1},{8,10},{9,11},{10,... | collective-permute-start | bytes 663560 | tf_op jit(solution)/shard_map/ppermute | solution.py:247
  8.3 1.0 prepare_own.4.refs_0_
  9.3 2.7 %collective-permute-start.8 = (bf16[32,3456]{1,0:T(8,128)(2,1)}, bf16[32,3456]{1,0:T(8,128)(2,1)S(1)}, u32[]{:S(2)}, u32[]{:S(2)}) collective-permute-start(bf16[32,3456]{1,0:T(8,128)(2,1)} %get-tuple-element.56), channel_id=1, source_target_pairs={{0,4},{1,5},{2,6},{3,7},{4,0},{5,1},{6,2},{7,3},{8,12},{9,13},{10,... | collective-permute-start | bytes 663560 | tf_op jit(solution)/shard_map/ppermute | solution.py:247
  12.0 0.0 collective-permute-done.other_ref
  12.0 1.4 %collective-permute-start.1 = (bf16[9,32,288]{2,1,0:T(8,128)(2,1)S(1)}, bf16[9,32,288]{2,1,0:T(8,128)(2,1)S(1)}, u32[]{:S(2)}, u32[]{:S(2)}) collective-permute-start(bf16[9,32,288]{2,1,0:T(8,128)(2,1)S(1)} %bitcast_select_fusion), channel_id=1, source_target_pairs={{0,6},{1,7},{2,0},{3,1},{4,2},{5,3},{6,4},{7,5},{8,14},{9,15},{10,... | collective-permute-start | bytes 497672 | tf_op jit(solution)/shard_map/ppermute | solution.py:247
  13.4 0.4 collective-permute-start.3
  13.9 3.1 %collective-permute-done.13.refs_0_ = bf16[32,3456]{1,0:T(8,128)(2,1)S(1)} collective-permute-done((bf16[32,3456]{1,0:T(8,128)(2,1)}, bf16[32,3456]{1,0:T(8,128)(2,1)S(1)}, u32[]{:S(2)}, u32[]{:S(2)}) %collective-permute-start.13) | collective-permute-done | bytes 221216 | tf_op jit(solution)/shard_map/ppermute | solution.py:247
  17.0 1.7 %collective-permute-start.15 = (bf16[32,3456]{1,0:T(8,128)(2,1)S(1)}, bf16[32,3456]{1,0:T(8,128)(2,1)S(1)}, u32[]{:S(2)}, u32[]{:S(2)}) collective-permute-start(bf16[32,3456]{1,0:T(8,128)(2,1)S(1)} %collective-permute-done.13.refs_0_), channel_id=1, source_target_pairs={{0,16},{1,9},{2,18},{3,11},{4,20},{5,13},{6,22},{7,15},{8,24},{9,1... | collective-permute-start | bytes 663560 | tf_op jit(solution)/shard_map/ppermute | solution.py:247
  18.6 1.5 %collective-permute-start.14 = (bf16[32,3456]{1,0:T(8,128)(2,1)S(1)}, bf16[32,3456]{1,0:T(8,128)(2,1)S(1)}, u32[]{:S(2)}, u32[]{:S(2)}) collective-permute-start(bf16[32,3456]{1,0:T(8,128)(2,1)S(1)} %collective-permute-done.13.refs_0_), channel_id=1, source_target_pairs={{0,8},{1,17},{2,10},{3,19},{4,12},{5,21},{6,14},{7,23},{8,0},{9,25... | collective-permute-start | bytes 663560 | tf_op jit(solution)/shard_map/ppermute | solution.py:247
  20.1 6.1 %collective-permute-done.8.refs_0_ = bf16[32,3456]{1,0:T(8,128)(2,1)S(1)} collective-permute-done((bf16[32,3456]{1,0:T(8,128)(2,1)}, bf16[32,3456]{1,0:T(8,128)(2,1)S(1)}, u32[]{:S(2)}, u32[]{:S(2)}) %collective-permute-start.8) | collective-permute-done | bytes 221216 | tf_op jit(solution)/shard_map/ppermute | solution.py:247
  26.3 1.5 %collective-permute-start.9 = (bf16[32,3456]{1,0:T(8,128)(2,1)S(1)}, bf16[32,3456]{1,0:T(8,128)(2,1)S(1)}, u32[]{:S(2)}, u32[]{:S(2)}) collective-permute-start(bf16[32,3456]{1,0:T(8,128)(2,1)S(1)} %collective-permute-done.8.refs_0_), channel_id=1, source_target_pairs={{0,8},{1,17},{2,10},{3,19},{4,12},{5,21},{6,14},{7,23},{8,0},{9,25... | collective-permute-start | bytes 663560 | tf_op jit(solution)/shard_map/ppermute | solution.py:247
  27.7 0.0 collective-permute-done.1.next_ref
  27.7 4.4 %band_matrices.1.x_ref = bf16[9,16,9216]{2,1,0:T(8,128)(2,1)S(1)} custom-call(s32[2,288]{1,0:T(2,128)S(1)} %copy-done.2, bf16[2,9,32,288]{3,2,1,0:T(8,128)(2,1)S(1)} %copy-done.1, bf16[9,32,288]{2,1,0:T(8,128)(2,1)S(1)} %collective-permute-done.other_ref, bf16[9,32,288]{2,1,0:T(8,128)(2,1)S(1)} %collective-permute-done.1.next_ref), custom_call_target="tpu_custom_call" | custom-call | flops 10000000000 | bytes 1000000 | tf_op jit(solution)/shard_map/band_matrices/pallas_call | solution.py:220
  32.1 0.6 collective-permute-start.4
  32.7 1.5 %collective-permute-start.16 = (bf16[32,3456]{1,0:T(8,128)(2,1)S(1)}, bf16[32,3456]{1,0:T(8,128)(2,1)S(1)}, u32[]{:S(2)}, u32[]{:S(2)}) collective-permute-start(bf16[32,3456]{1,0:T(8,128)(2,1)S(1)} %collective-permute-done.14.refs_1_), channel_id=1, source_target_pairs={{0,16},{1,9},{2,18},{3,11},{4,20},{5,13},{6,22},{7,15},{8,24},{9,1... | collective-permute-start | bytes 663560 | tf_op jit(solution)/shard_map/ppermute | solution.py:247
  34.3 0.5 collective-permute-start.10
  34.8 0.0 collective-permute-done.9.refs_1_
  34.8 1.5 %collective-permute-start.11 = (bf16[32,3456]{1,0:T(8,128)(2,1)S(1)}, bf16[32,3456]{1,0:T(8,128)(2,1)S(1)}, u32[]{:S(2)}, u32[]{:S(2)}) collective-permute-start(bf16[32,3456]{1,0:T(8,128)(2,1)S(1)} %collective-permute-done.9.refs_1_), channel_id=1, source_target_pairs={{0,16},{1,9},{2,18},{3,11},{4,20},{5,13},{6,22},{7,15},{8,24},{9,1... | collective-permute-start | bytes 663560 | tf_op jit(solution)/shard_map/ppermute | solution.py:247
  36.3 0.5 collective-permute-start.5
  36.8 3.7 %collective-permute-done.4.refs_1_ = bf16[32,3456]{1,0:T(8,128)(2,1)S(1)} collective-permute-done((bf16[32,3456]{1,0:T(8,128)(2,1)S(1)}, bf16[32,3456]{1,0:T(8,128)(2,1)S(1)}, u32[]{:S(2)}, u32[]{:S(2)}) %collective-permute-start.4) | collective-permute-done | bytes 221216 | tf_op jit(solution)/shard_map/ppermute | solution.py:247
  40.5 1.5 %collective-permute-start.6 = (bf16[32,3456]{1,0:T(8,128)(2,1)S(1)}, bf16[32,3456]{1,0:T(8,128)(2,1)S(1)}, u32[]{:S(2)}, u32[]{:S(2)}) collective-permute-start(bf16[32,3456]{1,0:T(8,128)(2,1)S(1)} %collective-permute-done.4.refs_1_), channel_id=1, source_target_pairs={{0,16},{1,9},{2,18},{3,11},{4,20},{5,13},{6,22},{7,15},{8,24},{9,1... | collective-permute-start | bytes 663560 | tf_op jit(solution)/shard_map/ppermute | solution.py:247
  42.0 0.0 collective-permute-done.16.refs_3_
  42.0 0.0 collective-permute-start.2
  42.0 1.1 prepare_other.7
  43.1 0.0 collective-permute-done.10.refs_2_
  43.1 0.6 collective-permute-start.17
  43.7 0.3 collective-permute-done.11.refs_3_
  44.0 1.1 prepare_other.6
  45.1 0.4 collective-permute-start.12
  45.5 0.9 collective-permute-done.5.refs_2_
  46.4 2.4 %collective-permute-done.6.refs_3_ = bf16[32,3456]{1,0:T(8,128)(2,1)S(1)} collective-permute-done((bf16[32,3456]{1,0:T(8,128)(2,1)S(1)}, bf16[32,3456]{1,0:T(8,128)(2,1)S(1)}, u32[]{:S(2)}, u32[]{:S(2)}) %collective-permute-start.6) | collective-permute-done | bytes 221216 | tf_op jit(solution)/shard_map/ppermute | solution.py:247
  48.7 1.1 prepare_other.5
  49.8 0.2 collective-permute-start.7
  50.0 1.1 prepare_own.6.refs_4_
  51.0 1.1 prepare_own.7.refs_6_
  52.1 1.1 prepare_own.5.refs_2_
  53.2 0.0 collective-permute-done.17.refs_7_
  53.2 0.0 collective-permute-done.12.refs_5_
  53.2 13.2 %products.3 = (f32[5,64,256]{2,1,0:T(8,128)S(1)}, bf16[5,64,256]{2,1,0:T(8,128)(2,1)S(1)}, bf16[5,64,256]{2,1,0:T(8,128)(2,1)S(1)}, bf16[5,64,256]{2,1,0:T(8,128)(2,1)S(1)}) custom-call(bf16[9,16,9216]{2,1,0:T(8,128)(2,1)S(1)} %band_matrices.1.x_ref, bf16[2,32,9216]{2,1,0:T(8,128)(2,1)S(1)} %prepare_own.4.refs_0_, ...), custom_call_target="tpu_custom_call" | custom-call | flops 12079595520 | bytes 9437184 | tf_op jit(solution)/shard_map/products/pallas_call | solution.py:147
  66.4 8.1 %collective-permute-start.18 = (bf16[5,64,256]{2,1,0:T(8,128)(2,1)S(1)}, bf16[5,64,256]{2,1,0:T(8,128)(2,1)S(1)}, u32[]{:S(2)}, u32[]{:S(2)}) collective-permute-start(bf16[5,64,256]{2,1,0:T(8,128)(2,1)S(1)} %get-tuple-element.67), channel_id=1, source_target_pairs={{0,2},{1,3},{2,4},{3,5},{4,6},{5,7},{6,0},{7,1},{8,10},{9,11},{10,... | collective-permute-start | bytes 491528 | tf_op jit(solution)/shard_map/ppermute | solution.py:247
  74.5 3.3 %collective-permute-start.19 = (bf16[5,64,256]{2,1,0:T(8,128)(2,1)S(1)}, bf16[5,64,256]{2,1,0:T(8,128)(2,1)S(1)}, u32[]{:S(2)}, u32[]{:S(2)}) collective-permute-start(bf16[5,64,256]{2,1,0:T(8,128)(2,1)S(1)} %get-tuple-element.68), channel_id=1, source_target_pairs={{0,4},{1,5},{2,6},{3,7},{4,0},{5,1},{6,2},{7,3},{8,12},{9,13},{10,... | collective-permute-start | bytes 491528 | tf_op jit(solution)/shard_map/ppermute | solution.py:247
  77.8 0.0 collective-permute-start.20
  77.8 8.0 %products.4 = (f32[3,64,256]{2,1,0:T(8,128)S(1)}, bf16[3,64,256]{2,1,0:T(8,128)(2,1)S(1)}, bf16[3,64,256]{2,1,0:T(8,128)(2,1)S(1)}, bf16[3,64,256]{2,1,0:T(8,128)(2,1)S(1)}) custom-call(bf16[9,16,9216]{2,1,0:T(8,128)(2,1)S(1)} %band_matrices.1.x_ref, bf16[2,32,9216]{2,1,0:T(8,128)(2,1)S(1)} %prepare_own.4.refs_0_, ...), custom_call_target="tpu_custom_call" | custom-call | flops 7247757312 | bytes 9437184 | tf_op jit(solution)/shard_map/products/pallas_call | solution.py:147
  85.8 2.1 %collective-permute-start.21 = (bf16[3,64,256]{2,1,0:T(8,128)(2,1)S(1)}, bf16[3,64,256]{2,1,0:T(8,128)(2,1)S(1)}, u32[]{:S(2)}, u32[]{:S(2)}) collective-permute-start(bf16[3,64,256]{2,1,0:T(8,128)(2,1)S(1)} %get-tuple-element.82), channel_id=1, source_target_pairs={{0,2},{1,3},{2,4},{3,5},{4,6},{5,7},{6,0},{7,1},{8,10},{9,11},{10,... | collective-permute-start | bytes 294920 | tf_op jit(solution)/shard_map/ppermute | solution.py:247
  87.8 0.0 collective-permute-start.22
  87.8 0.0 collective-permute-done.18
  87.9 2.4 %collective-permute-start.23 = (bf16[3,64,256]{2,1,0:T(8,128)(2,1)S(1)}, bf16[3,64,256]{2,1,0:T(8,128)(2,1)S(1)}, u32[]{:S(2)}, u32[]{:S(2)}) collective-permute-start(bf16[3,64,256]{2,1,0:T(8,128)(2,1)S(1)} %get-tuple-element.84), channel_id=1, source_target_pairs={{0,6},{1,7},{2,0},{3,1},{4,2},{5,3},{6,4},{7,5},{8,14},{9,15},{10,... | collective-permute-start | bytes 294920 | tf_op jit(solution)/shard_map/ppermute | solution.py:247
  90.3 0.0 collective-permute-done.19
  90.3 0.1 convert_add_fusion
  90.4 3.1 %products.5 = (f32[1,64,256]{2,1,0:T(8,128)S(1)}, bf16[1,64,256]{2,1,0:T(8,128)(2,1)S(1)}, bf16[1,64,256]{2,1,0:T(8,128)(2,1)S(1)}, bf16[1,64,256]{2,1,0:T(8,128)(2,1)S(1)}) custom-call(bf16[9,16,9216]{2,1,0:T(8,128)(2,1)S(1)} %band_matrices.1.x_ref, bf16[2,32,9216]{2,1,0:T(8,128)(2,1)S(1)} %prepare_own.4.refs_0_, ...), custom_call_target="tpu_custom_call" | custom-call | flops 2415919104 | bytes 9437184 | tf_op jit(solution)/shard_map/products/pallas_call | solution.py:147
  93.5 7.1 %collective-permute-start.24 = (bf16[1,64,256]{2,1,0:T(8,128)(2,1)S(1)}, bf16[1,64,256]{2,1,0:T(8,128)(2,1)S(1)}, u32[]{:S(2)}, u32[]{:S(2)}) collective-permute-start(bf16[1,64,256]{2,1,0:T(8,128)(2,1)S(1)} %get-tuple-element.90), channel_id=1, source_target_pairs={{0,2},{1,3},{2,4},{3,5},{4,6},{5,7},{6,0},{7,1},{8,10},{9,11},{10,... | collective-permute-start | bytes 98312 | tf_op jit(solution)/shard_map/ppermute | solution.py:247
  100.5 0.0 collective-permute-start.25
  100.5 2.4 %collective-permute-start.26 = (bf16[1,64,256]{2,1,0:T(8,128)(2,1)S(1)}, bf16[1,64,256]{2,1,0:T(8,128)(2,1)S(1)}, u32[]{:S(2)}, u32[]{:S(2)}) collective-permute-start(bf16[1,64,256]{2,1,0:T(8,128)(2,1)S(1)} %get-tuple-element.92), channel_id=1, source_target_pairs={{0,6},{1,7},{2,0},{3,1},{4,2},{5,3},{6,4},{7,5},{8,14},{9,15},{10,... | collective-permute-start | bytes 98312 | tf_op jit(solution)/shard_map/ppermute | solution.py:247
  103.1 0.1 collective-permute-start.28
  103.1 0.5 collective-permute-start.27
  103.6 1.7 %collective-permute-done.25 = bf16[1,64,256]{2,1,0:T(8,128)(2,1)S(1)} collective-permute-done((bf16[1,64,256]{2,1,0:T(8,128)(2,1)S(1)}, bf16[1,64,256]{2,1,0:T(8,128)(2,1)S(1)}, u32[]{:S(2)}, u32[]{:S(2)}) %collective-permute-start.25) | collective-permute-done | bytes 32800 | tf_op jit(solution)/shard_map/ppermute | solution.py:247
  105.4 0.1 collective-permute-start.29
  105.5 1.2 %collective-permute-done.29 = f32[1,32,256]{2,1,0:T(8,128)S(1)} collective-permute-done((f32[1,32,256]{2,1,0:T(8,128)S(1)}, f32[1,32,256]{2,1,0:T(8,128)S(1)}, u32[]{:S(2)}, u32[]{:S(2)}) %collective-permute-start.29) | collective-permute-done | bytes 32800 | tf_op jit(solution)/shard_map/ppermute | solution.py:247
  106.7 0.9 maximum_select_fusion
  (25 shorter events, 0.2 us)
Async XLA Ops:
  0.0 3.5 %copy-start.2 = (s32[2,288]{1,0:T(2,128)S(1)}, s32[2,288]{1,0:T(2,128)}, u32[]{:S(2)}) copy-start(s32[2,288]{1,0:T(2,128)} %kq_ref.17) | copy-start | bytes 6916
  2.9 9.0 %collective-permute-start = (bf16[9,32,288]{2,1,0:T(8,128)(2,1)}, bf16[9,32,288]{2,1,0:T(8,128)(2,1)S(1)}, u32[]{:S(2)}, u32[]{:S(2)}) collective-permute-start(bf16[9,32,288]{2,1,0:T(8,128)(2,1)} %get-tuple-element.49), channel_id=1, source_target_pairs={{0,1},{1,0},{2,3},{3,2},{4,5},{5,4},{6,7},{7,6},{8,9},{9,8},{10,11... | collective-permute-start | bytes 497672 | tf_op jit(solution)/shard_map/ppermute | solution.py:247
  3.5 1.2 %copy-start = (bf16[32,13824]{1,0:T(8,128)(2,1)S(1)}, bf16[32,13824]{1,0:T(8,128)(2,1)}, u32[]{:S(2)}) copy-start(bf16[32,13824]{1,0:T(8,128)(2,1)} %get-tuple-element.51.refs_0_) | copy-start | bytes 2654212
  5.6 6.3 %copy-start.1 = (bf16[2,9,32,288]{3,2,1,0:T(8,128)(2,1)S(1)}, bf16[2,9,32,288]{3,2,1,0:T(8,128)(2,1)}, u32[]{:S(2)}) copy-start(bf16[2,9,32,288]{3,2,1,0:T(8,128)(2,1)} %coupling_ref.3) | copy-start | bytes 995332
  5.7 11.3 %collective-permute-start.13 = (bf16[32,3456]{1,0:T(8,128)(2,1)}, bf16[32,3456]{1,0:T(8,128)(2,1)S(1)}, u32[]{:S(2)}, u32[]{:S(2)}) collective-permute-start(bf16[32,3456]{1,0:T(8,128)(2,1)} %get-tuple-element.59), channel_id=1, source_target_pairs={{0,2},{1,3},{2,4},{3,5},{4,6},{5,7},{6,0},{7,1},{8,10},{9,11},{10,... | collective-permute-start | bytes 663560 | tf_op jit(solution)/shard_map/ppermute | solution.py:247
  9.3 16.9 %collective-permute-start.8 = (bf16[32,3456]{1,0:T(8,128)(2,1)}, bf16[32,3456]{1,0:T(8,128)(2,1)S(1)}, u32[]{:S(2)}, u32[]{:S(2)}) collective-permute-start(bf16[32,3456]{1,0:T(8,128)(2,1)} %get-tuple-element.56), channel_id=1, source_target_pairs={{0,4},{1,5},{2,6},{3,7},{4,0},{5,1},{6,2},{7,3},{8,12},{9,13},{10,... | collective-permute-start | bytes 663560 | tf_op jit(solution)/shard_map/ppermute | solution.py:247
  12.0 15.7 %collective-permute-start.1 = (bf16[9,32,288]{2,1,0:T(8,128)(2,1)S(1)}, bf16[9,32,288]{2,1,0:T(8,128)(2,1)S(1)}, u32[]{:S(2)}, u32[]{:S(2)}) collective-permute-start(bf16[9,32,288]{2,1,0:T(8,128)(2,1)S(1)} %bitcast_select_fusion), channel_id=1, source_target_pairs={{0,6},{1,7},{2,0},{3,1},{4,2},{5,3},{6,4},{7,5},{8,14},{9,15},{10,... | collective-permute-start | bytes 497672 | tf_op jit(solution)/shard_map/ppermute | solution.py:247
  13.4 18.7 %collective-permute-start.3 = (bf16[32,3456]{1,0:T(8,128)(2,1)}, bf16[32,3456]{1,0:T(8,128)(2,1)S(1)}, u32[]{:S(2)}, u32[]{:S(2)}) collective-permute-start(bf16[32,3456]{1,0:T(8,128)(2,1)} %get-tuple-element.52), channel_id=1, source_target_pairs={{0,6},{1,7},{2,0},{3,1},{4,2},{5,3},{6,4},{7,5},{8,14},{9,15},{10,... | collective-permute-start | bytes 663560 | tf_op jit(solution)/shard_map/ppermute | solution.py:247
  17.0 19.3 %collective-permute-start.15 = (bf16[32,3456]{1,0:T(8,128)(2,1)S(1)}, bf16[32,3456]{1,0:T(8,128)(2,1)S(1)}, u32[]{:S(2)}, u32[]{:S(2)}) collective-permute-start(bf16[32,3456]{1,0:T(8,128)(2,1)S(1)} %collective-permute-done.13.refs_0_), channel_id=1, source_target_pairs={{0,16},{1,9},{2,18},{3,11},{4,20},{5,13},{6,22},{7,15},{8,24},{9,1... | collective-permute-start | bytes 663560 | tf_op jit(solution)/shard_map/ppermute | solution.py:247
  18.6 14.1 %collective-permute-start.14 = (bf16[32,3456]{1,0:T(8,128)(2,1)S(1)}, bf16[32,3456]{1,0:T(8,128)(2,1)S(1)}, u32[]{:S(2)}, u32[]{:S(2)}) collective-permute-start(bf16[32,3456]{1,0:T(8,128)(2,1)S(1)} %collective-permute-done.13.refs_0_), channel_id=1, source_target_pairs={{0,8},{1,17},{2,10},{3,19},{4,12},{5,21},{6,14},{7,23},{8,0},{9,25... | collective-permute-start | bytes 663560 | tf_op jit(solution)/shard_map/ppermute | solution.py:247
  26.3 8.5 %collective-permute-start.9 = (bf16[32,3456]{1,0:T(8,128)(2,1)S(1)}, bf16[32,3456]{1,0:T(8,128)(2,1)S(1)}, u32[]{:S(2)}, u32[]{:S(2)}) collective-permute-start(bf16[32,3456]{1,0:T(8,128)(2,1)S(1)} %collective-permute-done.8.refs_0_), channel_id=1, source_target_pairs={{0,8},{1,17},{2,10},{3,19},{4,12},{5,21},{6,14},{7,23},{8,0},{9,25... | collective-permute-start | bytes 663560 | tf_op jit(solution)/shard_map/ppermute | solution.py:247
  32.1 8.4 %collective-permute-start.4 = (bf16[32,3456]{1,0:T(8,128)(2,1)S(1)}, bf16[32,3456]{1,0:T(8,128)(2,1)S(1)}, u32[]{:S(2)}, u32[]{:S(2)}) collective-permute-start(bf16[32,3456]{1,0:T(8,128)(2,1)S(1)} %collective-permute-done.3.refs_0_), channel_id=1, source_target_pairs={{0,8},{1,17},{2,10},{3,19},{4,12},{5,21},{6,14},{7,23},{8,0},{9,25... | collective-permute-start | bytes 663560 | tf_op jit(solution)/shard_map/ppermute | solution.py:247
  32.7 9.3 %collective-permute-start.16 = (bf16[32,3456]{1,0:T(8,128)(2,1)S(1)}, bf16[32,3456]{1,0:T(8,128)(2,1)S(1)}, u32[]{:S(2)}, u32[]{:S(2)}) collective-permute-start(bf16[32,3456]{1,0:T(8,128)(2,1)S(1)} %collective-permute-done.14.refs_1_), channel_id=1, source_target_pairs={{0,16},{1,9},{2,18},{3,11},{4,20},{5,13},{6,22},{7,15},{8,24},{9,1... | collective-permute-start | bytes 663560 | tf_op jit(solution)/shard_map/ppermute | solution.py:247
  34.3 8.8 %collective-permute-start.10 = (bf16[32,3456]{1,0:T(8,128)(2,1)S(1)}, bf16[32,3456]{1,0:T(8,128)(2,1)S(1)}, u32[]{:S(2)}, u32[]{:S(2)}) collective-permute-start(bf16[32,3456]{1,0:T(8,128)(2,1)S(1)} %collective-permute-done.8.refs_0_), channel_id=1, source_target_pairs={{0,16},{1,9},{2,18},{3,11},{4,20},{5,13},{6,22},{7,15},{8,24},{9,1... | collective-permute-start | bytes 663560 | tf_op jit(solution)/shard_map/ppermute | solution.py:247
  34.8 9.2 %collective-permute-start.11 = (bf16[32,3456]{1,0:T(8,128)(2,1)S(1)}, bf16[32,3456]{1,0:T(8,128)(2,1)S(1)}, u32[]{:S(2)}, u32[]{:S(2)}) collective-permute-start(bf16[32,3456]{1,0:T(8,128)(2,1)S(1)} %collective-permute-done.9.refs_1_), channel_id=1, source_target_pairs={{0,16},{1,9},{2,18},{3,11},{4,20},{5,13},{6,22},{7,15},{8,24},{9,1... | collective-permute-start | bytes 663560 | tf_op jit(solution)/shard_map/ppermute | solution.py:247
  36.3 10.1 %collective-permute-start.5 = (bf16[32,3456]{1,0:T(8,128)(2,1)S(1)}, bf16[32,3456]{1,0:T(8,128)(2,1)S(1)}, u32[]{:S(2)}, u32[]{:S(2)}) collective-permute-start(bf16[32,3456]{1,0:T(8,128)(2,1)S(1)} %collective-permute-done.3.refs_0_), channel_id=1, source_target_pairs={{0,16},{1,9},{2,18},{3,11},{4,20},{5,13},{6,22},{7,15},{8,24},{9,1... | collective-permute-start | bytes 663560 | tf_op jit(solution)/shard_map/ppermute | solution.py:247
  40.5 8.2 %collective-permute-start.6 = (bf16[32,3456]{1,0:T(8,128)(2,1)S(1)}, bf16[32,3456]{1,0:T(8,128)(2,1)S(1)}, u32[]{:S(2)}, u32[]{:S(2)}) collective-permute-start(bf16[32,3456]{1,0:T(8,128)(2,1)S(1)} %collective-permute-done.4.refs_1_), channel_id=1, source_target_pairs={{0,16},{1,9},{2,18},{3,11},{4,20},{5,13},{6,22},{7,15},{8,24},{9,1... | collective-permute-start | bytes 663560 | tf_op jit(solution)/shard_map/ppermute | solution.py:247
  42.0 11.2 %collective-permute-start.2 = (bf16[2,32,9216]{2,1,0:T(8,128)(2,1)S(1)}, bf16[2,32,9216]{2,1,0:T(8,128)(2,1)S(1)}, u32[]{:S(2)}, u32[]{:S(2)}) collective-permute-start(bf16[2,32,9216]{2,1,0:T(8,128)(2,1)S(1)} %prepare_other.4), channel_id=1, source_target_pairs={{0,1},{1,0},{2,3},{3,2},{4,5},{5,4},{6,7},{7,6},{8,9},{9,8},{10,11... | collective-permute-start | bytes 3538952 | tf_op jit(solution)/shard_map/ppermute | solution.py:247
  43.1 10.1 %collective-permute-start.17 = (bf16[2,32,9216]{2,1,0:T(8,128)(2,1)S(1)}, bf16[2,32,9216]{2,1,0:T(8,128)(2,1)S(1)}, u32[]{:S(2)}, u32[]{:S(2)}) collective-permute-start(bf16[2,32,9216]{2,1,0:T(8,128)(2,1)S(1)} %prepare_other.7), channel_id=1, source_target_pairs={{0,1},{1,0},{2,3},{3,2},{4,5},{5,4},{6,7},{7,6},{8,9},{9,8},{10,11... | collective-permute-start | bytes 3538952 | tf_op jit(solution)/shard_map/ppermute | solution.py:247
  45.1 8.1 %collective-permute-start.12 = (bf16[2,32,9216]{2,1,0:T(8,128)(2,1)S(1)}, bf16[2,32,9216]{2,1,0:T(8,128)(2,1)S(1)}, u32[]{:S(2)}, u32[]{:S(2)}) collective-permute-start(bf16[2,32,9216]{2,1,0:T(8,128)(2,1)S(1)} %prepare_other.6), channel_id=1, source_target_pairs={{0,1},{1,0},{2,3},{3,2},{4,5},{5,4},{6,7},{7,6},{8,9},{9,8},{10,11... | collective-permute-start | bytes 3538952 | tf_op jit(solution)/shard_map/ppermute | solution.py:247
  49.8 3.4 %collective-permute-start.7 = (bf16[2,32,9216]{2,1,0:T(8,128)(2,1)S(1)}, bf16[2,32,9216]{2,1,0:T(8,128)(2,1)S(1)}, u32[]{:S(2)}, u32[]{:S(2)}) collective-permute-start(bf16[2,32,9216]{2,1,0:T(8,128)(2,1)S(1)} %prepare_other.5), channel_id=1, source_target_pairs={{0,1},{1,0},{2,3},{3,2},{4,5},{5,4},{6,7},{7,6},{8,9},{9,8},{10,11... | collective-permute-start | bytes 3538952 | tf_op jit(solution)/shard_map/ppermute | solution.py:247
  66.4 21.4 %collective-permute-start.18 = (bf16[5,64,256]{2,1,0:T(8,128)(2,1)S(1)}, bf16[5,64,256]{2,1,0:T(8,128)(2,1)S(1)}, u32[]{:S(2)}, u32[]{:S(2)}) collective-permute-start(bf16[5,64,256]{2,1,0:T(8,128)(2,1)S(1)} %get-tuple-element.67), channel_id=1, source_target_pairs={{0,2},{1,3},{2,4},{3,5},{4,6},{5,7},{6,0},{7,1},{8,10},{9,11},{10,... | collective-permute-start | bytes 491528 | tf_op jit(solution)/shard_map/ppermute | solution.py:247
  74.5 15.8 %collective-permute-start.19 = (bf16[5,64,256]{2,1,0:T(8,128)(2,1)S(1)}, bf16[5,64,256]{2,1,0:T(8,128)(2,1)S(1)}, u32[]{:S(2)}, u32[]{:S(2)}) collective-permute-start(bf16[5,64,256]{2,1,0:T(8,128)(2,1)S(1)} %get-tuple-element.68), channel_id=1, source_target_pairs={{0,4},{1,5},{2,6},{3,7},{4,0},{5,1},{6,2},{7,3},{8,12},{9,13},{10,... | collective-permute-start | bytes 491528 | tf_op jit(solution)/shard_map/ppermute | solution.py:247
  77.8 12.5 %collective-permute-start.20 = (bf16[5,64,256]{2,1,0:T(8,128)(2,1)S(1)}, bf16[5,64,256]{2,1,0:T(8,128)(2,1)S(1)}, u32[]{:S(2)}, u32[]{:S(2)}) collective-permute-start(bf16[5,64,256]{2,1,0:T(8,128)(2,1)S(1)} %get-tuple-element.69), channel_id=1, source_target_pairs={{0,6},{1,7},{2,0},{3,1},{4,2},{5,3},{6,4},{7,5},{8,14},{9,15},{10,... | collective-permute-start | bytes 491528 | tf_op jit(solution)/shard_map/ppermute | solution.py:247
  85.8 14.8 %collective-permute-start.21 = (bf16[3,64,256]{2,1,0:T(8,128)(2,1)S(1)}, bf16[3,64,256]{2,1,0:T(8,128)(2,1)S(1)}, u32[]{:S(2)}, u32[]{:S(2)}) collective-permute-start(bf16[3,64,256]{2,1,0:T(8,128)(2,1)S(1)} %get-tuple-element.82), channel_id=1, source_target_pairs={{0,2},{1,3},{2,4},{3,5},{4,6},{5,7},{6,0},{7,1},{8,10},{9,11},{10,... | collective-permute-start | bytes 294920 | tf_op jit(solution)/shard_map/ppermute | solution.py:247
  87.8 15.2 %collective-permute-start.22 = (bf16[3,64,256]{2,1,0:T(8,128)(2,1)S(1)}, bf16[3,64,256]{2,1,0:T(8,128)(2,1)S(1)}, u32[]{:S(2)}, u32[]{:S(2)}) collective-permute-start(bf16[3,64,256]{2,1,0:T(8,128)(2,1)S(1)} %get-tuple-element.83), channel_id=1, source_target_pairs={{0,4},{1,5},{2,6},{3,7},{4,0},{5,1},{6,2},{7,3},{8,12},{9,13},{10,... | collective-permute-start | bytes 294920 | tf_op jit(solution)/shard_map/ppermute | solution.py:247
  87.9 15.1 %collective-permute-start.23 = (bf16[3,64,256]{2,1,0:T(8,128)(2,1)S(1)}, bf16[3,64,256]{2,1,0:T(8,128)(2,1)S(1)}, u32[]{:S(2)}, u32[]{:S(2)}) collective-permute-start(bf16[3,64,256]{2,1,0:T(8,128)(2,1)S(1)} %get-tuple-element.84), channel_id=1, source_target_pairs={{0,6},{1,7},{2,0},{3,1},{4,2},{5,3},{6,4},{7,5},{8,14},{9,15},{10,... | collective-permute-start | bytes 294920 | tf_op jit(solution)/shard_map/ppermute | solution.py:247
  93.5 10.2 %collective-permute-start.24 = (bf16[1,64,256]{2,1,0:T(8,128)(2,1)S(1)}, bf16[1,64,256]{2,1,0:T(8,128)(2,1)S(1)}, u32[]{:S(2)}, u32[]{:S(2)}) collective-permute-start(bf16[1,64,256]{2,1,0:T(8,128)(2,1)S(1)} %get-tuple-element.90), channel_id=1, source_target_pairs={{0,2},{1,3},{2,4},{3,5},{4,6},{5,7},{6,0},{7,1},{8,10},{9,11},{10,... | collective-permute-start | bytes 98312 | tf_op jit(solution)/shard_map/ppermute | solution.py:247
  100.5 4.8 %collective-permute-start.25 = (bf16[1,64,256]{2,1,0:T(8,128)(2,1)S(1)}, bf16[1,64,256]{2,1,0:T(8,128)(2,1)S(1)}, u32[]{:S(2)}, u32[]{:S(2)}) collective-permute-start(bf16[1,64,256]{2,1,0:T(8,128)(2,1)S(1)} %get-tuple-element.91), channel_id=1, source_target_pairs={{0,4},{1,5},{2,6},{3,7},{4,0},{5,1},{6,2},{7,3},{8,12},{9,13},{10,... | collective-permute-start | bytes 98312 | tf_op jit(solution)/shard_map/ppermute | solution.py:247
  100.5 4.8 %collective-permute-start.26 = (bf16[1,64,256]{2,1,0:T(8,128)(2,1)S(1)}, bf16[1,64,256]{2,1,0:T(8,128)(2,1)S(1)}, u32[]{:S(2)}, u32[]{:S(2)}) collective-permute-start(bf16[1,64,256]{2,1,0:T(8,128)(2,1)S(1)} %get-tuple-element.92), channel_id=1, source_target_pairs={{0,6},{1,7},{2,0},{3,1},{4,2},{5,3},{6,4},{7,5},{8,14},{9,15},{10,... | collective-permute-start | bytes 98312 | tf_op jit(solution)/shard_map/ppermute | solution.py:247
  103.1 3.6 %collective-permute-start.28 = (f32[3,32,256]{2,1,0:T(8,128)S(1)}, f32[3,32,256]{2,1,0:T(8,128)S(1)}, u32[]{:S(2)}, u32[]{:S(2)}) collective-permute-start(f32[3,32,256]{2,1,0:T(8,128)S(1)} %get-tuple-element.96), channel_id=1, source_target_pairs={{0,1},{1,0},{2,3},{3,2},{4,5},{5,4},{6,7},{7,6},{8,9},{9,8},{10,11... | collective-permute-start | bytes 294920 | tf_op jit(solution)/shard_map/ppermute | solution.py:247
  103.1 3.5 %collective-permute-start.27 = (f32[5,32,256]{2,1,0:T(8,128)S(1)}, f32[5,32,256]{2,1,0:T(8,128)S(1)}, u32[]{:S(2)}, u32[]{:S(2)}) collective-permute-start(f32[5,32,256]{2,1,0:T(8,128)S(1)} %get-tuple-element.94), channel_id=1, source_target_pairs={{0,1},{1,0},{2,3},{3,2},{4,5},{5,4},{6,7},{7,6},{8,9},{9,8},{10,11... | collective-permute-start | bytes 491528 | tf_op jit(solution)/shard_map/ppermute | solution.py:247
  105.4 1.3 %collective-permute-start.29 = (f32[1,32,256]{2,1,0:T(8,128)S(1)}, f32[1,32,256]{2,1,0:T(8,128)S(1)}, u32[]{:S(2)}, u32[]{:S(2)}) collective-permute-start(f32[1,32,256]{2,1,0:T(8,128)S(1)} %get-tuple-element.98), channel_id=1, source_target_pairs={{0,1},{1,0},{2,3},{3,2},{4,5},{5,4},{6,7},{7,6},{8,9},{9,8},{10,11... | collective-permute-start | bytes 98312 | tf_op jit(solution)/shard_map/ppermute | solution.py:247

commit v6 on v5

--- a/solution.py
+++ b/solution.py
@@ -61,7 +61,7 @@
     rows = envelopes.shape[0]
     shape = functools.partial(jax.ShapeDtypeStruct, dtype=BF16)
     outs = [shape((rows, 3 * block // 4))] * (n_z - 1) + [shape((rows, 3 * block)), shape(coupling.shape[1:])]
-    *pieces, window, give = pl.pallas_call(
+    return pl.pallas_call(
         functools.partial(cut_kernel, block),
         in_specs=[pl.BlockSpec(memory_space=pl.ANY)] * 2,
         out_specs=[pl.BlockSpec(memory_space=pltpu.VMEM)] * len(outs),
@@ -69,10 +69,9 @@
         scratch_shapes=[pltpu.SemaphoreType.DMA((3 * n_z + 10,))],
         name="cut",
     )(envelopes, coupling)
-    return pieces, window, give
-
-
-def prep_kernel(block_lines, lines_all, for_other, kq_ref, *refs):
+
+
+def prep_kernel(block_lines, lines_all, for_other, direct, kq_ref, *refs):
     ins, (out_ref, window) = refs[:-2], refs[-2:]
     pb, _, core = place()
     q = 1 - core if for_other else core
@@ -80,7 +79,7 @@
     if len(ins) == 1:
         window = ins[0]
     else:
-        for rel, src in zip((0, 1 + core, 2 - core, 3), ins):
+        for rel, src in zip((0, 1, 2, 3) if direct else (0, 1 + core, 2 - core, 3), ins):
             size = src.shape[1]
             window[:, pl.ds(pl.multiple_of((pb ^ rel) * size, 128), size)] = src[...]
     for line in range(2 * block_lines):
@@ -90,10 +89,10 @@
         out_ref[1, :, to] = pltpu.roll(shifted, turn, 1).astype(BF16)
 
 
-def prepare(kq_map, ins, block, lines_all, for_other):
+def prepare(kq_map, ins, block, lines_all, for_other, direct):
     rows = ins[0].shape[0]
     return pl.pallas_call(
-        functools.partial(prep_kernel, block // LINE, lines_all, for_other),
+        functools.partial(prep_kernel, block // LINE, lines_all, for_other, direct),
         in_specs=[pl.BlockSpec(memory_space=pltpu.SMEM)] + [pl.BlockSpec(memory_space=pltpu.VMEM)] * len(ins),
         out_specs=pl.BlockSpec(memory_space=pltpu.VMEM),
         out_shape=jax.ShapeDtypeStruct((2, rows, 2 * block), BF16),
@@ -158,27 +157,40 @@
     )(x, *amps)
 
 
-def band_kernel(block_lines, lines_all, kq_ref, coupling_ref, other_ref, next_ref, x_ref):
+def iota(shape, dim):
+    return lax.broadcasted_iota(jnp.int32, shape, dim)
+
+
+def spread_kernel(_, out_ref):
+    _, rows, lanes = out_ref.shape
+    row, lane = iota((rows, lanes), 0), iota((rows, lanes), 1)
+    here = row % (rows // 4) == lane // BANDS
+    index = row // (rows // 4)
+    out_ref[0] = (here & (index == lane % 4)).astype(F32).astype(BF16)
+    out_ref[1] = (here & (index == lane % BANDS // 4)).astype(F32).astype(BF16)
+
+
+def spread_matrices(size, earlier):
+    return pl.pallas_call(
+        spread_kernel,
+        in_specs=[pl.BlockSpec(memory_space=pl.ANY)],
+        out_specs=pl.BlockSpec(memory_space=pltpu.VMEM),
+        out_shape=jax.ShapeDtypeStruct((2, 4 * size, size * BANDS), BF16),
+        compiler_params=pltpu.CompilerParams(vmem_limit_bytes=24 << 20),
+        cost_estimate=pl.CostEstimate(flops=3 * 10**9, bytes_accessed=10**6, transcendentals=0),
+        name="spread",
+    )(earlier)
+
+
+def band_kernel(block_lines, lines_all, kq_ref, spread, coupling_ref, other_ref, next_ref, x_ref):
     branches, _, count = other_ref.shape
     half = BANDS // 4
-    size = min(count, 128)
-
-    def iota(shape, dim):
-        return lax.broadcasted_iota(jnp.int32, shape, dim)
-
+    size = spread.shape[1] // 4
     shape = (8 * BANDS, 32)
     row, col = iota(shape, 0), iota(shape, 1)
     term, v, c = row // BANDS, row % BANDS // half, row % half
     choice = jnp.where(term < 4, 4 * term + c, 16 + 4 * v + (term - 4))
     pick = (choice == col).astype(F32).astype(BF16)
-    spread = []
-    for by_a in (False, True):
-        shape = (4 * size, size * BANDS)
-        row, lane = iota(shape, 0), iota(shape, 1)
-        band = lane % BANDS
-        index = band // half if by_a else band % half
-        hit = (row % size == lane // BANDS) & (row // size == index)
-        spread.append(hit.astype(F32).astype(BF16))
     shape = (branches * BANDS, size * BANDS)
     row, lane = iota(shape, 0) % BANDS, iota(shape, 1) % BANDS
     keep_cond = (row // half == lane // half).astype(F32)
@@ -208,24 +220,24 @@
                             slab = jnp.concatenate([slab, jnp.zeros((BANDS, size - width), BF16)], axis=1)
                         slabs.append(slab)
                     rows.append(jnp.concatenate(slabs, axis=1))
-                values.append(contract(jnp.concatenate(rows, axis=0), spread[kind][:, :lanes], 1, 0))
+                values.append(contract(jnp.concatenate(rows, axis=0), spread[kind, :, :lanes], 1, 0))
             total = (values[0] * keep_cond[:, :lanes] - values[1] * keep_val[:, :lanes]).astype(BF16)
             at = (part * count + start) * BANDS
             for branch in range(branches):
                 x_ref[branch, :, at : at + lanes] = total[branch * BANDS : (branch + 1) * BANDS]
 
 
-def band_matrices(kq_map, coupling, other, following, lines_all):
+def band_matrices(kq_map, spread, coupling, other, following, lines_all):
     branches, _, count = other.shape
     return pl.pallas_call(
         functools.partial(band_kernel, count // KY, lines_all),
-        in_specs=[pl.BlockSpec(memory_space=pltpu.SMEM)] + [pl.BlockSpec(memory_space=pltpu.VMEM)] * 3,
+        in_specs=[pl.BlockSpec(memory_space=pltpu.SMEM)] + [pl.BlockSpec(memory_space=pltpu.VMEM)] * 4,
         out_specs=pl.BlockSpec(memory_space=pltpu.VMEM),
         out_shape=jax.ShapeDtypeStruct((branches, BANDS, 2 * count * BANDS), BF16),
-        compiler_params=pltpu.CompilerParams(vmem_limit_bytes=40 << 20),
-        cost_estimate=pl.CostEstimate(flops=10**10, bytes_accessed=10**6, transcendentals=0),
+        compiler_params=pltpu.CompilerParams(vmem_limit_bytes=32 << 20),
+        cost_estimate=pl.CostEstimate(flops=3 * 10**9, bytes_accessed=10**6, transcendentals=0),
         name="band_matrices",
-    )(kq_map, coupling, other, following)
+    )(kq_map, spread, coupling, other, following)
 
 
 def shards(envelopes, coupling, kq_map):
@@ -255,36 +267,42 @@
     def passed_down(x, e):
         return permute(x, lambda p, zz, c: (p, zz - e, c))
 
-    def prepared(ins, for_other):
-        return prepare(kq_map, ins, block, lines_all, for_other)
+    def prepared(ins, for_other, direct=False):
+        return prepare(kq_map, ins, block, lines_all, for_other, direct)
 
     def after(x, *others):
         return lax.optimization_barrier((x, *others))[0]
 
-    pieces, window, give = cut(envelopes, coupling, n_z, block)
     near = sorted({1, n_z - 1})
     far = [e for e in range(2, n_z - 1)]
-    arrived = {1: passed_down(pieces[0], 1)}
-    pass_on = prepared([window], True)
-    if len(near) > 1:
-        arrived[n_z - 1] = passed_down(after(pieces[n_z - 2], pass_on), n_z - 1)
+    *pieces, window, give = cut(envelopes, coupling, n_z, block)
+    arrived = {e: passed_down(pieces[e - 1], e) for e in near}
+    other_table = sibling(give)
+    first_table = jnp.where(core == 0, lax.dynamic_index_in_dim(coupling, core, 0, keepdims=False), other_table)
+    next_table = passed_down(first_table, 1)
+    pass_on = prepared([after(window, first_table)], True)
     keep = prepared([after(window, pass_on)], False)
     for e in far:
         arrived[e] = passed_down(after(pieces[e - 1], keep), e)
+    spread = spread_matrices(min(coupling.shape[3], 128), keep)
     amps = {0: (keep, sibling(pass_on))}
-    other_table = sibling(give)
-    first_table = jnp.where(core == 0, lax.dynamic_index_in_dim(coupling, core, 0, keepdims=False), other_table)
-    next_table = passed_down(first_table, 1)
-    x = band_matrices(kq_map, coupling, other_table, next_table, lines_all)
-    arrived[1] = after(arrived[1], x)
-
-    for e in near + far:
+
+    parts, first_steps = {}, []
+    for e in near:
         piece = arrived[e]
         one = permute(piece, lambda p, zz, c: (p ^ (1 + c), zz, c))
         two = permute(piece, lambda p, zz, c: (p ^ (2 - c), zz, c))
-        three = permute(one, lambda p, zz, c: (p ^ (2 - c), zz, c))
-        pass_on = prepared([piece, one, two, three], True)
-        keep = prepared([after(piece, pass_on), one, two, three], False)
+        first_steps += [one, two]
+        parts[e] = [piece, one, two, permute(one, lambda p, zz, c: (p ^ (2 - c), zz, c))]
+    for e in far:
+        piece = after(arrived[e], next_table, *first_steps)
+        parts[e] = [piece] + [permute(piece, lambda p, zz, c: (p ^ i, zz, c)) for i in (1, 2, 3)]
+    late = [parts[e][0] for e in far]
+    x = band_matrices(kq_map, spread, coupling, other_table, after(next_table, *late), lines_all)
+    for e in near + far:
+        piece, *others = parts[e]
+        pass_on = prepared([after(piece, x)] + others, True, e in far)
+        keep = prepared([after(piece, pass_on)] + others, False, e in far)
         amps[e] = (keep, sibling(pass_on))
     amps = [half for e in range(n_z) for half in amps[e]]
 

time: 108 us -> 105 us (0.972)
  starting transfers between devices: 45.6 us -> 40.6 us
  waiting for transfers between devices: 19.5 us -> 21.1 us
    ppermute x30, starting transfers between devices: 45.6 us -> 40.6 us  [permute(): return lax.ppermute(x, ('pb', 'ka'), pairs)]
    ppermute x30, waiting for transfers between devices: 19.5 us -> 21.1 us  [permute(): return lax.ppermute(x, ('pb', 'ka'), pairs)]
  transfers between devices with their start and end apart: 30 -> 30, of which waited for: 8 -> 7; matrix products, arithmetic and copies ran while one was open for 0% -> 0% of each run, Pallas kernels for 22% -> 23%
where the time goes in v6:
time: 105 us
  starting transfers between devices  40.6 us (39%)
  Pallas kernels  40.5 us (39%)
  waiting for transfers between devices  21.1 us (20%)
  local copies, waits for them, and re-layouts  1.22 us (1%)
  other arithmetic  1.07 us (1%)
    ppermute x30, starting transfers between devices, permute(): return lax.ppermute(x, ('pb', 'ka'), pairs)  40.6 us
    pallas_call x3, Pallas kernels, products(): pl.pallas_call(functools.partial(main_kernel, sources, first, branches, f...  24.2 us
    ppermute x30, waiting for transfers between devices, permute(): return lax.ppermute(x, ('pb', 'ka'), pairs)  21.1 us
    pallas_call x8, Pallas kernels, prepare(): pl.pallas_call(functools.partial(prep_kernel, block // LINE, lines_all, f...  8.31 us
    pallas_call x1, Pallas kernels, band_matrices(): pl.pallas_call(functools.partial(band_kernel, count // KY, lines_all), in...  4.57 us
    pallas_call x1, Pallas kernels, cut(): pl.pallas_call(functools.partial(cut_kernel, block), in_specs=[pl.BlockSp...  2.98 us
  transfers between devices with their start and end apart: 30, of which 7 were waited for; matrix products, arithmetic and copies ran while one was open for 0% of the time, Pallas kernels for 23%

profile of v6, /device:TPU:0, one launch (start us, length us, event | category | flops | bytes accessed | tf_op | source)
XLA Modules:
  0.0 104.8 jit_solution(11210945883789755639)
XLA Ops:
  0.0 3.0 %cut.1 = (bf16[32,3456]{1,0:T(8,128)(2,1)}, bf16[32,3456]{1,0:T(8,128)(2,1)}, bf16[32,3456]{1,0:T(8,128)(2,1)}, bf16[32,13824]{1,0:T(8,128)(2,1)}, bf16[9,32,288]{2,1,0:T(8,128)(2,1)}) custom-call(bf16[32,36864]{1,0:T(8,128)(2,1)} %env_ref.1, bf16[2,9,32,288]{3,2,1,0:T(8,128)(2,1)} %coupling_ref.3), custom_call_target="tpu_custom_call" | custom-call | tf_op jit(solution)/shard_map/cut/pallas_call | solution.py:64
  3.0 0.5 collective-permute-start
  3.5 4.7 %collective-permute-start.3 = (bf16[32,3456]{1,0:T(8,128)(2,1)}, bf16[32,3456]{1,0:T(8,128)(2,1)S(1)}, u32[]{:S(2)}, u32[]{:S(2)}) collective-permute-start(bf16[32,3456]{1,0:T(8,128)(2,1)} %get-tuple-element.59), channel_id=1, source_target_pairs={{0,6},{1,7},{2,0},{3,1},{4,2},{5,3},{6,4},{7,5},{8,14},{9,15},{10,... | collective-permute-start | bytes 663560 | tf_op jit(solution)/shard_map/ppermute | solution.py:259
  8.2 0.0 collective-permute-start.6
  8.2 0.0 collective-permute-done.other_ref
  8.3 3.9 %collective-permute-start.1 = (bf16[9,32,288]{2,1,0:T(8,128)(2,1)S(1)}, bf16[9,32,288]{2,1,0:T(8,128)(2,1)S(1)}, u32[]{:S(2)}, u32[]{:S(2)}) collective-permute-start(bf16[9,32,288]{2,1,0:T(8,128)(2,1)S(1)} %bitcast_select_fusion), channel_id=1, source_target_pairs={{0,6},{1,7},{2,0},{3,1},{4,2},{5,3},{6,4},{7,5},{8,14},{9,15},{10,... | collective-permute-start | bytes 497672 | tf_op jit(solution)/shard_map/ppermute | solution.py:259
  12.1 1.2 %copy-done = bf16[32,13824]{1,0:T(8,128)(2,1)S(1)} copy-done((bf16[32,13824]{1,0:T(8,128)(2,1)S(1)}, bf16[32,13824]{1,0:T(8,128)(2,1)}, u32[]{:S(2)}) %copy-start) | copy-done | bytes 884760
  13.3 1.0 prepare_other.4
  14.3 1.0 prepare_own.4._.refs_0_
  15.3 0.1 collective-permute-start.2
  15.4 0.0 collective-permute-done.3.refs_0_
  15.4 1.6 %collective-permute-start.5 = (bf16[32,3456]{1,0:T(8,128)(2,1)S(1)}, bf16[32,3456]{1,0:T(8,128)(2,1)S(1)}, u32[]{:S(2)}, u32[]{:S(2)}) collective-permute-start(bf16[32,3456]{1,0:T(8,128)(2,1)S(1)} %collective-permute-done.3.refs_0_), channel_id=1, source_target_pairs={{0,16},{1,9},{2,18},{3,11},{4,20},{5,13},{6,22},{7,15},{8,24},{9,1... | collective-permute-start | bytes 663560 | tf_op jit(solution)/shard_map/ppermute | solution.py:259
  17.0 1.5 %collective-permute-start.4 = (bf16[32,3456]{1,0:T(8,128)(2,1)S(1)}, bf16[32,3456]{1,0:T(8,128)(2,1)S(1)}, u32[]{:S(2)}, u32[]{:S(2)}) collective-permute-start(bf16[32,3456]{1,0:T(8,128)(2,1)S(1)} %collective-permute-done.3.refs_0_), channel_id=1, source_target_pairs={{0,8},{1,17},{2,10},{3,19},{4,12},{5,21},{6,14},{7,23},{8,0},{9,25... | collective-permute-start | bytes 663560 | tf_op jit(solution)/shard_map/ppermute | solution.py:259
  18.5 1.4 %collective-permute-done.6.refs_0_ = bf16[32,3456]{1,0:T(8,128)(2,1)S(1)} collective-permute-done((bf16[32,3456]{1,0:T(8,128)(2,1)}, bf16[32,3456]{1,0:T(8,128)(2,1)S(1)}, u32[]{:S(2)}, u32[]{:S(2)}) %collective-permute-start.6) | collective-permute-done | bytes 221216 | tf_op jit(solution)/shard_map/ppermute | solution.py:259
  19.8 1.5 %collective-permute-start.8 = (bf16[32,3456]{1,0:T(8,128)(2,1)S(1)}, bf16[32,3456]{1,0:T(8,128)(2,1)S(1)}, u32[]{:S(2)}, u32[]{:S(2)}) collective-permute-start(bf16[32,3456]{1,0:T(8,128)(2,1)S(1)} %collective-permute-done.6.refs_0_), channel_id=1, source_target_pairs={{0,16},{1,9},{2,18},{3,11},{4,20},{5,13},{6,22},{7,15},{8,24},{9,1... | collective-permute-start | bytes 663560 | tf_op jit(solution)/shard_map/ppermute | solution.py:259
  21.4 2.3 %collective-permute-done.1.next_ref = bf16[9,32,288]{2,1,0:T(8,128)(2,1)S(1)} collective-permute-done((bf16[9,32,288]{2,1,0:T(8,128)(2,1)S(1)}, bf16[9,32,288]{2,1,0:T(8,128)(2,1)S(1)}, u32[]{:S(2)}, u32[]{:S(2)}) %collective-permute-start.1) | collective-permute-done | bytes 165920 | tf_op jit(solution)/shard_map/ppermute | solution.py:259
  23.7 1.5 %collective-permute-start.7 = (bf16[32,3456]{1,0:T(8,128)(2,1)S(1)}, bf16[32,3456]{1,0:T(8,128)(2,1)S(1)}, u32[]{:S(2)}, u32[]{:S(2)}) collective-permute-start(bf16[32,3456]{1,0:T(8,128)(2,1)S(1)} %collective-permute-done.6.refs_0_), channel_id=1, source_target_pairs={{0,8},{1,17},{2,10},{3,19},{4,12},{5,21},{6,14},{7,23},{8,0},{9,25... | collective-permute-start | bytes 663560 | tf_op jit(solution)/shard_map/ppermute | solution.py:259
  25.2 0.4 spread.1
  25.6 7.0 %collective-permute-done.2.refs_0_ = bf16[32,3456]{1,0:T(8,128)(2,1)S(1)} collective-permute-done((bf16[32,3456]{1,0:T(8,128)(2,1)S(1)}, bf16[32,3456]{1,0:T(8,128)(2,1)S(1)}, u32[]{:S(2)}, u32[]{:S(2)}) %collective-permute-start.2) | collective-permute-done | bytes 221216 | tf_op jit(solution)/shard_map/ppermute | solution.py:259
  32.6 0.0 collective-permute-done.5.refs_2_
  32.6 0.0 collective-permute-done.4.refs_1_
  32.6 0.0 collective-permute-done.8.refs_2_
  32.6 2.5 %collective-permute-start.14 = (bf16[32,3456]{1,0:T(8,128)(2,1)S(1)}, bf16[32,3456]{1,0:T(8,128)(2,1)S(1)}, u32[]{:S(2)}, u32[]{:S(2)}) collective-permute-start(bf16[32,3456]{1,0:T(8,128)(2,1)S(1)} %collective-permute-done.2.refs_0_), channel_id=1, source_target_pairs={{0,24},{1,25},{2,26},{3,27},{4,28},{5,29},{6,30},{7,31},{8,16},{9,... | collective-permute-start | bytes 663560 | tf_op jit(solution)/shard_map/ppermute | solution.py:259
  35.1 0.5 collective-permute-start.13
  35.6 0.5 collective-permute-start.12
  36.1 1.5 %collective-permute-start.10 = (bf16[32,3456]{1,0:T(8,128)(2,1)S(1)}, bf16[32,3456]{1,0:T(8,128)(2,1)S(1)}, u32[]{:S(2)}, u32[]{:S(2)}) collective-permute-start(bf16[32,3456]{1,0:T(8,128)(2,1)S(1)} %collective-permute-done.4.refs_1_), channel_id=1, source_target_pairs={{0,16},{1,9},{2,18},{3,11},{4,20},{5,13},{6,22},{7,15},{8,24},{9,1... | collective-permute-start | bytes 663560 | tf_op jit(solution)/shard_map/ppermute | solution.py:259
  37.7 0.5 collective-permute-start.16
  38.2 4.6 %band_matrices.1.x_ref = bf16[9,16,9216]{2,1,0:T(8,128)(2,1)S(1)} custom-call(s32[2,288]{1,0:T(2,128)S(1)} %copy-done.2, bf16[2,512,2048]{2,1,0:T(8,128)(2,1)S(1)} %spread.1, bf16[2,9,32,288]{3,2,1,0:T(8,128)(2,1)S(1)} %copy-done.1, bf16[9,32,288]{2,1,0:T(8,128)(2,1)S(1)} %collective-permute-done.other_ref, ...), custom_call_target="tpu_custom_call" | custom-call | flops 3000000000 | bytes 1000000 | tf_op jit(solution)/shard_map/band_matrices/pallas_call | solution.py:232
  42.7 7.3 %collective-permute-done.16.refs_3_ = bf16[32,3456]{1,0:T(8,128)(2,1)S(1)} collective-permute-done((bf16[32,3456]{1,0:T(8,128)(2,1)S(1)}, bf16[32,3456]{1,0:T(8,128)(2,1)S(1)}, u32[]{:S(2)}, u32[]{:S(2)}) %collective-permute-start.16) | collective-permute-done | bytes 221216 | tf_op jit(solution)/shard_map/ppermute | solution.py:259
  50.0 0.1 collective-permute-start.9
  50.1 1.0 %prepare_other.7 = bf16[2,32,9216]{2,1,0:T(8,128)(2,1)S(1)} custom-call(s32[2,288]{1,0:T(2,128)S(1)} %copy-done.2, bf16[32,3456]{1,0:T(8,128)(2,1)S(1)} %collective-permute-done.6.refs_0_, bf16[32,3456]{1,0:T(8,128)(2,1)S(1)} %collective-permute-done.7.refs_1_, bf16[32,3456]{1,0:T(8,128)(2,1)S(1)} %collective-permute-done.8.refs_2_, ...), custom_call_target="tpu_custom_call" | custom-call | tf_op jit(solution)/shard_map/prepare_other/pallas_call | solution.py:94
  51.2 0.0 collective-permute-done.14.refs_3_
  51.2 0.5 collective-permute-start.17
  51.7 0.0 collective-permute-done.13.refs_2_
  51.7 0.0 collective-permute-done.12.refs_1_
  51.7 1.1 %prepare_other.6 = bf16[2,32,9216]{2,1,0:T(8,128)(2,1)S(1)} custom-call(s32[2,288]{1,0:T(2,128)S(1)} %copy-done.2, bf16[32,3456]{1,0:T(8,128)(2,1)S(1)} %collective-permute-done.2.refs_0_, bf16[32,3456]{1,0:T(8,128)(2,1)S(1)} %collective-permute-done.12.refs_1_, bf16[32,3456]{1,0:T(8,128)(2,1)S(1)} %collective-permute-done.13.refs_2_, ...), custom_call_target="tpu_custom_call" | custom-call | tf_op jit(solution)/shard_map/prepare_other/pallas_call | solution.py:94
  52.7 0.2 collective-permute-start.15
  52.9 0.0 collective-permute-done.10.refs_3_
  52.9 1.1 %prepare_other.5 = bf16[2,32,9216]{2,1,0:T(8,128)(2,1)S(1)} custom-call(s32[2,288]{1,0:T(2,128)S(1)} %copy-done.2, bf16[32,3456]{1,0:T(8,128)(2,1)S(1)} %collective-permute-done.3.refs_0_, bf16[32,3456]{1,0:T(8,128)(2,1)S(1)} %collective-permute-done.4.refs_1_, bf16[32,3456]{1,0:T(8,128)(2,1)S(1)} %collective-permute-done.5.refs_2_, ...), custom_call_target="tpu_custom_call" | custom-call | tf_op jit(solution)/shard_map/prepare_other/pallas_call | solution.py:94
  54.0 0.5 collective-permute-start.11
  54.4 1.1 %prepare_own.5.refs_2_ = bf16[2,32,9216]{2,1,0:T(8,128)(2,1)S(1)} custom-call(s32[2,288]{1,0:T(2,128)S(1)} %copy-done.2, bf16[32,3456]{1,0:T(8,128)(2,1)S(1)} %collective-permute-done.3.refs_0_, bf16[32,3456]{1,0:T(8,128)(2,1)S(1)} %collective-permute-done.4.refs_1_, bf16[32,3456]{1,0:T(8,128)(2,1)S(1)} %collective-permute-done.5.refs_2_, ...), custom_call_target="tpu_custom_call" | custom-call | tf_op jit(solution)/shard_map/prepare_own/pallas_call | solution.py:94
  55.5 1.1 %prepare_own.6.refs_4_ = bf16[2,32,9216]{2,1,0:T(8,128)(2,1)S(1)} custom-call(s32[2,288]{1,0:T(2,128)S(1)} %copy-done.2, bf16[32,3456]{1,0:T(8,128)(2,1)S(1)} %collective-permute-done.2.refs_0_, bf16[32,3456]{1,0:T(8,128)(2,1)S(1)} %collective-permute-done.12.refs_1_, bf16[32,3456]{1,0:T(8,128)(2,1)S(1)} %collective-permute-done.13.refs_2_, ...), custom_call_target="tpu_custom_call" | custom-call | tf_op jit(solution)/shard_map/prepare_own/pallas_call | solution.py:94
  56.5 1.1 %prepare_own.7.refs_6_ = bf16[2,32,9216]{2,1,0:T(8,128)(2,1)S(1)} custom-call(s32[2,288]{1,0:T(2,128)S(1)} %copy-done.2, bf16[32,3456]{1,0:T(8,128)(2,1)S(1)} %collective-permute-done.6.refs_0_, bf16[32,3456]{1,0:T(8,128)(2,1)S(1)} %collective-permute-done.7.refs_1_, bf16[32,3456]{1,0:T(8,128)(2,1)S(1)} %collective-permute-done.8.refs_2_, ...), custom_call_target="tpu_custom_call" | custom-call | tf_op jit(solution)/shard_map/prepare_own/pallas_call | solution.py:94
  57.6 0.0 collective-permute-done.9.refs_1_
  57.6 0.0 collective-permute-done.17.refs_7_
  57.6 0.3 collective-permute-done.11.refs_3_
  57.9 13.2 %products.3 = (f32[5,64,256]{2,1,0:T(8,128)S(1)}, bf16[5,64,256]{2,1,0:T(8,128)(2,1)S(1)}, bf16[5,64,256]{2,1,0:T(8,128)(2,1)S(1)}, bf16[5,64,256]{2,1,0:T(8,128)(2,1)S(1)}) custom-call(bf16[9,16,9216]{2,1,0:T(8,128)(2,1)S(1)} %band_matrices.1.x_ref, bf16[2,32,9216]{2,1,0:T(8,128)(2,1)S(1)} %prepare_own.4._.refs_0_, ...), custom_call_target="tpu_custom_call" | custom-call | flops 12079595520 | bytes 9437184 | tf_op jit(solution)/shard_map/products/pallas_call | solution.py:146
  71.1 0.1 collective-permute-start.18
  71.2 2.9 %collective-permute-start.19 = (bf16[5,64,256]{2,1,0:T(8,128)(2,1)S(1)}, bf16[5,64,256]{2,1,0:T(8,128)(2,1)S(1)}, u32[]{:S(2)}, u32[]{:S(2)}) collective-permute-start(bf16[5,64,256]{2,1,0:T(8,128)(2,1)S(1)} %get-tuple-element.76), channel_id=1, source_target_pairs={{0,4},{1,5},{2,6},{3,7},{4,0},{5,1},{6,2},{7,3},{8,12},{9,13},{10,... | collective-permute-start | bytes 491528 | tf_op jit(solution)/shard_map/ppermute | solution.py:259
  74.1 0.9 collective-permute-start.20
  75.0 8.0 %products.4 = (f32[3,64,256]{2,1,0:T(8,128)S(1)}, bf16[3,64,256]{2,1,0:T(8,128)(2,1)S(1)}, bf16[3,64,256]{2,1,0:T(8,128)(2,1)S(1)}, bf16[3,64,256]{2,1,0:T(8,128)(2,1)S(1)}) custom-call(bf16[9,16,9216]{2,1,0:T(8,128)(2,1)S(1)} %band_matrices.1.x_ref, bf16[2,32,9216]{2,1,0:T(8,128)(2,1)S(1)} %prepare_own.4._.refs_0_, ...), custom_call_target="tpu_custom_call" | custom-call | flops 7247757312 | bytes 9437184 | tf_op jit(solution)/shard_map/products/pallas_call | solution.py:146
  83.0 1.2 %collective-permute-start.21 = (bf16[3,64,256]{2,1,0:T(8,128)(2,1)S(1)}, bf16[3,64,256]{2,1,0:T(8,128)(2,1)S(1)}, u32[]{:S(2)}, u32[]{:S(2)}) collective-permute-start(bf16[3,64,256]{2,1,0:T(8,128)(2,1)S(1)} %get-tuple-element.90), channel_id=1, source_target_pairs={{0,2},{1,3},{2,4},{3,5},{4,6},{5,7},{6,0},{7,1},{8,10},{9,11},{10,... | collective-permute-start | bytes 294920 | tf_op jit(solution)/shard_map/ppermute | solution.py:259
  84.2 1.0 collective-permute-start.22
  85.1 2.8 %collective-permute-start.23 = (bf16[3,64,256]{2,1,0:T(8,128)(2,1)S(1)}, bf16[3,64,256]{2,1,0:T(8,128)(2,1)S(1)}, u32[]{:S(2)}, u32[]{:S(2)}) collective-permute-start(bf16[3,64,256]{2,1,0:T(8,128)(2,1)S(1)} %get-tuple-element.92), channel_id=1, source_target_pairs={{0,6},{1,7},{2,0},{3,1},{4,2},{5,3},{6,4},{7,5},{8,14},{9,15},{10,... | collective-permute-start | bytes 294920 | tf_op jit(solution)/shard_map/ppermute | solution.py:259
  88.0 0.1 convert_add_fusion
  88.1 3.0 %products.5 = (f32[1,64,256]{2,1,0:T(8,128)S(1)}, bf16[1,64,256]{2,1,0:T(8,128)(2,1)S(1)}, bf16[1,64,256]{2,1,0:T(8,128)(2,1)S(1)}, bf16[1,64,256]{2,1,0:T(8,128)(2,1)S(1)}) custom-call(bf16[9,16,9216]{2,1,0:T(8,128)(2,1)S(1)} %band_matrices.1.x_ref, bf16[2,32,9216]{2,1,0:T(8,128)(2,1)S(1)} %prepare_own.4._.refs_0_, ...), custom_call_target="tpu_custom_call" | custom-call | flops 2415919104 | bytes 9437184 | tf_op jit(solution)/shard_map/products/pallas_call | solution.py:146
  91.2 6.6 %collective-permute-start.24 = (bf16[1,64,256]{2,1,0:T(8,128)(2,1)S(1)}, bf16[1,64,256]{2,1,0:T(8,128)(2,1)S(1)}, u32[]{:S(2)}, u32[]{:S(2)}) collective-permute-start(bf16[1,64,256]{2,1,0:T(8,128)(2,1)S(1)} %get-tuple-element.98), channel_id=1, source_target_pairs={{0,2},{1,3},{2,4},{3,5},{4,6},{5,7},{6,0},{7,1},{8,10},{9,11},{10,... | collective-permute-start | bytes 98312 | tf_op jit(solution)/shard_map/ppermute | solution.py:259
  97.8 2.4 %collective-permute-start.26 = (bf16[1,64,256]{2,1,0:T(8,128)(2,1)S(1)}, bf16[1,64,256]{2,1,0:T(8,128)(2,1)S(1)}, u32[]{:S(2)}, u32[]{:S(2)}) collective-permute-start(bf16[1,64,256]{2,1,0:T(8,128)(2,1)S(1)} %get-tuple-element.100), channel_id=1, source_target_pairs={{0,6},{1,7},{2,0},{3,1},{4,2},{5,3},{6,4},{7,5},{8,14},{9,15},{10,... | collective-permute-start | bytes 98312 | tf_op jit(solution)/shard_map/ppermute | solution.py:259
  100.3 0.1 collective-permute-start.28
  100.4 0.5 collective-permute-start.27
  100.9 1.7 %collective-permute-done.25 = bf16[1,64,256]{2,1,0:T(8,128)(2,1)S(1)} collective-permute-done((bf16[1,64,256]{2,1,0:T(8,128)(2,1)S(1)}, bf16[1,64,256]{2,1,0:T(8,128)(2,1)S(1)}, u32[]{:S(2)}, u32[]{:S(2)}) %collective-permute-start.25) | collective-permute-done | bytes 32800 | tf_op jit(solution)/shard_map/ppermute | solution.py:259
  102.6 0.1 collective-permute-start.29
  102.7 1.2 %collective-permute-done.29 = f32[1,32,256]{2,1,0:T(8,128)S(1)} collective-permute-done((f32[1,32,256]{2,1,0:T(8,128)S(1)}, f32[1,32,256]{2,1,0:T(8,128)S(1)}, u32[]{:S(2)}, u32[]{:S(2)}) %collective-permute-start.29) | collective-permute-done | bytes 32800 | tf_op jit(solution)/shard_map/ppermute | solution.py:259
  103.9 0.9 maximum_select_fusion
  (28 shorter events, 0.2 us)
Async XLA Ops:
  0.0 8.2 %copy-start.1 = (bf16[2,9,32,288]{3,2,1,0:T(8,128)(2,1)S(1)}, bf16[2,9,32,288]{3,2,1,0:T(8,128)(2,1)}, u32[]{:S(2)}) copy-start(bf16[2,9,32,288]{3,2,1,0:T(8,128)(2,1)} %coupling_ref.3) | copy-start | bytes 995332
  0.0 12.1 %copy-start.2 = (s32[2,288]{1,0:T(2,128)S(1)}, s32[2,288]{1,0:T(2,128)}, u32[]{:S(2)}) copy-start(s32[2,288]{1,0:T(2,128)} %kq_ref.17) | copy-start | bytes 6916
  3.0 5.2 %collective-permute-start = (bf16[9,32,288]{2,1,0:T(8,128)(2,1)}, bf16[9,32,288]{2,1,0:T(8,128)(2,1)S(1)}, u32[]{:S(2)}, u32[]{:S(2)}) collective-permute-start(bf16[9,32,288]{2,1,0:T(8,128)(2,1)} %get-tuple-element.54), channel_id=1, source_target_pairs={{0,1},{1,0},{2,3},{3,2},{4,5},{5,4},{6,7},{7,6},{8,9},{9,8},{10,11... | collective-permute-start | bytes 497672 | tf_op jit(solution)/shard_map/ppermute | solution.py:259
  3.5 11.9 %collective-permute-start.3 = (bf16[32,3456]{1,0:T(8,128)(2,1)}, bf16[32,3456]{1,0:T(8,128)(2,1)S(1)}, u32[]{:S(2)}, u32[]{:S(2)}) collective-permute-start(bf16[32,3456]{1,0:T(8,128)(2,1)} %get-tuple-element.59), channel_id=1, source_target_pairs={{0,6},{1,7},{2,0},{3,1},{4,2},{5,3},{6,4},{7,5},{8,14},{9,15},{10,... | collective-permute-start | bytes 663560 | tf_op jit(solution)/shard_map/ppermute | solution.py:259
  8.2 11.6 %collective-permute-start.6 = (bf16[32,3456]{1,0:T(8,128)(2,1)}, bf16[32,3456]{1,0:T(8,128)(2,1)S(1)}, u32[]{:S(2)}, u32[]{:S(2)}) collective-permute-start(bf16[32,3456]{1,0:T(8,128)(2,1)} %get-tuple-element.60), channel_id=1, source_target_pairs={{0,2},{1,3},{2,4},{3,5},{4,6},{5,7},{6,0},{7,1},{8,10},{9,11},{10,... | collective-permute-start | bytes 663560 | tf_op jit(solution)/shard_map/ppermute | solution.py:259
  8.3 15.4 %collective-permute-start.1 = (bf16[9,32,288]{2,1,0:T(8,128)(2,1)S(1)}, bf16[9,32,288]{2,1,0:T(8,128)(2,1)S(1)}, u32[]{:S(2)}, u32[]{:S(2)}) collective-permute-start(bf16[9,32,288]{2,1,0:T(8,128)(2,1)S(1)} %bitcast_select_fusion), channel_id=1, source_target_pairs={{0,6},{1,7},{2,0},{3,1},{4,2},{5,3},{6,4},{7,5},{8,14},{9,15},{10,... | collective-permute-start | bytes 497672 | tf_op jit(solution)/shard_map/ppermute | solution.py:259
  12.1 1.2 %copy-start = (bf16[32,13824]{1,0:T(8,128)(2,1)S(1)}, bf16[32,13824]{1,0:T(8,128)(2,1)}, u32[]{:S(2)}) copy-start(bf16[32,13824]{1,0:T(8,128)(2,1)} %get-tuple-element.56.refs_0_) | copy-start | bytes 2654212
  14.3 1.0 copy-start.3
  15.3 17.2 %collective-permute-start.2 = (bf16[32,3456]{1,0:T(8,128)(2,1)S(1)}, bf16[32,3456]{1,0:T(8,128)(2,1)S(1)}, u32[]{:S(2)}, u32[]{:S(2)}) collective-permute-start(bf16[32,3456]{1,0:T(8,128)(2,1)S(1)} %copy-done.3), channel_id=1, source_target_pairs={{0,4},{1,5},{2,6},{3,7},{4,0},{5,1},{6,2},{7,3},{8,12},{9,13},{10,... | collective-permute-start | bytes 663560 | tf_op jit(solution)/shard_map/ppermute | solution.py:259
  15.4 17.2 %collective-permute-start.5 = (bf16[32,3456]{1,0:T(8,128)(2,1)S(1)}, bf16[32,3456]{1,0:T(8,128)(2,1)S(1)}, u32[]{:S(2)}, u32[]{:S(2)}) collective-permute-start(bf16[32,3456]{1,0:T(8,128)(2,1)S(1)} %collective-permute-done.3.refs_0_), channel_id=1, source_target_pairs={{0,16},{1,9},{2,18},{3,11},{4,20},{5,13},{6,22},{7,15},{8,24},{9,1... | collective-permute-start | bytes 663560 | tf_op jit(solution)/shard_map/ppermute | solution.py:259
  17.0 15.6 %collective-permute-start.4 = (bf16[32,3456]{1,0:T(8,128)(2,1)S(1)}, bf16[32,3456]{1,0:T(8,128)(2,1)S(1)}, u32[]{:S(2)}, u32[]{:S(2)}) collective-permute-start(bf16[32,3456]{1,0:T(8,128)(2,1)S(1)} %collective-permute-done.3.refs_0_), channel_id=1, source_target_pairs={{0,8},{1,17},{2,10},{3,19},{4,12},{5,21},{6,14},{7,23},{8,0},{9,25... | collective-permute-start | bytes 663560 | tf_op jit(solution)/shard_map/ppermute | solution.py:259
  19.8 12.7 %collective-permute-start.8 = (bf16[32,3456]{1,0:T(8,128)(2,1)S(1)}, bf16[32,3456]{1,0:T(8,128)(2,1)S(1)}, u32[]{:S(2)}, u32[]{:S(2)}) collective-permute-start(bf16[32,3456]{1,0:T(8,128)(2,1)S(1)} %collective-permute-done.6.refs_0_), channel_id=1, source_target_pairs={{0,16},{1,9},{2,18},{3,11},{4,20},{5,13},{6,22},{7,15},{8,24},{9,1... | collective-permute-start | bytes 663560 | tf_op jit(solution)/shard_map/ppermute | solution.py:259
  23.7 8.9 %collective-permute-start.7 = (bf16[32,3456]{1,0:T(8,128)(2,1)S(1)}, bf16[32,3456]{1,0:T(8,128)(2,1)S(1)}, u32[]{:S(2)}, u32[]{:S(2)}) collective-permute-start(bf16[32,3456]{1,0:T(8,128)(2,1)S(1)} %collective-permute-done.6.refs_0_), channel_id=1, source_target_pairs={{0,8},{1,17},{2,10},{3,19},{4,12},{5,21},{6,14},{7,23},{8,0},{9,25... | collective-permute-start | bytes 663560 | tf_op jit(solution)/shard_map/ppermute | solution.py:259
  32.6 18.6 %collective-permute-start.14 = (bf16[32,3456]{1,0:T(8,128)(2,1)S(1)}, bf16[32,3456]{1,0:T(8,128)(2,1)S(1)}, u32[]{:S(2)}, u32[]{:S(2)}) collective-permute-start(bf16[32,3456]{1,0:T(8,128)(2,1)S(1)} %collective-permute-done.2.refs_0_), channel_id=1, source_target_pairs={{0,24},{1,25},{2,26},{3,27},{4,28},{5,29},{6,30},{7,31},{8,16},{9,... | collective-permute-start | bytes 663560 | tf_op jit(solution)/shard_map/ppermute | solution.py:259
  35.1 16.6 %collective-permute-start.13 = (bf16[32,3456]{1,0:T(8,128)(2,1)S(1)}, bf16[32,3456]{1,0:T(8,128)(2,1)S(1)}, u32[]{:S(2)}, u32[]{:S(2)}) collective-permute-start(bf16[32,3456]{1,0:T(8,128)(2,1)S(1)} %collective-permute-done.2.refs_0_), channel_id=1, source_target_pairs={{0,16},{1,17},{2,18},{3,19},{4,20},{5,21},{6,22},{7,23},{8,24},{9,... | collective-permute-start | bytes 663560 | tf_op jit(solution)/shard_map/ppermute | solution.py:259
  35.6 16.1 %collective-permute-start.12 = (bf16[32,3456]{1,0:T(8,128)(2,1)S(1)}, bf16[32,3456]{1,0:T(8,128)(2,1)S(1)}, u32[]{:S(2)}, u32[]{:S(2)}) collective-permute-start(bf16[32,3456]{1,0:T(8,128)(2,1)S(1)} %collective-permute-done.2.refs_0_), channel_id=1, source_target_pairs={{0,8},{1,9},{2,10},{3,11},{4,12},{5,13},{6,14},{7,15},{8,0},{9,1},... | collective-permute-start | bytes 663560 | tf_op jit(solution)/shard_map/ppermute | solution.py:259
  36.1 16.8 %collective-permute-start.10 = (bf16[32,3456]{1,0:T(8,128)(2,1)S(1)}, bf16[32,3456]{1,0:T(8,128)(2,1)S(1)}, u32[]{:S(2)}, u32[]{:S(2)}) collective-permute-start(bf16[32,3456]{1,0:T(8,128)(2,1)S(1)} %collective-permute-done.4.refs_1_), channel_id=1, source_target_pairs={{0,16},{1,9},{2,18},{3,11},{4,20},{5,13},{6,22},{7,15},{8,24},{9,1... | collective-permute-start | bytes 663560 | tf_op jit(solution)/shard_map/ppermute | solution.py:259
  37.7 12.4 %collective-permute-start.16 = (bf16[32,3456]{1,0:T(8,128)(2,1)S(1)}, bf16[32,3456]{1,0:T(8,128)(2,1)S(1)}, u32[]{:S(2)}, u32[]{:S(2)}) collective-permute-start(bf16[32,3456]{1,0:T(8,128)(2,1)S(1)} %collective-permute-done.7.refs_1_), channel_id=1, source_target_pairs={{0,16},{1,9},{2,18},{3,11},{4,20},{5,13},{6,22},{7,15},{8,24},{9,1... | collective-permute-start | bytes 663560 | tf_op jit(solution)/shard_map/ppermute | solution.py:259
  50.0 7.6 %collective-permute-start.9 = (bf16[2,32,9216]{2,1,0:T(8,128)(2,1)S(1)}, bf16[2,32,9216]{2,1,0:T(8,128)(2,1)S(1)}, u32[]{:S(2)}, u32[]{:S(2)}) collective-permute-start(bf16[2,32,9216]{2,1,0:T(8,128)(2,1)S(1)} %prepare_other.4), channel_id=1, source_target_pairs={{0,1},{1,0},{2,3},{3,2},{4,5},{5,4},{6,7},{7,6},{8,9},{9,8},{10,11... | collective-permute-start | bytes 3538952 | tf_op jit(solution)/shard_map/ppermute | solution.py:259
  51.2 6.4 %collective-permute-start.17 = (bf16[2,32,9216]{2,1,0:T(8,128)(2,1)S(1)}, bf16[2,32,9216]{2,1,0:T(8,128)(2,1)S(1)}, u32[]{:S(2)}, u32[]{:S(2)}) collective-permute-start(bf16[2,32,9216]{2,1,0:T(8,128)(2,1)S(1)} %prepare_other.7), channel_id=1, source_target_pairs={{0,1},{1,0},{2,3},{3,2},{4,5},{5,4},{6,7},{7,6},{8,9},{9,8},{10,11... | collective-permute-start | bytes 3538952 | tf_op jit(solution)/shard_map/ppermute | solution.py:259
  52.7 4.9 %collective-permute-start.15 = (bf16[2,32,9216]{2,1,0:T(8,128)(2,1)S(1)}, bf16[2,32,9216]{2,1,0:T(8,128)(2,1)S(1)}, u32[]{:S(2)}, u32[]{:S(2)}) collective-permute-start(bf16[2,32,9216]{2,1,0:T(8,128)(2,1)S(1)} %prepare_other.6), channel_id=1, source_target_pairs={{0,1},{1,0},{2,3},{3,2},{4,5},{5,4},{6,7},{7,6},{8,9},{9,8},{10,11... | collective-permute-start | bytes 3538952 | tf_op jit(solution)/shard_map/ppermute | solution.py:259
  54.0 4.0 %collective-permute-start.11 = (bf16[2,32,9216]{2,1,0:T(8,128)(2,1)S(1)}, bf16[2,32,9216]{2,1,0:T(8,128)(2,1)S(1)}, u32[]{:S(2)}, u32[]{:S(2)}) collective-permute-start(bf16[2,32,9216]{2,1,0:T(8,128)(2,1)S(1)} %prepare_other.5), channel_id=1, source_target_pairs={{0,1},{1,0},{2,3},{3,2},{4,5},{5,4},{6,7},{7,6},{8,9},{9,8},{10,11... | collective-permute-start | bytes 3538952 | tf_op jit(solution)/shard_map/ppermute | solution.py:259
  71.1 14.0 %collective-permute-start.18 = (bf16[5,64,256]{2,1,0:T(8,128)(2,1)S(1)}, bf16[5,64,256]{2,1,0:T(8,128)(2,1)S(1)}, u32[]{:S(2)}, u32[]{:S(2)}) collective-permute-start(bf16[5,64,256]{2,1,0:T(8,128)(2,1)S(1)} %get-tuple-element.75), channel_id=1, source_target_pairs={{0,2},{1,3},{2,4},{3,5},{4,6},{5,7},{6,0},{7,1},{8,10},{9,11},{10,... | collective-permute-start | bytes 491528 | tf_op jit(solution)/shard_map/ppermute | solution.py:259
  71.2 16.8 %collective-permute-start.19 = (bf16[5,64,256]{2,1,0:T(8,128)(2,1)S(1)}, bf16[5,64,256]{2,1,0:T(8,128)(2,1)S(1)}, u32[]{:S(2)}, u32[]{:S(2)}) collective-permute-start(bf16[5,64,256]{2,1,0:T(8,128)(2,1)S(1)} %get-tuple-element.76), channel_id=1, source_target_pairs={{0,4},{1,5},{2,6},{3,7},{4,0},{5,1},{6,2},{7,3},{8,12},{9,13},{10,... | collective-permute-start | bytes 491528 | tf_op jit(solution)/shard_map/ppermute | solution.py:259
  74.1 13.9 %collective-permute-start.20 = (bf16[5,64,256]{2,1,0:T(8,128)(2,1)S(1)}, bf16[5,64,256]{2,1,0:T(8,128)(2,1)S(1)}, u32[]{:S(2)}, u32[]{:S(2)}) collective-permute-start(bf16[5,64,256]{2,1,0:T(8,128)(2,1)S(1)} %get-tuple-element.77), channel_id=1, source_target_pairs={{0,6},{1,7},{2,0},{3,1},{4,2},{5,3},{6,4},{7,5},{8,14},{9,15},{10,... | collective-permute-start | bytes 491528 | tf_op jit(solution)/shard_map/ppermute | solution.py:259
  83.0 14.8 %collective-permute-start.21 = (bf16[3,64,256]{2,1,0:T(8,128)(2,1)S(1)}, bf16[3,64,256]{2,1,0:T(8,128)(2,1)S(1)}, u32[]{:S(2)}, u32[]{:S(2)}) collective-permute-start(bf16[3,64,256]{2,1,0:T(8,128)(2,1)S(1)} %get-tuple-element.90), channel_id=1, source_target_pairs={{0,2},{1,3},{2,4},{3,5},{4,6},{5,7},{6,0},{7,1},{8,10},{9,11},{10,... | collective-permute-start | bytes 294920 | tf_op jit(solution)/shard_map/ppermute | solution.py:259
  84.2 16.0 %collective-permute-start.22 = (bf16[3,64,256]{2,1,0:T(8,128)(2,1)S(1)}, bf16[3,64,256]{2,1,0:T(8,128)(2,1)S(1)}, u32[]{:S(2)}, u32[]{:S(2)}) collective-permute-start(bf16[3,64,256]{2,1,0:T(8,128)(2,1)S(1)} %get-tuple-element.91), channel_id=1, source_target_pairs={{0,4},{1,5},{2,6},{3,7},{4,0},{5,1},{6,2},{7,3},{8,12},{9,13},{10,... | collective-permute-start | bytes 294920 | tf_op jit(solution)/shard_map/ppermute | solution.py:259
  85.1 15.1 %collective-permute-start.23 = (bf16[3,64,256]{2,1,0:T(8,128)(2,1)S(1)}, bf16[3,64,256]{2,1,0:T(8,128)(2,1)S(1)}, u32[]{:S(2)}, u32[]{:S(2)}) collective-permute-start(bf16[3,64,256]{2,1,0:T(8,128)(2,1)S(1)} %get-tuple-element.92), channel_id=1, source_target_pairs={{0,6},{1,7},{2,0},{3,1},{4,2},{5,3},{6,4},{7,5},{8,14},{9,15},{10,... | collective-permute-start | bytes 294920 | tf_op jit(solution)/shard_map/ppermute | solution.py:259
  91.2 9.7 %collective-permute-start.24 = (bf16[1,64,256]{2,1,0:T(8,128)(2,1)S(1)}, bf16[1,64,256]{2,1,0:T(8,128)(2,1)S(1)}, u32[]{:S(2)}, u32[]{:S(2)}) collective-permute-start(bf16[1,64,256]{2,1,0:T(8,128)(2,1)S(1)} %get-tuple-element.98), channel_id=1, source_target_pairs={{0,2},{1,3},{2,4},{3,5},{4,6},{5,7},{6,0},{7,1},{8,10},{9,11},{10,... | collective-permute-start | bytes 98312 | tf_op jit(solution)/shard_map/ppermute | solution.py:259
  97.8 4.8 %collective-permute-start.25 = (bf16[1,64,256]{2,1,0:T(8,128)(2,1)S(1)}, bf16[1,64,256]{2,1,0:T(8,128)(2,1)S(1)}, u32[]{:S(2)}, u32[]{:S(2)}) collective-permute-start(bf16[1,64,256]{2,1,0:T(8,128)(2,1)S(1)} %get-tuple-element.99), channel_id=1, source_target_pairs={{0,4},{1,5},{2,6},{3,7},{4,0},{5,1},{6,2},{7,3},{8,12},{9,13},{10,... | collective-permute-start | bytes 98312 | tf_op jit(solution)/shard_map/ppermute | solution.py:259
  97.8 4.8 %collective-permute-start.26 = (bf16[1,64,256]{2,1,0:T(8,128)(2,1)S(1)}, bf16[1,64,256]{2,1,0:T(8,128)(2,1)S(1)}, u32[]{:S(2)}, u32[]{:S(2)}) collective-permute-start(bf16[1,64,256]{2,1,0:T(8,128)(2,1)S(1)} %get-tuple-element.100), channel_id=1, source_target_pairs={{0,6},{1,7},{2,0},{3,1},{4,2},{5,3},{6,4},{7,5},{8,14},{9,15},{10,... | collective-permute-start | bytes 98312 | tf_op jit(solution)/shard_map/ppermute | solution.py:259
  100.3 3.6 %collective-permute-start.28 = (f32[3,32,256]{2,1,0:T(8,128)S(1)}, f32[3,32,256]{2,1,0:T(8,128)S(1)}, u32[]{:S(2)}, u32[]{:S(2)}) collective-permute-start(f32[3,32,256]{2,1,0:T(8,128)S(1)} %get-tuple-element.104), channel_id=1, source_target_pairs={{0,1},{1,0},{2,3},{3,2},{4,5},{5,4},{6,7},{7,6},{8,9},{9,8},{10,11... | collective-permute-start | bytes 294920 | tf_op jit(solution)/shard_map/ppermute | solution.py:259
  100.4 3.5 %collective-permute-start.27 = (f32[5,32,256]{2,1,0:T(8,128)S(1)}, f32[5,32,256]{2,1,0:T(8,128)S(1)}, u32[]{:S(2)}, u32[]{:S(2)}) collective-permute-start(f32[5,32,256]{2,1,0:T(8,128)S(1)} %get-tuple-element.102), channel_id=1, source_target_pairs={{0,1},{1,0},{2,3},{3,2},{4,5},{5,4},{6,7},{7,6},{8,9},{9,8},{10,11... | collective-permute-start | bytes 491528 | tf_op jit(solution)/shard_map/ppermute | solution.py:259
  102.6 1.3 %collective-permute-start.29 = (f32[1,32,256]{2,1,0:T(8,128)S(1)}, f32[1,32,256]{2,1,0:T(8,128)S(1)}, u32[]{:S(2)}, u32[]{:S(2)}) collective-permute-start(f32[1,32,256]{2,1,0:T(8,128)S(1)} %get-tuple-element.106), channel_id=1, source_target_pairs={{0,1},{1,0},{2,3},{3,2},{4,5},{5,4},{6,7},{7,6},{8,9},{9,8},{10,11... | collective-permute-start | bytes 98312 | tf_op jit(solution)/shard_map/ppermute | solution.py:259

commit v7 on v6

--- a/solution.py
+++ b/solution.py
@@ -13,6 +13,7 @@
 LINE = KY * BANDS
 GROUPS = (5, 8)
 F32 = jnp.float32
+SMALL = pl.CostEstimate(flops=1, bytes_accessed=1, transcendentals=0)
 BF16 = jnp.bfloat16
 
 
@@ -67,6 +68,7 @@
         out_specs=[pl.BlockSpec(memory_space=pltpu.VMEM)] * len(outs),
         out_shape=outs,
         scratch_shapes=[pltpu.SemaphoreType.DMA((3 * n_z + 10,))],
+        cost_estimate=SMALL,
         name="cut",
     )(envelopes, coupling)
 
@@ -98,6 +100,7 @@
         out_shape=jax.ShapeDtypeStruct((2, rows, 2 * block), BF16),
         scratch_shapes=[pltpu.VMEM((rows, 3 * block), BF16)],
         compiler_params=pltpu.CompilerParams(vmem_limit_bytes=16 << 20),
+        cost_estimate=SMALL,
         name="prepare_other" if for_other else "prepare_own",
     )(kq_map, *ins)
 
@@ -177,7 +180,7 @@
         out_specs=pl.BlockSpec(memory_space=pltpu.VMEM),
         out_shape=jax.ShapeDtypeStruct((2, 4 * size, size * BANDS), BF16),
         compiler_params=pltpu.CompilerParams(vmem_limit_bytes=24 << 20),
-        cost_estimate=pl.CostEstimate(flops=3 * 10**9, bytes_accessed=10**6, transcendentals=0),
+        cost_estimate=SMALL,
         name="spread",
     )(earlier)
 
@@ -235,7 +238,7 @@
         out_specs=pl.BlockSpec(memory_space=pltpu.VMEM),
         out_shape=jax.ShapeDtypeStruct((branches, BANDS, 2 * count * BANDS), BF16),
         compiler_params=pltpu.CompilerParams(vmem_limit_bytes=32 << 20),
-        cost_estimate=pl.CostEstimate(flops=3 * 10**9, bytes_accessed=10**6, transcendentals=0),
+        cost_estimate=SMALL,
         name="band_matrices",
     )(kq_map, spread, coupling, other, following)
 
@@ -277,14 +280,11 @@
     far = [e for e in range(2, n_z - 1)]
     *pieces, window, give = cut(envelopes, coupling, n_z, block)
     arrived = {e: passed_down(pieces[e - 1], e) for e in near}
-    other_table = sibling(give)
-    first_table = jnp.where(core == 0, lax.dynamic_index_in_dim(coupling, core, 0, keepdims=False), other_table)
-    next_table = passed_down(first_table, 1)
-    pass_on = prepared([after(window, first_table)], True)
+    pass_on = prepared([window], True)
     keep = prepared([after(window, pass_on)], False)
     for e in far:
         arrived[e] = passed_down(after(pieces[e - 1], keep), e)
-    spread = spread_matrices(min(coupling.shape[3], 128), keep)
+    spread = spread_matrices(min(coupling.shape[3], 64), keep)
     amps = {0: (keep, sibling(pass_on))}
 
     parts, first_steps = {}, []
@@ -292,13 +292,17 @@
         piece = arrived[e]
         one = permute(piece, lambda p, zz, c: (p ^ (1 + c), zz, c))
         two = permute(piece, lambda p, zz, c: (p ^ (2 - c), zz, c))
-        first_steps += [one, two]
-        parts[e] = [piece, one, two, permute(one, lambda p, zz, c: (p ^ (2 - c), zz, c))]
+        three = permute(one, lambda p, zz, c: (p ^ (2 - c), zz, c))
+        first_steps += [one, two, three] if e == 1 else [one, two]
+        parts[e] = [piece, one, two, three]
     for e in far:
-        piece = after(arrived[e], next_table, *first_steps)
+        piece = after(arrived[e], *first_steps)
         parts[e] = [piece] + [permute(piece, lambda p, zz, c: (p ^ i, zz, c)) for i in (1, 2, 3)]
-    late = [parts[e][0] for e in far]
-    x = band_matrices(kq_map, spread, coupling, other_table, after(next_table, *late), lines_all)
+    other_table = sibling(give)
+    first_table = jnp.where(core == 0, lax.dynamic_index_in_dim(coupling, core, 0, keepdims=False), other_table)
+    next_table = passed_down(after(first_table, *[arrived[e] for e in near[1:]]), 1)
+    next_table = after(next_table, *[parts[e][0] for e in far])
+    x = band_matrices(kq_map, spread, coupling, other_table, next_table, lines_all)
     for e in near + far:
         piece, *others = parts[e]
         pass_on = prepared([after(piece, x)] + others, True, e in far)

time: 105 us -> 104 us (level)
  Pallas kernels: 40.5 us -> 41.8 us
    pallas_call x8, Pallas kernels: 8.31 us -> 10.4 us  [prepare(): pl.pallas_call(functools.partial(prep_kernel, block // LINE, lines_all, f...]
  transfers between devices with their start and end apart: 30 -> 30, of which waited for: 7 -> 6; matrix products, arithmetic and copies ran while one was open for 0% -> 0% of each run, Pallas kernels for 23% -> 25%
where the time goes in v7:
time: 104 us
  Pallas kernels  41.8 us (40%)
  starting transfers between devices  39.6 us (38%)
  waiting for transfers between devices  20.2 us (19%)
  local copies, waits for them, and re-layouts  1.23 us (1%)
  other arithmetic  1.07 us (1%)
    ppermute x30, starting transfers between devices, permute(): return lax.ppermute(x, ('pb', 'ka'), pairs)  39.6 us
    pallas_call x3, Pallas kernels, products(): pl.pallas_call(functools.partial(main_kernel, sources, first, branches, f...  24.2 us
    ppermute x30, waiting for transfers between devices, permute(): return lax.ppermute(x, ('pb', 'ka'), pairs)  20.2 us
    pallas_call x8, Pallas kernels, prepare(): pl.pallas_call(functools.partial(prep_kernel, block // LINE, lines_all, f...  10.4 us
    pallas_call x1, Pallas kernels, band_matrices(): pl.pallas_call(functools.partial(band_kernel, count // KY, lines_all), in...  4.05 us
    pallas_call x1, Pallas kernels, cut(): pl.pallas_call(functools.partial(cut_kernel, block), in_specs=[pl.BlockSp...  2.95 us
  transfers between devices with their start and end apart: 30, of which 6 were waited for; matrix products, arithmetic and copies ran while one was open for 0% of the time, Pallas kernels for 25%

profile of v7, /device:TPU:0, one launch (start us, length us, event | category | flops | bytes accessed | tf_op | source)
XLA Modules:
  0.0 104.1 jit_solution(14595705947578134920)
XLA Ops:
  0.0 2.9 %cut.1 = (bf16[32,3456]{1,0:T(8,128)(2,1)}, bf16[32,3456]{1,0:T(8,128)(2,1)}, bf16[32,3456]{1,0:T(8,128)(2,1)}, bf16[32,13824]{1,0:T(8,128)(2,1)}, bf16[9,32,288]{2,1,0:T(8,128)(2,1)}) custom-call(bf16[32,36864]{1,0:T(8,128)(2,1)} %env_ref.1, bf16[2,9,32,288]{3,2,1,0:T(8,128)(2,1)} %coupling_ref.3), custom_call_target="tpu_custom_call" | custom-call | flops 1 | bytes 1 | tf_op jit(solution)/shard_map/cut/pallas_call | solution.py:65
  3.0 5.1 %collective-permute-start.4 = (bf16[32,3456]{1,0:T(8,128)(2,1)}, bf16[32,3456]{1,0:T(8,128)(2,1)S(1)}, u32[]{:S(2)}, u32[]{:S(2)}) collective-permute-start(bf16[32,3456]{1,0:T(8,128)(2,1)} %get-tuple-element.60), channel_id=1, source_target_pairs={{0,6},{1,7},{2,0},{3,1},{4,2},{5,3},{6,4},{7,5},{8,14},{9,15},{10,... | collective-permute-start | bytes 663560 | tf_op jit(solution)/shard_map/ppermute | solution.py:262
  8.1 6.1 %collective-permute-done.4.refs_0_ = bf16[32,3456]{1,0:T(8,128)(2,1)S(1)} collective-permute-done((bf16[32,3456]{1,0:T(8,128)(2,1)}, bf16[32,3456]{1,0:T(8,128)(2,1)S(1)}, u32[]{:S(2)}, u32[]{:S(2)}) %collective-permute-start.4) | collective-permute-done | bytes 221216 | tf_op jit(solution)/shard_map/ppermute | solution.py:262
  14.2 1.5 %collective-permute-start.5 = (bf16[32,3456]{1,0:T(8,128)(2,1)S(1)}, bf16[32,3456]{1,0:T(8,128)(2,1)}, u32[]{:S(2)}, u32[]{:S(2)}) collective-permute-start(bf16[32,3456]{1,0:T(8,128)(2,1)S(1)} %collective-permute-done.4.refs_0_), channel_id=1, source_target_pairs={{0,8},{1,17},{2,10},{3,19},{4,12},{5,21},{6,14},{7,23},{8,0},{9,25... | collective-permute-start | bytes 663560 | tf_op jit(solution)/shard_map/ppermute | solution.py:262
  15.7 1.2 %copy-done = bf16[32,13824]{1,0:T(8,128)(2,1)S(1)} copy-done((bf16[32,13824]{1,0:T(8,128)(2,1)S(1)}, bf16[32,13824]{1,0:T(8,128)(2,1)}, u32[]{:S(2)}) %copy-start) | copy-done | bytes 884760
  16.9 1.0 prepare_other.4
  17.9 0.0 copy-start.1
  17.9 1.0 prepare_own.4._.refs_0_
  18.9 1.4 %collective-permute-start.3 = (bf16[32,3456]{1,0:T(8,128)(2,1)S(1)}, bf16[32,3456]{1,0:T(8,128)(2,1)S(1)}, u32[]{:S(2)}, u32[]{:S(2)}) collective-permute-start(bf16[32,3456]{1,0:T(8,128)(2,1)S(1)} %copy-done.3), channel_id=1, source_target_pairs={{0,4},{1,5},{2,6},{3,7},{4,0},{5,1},{6,2},{7,3},{8,12},{9,13},{10,... | collective-permute-start | bytes 663560 | tf_op jit(solution)/shard_map/ppermute | solution.py:262
  20.3 0.0 collective-permute-done.1.refs_0_
  20.3 0.5 collective-permute-start.8
  20.9 1.5 %collective-permute-start.9 = (bf16[32,3456]{1,0:T(8,128)(2,1)S(1)}, bf16[32,3456]{1,0:T(8,128)(2,1)}, u32[]{:S(2)}, u32[]{:S(2)}) collective-permute-start(bf16[32,3456]{1,0:T(8,128)(2,1)S(1)} %collective-permute-done.1.refs_0_), channel_id=1, source_target_pairs={{0,16},{1,9},{2,18},{3,11},{4,20},{5,13},{6,22},{7,15},{8,24},{9,1... | collective-permute-start | bytes 663560 | tf_op jit(solution)/shard_map/ppermute | solution.py:262
  22.4 0.5 collective-permute-start.6
  22.9 0.0 collective-permute-done.5.refs_1_
  22.9 1.5 %collective-permute-start.7 = (bf16[32,3456]{1,0:T(8,128)(2,1)}, bf16[32,3456]{1,0:T(8,128)(2,1)}, u32[]{:S(2)}, u32[]{:S(2)}) collective-permute-start(bf16[32,3456]{1,0:T(8,128)(2,1)} %collective-permute-done.5.refs_1_), channel_id=1, source_target_pairs={{0,16},{1,9},{2,18},{3,11},{4,20},{5,13},{6,22},{7,15},{8,24},{9,1... | collective-permute-start | bytes 663560 | tf_op jit(solution)/shard_map/ppermute | solution.py:262
  24.4 5.2 %collective-permute-done.3.refs_0_ = bf16[32,3456]{1,0:T(8,128)(2,1)S(1)} collective-permute-done((bf16[32,3456]{1,0:T(8,128)(2,1)S(1)}, bf16[32,3456]{1,0:T(8,128)(2,1)S(1)}, u32[]{:S(2)}, u32[]{:S(2)}) %collective-permute-start.3) | collective-permute-done | bytes 221216 | tf_op jit(solution)/shard_map/ppermute | solution.py:262
  29.6 0.0 collective-permute-start
  29.6 0.0 collective-permute-done.8.refs_1_
  29.6 0.7 collective-permute-start.16
  30.3 0.0 collective-permute-done.9.refs_2_
  30.3 0.0 collective-permute-done.6.refs_2_
  30.3 1.3 %collective-permute-done.7.refs_3_ = bf16[32,3456]{1,0:T(8,128)(2,1)} collective-permute-done((bf16[32,3456]{1,0:T(8,128)(2,1)}, bf16[32,3456]{1,0:T(8,128)(2,1)}, u32[]{:S(2)}, u32[]{:S(2)}) %collective-permute-start.7) | collective-permute-done | bytes 221216 | tf_op jit(solution)/shard_map/ppermute | solution.py:262
  31.7 2.4 %collective-permute-start.14 = (bf16[32,3456]{1,0:T(8,128)(2,1)S(1)}, bf16[32,3456]{1,0:T(8,128)(2,1)S(1)}, u32[]{:S(2)}, u32[]{:S(2)}) collective-permute-start(bf16[32,3456]{1,0:T(8,128)(2,1)S(1)} %collective-permute-done.3.refs_0_), channel_id=1, source_target_pairs={{0,24},{1,25},{2,26},{3,27},{4,28},{5,29},{6,30},{7,31},{8,16},{9,... | collective-permute-start | bytes 663560 | tf_op jit(solution)/shard_map/ppermute | solution.py:262
  34.1 0.5 collective-permute-start.13
  34.6 0.5 collective-permute-start.12
  35.1 0.0 collective-permute-done.other_ref
  35.2 3.1 %collective-permute-start.2 = (bf16[9,32,288]{2,1,0:T(8,128)(2,1)S(1)}, bf16[9,32,288]{2,1,0:T(8,128)(2,1)S(1)}, u32[]{:S(2)}, u32[]{:S(2)}) collective-permute-start(bf16[9,32,288]{2,1,0:T(8,128)(2,1)S(1)} %bitcast_select_fusion), channel_id=1, source_target_pairs={{0,6},{1,7},{2,0},{3,1},{4,2},{5,3},{6,4},{7,5},{8,14},{9,15},{10,... | collective-permute-start | bytes 497672 | tf_op jit(solution)/shard_map/ppermute | solution.py:262
  38.3 0.1 spread.1
  38.5 4.6 %collective-permute-done.2.next_ref = bf16[9,32,288]{2,1,0:T(8,128)(2,1)S(1)} collective-permute-done((bf16[9,32,288]{2,1,0:T(8,128)(2,1)S(1)}, bf16[9,32,288]{2,1,0:T(8,128)(2,1)S(1)}, u32[]{:S(2)}, u32[]{:S(2)}) %collective-permute-start.2) | collective-permute-done | bytes 165920 | tf_op jit(solution)/shard_map/ppermute | solution.py:262
  43.1 4.0 %band_matrices.1.x_ref = bf16[9,16,9216]{2,1,0:T(8,128)(2,1)S(1)} custom-call(s32[2,288]{1,0:T(2,128)S(1)} %copy-done.2, bf16[2,256,1024]{2,1,0:T(8,128)(2,1)S(1)} %spread.1, bf16[2,9,32,288]{3,2,1,0:T(8,128)(2,1)S(1)} %copy-done.1, bf16[9,32,288]{2,1,0:T(8,128)(2,1)} %collective-permute-done.other_ref, bf16[9,32,288]{2,1,0:T(8,128)(2,1)S(1)} %collective-permute-done.2.next_ref), custom_call_target="tpu_custom_call" | custom-call | flops 1 | bytes 1 | tf_op jit(solution)/shard_map/band_matrices/pallas_call | solution.py:235
  47.1 0.0 collective-permute-done.16.refs_3_
  47.1 1.5 %prepare_other.7 = bf16[2,32,9216]{2,1,0:T(8,128)(2,1)S(1)} custom-call(s32[2,288]{1,0:T(2,128)S(1)} %copy-done.2, bf16[32,3456]{1,0:T(8,128)(2,1)S(1)} %collective-permute-done.1.refs_0_, bf16[32,3456]{1,0:T(8,128)(2,1)} %collective-permute-done.8.refs_1_, bf16[32,3456]{1,0:T(8,128)(2,1)} %collective-permute-done.9.refs_2_, ...), custom_call_target="tpu_custom_call" | custom-call | flops 1 | bytes 1 | tf_op jit(solution)/shard_map/prepare_other/pallas_call | solution.py:96
  48.7 0.6 collective-permute-start.17
  49.2 1.6 %prepare_other.5 = bf16[2,32,9216]{2,1,0:T(8,128)(2,1)S(1)} custom-call(s32[2,288]{1,0:T(2,128)S(1)} %copy-done.2, bf16[32,3456]{1,0:T(8,128)(2,1)S(1)} %collective-permute-done.4.refs_0_, bf16[32,3456]{1,0:T(8,128)(2,1)} %collective-permute-done.5.refs_1_, bf16[32,3456]{1,0:T(8,128)(2,1)} %collective-permute-done.6.refs_2_, ...), custom_call_target="tpu_custom_call" | custom-call | flops 1 | bytes 1 | tf_op jit(solution)/shard_map/prepare_other/pallas_call | solution.py:96
  50.9 0.1 collective-permute-start.11
  51.0 0.0 collective-permute-done.13.refs_2_
  51.0 1.1 %prepare_other.6 = bf16[2,32,9216]{2,1,0:T(8,128)(2,1)S(1)} custom-call(s32[2,288]{1,0:T(2,128)S(1)} %copy-done.2, bf16[32,3456]{1,0:T(8,128)(2,1)S(1)} %collective-permute-done.3.refs_0_, bf16[32,3456]{1,0:T(8,128)(2,1)S(1)} %collective-permute-done.12.refs_1_, bf16[32,3456]{1,0:T(8,128)(2,1)S(1)} %collective-permute-done.13.refs_2_, ...), custom_call_target="tpu_custom_call" | custom-call | flops 1 | bytes 1 | tf_op jit(solution)/shard_map/prepare_other/pallas_call | solution.py:96
  52.0 0.5 collective-permute-start.15
  52.6 1.6 %prepare_own.5.refs_2_ = bf16[2,32,9216]{2,1,0:T(8,128)(2,1)S(1)} custom-call(s32[2,288]{1,0:T(2,128)S(1)} %copy-done.2, bf16[32,3456]{1,0:T(8,128)(2,1)S(1)} %collective-permute-done.4.refs_0_, bf16[32,3456]{1,0:T(8,128)(2,1)} %collective-permute-done.5.refs_1_, bf16[32,3456]{1,0:T(8,128)(2,1)} %collective-permute-done.6.refs_2_, ...), custom_call_target="tpu_custom_call" | custom-call | flops 1 | bytes 1 | tf_op jit(solution)/shard_map/prepare_own/pallas_call | solution.py:96
  54.2 1.5 %prepare_own.7.refs_6_ = bf16[2,32,9216]{2,1,0:T(8,128)(2,1)S(1)} custom-call(s32[2,288]{1,0:T(2,128)S(1)} %copy-done.2, bf16[32,3456]{1,0:T(8,128)(2,1)S(1)} %collective-permute-done.1.refs_0_, bf16[32,3456]{1,0:T(8,128)(2,1)} %collective-permute-done.8.refs_1_, bf16[32,3456]{1,0:T(8,128)(2,1)} %collective-permute-done.9.refs_2_, ...), custom_call_target="tpu_custom_call" | custom-call | flops 1 | bytes 1 | tf_op jit(solution)/shard_map/prepare_own/pallas_call | solution.py:96
  55.8 1.1 %prepare_own.6.refs_4_ = bf16[2,32,9216]{2,1,0:T(8,128)(2,1)S(1)} custom-call(s32[2,288]{1,0:T(2,128)S(1)} %copy-done.2, bf16[32,3456]{1,0:T(8,128)(2,1)S(1)} %collective-permute-done.3.refs_0_, bf16[32,3456]{1,0:T(8,128)(2,1)S(1)} %collective-permute-done.12.refs_1_, bf16[32,3456]{1,0:T(8,128)(2,1)S(1)} %collective-permute-done.13.refs_2_, ...), custom_call_target="tpu_custom_call" | custom-call | flops 1 | bytes 1 | tf_op jit(solution)/shard_map/prepare_own/pallas_call | solution.py:96
  56.8 0.0 collective-permute-done.17.refs_7_
  56.9 13.2 %products.3 = (f32[5,64,256]{2,1,0:T(8,128)S(1)}, bf16[5,64,256]{2,1,0:T(8,128)(2,1)S(1)}, bf16[5,64,256]{2,1,0:T(8,128)(2,1)S(1)}, bf16[5,64,256]{2,1,0:T(8,128)(2,1)S(1)}) custom-call(bf16[9,16,9216]{2,1,0:T(8,128)(2,1)S(1)} %band_matrices.1.x_ref, bf16[2,32,9216]{2,1,0:T(8,128)(2,1)S(1)} %prepare_own.4._.refs_0_, ...), custom_call_target="tpu_custom_call" | custom-call | flops 12079595520 | bytes 9437184 | tf_op jit(solution)/shard_map/products/pallas_call | solution.py:149
  70.1 1.8 %collective-permute-start.18 = (bf16[5,64,256]{2,1,0:T(8,128)(2,1)S(1)}, bf16[5,64,256]{2,1,0:T(8,128)(2,1)S(1)}, u32[]{:S(2)}, u32[]{:S(2)}) collective-permute-start(bf16[5,64,256]{2,1,0:T(8,128)(2,1)S(1)} %get-tuple-element.75), channel_id=1, source_target_pairs={{0,2},{1,3},{2,4},{3,5},{4,6},{5,7},{6,0},{7,1},{8,10},{9,11},{10,... | collective-permute-start | bytes 491528 | tf_op jit(solution)/shard_map/ppermute | solution.py:262
  71.9 2.8 %collective-permute-start.19 = (bf16[5,64,256]{2,1,0:T(8,128)(2,1)S(1)}, bf16[5,64,256]{2,1,0:T(8,128)(2,1)S(1)}, u32[]{:S(2)}, u32[]{:S(2)}) collective-permute-start(bf16[5,64,256]{2,1,0:T(8,128)(2,1)S(1)} %get-tuple-element.76), channel_id=1, source_target_pairs={{0,4},{1,5},{2,6},{3,7},{4,0},{5,1},{6,2},{7,3},{8,12},{9,13},{10,... | collective-permute-start | bytes 491528 | tf_op jit(solution)/shard_map/ppermute | solution.py:262
  74.6 0.0 collective-permute-start.20
  74.7 8.0 %products.4 = (f32[3,64,256]{2,1,0:T(8,128)S(1)}, bf16[3,64,256]{2,1,0:T(8,128)(2,1)S(1)}, bf16[3,64,256]{2,1,0:T(8,128)(2,1)S(1)}, bf16[3,64,256]{2,1,0:T(8,128)(2,1)S(1)}) custom-call(bf16[9,16,9216]{2,1,0:T(8,128)(2,1)S(1)} %band_matrices.1.x_ref, bf16[2,32,9216]{2,1,0:T(8,128)(2,1)S(1)} %prepare_own.4._.refs_0_, ...), custom_call_target="tpu_custom_call" | custom-call | flops 7247757312 | bytes 9437184 | tf_op jit(solution)/shard_map/products/pallas_call | solution.py:149
  82.6 2.1 %collective-permute-start.21 = (bf16[3,64,256]{2,1,0:T(8,128)(2,1)S(1)}, bf16[3,64,256]{2,1,0:T(8,128)(2,1)S(1)}, u32[]{:S(2)}, u32[]{:S(2)}) collective-permute-start(bf16[3,64,256]{2,1,0:T(8,128)(2,1)S(1)} %get-tuple-element.90), channel_id=1, source_target_pairs={{0,2},{1,3},{2,4},{3,5},{4,6},{5,7},{6,0},{7,1},{8,10},{9,11},{10,... | collective-permute-start | bytes 294920 | tf_op jit(solution)/shard_map/ppermute | solution.py:262
  84.7 0.2 collective-permute-start.22
  84.9 0.0 collective-permute-done.18
  84.9 2.3 %collective-permute-start.23 = (bf16[3,64,256]{2,1,0:T(8,128)(2,1)S(1)}, bf16[3,64,256]{2,1,0:T(8,128)(2,1)S(1)}, u32[]{:S(2)}, u32[]{:S(2)}) collective-permute-start(bf16[3,64,256]{2,1,0:T(8,128)(2,1)S(1)} %get-tuple-element.92), channel_id=1, source_target_pairs={{0,6},{1,7},{2,0},{3,1},{4,2},{5,3},{6,4},{7,5},{8,14},{9,15},{10,... | collective-permute-start | bytes 294920 | tf_op jit(solution)/shard_map/ppermute | solution.py:262
  87.2 0.0 collective-permute-done.20
  87.2 0.1 convert_add_fusion
  87.3 3.0 %products.5 = (f32[1,64,256]{2,1,0:T(8,128)S(1)}, bf16[1,64,256]{2,1,0:T(8,128)(2,1)S(1)}, bf16[1,64,256]{2,1,0:T(8,128)(2,1)S(1)}, bf16[1,64,256]{2,1,0:T(8,128)(2,1)S(1)}) custom-call(bf16[9,16,9216]{2,1,0:T(8,128)(2,1)S(1)} %band_matrices.1.x_ref, bf16[2,32,9216]{2,1,0:T(8,128)(2,1)S(1)} %prepare_own.4._.refs_0_, ...), custom_call_target="tpu_custom_call" | custom-call | flops 2415919104 | bytes 9437184 | tf_op jit(solution)/shard_map/products/pallas_call | solution.py:149
  90.3 6.8 %collective-permute-start.24 = (bf16[1,64,256]{2,1,0:T(8,128)(2,1)S(1)}, bf16[1,64,256]{2,1,0:T(8,128)(2,1)S(1)}, u32[]{:S(2)}, u32[]{:S(2)}) collective-permute-start(bf16[1,64,256]{2,1,0:T(8,128)(2,1)S(1)} %get-tuple-element.98), channel_id=1, source_target_pairs={{0,2},{1,3},{2,4},{3,5},{4,6},{5,7},{6,0},{7,1},{8,10},{9,11},{10,... | collective-permute-start | bytes 98312 | tf_op jit(solution)/shard_map/ppermute | solution.py:262
  97.1 0.0 collective-permute-start.25
  97.1 0.0 collective-permute-done.21
  97.1 2.4 %collective-permute-start.26 = (bf16[1,64,256]{2,1,0:T(8,128)(2,1)S(1)}, bf16[1,64,256]{2,1,0:T(8,128)(2,1)S(1)}, u32[]{:S(2)}, u32[]{:S(2)}) collective-permute-start(bf16[1,64,256]{2,1,0:T(8,128)(2,1)S(1)} %get-tuple-element.100), channel_id=1, source_target_pairs={{0,6},{1,7},{2,0},{3,1},{4,2},{5,3},{6,4},{7,5},{8,14},{9,15},{10,... | collective-permute-start | bytes 98312 | tf_op jit(solution)/shard_map/ppermute | solution.py:262
  99.6 0.1 collective-permute-start.28
  99.7 0.5 collective-permute-start.27
  100.2 1.7 %collective-permute-done.25 = bf16[1,64,256]{2,1,0:T(8,128)(2,1)S(1)} collective-permute-done((bf16[1,64,256]{2,1,0:T(8,128)(2,1)S(1)}, bf16[1,64,256]{2,1,0:T(8,128)(2,1)S(1)}, u32[]{:S(2)}, u32[]{:S(2)}) %collective-permute-start.25) | collective-permute-done | bytes 32800 | tf_op jit(solution)/shard_map/ppermute | solution.py:262
  101.9 0.1 collective-permute-start.29
  102.0 1.2 %collective-permute-done.29 = f32[1,32,256]{2,1,0:T(8,128)S(1)} collective-permute-done((f32[1,32,256]{2,1,0:T(8,128)S(1)}, f32[1,32,256]{2,1,0:T(8,128)S(1)}, u32[]{:S(2)}, u32[]{:S(2)}) %collective-permute-start.29) | collective-permute-done | bytes 32800 | tf_op jit(solution)/shard_map/ppermute | solution.py:262
  103.2 0.9 maximum_select_fusion
  (28 shorter events, 0.2 us)
Async XLA Ops:
  0.0 15.7 %copy-start.2 = (s32[2,288]{1,0:T(2,128)S(1)}, s32[2,288]{1,0:T(2,128)}, u32[]{:S(2)}) copy-start(s32[2,288]{1,0:T(2,128)} %kq_ref.17) | copy-start | bytes 6916
  3.0 11.3 %collective-permute-start.4 = (bf16[32,3456]{1,0:T(8,128)(2,1)}, bf16[32,3456]{1,0:T(8,128)(2,1)S(1)}, u32[]{:S(2)}, u32[]{:S(2)}) collective-permute-start(bf16[32,3456]{1,0:T(8,128)(2,1)} %get-tuple-element.60), channel_id=1, source_target_pairs={{0,6},{1,7},{2,0},{3,1},{4,2},{5,3},{6,4},{7,5},{8,14},{9,15},{10,... | collective-permute-start | bytes 663560 | tf_op jit(solution)/shard_map/ppermute | solution.py:262
  8.1 12.3 %collective-permute-start.1 = (bf16[32,3456]{1,0:T(8,128)(2,1)}, bf16[32,3456]{1,0:T(8,128)(2,1)S(1)}, u32[]{:S(2)}, u32[]{:S(2)}) collective-permute-start(bf16[32,3456]{1,0:T(8,128)(2,1)} %get-tuple-element.56), channel_id=1, source_target_pairs={{0,2},{1,3},{2,4},{3,5},{4,6},{5,7},{6,0},{7,1},{8,10},{9,11},{10,... | collective-permute-start | bytes 663560 | tf_op jit(solution)/shard_map/ppermute | solution.py:262
  14.2 8.7 %collective-permute-start.5 = (bf16[32,3456]{1,0:T(8,128)(2,1)S(1)}, bf16[32,3456]{1,0:T(8,128)(2,1)}, u32[]{:S(2)}, u32[]{:S(2)}) collective-permute-start(bf16[32,3456]{1,0:T(8,128)(2,1)S(1)} %collective-permute-done.4.refs_0_), channel_id=1, source_target_pairs={{0,8},{1,17},{2,10},{3,19},{4,12},{5,21},{6,14},{7,23},{8,0},{9,25... | collective-permute-start | bytes 663560 | tf_op jit(solution)/shard_map/ppermute | solution.py:262
  15.7 1.2 %copy-start = (bf16[32,13824]{1,0:T(8,128)(2,1)S(1)}, bf16[32,13824]{1,0:T(8,128)(2,1)}, u32[]{:S(2)}) copy-start(bf16[32,13824]{1,0:T(8,128)(2,1)} %get-tuple-element.54.refs_0_) | copy-start | bytes 2654212
  17.9 1.0 copy-start.3
  17.9 17.3 %copy-start.1 = (bf16[2,9,32,288]{3,2,1,0:T(8,128)(2,1)S(1)}, bf16[2,9,32,288]{3,2,1,0:T(8,128)(2,1)}, u32[]{:S(2)}) copy-start(bf16[2,9,32,288]{3,2,1,0:T(8,128)(2,1)} %coupling_ref.3) | copy-start | bytes 995332
  18.9 10.7 %collective-permute-start.3 = (bf16[32,3456]{1,0:T(8,128)(2,1)S(1)}, bf16[32,3456]{1,0:T(8,128)(2,1)S(1)}, u32[]{:S(2)}, u32[]{:S(2)}) collective-permute-start(bf16[32,3456]{1,0:T(8,128)(2,1)S(1)} %copy-done.3), channel_id=1, source_target_pairs={{0,4},{1,5},{2,6},{3,7},{4,0},{5,1},{6,2},{7,3},{8,12},{9,13},{10,... | collective-permute-start | bytes 663560 | tf_op jit(solution)/shard_map/ppermute | solution.py:262
  20.3 9.3 %collective-permute-start.8 = (bf16[32,3456]{1,0:T(8,128)(2,1)S(1)}, bf16[32,3456]{1,0:T(8,128)(2,1)}, u32[]{:S(2)}, u32[]{:S(2)}) collective-permute-start(bf16[32,3456]{1,0:T(8,128)(2,1)S(1)} %collective-permute-done.1.refs_0_), channel_id=1, source_target_pairs={{0,8},{1,17},{2,10},{3,19},{4,12},{5,21},{6,14},{7,23},{8,0},{9,25... | collective-permute-start | bytes 663560 | tf_op jit(solution)/shard_map/ppermute | solution.py:262
  20.9 9.5 %collective-permute-start.9 = (bf16[32,3456]{1,0:T(8,128)(2,1)S(1)}, bf16[32,3456]{1,0:T(8,128)(2,1)}, u32[]{:S(2)}, u32[]{:S(2)}) collective-permute-start(bf16[32,3456]{1,0:T(8,128)(2,1)S(1)} %collective-permute-done.1.refs_0_), channel_id=1, source_target_pairs={{0,16},{1,9},{2,18},{3,11},{4,20},{5,13},{6,22},{7,15},{8,24},{9,1... | collective-permute-start | bytes 663560 | tf_op jit(solution)/shard_map/ppermute | solution.py:262
  22.4 7.9 %collective-permute-start.6 = (bf16[32,3456]{1,0:T(8,128)(2,1)S(1)}, bf16[32,3456]{1,0:T(8,128)(2,1)}, u32[]{:S(2)}, u32[]{:S(2)}) collective-permute-start(bf16[32,3456]{1,0:T(8,128)(2,1)S(1)} %collective-permute-done.4.refs_0_), channel_id=1, source_target_pairs={{0,16},{1,9},{2,18},{3,11},{4,20},{5,13},{6,22},{7,15},{8,24},{9,1... | collective-permute-start | bytes 663560 | tf_op jit(solution)/shard_map/ppermute | solution.py:262
  22.9 8.7 %collective-permute-start.7 = (bf16[32,3456]{1,0:T(8,128)(2,1)}, bf16[32,3456]{1,0:T(8,128)(2,1)}, u32[]{:S(2)}, u32[]{:S(2)}) collective-permute-start(bf16[32,3456]{1,0:T(8,128)(2,1)} %collective-permute-done.5.refs_1_), channel_id=1, source_target_pairs={{0,16},{1,9},{2,18},{3,11},{4,20},{5,13},{6,22},{7,15},{8,24},{9,1... | collective-permute-start | bytes 663560 | tf_op jit(solution)/shard_map/ppermute | solution.py:262
  29.6 5.5 %collective-permute-start = (bf16[9,32,288]{2,1,0:T(8,128)(2,1)}, bf16[9,32,288]{2,1,0:T(8,128)(2,1)}, u32[]{:S(2)}, u32[]{:S(2)}) collective-permute-start(bf16[9,32,288]{2,1,0:T(8,128)(2,1)} %get-tuple-element.55), channel_id=1, source_target_pairs={{0,1},{1,0},{2,3},{3,2},{4,5},{5,4},{6,7},{7,6},{8,9},{9,8},{10,11... | collective-permute-start | bytes 497672 | tf_op jit(solution)/shard_map/ppermute | solution.py:262
  29.6 17.5 %collective-permute-start.16 = (bf16[32,3456]{1,0:T(8,128)(2,1)}, bf16[32,3456]{1,0:T(8,128)(2,1)S(1)}, u32[]{:S(2)}, u32[]{:S(2)}) collective-permute-start(bf16[32,3456]{1,0:T(8,128)(2,1)} %collective-permute-done.8.refs_1_), channel_id=1, source_target_pairs={{0,16},{1,9},{2,18},{3,11},{4,20},{5,13},{6,22},{7,15},{8,24},{9,1... | collective-permute-start | bytes 663560 | tf_op jit(solution)/shard_map/ppermute | solution.py:262
  31.7 19.2 %collective-permute-start.14 = (bf16[32,3456]{1,0:T(8,128)(2,1)S(1)}, bf16[32,3456]{1,0:T(8,128)(2,1)S(1)}, u32[]{:S(2)}, u32[]{:S(2)}) collective-permute-start(bf16[32,3456]{1,0:T(8,128)(2,1)S(1)} %collective-permute-done.3.refs_0_), channel_id=1, source_target_pairs={{0,24},{1,25},{2,26},{3,27},{4,28},{5,29},{6,30},{7,31},{8,16},{9,... | collective-permute-start | bytes 663560 | tf_op jit(solution)/shard_map/ppermute | solution.py:262
  34.1 16.9 %collective-permute-start.13 = (bf16[32,3456]{1,0:T(8,128)(2,1)S(1)}, bf16[32,3456]{1,0:T(8,128)(2,1)S(1)}, u32[]{:S(2)}, u32[]{:S(2)}) collective-permute-start(bf16[32,3456]{1,0:T(8,128)(2,1)S(1)} %collective-permute-done.3.refs_0_), channel_id=1, source_target_pairs={{0,16},{1,17},{2,18},{3,19},{4,20},{5,21},{6,22},{7,23},{8,24},{9,... | collective-permute-start | bytes 663560 | tf_op jit(solution)/shard_map/ppermute | solution.py:262
  34.6 16.4 %collective-permute-start.12 = (bf16[32,3456]{1,0:T(8,128)(2,1)S(1)}, bf16[32,3456]{1,0:T(8,128)(2,1)S(1)}, u32[]{:S(2)}, u32[]{:S(2)}) collective-permute-start(bf16[32,3456]{1,0:T(8,128)(2,1)S(1)} %collective-permute-done.3.refs_0_), channel_id=1, source_target_pairs={{0,8},{1,9},{2,10},{3,11},{4,12},{5,13},{6,14},{7,15},{8,0},{9,1},... | collective-permute-start | bytes 663560 | tf_op jit(solution)/shard_map/ppermute | solution.py:262
  35.2 7.9 %collective-permute-start.2 = (bf16[9,32,288]{2,1,0:T(8,128)(2,1)S(1)}, bf16[9,32,288]{2,1,0:T(8,128)(2,1)S(1)}, u32[]{:S(2)}, u32[]{:S(2)}) collective-permute-start(bf16[9,32,288]{2,1,0:T(8,128)(2,1)S(1)} %bitcast_select_fusion), channel_id=1, source_target_pairs={{0,6},{1,7},{2,0},{3,1},{4,2},{5,3},{6,4},{7,5},{8,14},{9,15},{10,... | collective-permute-start | bytes 497672 | tf_op jit(solution)/shard_map/ppermute | solution.py:262
  43.1 13.7 %collective-permute-start.10 = (bf16[2,32,9216]{2,1,0:T(8,128)(2,1)S(1)}, bf16[2,32,9216]{2,1,0:T(8,128)(2,1)S(1)}, u32[]{:S(2)}, u32[]{:S(2)}) collective-permute-start(bf16[2,32,9216]{2,1,0:T(8,128)(2,1)S(1)} %prepare_other.4), channel_id=1, source_target_pairs={{0,1},{1,0},{2,3},{3,2},{4,5},{5,4},{6,7},{7,6},{8,9},{9,8},{10,11... | collective-permute-start | bytes 3538952 | tf_op jit(solution)/shard_map/ppermute | solution.py:262
  48.7 8.2 %collective-permute-start.17 = (bf16[2,32,9216]{2,1,0:T(8,128)(2,1)S(1)}, bf16[2,32,9216]{2,1,0:T(8,128)(2,1)S(1)}, u32[]{:S(2)}, u32[]{:S(2)}) collective-permute-start(bf16[2,32,9216]{2,1,0:T(8,128)(2,1)S(1)} %prepare_other.7), channel_id=1, source_target_pairs={{0,1},{1,0},{2,3},{3,2},{4,5},{5,4},{6,7},{7,6},{8,9},{9,8},{10,11... | collective-permute-start | bytes 3538952 | tf_op jit(solution)/shard_map/ppermute | solution.py:262
  50.9 5.9 %collective-permute-start.11 = (bf16[2,32,9216]{2,1,0:T(8,128)(2,1)S(1)}, bf16[2,32,9216]{2,1,0:T(8,128)(2,1)S(1)}, u32[]{:S(2)}, u32[]{:S(2)}) collective-permute-start(bf16[2,32,9216]{2,1,0:T(8,128)(2,1)S(1)} %prepare_other.5), channel_id=1, source_target_pairs={{0,1},{1,0},{2,3},{3,2},{4,5},{5,4},{6,7},{7,6},{8,9},{9,8},{10,11... | collective-permute-start | bytes 3538952 | tf_op jit(solution)/shard_map/ppermute | solution.py:262
  52.0 4.8 %collective-permute-start.15 = (bf16[2,32,9216]{2,1,0:T(8,128)(2,1)S(1)}, bf16[2,32,9216]{2,1,0:T(8,128)(2,1)S(1)}, u32[]{:S(2)}, u32[]{:S(2)}) collective-permute-start(bf16[2,32,9216]{2,1,0:T(8,128)(2,1)S(1)} %prepare_other.6), channel_id=1, source_target_pairs={{0,1},{1,0},{2,3},{3,2},{4,5},{5,4},{6,7},{7,6},{8,9},{9,8},{10,11... | collective-permute-start | bytes 3538952 | tf_op jit(solution)/shard_map/ppermute | solution.py:262
  70.1 14.8 %collective-permute-start.18 = (bf16[5,64,256]{2,1,0:T(8,128)(2,1)S(1)}, bf16[5,64,256]{2,1,0:T(8,128)(2,1)S(1)}, u32[]{:S(2)}, u32[]{:S(2)}) collective-permute-start(bf16[5,64,256]{2,1,0:T(8,128)(2,1)S(1)} %get-tuple-element.75), channel_id=1, source_target_pairs={{0,2},{1,3},{2,4},{3,5},{4,6},{5,7},{6,0},{7,1},{8,10},{9,11},{10,... | collective-permute-start | bytes 491528 | tf_op jit(solution)/shard_map/ppermute | solution.py:262
  71.9 15.3 %collective-permute-start.19 = (bf16[5,64,256]{2,1,0:T(8,128)(2,1)S(1)}, bf16[5,64,256]{2,1,0:T(8,128)(2,1)S(1)}, u32[]{:S(2)}, u32[]{:S(2)}) collective-permute-start(bf16[5,64,256]{2,1,0:T(8,128)(2,1)S(1)} %get-tuple-element.76), channel_id=1, source_target_pairs={{0,4},{1,5},{2,6},{3,7},{4,0},{5,1},{6,2},{7,3},{8,12},{9,13},{10,... | collective-permute-start | bytes 491528 | tf_op jit(solution)/shard_map/ppermute | solution.py:262
  74.6 12.5 %collective-permute-start.20 = (bf16[5,64,256]{2,1,0:T(8,128)(2,1)S(1)}, bf16[5,64,256]{2,1,0:T(8,128)(2,1)S(1)}, u32[]{:S(2)}, u32[]{:S(2)}) collective-permute-start(bf16[5,64,256]{2,1,0:T(8,128)(2,1)S(1)} %get-tuple-element.77), channel_id=1, source_target_pairs={{0,6},{1,7},{2,0},{3,1},{4,2},{5,3},{6,4},{7,5},{8,14},{9,15},{10,... | collective-permute-start | bytes 491528 | tf_op jit(solution)/shard_map/ppermute | solution.py:262
  82.6 14.5 %collective-permute-start.21 = (bf16[3,64,256]{2,1,0:T(8,128)(2,1)S(1)}, bf16[3,64,256]{2,1,0:T(8,128)(2,1)S(1)}, u32[]{:S(2)}, u32[]{:S(2)}) collective-permute-start(bf16[3,64,256]{2,1,0:T(8,128)(2,1)S(1)} %get-tuple-element.90), channel_id=1, source_target_pairs={{0,2},{1,3},{2,4},{3,5},{4,6},{5,7},{6,0},{7,1},{8,10},{9,11},{10,... | collective-permute-start | bytes 294920 | tf_op jit(solution)/shard_map/ppermute | solution.py:262
  84.7 14.8 %collective-permute-start.22 = (bf16[3,64,256]{2,1,0:T(8,128)(2,1)S(1)}, bf16[3,64,256]{2,1,0:T(8,128)(2,1)S(1)}, u32[]{:S(2)}, u32[]{:S(2)}) collective-permute-start(bf16[3,64,256]{2,1,0:T(8,128)(2,1)S(1)} %get-tuple-element.91), channel_id=1, source_target_pairs={{0,4},{1,5},{2,6},{3,7},{4,0},{5,1},{6,2},{7,3},{8,12},{9,13},{10,... | collective-permute-start | bytes 294920 | tf_op jit(solution)/shard_map/ppermute | solution.py:262
  84.9 14.7 %collective-permute-start.23 = (bf16[3,64,256]{2,1,0:T(8,128)(2,1)S(1)}, bf16[3,64,256]{2,1,0:T(8,128)(2,1)S(1)}, u32[]{:S(2)}, u32[]{:S(2)}) collective-permute-start(bf16[3,64,256]{2,1,0:T(8,128)(2,1)S(1)} %get-tuple-element.92), channel_id=1, source_target_pairs={{0,6},{1,7},{2,0},{3,1},{4,2},{5,3},{6,4},{7,5},{8,14},{9,15},{10,... | collective-permute-start | bytes 294920 | tf_op jit(solution)/shard_map/ppermute | solution.py:262
  90.3 9.9 %collective-permute-start.24 = (bf16[1,64,256]{2,1,0:T(8,128)(2,1)S(1)}, bf16[1,64,256]{2,1,0:T(8,128)(2,1)S(1)}, u32[]{:S(2)}, u32[]{:S(2)}) collective-permute-start(bf16[1,64,256]{2,1,0:T(8,128)(2,1)S(1)} %get-tuple-element.98), channel_id=1, source_target_pairs={{0,2},{1,3},{2,4},{3,5},{4,6},{5,7},{6,0},{7,1},{8,10},{9,11},{10,... | collective-permute-start | bytes 98312 | tf_op jit(solution)/shard_map/ppermute | solution.py:262
  97.1 4.8 %collective-permute-start.25 = (bf16[1,64,256]{2,1,0:T(8,128)(2,1)S(1)}, bf16[1,64,256]{2,1,0:T(8,128)(2,1)S(1)}, u32[]{:S(2)}, u32[]{:S(2)}) collective-permute-start(bf16[1,64,256]{2,1,0:T(8,128)(2,1)S(1)} %get-tuple-element.99), channel_id=1, source_target_pairs={{0,4},{1,5},{2,6},{3,7},{4,0},{5,1},{6,2},{7,3},{8,12},{9,13},{10,... | collective-permute-start | bytes 98312 | tf_op jit(solution)/shard_map/ppermute | solution.py:262
  97.1 4.8 %collective-permute-start.26 = (bf16[1,64,256]{2,1,0:T(8,128)(2,1)S(1)}, bf16[1,64,256]{2,1,0:T(8,128)(2,1)S(1)}, u32[]{:S(2)}, u32[]{:S(2)}) collective-permute-start(bf16[1,64,256]{2,1,0:T(8,128)(2,1)S(1)} %get-tuple-element.100), channel_id=1, source_target_pairs={{0,6},{1,7},{2,0},{3,1},{4,2},{5,3},{6,4},{7,5},{8,14},{9,15},{10,... | collective-permute-start | bytes 98312 | tf_op jit(solution)/shard_map/ppermute | solution.py:262
  99.6 3.6 %collective-permute-start.28 = (f32[3,32,256]{2,1,0:T(8,128)S(1)}, f32[3,32,256]{2,1,0:T(8,128)S(1)}, u32[]{:S(2)}, u32[]{:S(2)}) collective-permute-start(f32[3,32,256]{2,1,0:T(8,128)S(1)} %get-tuple-element.104), channel_id=1, source_target_pairs={{0,1},{1,0},{2,3},{3,2},{4,5},{5,4},{6,7},{7,6},{8,9},{9,8},{10,11... | collective-permute-start | bytes 294920 | tf_op jit(solution)/shard_map/ppermute | solution.py:262
  99.7 3.5 %collective-permute-start.27 = (f32[5,32,256]{2,1,0:T(8,128)S(1)}, f32[5,32,256]{2,1,0:T(8,128)S(1)}, u32[]{:S(2)}, u32[]{:S(2)}) collective-permute-start(f32[5,32,256]{2,1,0:T(8,128)S(1)} %get-tuple-element.102), channel_id=1, source_target_pairs={{0,1},{1,0},{2,3},{3,2},{4,5},{5,4},{6,7},{7,6},{8,9},{9,8},{10,11... | collective-permute-start | bytes 491528 | tf_op jit(solution)/shard_map/ppermute | solution.py:262
  101.9 1.3 %collective-permute-start.29 = (f32[1,32,256]{2,1,0:T(8,128)S(1)}, f32[1,32,256]{2,1,0:T(8,128)S(1)}, u32[]{:S(2)}, u32[]{:S(2)}) collective-permute-start(f32[1,32,256]{2,1,0:T(8,128)S(1)} %get-tuple-element.106), channel_id=1, source_target_pairs={{0,1},{1,0},{2,3},{3,2},{4,5},{5,4},{6,7},{7,6},{8,9},{9,8},{10,11... | collective-permute-start | bytes 98312 | tf_op jit(solution)/shard_map/ppermute | solution.py:262

commit v8 on v7

--- a/solution.py
+++ b/solution.py
@@ -287,25 +287,28 @@
     spread = spread_matrices(min(coupling.shape[3], 64), keep)
     amps = {0: (keep, sibling(pass_on))}
 
+    other_table = sibling(give)
+    first_table = jnp.where(core == 0, lax.dynamic_index_in_dim(coupling, core, 0, keepdims=False), other_table)
+    next_table = passed_down(first_table, 1)
+
     parts, first_steps = {}, []
     for e in near:
         piece = arrived[e]
         one = permute(piece, lambda p, zz, c: (p ^ (1 + c), zz, c))
         two = permute(piece, lambda p, zz, c: (p ^ (2 - c), zz, c))
+        if e == 1:
+            one = after(one, next_table)
         three = permute(one, lambda p, zz, c: (p ^ (2 - c), zz, c))
-        first_steps += [one, two, three] if e == 1 else [one, two]
+        first_steps += [one, two]
         parts[e] = [piece, one, two, three]
     for e in far:
-        piece = after(arrived[e], *first_steps)
+        piece = after(arrived[e], next_table, *first_steps)
         parts[e] = [piece] + [permute(piece, lambda p, zz, c: (p ^ i, zz, c)) for i in (1, 2, 3)]
-    other_table = sibling(give)
-    first_table = jnp.where(core == 0, lax.dynamic_index_in_dim(coupling, core, 0, keepdims=False), other_table)
-    next_table = passed_down(after(first_table, *[arrived[e] for e in near[1:]]), 1)
-    next_table = after(next_table, *[parts[e][0] for e in far])
-    x = band_matrices(kq_map, spread, coupling, other_table, next_table, lines_all)
+    x = band_matrices(kq_map, spread, coupling, other_table, after(next_table, *[parts[e][0] for e in far]), lines_all)
     for e in near + far:
         piece, *others = parts[e]
-        pass_on = prepared([after(piece, x)] + others, True, e in far)
+        done = [x] if e in near else [x, amps[1][0]]
+        pass_on = prepared([after(piece, *done)] + others, True, e in far)
         keep = prepared([after(piece, pass_on)] + others, False, e in far)
         amps[e] = (keep, sibling(pass_on))
     amps = [half for e in range(n_z) for half in amps[e]]

time: 104 us -> 99.3 us (0.955)
  waiting for transfers between devices: 20.2 us -> 15.4 us
  Pallas kernels: 41.8 us -> 39.3 us
  starting transfers between devices: 39.6 us -> 41.8 us
    ppermute x30, waiting for transfers between devices: 20.2 us -> 15.4 us  [permute(): return lax.ppermute(x, ('pb', 'ka'), pairs)]
    ppermute x30, starting transfers between devices: 39.6 us -> 41.8 us  [permute(): return lax.ppermute(x, ('pb', 'ka'), pairs)]
    pallas_call x8, Pallas kernels: 10.4 us -> 8.31 us  [prepare(): pl.pallas_call(functools.partial(prep_kernel, block // LINE, lines_all, f...]
  transfers between devices with their start and end apart: 30 -> 30, of which waited for: 6 -> 9; matrix products, arithmetic and copies ran while one was open for 0% -> 0% of each run, Pallas kernels for 25% -> 23%
where the time goes in v8:
time: 99.3 us; the launch traced here: 99.1 us
  starting transfers between devices  41.8 us (42%)
  Pallas kernels  39.3 us (40%)
  waiting for transfers between devices  15.4 us (16%)
  local copies, waits for them, and re-layouts  1.22 us (1%)
  other arithmetic  1.07 us (1%)
    ppermute x30, starting transfers between devices, permute(): return lax.ppermute(x, ('pb', 'ka'), pairs)  41.8 us
    pallas_call x3, Pallas kernels, products(): pl.pallas_call(functools.partial(main_kernel, sources, first, branches, f...  24.2 us
    ppermute x30, waiting for transfers between devices, permute(): return lax.ppermute(x, ('pb', 'ka'), pairs)  15.4 us
    pallas_call x8, Pallas kernels, prepare(): pl.pallas_call(functools.partial(prep_kernel, block // LINE, lines_all, f...  8.31 us
    pallas_call x1, Pallas kernels, band_matrices(): pl.pallas_call(functools.partial(band_kernel, count // KY, lines_all), in...  3.71 us
    pallas_call x1, Pallas kernels, cut(): pl.pallas_call(functools.partial(cut_kernel, block), in_specs=[pl.BlockSp...  2.98 us
  transfers between devices with their start and end apart: 30, of which 9 were waited for; matrix products, arithmetic and copies ran while one was open for 0% of the time, Pallas kernels for 23%

profile of v8, /device:TPU:0, one launch (start us, length us, event | category | flops | bytes accessed | tf_op | source)
XLA Modules:
  0.0 99.1 jit_solution(12451396330679586711)
XLA Ops:
  0.0 3.0 %cut.1 = (bf16[32,3456]{1,0:T(8,128)(2,1)}, bf16[32,3456]{1,0:T(8,128)(2,1)}, bf16[32,3456]{1,0:T(8,128)(2,1)}, bf16[32,13824]{1,0:T(8,128)(2,1)}, bf16[9,32,288]{2,1,0:T(8,128)(2,1)}) custom-call(bf16[32,36864]{1,0:T(8,128)(2,1)} %env_ref.1, bf16[2,9,32,288]{3,2,1,0:T(8,128)(2,1)} %coupling_ref.3), custom_call_target="tpu_custom_call" | custom-call | flops 1 | bytes 1 | tf_op jit(solution)/shard_map/cut/pallas_call | solution.py:65
  3.0 0.5 collective-permute-start
  3.5 4.7 %collective-permute-start.3 = (bf16[32,3456]{1,0:T(8,128)(2,1)}, bf16[32,3456]{1,0:T(8,128)(2,1)S(1)}, u32[]{:S(2)}, u32[]{:S(2)}) collective-permute-start(bf16[32,3456]{1,0:T(8,128)(2,1)} %get-tuple-element.58), channel_id=1, source_target_pairs={{0,6},{1,7},{2,0},{3,1},{4,2},{5,3},{6,4},{7,5},{8,14},{9,15},{10,... | collective-permute-start | bytes 663560 | tf_op jit(solution)/shard_map/ppermute | solution.py:262
  8.2 0.0 collective-permute-start.6
  8.2 0.0 collective-permute-done.other_ref
  8.3 3.9 %collective-permute-start.1 = (bf16[9,32,288]{2,1,0:T(8,128)(2,1)S(1)}, bf16[9,32,288]{2,1,0:T(8,128)(2,1)S(1)}, u32[]{:S(2)}, u32[]{:S(2)}) collective-permute-start(bf16[9,32,288]{2,1,0:T(8,128)(2,1)S(1)} %bitcast_select_fusion), channel_id=1, source_target_pairs={{0,6},{1,7},{2,0},{3,1},{4,2},{5,3},{6,4},{7,5},{8,14},{9,15},{10,... | collective-permute-start | bytes 497672 | tf_op jit(solution)/shard_map/ppermute | solution.py:262
  12.1 1.2 %copy-done = bf16[32,13824]{1,0:T(8,128)(2,1)S(1)} copy-done((bf16[32,13824]{1,0:T(8,128)(2,1)S(1)}, bf16[32,13824]{1,0:T(8,128)(2,1)}, u32[]{:S(2)}) %copy-start) | copy-done | bytes 884760
  13.3 1.0 %prepare_other.4 = bf16[2,32,9216]{2,1,0:T(8,128)(2,1)S(1)} custom-call(s32[2,288]{1,0:T(2,128)S(1)} %copy-done.2, bf16[32,13824]{1,0:T(8,128)(2,1)S(1)} %copy-done), custom_call_target="tpu_custom_call" | custom-call | flops 1 | bytes 1 | tf_op jit(solution)/shard_map/prepare_other/pallas_call | solution.py:96
  14.3 0.0 collective-permute-done.3.refs_0_
  14.3 1.6 %collective-permute-start.4 = (bf16[32,3456]{1,0:T(8,128)(2,1)S(1)}, bf16[32,3456]{1,0:T(8,128)(2,1)S(1)}, u32[]{:S(2)}, u32[]{:S(2)}) collective-permute-start(bf16[32,3456]{1,0:T(8,128)(2,1)S(1)} %collective-permute-done.3.refs_0_), channel_id=1, source_target_pairs={{0,8},{1,17},{2,10},{3,19},{4,12},{5,21},{6,14},{7,23},{8,0},{9,25... | collective-permute-start | bytes 663560 | tf_op jit(solution)/shard_map/ppermute | solution.py:262
  15.9 1.0 %prepare_own.4._.refs_0_ = bf16[2,32,9216]{2,1,0:T(8,128)(2,1)S(1)} custom-call(s32[2,288]{1,0:T(2,128)S(1)} %copy-done.2, bf16[32,13824]{1,0:T(8,128)(2,1)S(1)} %copy-done), custom_call_target="tpu_custom_call" | custom-call | flops 1 | bytes 1 | tf_op jit(solution)/shard_map/prepare_own/pallas_call | solution.py:96
  16.9 3.0 %collective-permute-done.6.refs_0_ = bf16[32,3456]{1,0:T(8,128)(2,1)S(1)} collective-permute-done((bf16[32,3456]{1,0:T(8,128)(2,1)}, bf16[32,3456]{1,0:T(8,128)(2,1)S(1)}, u32[]{:S(2)}, u32[]{:S(2)}) %collective-permute-start.6) | collective-permute-done | bytes 221216 | tf_op jit(solution)/shard_map/ppermute | solution.py:262
  19.8 1.5 %collective-permute-start.7 = (bf16[32,3456]{1,0:T(8,128)(2,1)S(1)}, bf16[32,3456]{1,0:T(8,128)(2,1)S(1)}, u32[]{:S(2)}, u32[]{:S(2)}) collective-permute-start(bf16[32,3456]{1,0:T(8,128)(2,1)S(1)} %collective-permute-done.6.refs_0_), channel_id=1, source_target_pairs={{0,8},{1,17},{2,10},{3,19},{4,12},{5,21},{6,14},{7,23},{8,0},{9,25... | collective-permute-start | bytes 663560 | tf_op jit(solution)/shard_map/ppermute | solution.py:262
  21.3 0.2 collective-permute-start.2
  21.6 1.5 %collective-permute-start.5 = (bf16[32,3456]{1,0:T(8,128)(2,1)S(1)}, bf16[32,3456]{1,0:T(8,128)(2,1)S(1)}, u32[]{:S(2)}, u32[]{:S(2)}) collective-permute-start(bf16[32,3456]{1,0:T(8,128)(2,1)S(1)} %collective-permute-done.3.refs_0_), channel_id=1, source_target_pairs={{0,16},{1,9},{2,18},{3,11},{4,20},{5,13},{6,22},{7,15},{8,24},{9,1... | collective-permute-start | bytes 663560 | tf_op jit(solution)/shard_map/ppermute | solution.py:262
  23.1 0.6 collective-permute-done.1.next_ref
  23.7 1.5 %collective-permute-start.8 = (bf16[32,3456]{1,0:T(8,128)(2,1)S(1)}, bf16[32,3456]{1,0:T(8,128)(2,1)S(1)}, u32[]{:S(2)}, u32[]{:S(2)}) collective-permute-start(bf16[32,3456]{1,0:T(8,128)(2,1)S(1)} %collective-permute-done.6.refs_0_), channel_id=1, source_target_pairs={{0,16},{1,9},{2,18},{3,11},{4,20},{5,13},{6,22},{7,15},{8,24},{9,1... | collective-permute-start | bytes 663560 | tf_op jit(solution)/shard_map/ppermute | solution.py:262
  25.2 0.5 collective-permute-start.10
  25.8 2.3 %collective-permute-done.7.refs_1_ = bf16[32,3456]{1,0:T(8,128)(2,1)S(1)} collective-permute-done((bf16[32,3456]{1,0:T(8,128)(2,1)S(1)}, bf16[32,3456]{1,0:T(8,128)(2,1)S(1)}, u32[]{:S(2)}, u32[]{:S(2)}) %collective-permute-start.7) | collective-permute-done | bytes 221216 | tf_op jit(solution)/shard_map/ppermute | solution.py:262
  28.1 1.3 %collective-permute-start.16 = (bf16[32,3456]{1,0:T(8,128)(2,1)S(1)}, bf16[32,3456]{1,0:T(8,128)(2,1)S(1)}, u32[]{:S(2)}, u32[]{:S(2)}) collective-permute-start(bf16[32,3456]{1,0:T(8,128)(2,1)S(1)} %collective-permute-done.7.refs_1_), channel_id=1, source_target_pairs={{0,16},{1,9},{2,18},{3,11},{4,20},{5,13},{6,22},{7,15},{8,24},{9,1... | collective-permute-start | bytes 663560 | tf_op jit(solution)/shard_map/ppermute | solution.py:262
  29.3 3.9 %collective-permute-done.2.refs_0_ = bf16[32,3456]{1,0:T(8,128)(2,1)S(1)} collective-permute-done((bf16[32,3456]{1,0:T(8,128)(2,1)S(1)}, bf16[32,3456]{1,0:T(8,128)(2,1)S(1)}, u32[]{:S(2)}, u32[]{:S(2)}) %collective-permute-start.2) | collective-permute-done | bytes 221216 | tf_op jit(solution)/shard_map/ppermute | solution.py:262
  33.3 1.7 %collective-permute-start.14 = (bf16[32,3456]{1,0:T(8,128)(2,1)S(1)}, bf16[32,3456]{1,0:T(8,128)(2,1)S(1)}, u32[]{:S(2)}, u32[]{:S(2)}) collective-permute-start(bf16[32,3456]{1,0:T(8,128)(2,1)S(1)} %collective-permute-done.2.refs_0_), channel_id=1, source_target_pairs={{0,24},{1,25},{2,26},{3,27},{4,28},{5,29},{6,30},{7,31},{8,16},{9,... | collective-permute-start | bytes 663560 | tf_op jit(solution)/shard_map/ppermute | solution.py:262
  35.0 1.2 %collective-permute-start.13 = (bf16[32,3456]{1,0:T(8,128)(2,1)S(1)}, bf16[32,3456]{1,0:T(8,128)(2,1)S(1)}, u32[]{:S(2)}, u32[]{:S(2)}) collective-permute-start(bf16[32,3456]{1,0:T(8,128)(2,1)S(1)} %collective-permute-done.2.refs_0_), channel_id=1, source_target_pairs={{0,16},{1,17},{2,18},{3,19},{4,20},{5,21},{6,22},{7,23},{8,24},{9,... | collective-permute-start | bytes 663560 | tf_op jit(solution)/shard_map/ppermute | solution.py:262
  36.2 0.5 collective-permute-start.12
  36.8 0.1 spread.1
  36.9 3.7 %band_matrices.1.x_ref = bf16[9,16,9216]{2,1,0:T(8,128)(2,1)S(1)} custom-call(s32[2,288]{1,0:T(2,128)S(1)} %copy-done.2, bf16[2,256,1024]{2,1,0:T(8,128)(2,1)S(1)} %spread.1, bf16[2,9,32,288]{3,2,1,0:T(8,128)(2,1)S(1)} %copy-done.1, bf16[9,32,288]{2,1,0:T(8,128)(2,1)S(1)} %collective-permute-done.other_ref, ...), custom_call_target="tpu_custom_call" | custom-call | flops 1 | bytes 1 | tf_op jit(solution)/shard_map/band_matrices/pallas_call | solution.py:235
  40.6 0.1 collective-permute-start.9
  40.7 1.1 %prepare_other.5 = bf16[2,32,9216]{2,1,0:T(8,128)(2,1)S(1)} custom-call(s32[2,288]{1,0:T(2,128)S(1)} %copy-done.2, bf16[32,3456]{1,0:T(8,128)(2,1)S(1)} %collective-permute-done.3.refs_0_, bf16[32,3456]{1,0:T(8,128)(2,1)S(1)} %collective-permute-done.4.refs_1_, bf16[32,3456]{1,0:T(8,128)(2,1)S(1)} %collective-permute-done.5.refs_2_, ...), custom_call_target="tpu_custom_call" | custom-call | flops 1 | bytes 1 | tf_op jit(solution)/shard_map/prepare_other/pallas_call | solution.py:96
  41.8 1.1 %prepare_own.5.refs_2_ = bf16[2,32,9216]{2,1,0:T(8,128)(2,1)S(1)} custom-call(s32[2,288]{1,0:T(2,128)S(1)} %copy-done.2, bf16[32,3456]{1,0:T(8,128)(2,1)S(1)} %collective-permute-done.3.refs_0_, bf16[32,3456]{1,0:T(8,128)(2,1)S(1)} %collective-permute-done.4.refs_1_, bf16[32,3456]{1,0:T(8,128)(2,1)S(1)} %collective-permute-done.5.refs_2_, ...), custom_call_target="tpu_custom_call" | custom-call | flops 1 | bytes 1 | tf_op jit(solution)/shard_map/prepare_own/pallas_call | solution.py:96
  42.8 0.0 collective-permute-done.16.refs_3_
  42.9 1.1 %prepare_other.7 = bf16[2,32,9216]{2,1,0:T(8,128)(2,1)S(1)} custom-call(s32[2,288]{1,0:T(2,128)S(1)} %copy-done.2, bf16[32,3456]{1,0:T(8,128)(2,1)S(1)} %collective-permute-done.6.refs_0_, bf16[32,3456]{1,0:T(8,128)(2,1)S(1)} %collective-permute-done.7.refs_1_, bf16[32,3456]{1,0:T(8,128)(2,1)S(1)} %collective-permute-done.8.refs_2_, ...), custom_call_target="tpu_custom_call" | custom-call | flops 1 | bytes 1 | tf_op jit(solution)/shard_map/prepare_other/pallas_call | solution.py:96
  43.9 0.6 collective-permute-start.17
  44.5 0.0 collective-permute-done.14.refs_3_
  44.5 0.7 collective-permute-done.13.refs_2_
  45.2 1.0 %prepare_other.6 = bf16[2,32,9216]{2,1,0:T(8,128)(2,1)S(1)} custom-call(s32[2,288]{1,0:T(2,128)S(1)} %copy-done.2, bf16[32,3456]{1,0:T(8,128)(2,1)S(1)} %collective-permute-done.2.refs_0_, bf16[32,3456]{1,0:T(8,128)(2,1)S(1)} %collective-permute-done.12.refs_1_, bf16[32,3456]{1,0:T(8,128)(2,1)S(1)} %collective-permute-done.13.refs_2_, ...), custom_call_target="tpu_custom_call" | custom-call | flops 1 | bytes 1 | tf_op jit(solution)/shard_map/prepare_other/pallas_call | solution.py:96
  46.2 0.1 collective-permute-start.15
  46.3 0.5 collective-permute-start.11
  46.8 1.0 %prepare_own.6.refs_4_ = bf16[2,32,9216]{2,1,0:T(8,128)(2,1)S(1)} custom-call(s32[2,288]{1,0:T(2,128)S(1)} %copy-done.2, bf16[32,3456]{1,0:T(8,128)(2,1)S(1)} %collective-permute-done.2.refs_0_, bf16[32,3456]{1,0:T(8,128)(2,1)S(1)} %collective-permute-done.12.refs_1_, bf16[32,3456]{1,0:T(8,128)(2,1)S(1)} %collective-permute-done.13.refs_2_, ...), custom_call_target="tpu_custom_call" | custom-call | flops 1 | bytes 1 | tf_op jit(solution)/shard_map/prepare_own/pallas_call | solution.py:96
  47.9 1.1 %prepare_own.7.refs_6_ = bf16[2,32,9216]{2,1,0:T(8,128)(2,1)S(1)} custom-call(s32[2,288]{1,0:T(2,128)S(1)} %copy-done.2, bf16[32,3456]{1,0:T(8,128)(2,1)S(1)} %collective-permute-done.6.refs_0_, bf16[32,3456]{1,0:T(8,128)(2,1)S(1)} %collective-permute-done.7.refs_1_, bf16[32,3456]{1,0:T(8,128)(2,1)S(1)} %collective-permute-done.8.refs_2_, ...), custom_call_target="tpu_custom_call" | custom-call | flops 1 | bytes 1 | tf_op jit(solution)/shard_map/prepare_own/pallas_call | solution.py:96
  48.9 0.0 collective-permute-done.9.refs_1_
  49.0 0.2 collective-permute-done.15.refs_5_
  49.2 1.7 %collective-permute-done.11.refs_3_ = bf16[2,32,9216]{2,1,0:T(8,128)(2,1)S(1)} collective-permute-done((bf16[2,32,9216]{2,1,0:T(8,128)(2,1)S(1)}, bf16[2,32,9216]{2,1,0:T(8,128)(2,1)S(1)}, u32[]{:S(2)}, u32[]{:S(2)}) %collective-permute-start.11) | collective-permute-done | bytes 1179680 | tf_op jit(solution)/shard_map/ppermute | solution.py:262
  50.8 13.2 %products.3 = (f32[5,64,256]{2,1,0:T(8,128)S(1)}, bf16[5,64,256]{2,1,0:T(8,128)(2,1)S(1)}, bf16[5,64,256]{2,1,0:T(8,128)(2,1)S(1)}, bf16[5,64,256]{2,1,0:T(8,128)(2,1)S(1)}) custom-call(bf16[9,16,9216]{2,1,0:T(8,128)(2,1)S(1)} %band_matrices.1.x_ref, bf16[2,32,9216]{2,1,0:T(8,128)(2,1)S(1)} %prepare_own.4._.refs_0_, ...), custom_call_target="tpu_custom_call" | custom-call | flops 12079595520 | bytes 9437184 | tf_op jit(solution)/shard_map/products/pallas_call | solution.py:149
  64.0 2.1 %collective-permute-start.18 = (bf16[5,64,256]{2,1,0:T(8,128)(2,1)S(1)}, bf16[5,64,256]{2,1,0:T(8,128)(2,1)S(1)}, u32[]{:S(2)}, u32[]{:S(2)}) collective-permute-start(bf16[5,64,256]{2,1,0:T(8,128)(2,1)S(1)} %get-tuple-element.75), channel_id=1, source_target_pairs={{0,2},{1,3},{2,4},{3,5},{4,6},{5,7},{6,0},{7,1},{8,10},{9,11},{10,... | collective-permute-start | bytes 491528 | tf_op jit(solution)/shard_map/ppermute | solution.py:262
  66.2 3.4 %collective-permute-start.19 = (bf16[5,64,256]{2,1,0:T(8,128)(2,1)S(1)}, bf16[5,64,256]{2,1,0:T(8,128)(2,1)S(1)}, u32[]{:S(2)}, u32[]{:S(2)}) collective-permute-start(bf16[5,64,256]{2,1,0:T(8,128)(2,1)S(1)} %get-tuple-element.76), channel_id=1, source_target_pairs={{0,4},{1,5},{2,6},{3,7},{4,0},{5,1},{6,2},{7,3},{8,12},{9,13},{10,... | collective-permute-start | bytes 491528 | tf_op jit(solution)/shard_map/ppermute | solution.py:262
  69.6 0.0 collective-permute-start.20
  69.6 8.0 %products.4 = (f32[3,64,256]{2,1,0:T(8,128)S(1)}, bf16[3,64,256]{2,1,0:T(8,128)(2,1)S(1)}, bf16[3,64,256]{2,1,0:T(8,128)(2,1)S(1)}, bf16[3,64,256]{2,1,0:T(8,128)(2,1)S(1)}) custom-call(bf16[9,16,9216]{2,1,0:T(8,128)(2,1)S(1)} %band_matrices.1.x_ref, bf16[2,32,9216]{2,1,0:T(8,128)(2,1)S(1)} %prepare_own.4._.refs_0_, ...), custom_call_target="tpu_custom_call" | custom-call | flops 7247757312 | bytes 9437184 | tf_op jit(solution)/shard_map/products/pallas_call | solution.py:149
  77.5 2.1 %collective-permute-start.21 = (bf16[3,64,256]{2,1,0:T(8,128)(2,1)S(1)}, bf16[3,64,256]{2,1,0:T(8,128)(2,1)S(1)}, u32[]{:S(2)}, u32[]{:S(2)}) collective-permute-start(bf16[3,64,256]{2,1,0:T(8,128)(2,1)S(1)} %get-tuple-element.90), channel_id=1, source_target_pairs={{0,2},{1,3},{2,4},{3,5},{4,6},{5,7},{6,0},{7,1},{8,10},{9,11},{10,... | collective-permute-start | bytes 294920 | tf_op jit(solution)/shard_map/ppermute | solution.py:262
  79.6 0.0 collective-permute-start.22
  79.6 0.0 collective-permute-done.18
  79.6 2.4 %collective-permute-start.23 = (bf16[3,64,256]{2,1,0:T(8,128)(2,1)S(1)}, bf16[3,64,256]{2,1,0:T(8,128)(2,1)S(1)}, u32[]{:S(2)}, u32[]{:S(2)}) collective-permute-start(bf16[3,64,256]{2,1,0:T(8,128)(2,1)S(1)} %get-tuple-element.92), channel_id=1, source_target_pairs={{0,6},{1,7},{2,0},{3,1},{4,2},{5,3},{6,4},{7,5},{8,14},{9,15},{10,... | collective-permute-start | bytes 294920 | tf_op jit(solution)/shard_map/ppermute | solution.py:262
  82.1 0.1 convert_add_fusion
  82.2 3.0 %products.5 = (f32[1,64,256]{2,1,0:T(8,128)S(1)}, bf16[1,64,256]{2,1,0:T(8,128)(2,1)S(1)}, bf16[1,64,256]{2,1,0:T(8,128)(2,1)S(1)}, bf16[1,64,256]{2,1,0:T(8,128)(2,1)S(1)}) custom-call(bf16[9,16,9216]{2,1,0:T(8,128)(2,1)S(1)} %band_matrices.1.x_ref, bf16[2,32,9216]{2,1,0:T(8,128)(2,1)S(1)} %prepare_own.4._.refs_0_, ...), custom_call_target="tpu_custom_call" | custom-call | flops 2415919104 | bytes 9437184 | tf_op jit(solution)/shard_map/products/pallas_call | solution.py:149
  85.2 6.9 %collective-permute-start.24 = (bf16[1,64,256]{2,1,0:T(8,128)(2,1)S(1)}, bf16[1,64,256]{2,1,0:T(8,128)(2,1)S(1)}, u32[]{:S(2)}, u32[]{:S(2)}) collective-permute-start(bf16[1,64,256]{2,1,0:T(8,128)(2,1)S(1)} %get-tuple-element.98), channel_id=1, source_target_pairs={{0,2},{1,3},{2,4},{3,5},{4,6},{5,7},{6,0},{7,1},{8,10},{9,11},{10,... | collective-permute-start | bytes 98312 | tf_op jit(solution)/shard_map/ppermute | solution.py:262
  92.1 2.4 %collective-permute-start.26 = (bf16[1,64,256]{2,1,0:T(8,128)(2,1)S(1)}, bf16[1,64,256]{2,1,0:T(8,128)(2,1)S(1)}, u32[]{:S(2)}, u32[]{:S(2)}) collective-permute-start(bf16[1,64,256]{2,1,0:T(8,128)(2,1)S(1)} %get-tuple-element.100), channel_id=1, source_target_pairs={{0,6},{1,7},{2,0},{3,1},{4,2},{5,3},{6,4},{7,5},{8,14},{9,15},{10,... | collective-permute-start | bytes 98312 | tf_op jit(solution)/shard_map/ppermute | solution.py:262
  94.5 0.0 collective-permute-done.22
  94.5 0.0 collective-permute-done.23
  94.6 0.1 collective-permute-start.28
  94.7 0.5 collective-permute-start.27
  95.2 0.0 collective-permute-done.24
  95.2 1.7 %collective-permute-done.25 = bf16[1,64,256]{2,1,0:T(8,128)(2,1)S(1)} collective-permute-done((bf16[1,64,256]{2,1,0:T(8,128)(2,1)S(1)}, bf16[1,64,256]{2,1,0:T(8,128)(2,1)S(1)}, u32[]{:S(2)}, u32[]{:S(2)}) %collective-permute-start.25) | collective-permute-done | bytes 32800 | tf_op jit(solution)/shard_map/ppermute | solution.py:262
  96.9 0.1 collective-permute-start.29
  97.0 1.2 %collective-permute-done.29 = f32[1,32,256]{2,1,0:T(8,128)S(1)} collective-permute-done((f32[1,32,256]{2,1,0:T(8,128)S(1)}, f32[1,32,256]{2,1,0:T(8,128)S(1)}, u32[]{:S(2)}, u32[]{:S(2)}) %collective-permute-start.29) | collective-permute-done | bytes 32800 | tf_op jit(solution)/shard_map/ppermute | solution.py:262
  98.2 0.9 maximum_select_fusion
  (28 shorter events, 0.2 us)
Async XLA Ops:
  0.0 8.2 %copy-start.1 = (bf16[2,9,32,288]{3,2,1,0:T(8,128)(2,1)S(1)}, bf16[2,9,32,288]{3,2,1,0:T(8,128)(2,1)}, u32[]{:S(2)}) copy-start(bf16[2,9,32,288]{3,2,1,0:T(8,128)(2,1)} %coupling_ref.3) | copy-start | bytes 995332
  0.0 12.1 %copy-start.2 = (s32[2,288]{1,0:T(2,128)S(1)}, s32[2,288]{1,0:T(2,128)}, u32[]{:S(2)}) copy-start(s32[2,288]{1,0:T(2,128)} %kq_ref.17) | copy-start | bytes 6916
  3.0 5.2 %collective-permute-start = (bf16[9,32,288]{2,1,0:T(8,128)(2,1)}, bf16[9,32,288]{2,1,0:T(8,128)(2,1)S(1)}, u32[]{:S(2)}, u32[]{:S(2)}) collective-permute-start(bf16[9,32,288]{2,1,0:T(8,128)(2,1)} %get-tuple-element.55), channel_id=1, source_target_pairs={{0,1},{1,0},{2,3},{3,2},{4,5},{5,4},{6,7},{7,6},{8,9},{9,8},{10,11... | collective-permute-start | bytes 497672 | tf_op jit(solution)/shard_map/ppermute | solution.py:262
  3.5 10.8 %collective-permute-start.3 = (bf16[32,3456]{1,0:T(8,128)(2,1)}, bf16[32,3456]{1,0:T(8,128)(2,1)S(1)}, u32[]{:S(2)}, u32[]{:S(2)}) collective-permute-start(bf16[32,3456]{1,0:T(8,128)(2,1)} %get-tuple-element.58), channel_id=1, source_target_pairs={{0,6},{1,7},{2,0},{3,1},{4,2},{5,3},{6,4},{7,5},{8,14},{9,15},{10,... | collective-permute-start | bytes 663560 | tf_op jit(solution)/shard_map/ppermute | solution.py:262
  8.2 11.6 %collective-permute-start.6 = (bf16[32,3456]{1,0:T(8,128)(2,1)}, bf16[32,3456]{1,0:T(8,128)(2,1)S(1)}, u32[]{:S(2)}, u32[]{:S(2)}) collective-permute-start(bf16[32,3456]{1,0:T(8,128)(2,1)} %get-tuple-element.60), channel_id=1, source_target_pairs={{0,2},{1,3},{2,4},{3,5},{4,6},{5,7},{6,0},{7,1},{8,10},{9,11},{10,... | collective-permute-start | bytes 663560 | tf_op jit(solution)/shard_map/ppermute | solution.py:262
  8.3 15.5 %collective-permute-start.1 = (bf16[9,32,288]{2,1,0:T(8,128)(2,1)S(1)}, bf16[9,32,288]{2,1,0:T(8,128)(2,1)S(1)}, u32[]{:S(2)}, u32[]{:S(2)}) collective-permute-start(bf16[9,32,288]{2,1,0:T(8,128)(2,1)S(1)} %bitcast_select_fusion), channel_id=1, source_target_pairs={{0,6},{1,7},{2,0},{3,1},{4,2},{5,3},{6,4},{7,5},{8,14},{9,15},{10,... | collective-permute-start | bytes 497672 | tf_op jit(solution)/shard_map/ppermute | solution.py:262
  12.1 1.2 %copy-start = (bf16[32,13824]{1,0:T(8,128)(2,1)S(1)}, bf16[32,13824]{1,0:T(8,128)(2,1)}, u32[]{:S(2)}) copy-start(bf16[32,13824]{1,0:T(8,128)(2,1)} %get-tuple-element.54.refs_0_) | copy-start | bytes 2654212
  14.3 7.1 %copy-start.3 = (bf16[32,3456]{1,0:T(8,128)(2,1)S(1)}, bf16[32,3456]{1,0:T(8,128)(2,1)}, u32[]{:S(2)}) copy-start(bf16[32,3456]{1,0:T(8,128)(2,1)} %get-tuple-element.57) | copy-start | bytes 663556
  14.3 10.9 %collective-permute-start.4 = (bf16[32,3456]{1,0:T(8,128)(2,1)S(1)}, bf16[32,3456]{1,0:T(8,128)(2,1)S(1)}, u32[]{:S(2)}, u32[]{:S(2)}) collective-permute-start(bf16[32,3456]{1,0:T(8,128)(2,1)S(1)} %collective-permute-done.3.refs_0_), channel_id=1, source_target_pairs={{0,8},{1,17},{2,10},{3,19},{4,12},{5,21},{6,14},{7,23},{8,0},{9,25... | collective-permute-start | bytes 663560 | tf_op jit(solution)/shard_map/ppermute | solution.py:262
  19.8 8.2 %collective-permute-start.7 = (bf16[32,3456]{1,0:T(8,128)(2,1)S(1)}, bf16[32,3456]{1,0:T(8,128)(2,1)S(1)}, u32[]{:S(2)}, u32[]{:S(2)}) collective-permute-start(bf16[32,3456]{1,0:T(8,128)(2,1)S(1)} %collective-permute-done.6.refs_0_), channel_id=1, source_target_pairs={{0,8},{1,17},{2,10},{3,19},{4,12},{5,21},{6,14},{7,23},{8,0},{9,25... | collective-permute-start | bytes 663560 | tf_op jit(solution)/shard_map/ppermute | solution.py:262
  21.3 11.9 %collective-permute-start.2 = (bf16[32,3456]{1,0:T(8,128)(2,1)S(1)}, bf16[32,3456]{1,0:T(8,128)(2,1)S(1)}, u32[]{:S(2)}, u32[]{:S(2)}) collective-permute-start(bf16[32,3456]{1,0:T(8,128)(2,1)S(1)} %copy-done.3), channel_id=1, source_target_pairs={{0,4},{1,5},{2,6},{3,7},{4,0},{5,1},{6,2},{7,3},{8,12},{9,13},{10,... | collective-permute-start | bytes 663560 | tf_op jit(solution)/shard_map/ppermute | solution.py:262
  21.6 11.7 %collective-permute-start.5 = (bf16[32,3456]{1,0:T(8,128)(2,1)S(1)}, bf16[32,3456]{1,0:T(8,128)(2,1)S(1)}, u32[]{:S(2)}, u32[]{:S(2)}) collective-permute-start(bf16[32,3456]{1,0:T(8,128)(2,1)S(1)} %collective-permute-done.3.refs_0_), channel_id=1, source_target_pairs={{0,16},{1,9},{2,18},{3,11},{4,20},{5,13},{6,22},{7,15},{8,24},{9,1... | collective-permute-start | bytes 663560 | tf_op jit(solution)/shard_map/ppermute | solution.py:262
  23.7 9.6 %collective-permute-start.8 = (bf16[32,3456]{1,0:T(8,128)(2,1)S(1)}, bf16[32,3456]{1,0:T(8,128)(2,1)S(1)}, u32[]{:S(2)}, u32[]{:S(2)}) collective-permute-start(bf16[32,3456]{1,0:T(8,128)(2,1)S(1)} %collective-permute-done.6.refs_0_), channel_id=1, source_target_pairs={{0,16},{1,9},{2,18},{3,11},{4,20},{5,13},{6,22},{7,15},{8,24},{9,1... | collective-permute-start | bytes 663560 | tf_op jit(solution)/shard_map/ppermute | solution.py:262
  25.2 15.4 %collective-permute-start.10 = (bf16[32,3456]{1,0:T(8,128)(2,1)S(1)}, bf16[32,3456]{1,0:T(8,128)(2,1)S(1)}, u32[]{:S(2)}, u32[]{:S(2)}) collective-permute-start(bf16[32,3456]{1,0:T(8,128)(2,1)S(1)} %collective-permute-done.4.refs_1_), channel_id=1, source_target_pairs={{0,16},{1,9},{2,18},{3,11},{4,20},{5,13},{6,22},{7,15},{8,24},{9,1... | collective-permute-start | bytes 663560 | tf_op jit(solution)/shard_map/ppermute | solution.py:262
  28.1 14.8 %collective-permute-start.16 = (bf16[32,3456]{1,0:T(8,128)(2,1)S(1)}, bf16[32,3456]{1,0:T(8,128)(2,1)S(1)}, u32[]{:S(2)}, u32[]{:S(2)}) collective-permute-start(bf16[32,3456]{1,0:T(8,128)(2,1)S(1)} %collective-permute-done.7.refs_1_), channel_id=1, source_target_pairs={{0,16},{1,9},{2,18},{3,11},{4,20},{5,13},{6,22},{7,15},{8,24},{9,1... | collective-permute-start | bytes 663560 | tf_op jit(solution)/shard_map/ppermute | solution.py:262
  33.3 11.2 %collective-permute-start.14 = (bf16[32,3456]{1,0:T(8,128)(2,1)S(1)}, bf16[32,3456]{1,0:T(8,128)(2,1)S(1)}, u32[]{:S(2)}, u32[]{:S(2)}) collective-permute-start(bf16[32,3456]{1,0:T(8,128)(2,1)S(1)} %collective-permute-done.2.refs_0_), channel_id=1, source_target_pairs={{0,24},{1,25},{2,26},{3,27},{4,28},{5,29},{6,30},{7,31},{8,16},{9,... | collective-permute-start | bytes 663560 | tf_op jit(solution)/shard_map/ppermute | solution.py:262
  35.0 10.2 %collective-permute-start.13 = (bf16[32,3456]{1,0:T(8,128)(2,1)S(1)}, bf16[32,3456]{1,0:T(8,128)(2,1)S(1)}, u32[]{:S(2)}, u32[]{:S(2)}) collective-permute-start(bf16[32,3456]{1,0:T(8,128)(2,1)S(1)} %collective-permute-done.2.refs_0_), channel_id=1, source_target_pairs={{0,16},{1,17},{2,18},{3,19},{4,20},{5,21},{6,22},{7,23},{8,24},{9,... | collective-permute-start | bytes 663560 | tf_op jit(solution)/shard_map/ppermute | solution.py:262
  36.2 9.0 %collective-permute-start.12 = (bf16[32,3456]{1,0:T(8,128)(2,1)S(1)}, bf16[32,3456]{1,0:T(8,128)(2,1)S(1)}, u32[]{:S(2)}, u32[]{:S(2)}) collective-permute-start(bf16[32,3456]{1,0:T(8,128)(2,1)S(1)} %collective-permute-done.2.refs_0_), channel_id=1, source_target_pairs={{0,8},{1,9},{2,10},{3,11},{4,12},{5,13},{6,14},{7,15},{8,0},{9,1},... | collective-permute-start | bytes 663560 | tf_op jit(solution)/shard_map/ppermute | solution.py:262
  40.6 8.3 %collective-permute-start.9 = (bf16[2,32,9216]{2,1,0:T(8,128)(2,1)S(1)}, bf16[2,32,9216]{2,1,0:T(8,128)(2,1)S(1)}, u32[]{:S(2)}, u32[]{:S(2)}) collective-permute-start(bf16[2,32,9216]{2,1,0:T(8,128)(2,1)S(1)} %prepare_other.4), channel_id=1, source_target_pairs={{0,1},{1,0},{2,3},{3,2},{4,5},{5,4},{6,7},{7,6},{8,9},{9,8},{10,11... | collective-permute-start | bytes 3538952 | tf_op jit(solution)/shard_map/ppermute | solution.py:262
  43.9 5.0 %collective-permute-start.17 = (bf16[2,32,9216]{2,1,0:T(8,128)(2,1)S(1)}, bf16[2,32,9216]{2,1,0:T(8,128)(2,1)S(1)}, u32[]{:S(2)}, u32[]{:S(2)}) collective-permute-start(bf16[2,32,9216]{2,1,0:T(8,128)(2,1)S(1)} %prepare_other.7), channel_id=1, source_target_pairs={{0,1},{1,0},{2,3},{3,2},{4,5},{5,4},{6,7},{7,6},{8,9},{9,8},{10,11... | collective-permute-start | bytes 3538952 | tf_op jit(solution)/shard_map/ppermute | solution.py:262
  46.2 2.9 %collective-permute-start.15 = (bf16[2,32,9216]{2,1,0:T(8,128)(2,1)S(1)}, bf16[2,32,9216]{2,1,0:T(8,128)(2,1)S(1)}, u32[]{:S(2)}, u32[]{:S(2)}) collective-permute-start(bf16[2,32,9216]{2,1,0:T(8,128)(2,1)S(1)} %prepare_other.6), channel_id=1, source_target_pairs={{0,1},{1,0},{2,3},{3,2},{4,5},{5,4},{6,7},{7,6},{8,9},{9,8},{10,11... | collective-permute-start | bytes 3538952 | tf_op jit(solution)/shard_map/ppermute | solution.py:262
  46.3 4.5 %collective-permute-start.11 = (bf16[2,32,9216]{2,1,0:T(8,128)(2,1)S(1)}, bf16[2,32,9216]{2,1,0:T(8,128)(2,1)S(1)}, u32[]{:S(2)}, u32[]{:S(2)}) collective-permute-start(bf16[2,32,9216]{2,1,0:T(8,128)(2,1)S(1)} %prepare_other.5), channel_id=1, source_target_pairs={{0,1},{1,0},{2,3},{3,2},{4,5},{5,4},{6,7},{7,6},{8,9},{9,8},{10,11... | collective-permute-start | bytes 3538952 | tf_op jit(solution)/shard_map/ppermute | solution.py:262
  64.0 15.6 %collective-permute-start.18 = (bf16[5,64,256]{2,1,0:T(8,128)(2,1)S(1)}, bf16[5,64,256]{2,1,0:T(8,128)(2,1)S(1)}, u32[]{:S(2)}, u32[]{:S(2)}) collective-permute-start(bf16[5,64,256]{2,1,0:T(8,128)(2,1)S(1)} %get-tuple-element.75), channel_id=1, source_target_pairs={{0,2},{1,3},{2,4},{3,5},{4,6},{5,7},{6,0},{7,1},{8,10},{9,11},{10,... | collective-permute-start | bytes 491528 | tf_op jit(solution)/shard_map/ppermute | solution.py:262
  66.2 15.9 %collective-permute-start.19 = (bf16[5,64,256]{2,1,0:T(8,128)(2,1)S(1)}, bf16[5,64,256]{2,1,0:T(8,128)(2,1)S(1)}, u32[]{:S(2)}, u32[]{:S(2)}) collective-permute-start(bf16[5,64,256]{2,1,0:T(8,128)(2,1)S(1)} %get-tuple-element.76), channel_id=1, source_target_pairs={{0,4},{1,5},{2,6},{3,7},{4,0},{5,1},{6,2},{7,3},{8,12},{9,13},{10,... | collective-permute-start | bytes 491528 | tf_op jit(solution)/shard_map/ppermute | solution.py:262
  69.6 12.5 %collective-permute-start.20 = (bf16[5,64,256]{2,1,0:T(8,128)(2,1)S(1)}, bf16[5,64,256]{2,1,0:T(8,128)(2,1)S(1)}, u32[]{:S(2)}, u32[]{:S(2)}) collective-permute-start(bf16[5,64,256]{2,1,0:T(8,128)(2,1)S(1)} %get-tuple-element.77), channel_id=1, source_target_pairs={{0,6},{1,7},{2,0},{3,1},{4,2},{5,3},{6,4},{7,5},{8,14},{9,15},{10,... | collective-permute-start | bytes 491528 | tf_op jit(solution)/shard_map/ppermute | solution.py:262
  77.5 14.5 %collective-permute-start.21 = (bf16[3,64,256]{2,1,0:T(8,128)(2,1)S(1)}, bf16[3,64,256]{2,1,0:T(8,128)(2,1)S(1)}, u32[]{:S(2)}, u32[]{:S(2)}) collective-permute-start(bf16[3,64,256]{2,1,0:T(8,128)(2,1)S(1)} %get-tuple-element.90), channel_id=1, source_target_pairs={{0,2},{1,3},{2,4},{3,5},{4,6},{5,7},{6,0},{7,1},{8,10},{9,11},{10,... | collective-permute-start | bytes 294920 | tf_op jit(solution)/shard_map/ppermute | solution.py:262
  79.6 14.9 %collective-permute-start.22 = (bf16[3,64,256]{2,1,0:T(8,128)(2,1)S(1)}, bf16[3,64,256]{2,1,0:T(8,128)(2,1)S(1)}, u32[]{:S(2)}, u32[]{:S(2)}) collective-permute-start(bf16[3,64,256]{2,1,0:T(8,128)(2,1)S(1)} %get-tuple-element.91), channel_id=1, source_target_pairs={{0,4},{1,5},{2,6},{3,7},{4,0},{5,1},{6,2},{7,3},{8,12},{9,13},{10,... | collective-permute-start | bytes 294920 | tf_op jit(solution)/shard_map/ppermute | solution.py:262
  79.6 14.9 %collective-permute-start.23 = (bf16[3,64,256]{2,1,0:T(8,128)(2,1)S(1)}, bf16[3,64,256]{2,1,0:T(8,128)(2,1)S(1)}, u32[]{:S(2)}, u32[]{:S(2)}) collective-permute-start(bf16[3,64,256]{2,1,0:T(8,128)(2,1)S(1)} %get-tuple-element.92), channel_id=1, source_target_pairs={{0,6},{1,7},{2,0},{3,1},{4,2},{5,3},{6,4},{7,5},{8,14},{9,15},{10,... | collective-permute-start | bytes 294920 | tf_op jit(solution)/shard_map/ppermute | solution.py:262
  85.2 10.0 %collective-permute-start.24 = (bf16[1,64,256]{2,1,0:T(8,128)(2,1)S(1)}, bf16[1,64,256]{2,1,0:T(8,128)(2,1)S(1)}, u32[]{:S(2)}, u32[]{:S(2)}) collective-permute-start(bf16[1,64,256]{2,1,0:T(8,128)(2,1)S(1)} %get-tuple-element.98), channel_id=1, source_target_pairs={{0,2},{1,3},{2,4},{3,5},{4,6},{5,7},{6,0},{7,1},{8,10},{9,11},{10,... | collective-permute-start | bytes 98312 | tf_op jit(solution)/shard_map/ppermute | solution.py:262
  92.1 4.8 %collective-permute-start.25 = (bf16[1,64,256]{2,1,0:T(8,128)(2,1)S(1)}, bf16[1,64,256]{2,1,0:T(8,128)(2,1)S(1)}, u32[]{:S(2)}, u32[]{:S(2)}) collective-permute-start(bf16[1,64,256]{2,1,0:T(8,128)(2,1)S(1)} %get-tuple-element.99), channel_id=1, source_target_pairs={{0,4},{1,5},{2,6},{3,7},{4,0},{5,1},{6,2},{7,3},{8,12},{9,13},{10,... | collective-permute-start | bytes 98312 | tf_op jit(solution)/shard_map/ppermute | solution.py:262
  92.1 4.8 %collective-permute-start.26 = (bf16[1,64,256]{2,1,0:T(8,128)(2,1)S(1)}, bf16[1,64,256]{2,1,0:T(8,128)(2,1)S(1)}, u32[]{:S(2)}, u32[]{:S(2)}) collective-permute-start(bf16[1,64,256]{2,1,0:T(8,128)(2,1)S(1)} %get-tuple-element.100), channel_id=1, source_target_pairs={{0,6},{1,7},{2,0},{3,1},{4,2},{5,3},{6,4},{7,5},{8,14},{9,15},{10,... | collective-permute-start | bytes 98312 | tf_op jit(solution)/shard_map/ppermute | solution.py:262
  94.6 3.6 %collective-permute-start.28 = (f32[3,32,256]{2,1,0:T(8,128)S(1)}, f32[3,32,256]{2,1,0:T(8,128)S(1)}, u32[]{:S(2)}, u32[]{:S(2)}) collective-permute-start(f32[3,32,256]{2,1,0:T(8,128)S(1)} %get-tuple-element.104), channel_id=1, source_target_pairs={{0,1},{1,0},{2,3},{3,2},{4,5},{5,4},{6,7},{7,6},{8,9},{9,8},{10,11... | collective-permute-start | bytes 294920 | tf_op jit(solution)/shard_map/ppermute | solution.py:262
  94.7 3.5 %collective-permute-start.27 = (f32[5,32,256]{2,1,0:T(8,128)S(1)}, f32[5,32,256]{2,1,0:T(8,128)S(1)}, u32[]{:S(2)}, u32[]{:S(2)}) collective-permute-start(f32[5,32,256]{2,1,0:T(8,128)S(1)} %get-tuple-element.102), channel_id=1, source_target_pairs={{0,1},{1,0},{2,3},{3,2},{4,5},{5,4},{6,7},{7,6},{8,9},{9,8},{10,11... | collective-permute-start | bytes 491528 | tf_op jit(solution)/shard_map/ppermute | solution.py:262
  96.9 1.3 %collective-permute-start.29 = (f32[1,32,256]{2,1,0:T(8,128)S(1)}, f32[1,32,256]{2,1,0:T(8,128)S(1)}, u32[]{:S(2)}, u32[]{:S(2)}) collective-permute-start(f32[1,32,256]{2,1,0:T(8,128)S(1)} %get-tuple-element.106), channel_id=1, source_target_pairs={{0,1},{1,0},{2,3},{3,2},{4,5},{5,4},{6,7},{7,6},{8,9},{9,8},{10,11... | collective-permute-start | bytes 98312 | tf_op jit(solution)/shard_map/ppermute | solution.py:262

commit v9 on v8

--- a/solution.py
+++ b/solution.py
@@ -11,7 +11,7 @@
 KY = 96
 BANDS = 16
 LINE = KY * BANDS
-GROUPS = (5, 8)
+GROUPS = (4, 8)
 F32 = jnp.float32
 SMALL = pl.CostEstimate(flops=1, bytes_accessed=1, transcendentals=0)
 BF16 = jnp.bfloat16

time: 99.3 us -> 97.2 us (0.979)
  starting transfers between devices: 41.8 us -> 36.9 us
  waiting for transfers between devices: 15.4 us -> 18.4 us
    ppermute x30, starting transfers between devices: 41.8 us -> 36.9 us  [permute(): return lax.ppermute(x, ('pb', 'ka'), pairs)]
    ppermute x30, waiting for transfers between devices: 15.4 us -> 18.4 us  [permute(): return lax.ppermute(x, ('pb', 'ka'), pairs)]
  transfers between devices with their start and end apart: 30 -> 30, of which waited for: 9 -> 10; matrix products, arithmetic and copies ran while one was open for 0% -> 0% of each run, Pallas kernels for 23% -> 26%
where the time goes in v9:
time: 97.2 us; the launch traced here: 97 us
  Pallas kernels  39.2 us (40%)
  starting transfers between devices  36.9 us (38%)
  waiting for transfers between devices  18.4 us (19%)
  local copies, waits for them, and re-layouts  1.22 us (1%)
  other arithmetic  1.08 us (1%)
    ppermute x30, starting transfers between devices, permute(): return lax.ppermute(x, ('pb', 'ka'), pairs)  36.9 us
    pallas_call x3, Pallas kernels, products(): pl.pallas_call(functools.partial(main_kernel, sources, first, branches, f...  24 us
    ppermute x30, waiting for transfers between devices, permute(): return lax.ppermute(x, ('pb', 'ka'), pairs)  18.4 us
    pallas_call x8, Pallas kernels, prepare(): pl.pallas_call(functools.partial(prep_kernel, block // LINE, lines_all, f...  8.31 us
    pallas_call x1, Pallas kernels, band_matrices(): pl.pallas_call(functools.partial(band_kernel, count // KY, lines_all), in...  3.73 us
    pallas_call x1, Pallas kernels, cut(): pl.pallas_call(functools.partial(cut_kernel, block), in_specs=[pl.BlockSp...  2.97 us
  transfers between devices with their start and end apart: 30, of which 10 were waited for; matrix products, arithmetic and copies ran while one was open for 0% of the time, Pallas kernels for 26%

profile of v9, /device:TPU:0, one launch (start us, length us, event | category | flops | bytes accessed | tf_op | source)
XLA Modules:
  0.0 97.0 jit_solution(5750352760843336019)
XLA Ops:
  0.0 3.0 %cut.1 = (bf16[32,3456]{1,0:T(8,128)(2,1)}, bf16[32,3456]{1,0:T(8,128)(2,1)}, bf16[32,3456]{1,0:T(8,128)(2,1)}, bf16[32,13824]{1,0:T(8,128)(2,1)}, bf16[9,32,288]{2,1,0:T(8,128)(2,1)}) custom-call(bf16[32,36864]{1,0:T(8,128)(2,1)} %env_ref.1, bf16[2,9,32,288]{3,2,1,0:T(8,128)(2,1)} %coupling_ref.3), custom_call_target="tpu_custom_call" | custom-call | flops 1 | bytes 1 | tf_op jit(solution)/shard_map/cut/pallas_call | solution.py:65
  3.0 0.5 collective-permute-start
  3.5 4.7 %collective-permute-start.3 = (bf16[32,3456]{1,0:T(8,128)(2,1)}, bf16[32,3456]{1,0:T(8,128)(2,1)S(1)}, u32[]{:S(2)}, u32[]{:S(2)}) collective-permute-start(bf16[32,3456]{1,0:T(8,128)(2,1)} %get-tuple-element.58), channel_id=1, source_target_pairs={{0,6},{1,7},{2,0},{3,1},{4,2},{5,3},{6,4},{7,5},{8,14},{9,15},{10,... | collective-permute-start | bytes 663560 | tf_op jit(solution)/shard_map/ppermute | solution.py:262
  8.2 0.0 collective-permute-start.6
  8.2 0.0 collective-permute-done.other_ref
  8.2 3.9 %collective-permute-start.1 = (bf16[9,32,288]{2,1,0:T(8,128)(2,1)S(1)}, bf16[9,32,288]{2,1,0:T(8,128)(2,1)S(1)}, u32[]{:S(2)}, u32[]{:S(2)}) collective-permute-start(bf16[9,32,288]{2,1,0:T(8,128)(2,1)S(1)} %bitcast_select_fusion), channel_id=1, source_target_pairs={{0,6},{1,7},{2,0},{3,1},{4,2},{5,3},{6,4},{7,5},{8,14},{9,15},{10,... | collective-permute-start | bytes 497672 | tf_op jit(solution)/shard_map/ppermute | solution.py:262
  12.1 1.2 %copy-done = bf16[32,13824]{1,0:T(8,128)(2,1)S(1)} copy-done((bf16[32,13824]{1,0:T(8,128)(2,1)S(1)}, bf16[32,13824]{1,0:T(8,128)(2,1)}, u32[]{:S(2)}) %copy-start) | copy-done | bytes 884760
  13.3 1.0 %prepare_other.4 = bf16[2,32,9216]{2,1,0:T(8,128)(2,1)S(1)} custom-call(s32[2,288]{1,0:T(2,128)S(1)} %copy-done.2, bf16[32,13824]{1,0:T(8,128)(2,1)S(1)} %copy-done), custom_call_target="tpu_custom_call" | custom-call | flops 1 | bytes 1 | tf_op jit(solution)/shard_map/prepare_other/pallas_call | solution.py:96
  14.3 0.0 collective-permute-done.3.refs_0_
  14.3 1.6 %collective-permute-start.4 = (bf16[32,3456]{1,0:T(8,128)(2,1)S(1)}, bf16[32,3456]{1,0:T(8,128)(2,1)S(1)}, u32[]{:S(2)}, u32[]{:S(2)}) collective-permute-start(bf16[32,3456]{1,0:T(8,128)(2,1)S(1)} %collective-permute-done.3.refs_0_), channel_id=1, source_target_pairs={{0,8},{1,17},{2,10},{3,19},{4,12},{5,21},{6,14},{7,23},{8,0},{9,25... | collective-permute-start | bytes 663560 | tf_op jit(solution)/shard_map/ppermute | solution.py:262
  15.9 1.0 %prepare_own.4._.refs_0_ = bf16[2,32,9216]{2,1,0:T(8,128)(2,1)S(1)} custom-call(s32[2,288]{1,0:T(2,128)S(1)} %copy-done.2, bf16[32,13824]{1,0:T(8,128)(2,1)S(1)} %copy-done), custom_call_target="tpu_custom_call" | custom-call | flops 1 | bytes 1 | tf_op jit(solution)/shard_map/prepare_own/pallas_call | solution.py:96
  16.9 3.0 %collective-permute-done.6.refs_0_ = bf16[32,3456]{1,0:T(8,128)(2,1)S(1)} collective-permute-done((bf16[32,3456]{1,0:T(8,128)(2,1)}, bf16[32,3456]{1,0:T(8,128)(2,1)S(1)}, u32[]{:S(2)}, u32[]{:S(2)}) %collective-permute-start.6) | collective-permute-done | bytes 221216 | tf_op jit(solution)/shard_map/ppermute | solution.py:262
  19.8 1.5 %collective-permute-start.7 = (bf16[32,3456]{1,0:T(8,128)(2,1)S(1)}, bf16[32,3456]{1,0:T(8,128)(2,1)S(1)}, u32[]{:S(2)}, u32[]{:S(2)}) collective-permute-start(bf16[32,3456]{1,0:T(8,128)(2,1)S(1)} %collective-permute-done.6.refs_0_), channel_id=1, source_target_pairs={{0,8},{1,17},{2,10},{3,19},{4,12},{5,21},{6,14},{7,23},{8,0},{9,25... | collective-permute-start | bytes 663560 | tf_op jit(solution)/shard_map/ppermute | solution.py:262
  21.3 0.2 collective-permute-start.2
  21.6 1.5 %collective-permute-start.5 = (bf16[32,3456]{1,0:T(8,128)(2,1)S(1)}, bf16[32,3456]{1,0:T(8,128)(2,1)S(1)}, u32[]{:S(2)}, u32[]{:S(2)}) collective-permute-start(bf16[32,3456]{1,0:T(8,128)(2,1)S(1)} %collective-permute-done.3.refs_0_), channel_id=1, source_target_pairs={{0,16},{1,9},{2,18},{3,11},{4,20},{5,13},{6,22},{7,15},{8,24},{9,1... | collective-permute-start | bytes 663560 | tf_op jit(solution)/shard_map/ppermute | solution.py:262
  23.1 0.6 collective-permute-done.1.next_ref
  23.7 1.5 %collective-permute-start.8 = (bf16[32,3456]{1,0:T(8,128)(2,1)S(1)}, bf16[32,3456]{1,0:T(8,128)(2,1)S(1)}, u32[]{:S(2)}, u32[]{:S(2)}) collective-permute-start(bf16[32,3456]{1,0:T(8,128)(2,1)S(1)} %collective-permute-done.6.refs_0_), channel_id=1, source_target_pairs={{0,16},{1,9},{2,18},{3,11},{4,20},{5,13},{6,22},{7,15},{8,24},{9,1... | collective-permute-start | bytes 663560 | tf_op jit(solution)/shard_map/ppermute | solution.py:262
  25.2 0.5 collective-permute-start.10
  25.7 2.3 %collective-permute-done.7.refs_1_ = bf16[32,3456]{1,0:T(8,128)(2,1)S(1)} collective-permute-done((bf16[32,3456]{1,0:T(8,128)(2,1)S(1)}, bf16[32,3456]{1,0:T(8,128)(2,1)S(1)}, u32[]{:S(2)}, u32[]{:S(2)}) %collective-permute-start.7) | collective-permute-done | bytes 221216 | tf_op jit(solution)/shard_map/ppermute | solution.py:262
  28.1 1.3 %collective-permute-start.16 = (bf16[32,3456]{1,0:T(8,128)(2,1)S(1)}, bf16[32,3456]{1,0:T(8,128)(2,1)S(1)}, u32[]{:S(2)}, u32[]{:S(2)}) collective-permute-start(bf16[32,3456]{1,0:T(8,128)(2,1)S(1)} %collective-permute-done.7.refs_1_), channel_id=1, source_target_pairs={{0,16},{1,9},{2,18},{3,11},{4,20},{5,13},{6,22},{7,15},{8,24},{9,1... | collective-permute-start | bytes 663560 | tf_op jit(solution)/shard_map/ppermute | solution.py:262
  29.3 3.9 %collective-permute-done.2.refs_0_ = bf16[32,3456]{1,0:T(8,128)(2,1)S(1)} collective-permute-done((bf16[32,3456]{1,0:T(8,128)(2,1)S(1)}, bf16[32,3456]{1,0:T(8,128)(2,1)S(1)}, u32[]{:S(2)}, u32[]{:S(2)}) %collective-permute-start.2) | collective-permute-done | bytes 221216 | tf_op jit(solution)/shard_map/ppermute | solution.py:262
  33.3 1.7 %collective-permute-start.14 = (bf16[32,3456]{1,0:T(8,128)(2,1)S(1)}, bf16[32,3456]{1,0:T(8,128)(2,1)S(1)}, u32[]{:S(2)}, u32[]{:S(2)}) collective-permute-start(bf16[32,3456]{1,0:T(8,128)(2,1)S(1)} %collective-permute-done.2.refs_0_), channel_id=1, source_target_pairs={{0,24},{1,25},{2,26},{3,27},{4,28},{5,29},{6,30},{7,31},{8,16},{9,... | collective-permute-start | bytes 663560 | tf_op jit(solution)/shard_map/ppermute | solution.py:262
  35.0 1.2 %collective-permute-start.13 = (bf16[32,3456]{1,0:T(8,128)(2,1)S(1)}, bf16[32,3456]{1,0:T(8,128)(2,1)S(1)}, u32[]{:S(2)}, u32[]{:S(2)}) collective-permute-start(bf16[32,3456]{1,0:T(8,128)(2,1)S(1)} %collective-permute-done.2.refs_0_), channel_id=1, source_target_pairs={{0,16},{1,17},{2,18},{3,19},{4,20},{5,21},{6,22},{7,23},{8,24},{9,... | collective-permute-start | bytes 663560 | tf_op jit(solution)/shard_map/ppermute | solution.py:262
  36.2 0.5 collective-permute-start.12
  36.8 0.1 spread.1
  36.9 3.7 %band_matrices.1.x_ref = bf16[9,16,9216]{2,1,0:T(8,128)(2,1)S(1)} custom-call(s32[2,288]{1,0:T(2,128)S(1)} %copy-done.2, bf16[2,256,1024]{2,1,0:T(8,128)(2,1)S(1)} %spread.1, bf16[2,9,32,288]{3,2,1,0:T(8,128)(2,1)S(1)} %copy-done.1, bf16[9,32,288]{2,1,0:T(8,128)(2,1)S(1)} %collective-permute-done.other_ref, ...), custom_call_target="tpu_custom_call" | custom-call | flops 1 | bytes 1 | tf_op jit(solution)/shard_map/band_matrices/pallas_call | solution.py:235
  40.6 0.1 collective-permute-start.9
  40.7 1.1 %prepare_other.5 = bf16[2,32,9216]{2,1,0:T(8,128)(2,1)S(1)} custom-call(s32[2,288]{1,0:T(2,128)S(1)} %copy-done.2, bf16[32,3456]{1,0:T(8,128)(2,1)S(1)} %collective-permute-done.3.refs_0_, bf16[32,3456]{1,0:T(8,128)(2,1)S(1)} %collective-permute-done.4.refs_1_, bf16[32,3456]{1,0:T(8,128)(2,1)S(1)} %collective-permute-done.5.refs_2_, ...), custom_call_target="tpu_custom_call" | custom-call | flops 1 | bytes 1 | tf_op jit(solution)/shard_map/prepare_other/pallas_call | solution.py:96
  41.8 1.1 %prepare_own.5.refs_2_ = bf16[2,32,9216]{2,1,0:T(8,128)(2,1)S(1)} custom-call(s32[2,288]{1,0:T(2,128)S(1)} %copy-done.2, bf16[32,3456]{1,0:T(8,128)(2,1)S(1)} %collective-permute-done.3.refs_0_, bf16[32,3456]{1,0:T(8,128)(2,1)S(1)} %collective-permute-done.4.refs_1_, bf16[32,3456]{1,0:T(8,128)(2,1)S(1)} %collective-permute-done.5.refs_2_, ...), custom_call_target="tpu_custom_call" | custom-call | flops 1 | bytes 1 | tf_op jit(solution)/shard_map/prepare_own/pallas_call | solution.py:96
  42.9 1.1 %prepare_other.7 = bf16[2,32,9216]{2,1,0:T(8,128)(2,1)S(1)} custom-call(s32[2,288]{1,0:T(2,128)S(1)} %copy-done.2, bf16[32,3456]{1,0:T(8,128)(2,1)S(1)} %collective-permute-done.6.refs_0_, bf16[32,3456]{1,0:T(8,128)(2,1)S(1)} %collective-permute-done.7.refs_1_, bf16[32,3456]{1,0:T(8,128)(2,1)S(1)} %collective-permute-done.8.refs_2_, ...), custom_call_target="tpu_custom_call" | custom-call | flops 1 | bytes 1 | tf_op jit(solution)/shard_map/prepare_other/pallas_call | solution.py:96
  43.9 0.6 collective-permute-start.17
  44.5 0.0 collective-permute-done.14.refs_3_
  44.5 0.7 collective-permute-done.13.refs_2_
  45.2 1.0 %prepare_other.6 = bf16[2,32,9216]{2,1,0:T(8,128)(2,1)S(1)} custom-call(s32[2,288]{1,0:T(2,128)S(1)} %copy-done.2, bf16[32,3456]{1,0:T(8,128)(2,1)S(1)} %collective-permute-done.2.refs_0_, bf16[32,3456]{1,0:T(8,128)(2,1)S(1)} %collective-permute-done.12.refs_1_, bf16[32,3456]{1,0:T(8,128)(2,1)S(1)} %collective-permute-done.13.refs_2_, ...), custom_call_target="tpu_custom_call" | custom-call | flops 1 | bytes 1 | tf_op jit(solution)/shard_map/prepare_other/pallas_call | solution.py:96
  46.2 0.1 collective-permute-start.15
  46.3 0.5 collective-permute-start.11
  46.8 1.0 %prepare_own.6.refs_4_ = bf16[2,32,9216]{2,1,0:T(8,128)(2,1)S(1)} custom-call(s32[2,288]{1,0:T(2,128)S(1)} %copy-done.2, bf16[32,3456]{1,0:T(8,128)(2,1)S(1)} %collective-permute-done.2.refs_0_, bf16[32,3456]{1,0:T(8,128)(2,1)S(1)} %collective-permute-done.12.refs_1_, bf16[32,3456]{1,0:T(8,128)(2,1)S(1)} %collective-permute-done.13.refs_2_, ...), custom_call_target="tpu_custom_call" | custom-call | flops 1 | bytes 1 | tf_op jit(solution)/shard_map/prepare_own/pallas_call | solution.py:96
  47.9 1.1 %prepare_own.7.refs_6_ = bf16[2,32,9216]{2,1,0:T(8,128)(2,1)S(1)} custom-call(s32[2,288]{1,0:T(2,128)S(1)} %copy-done.2, bf16[32,3456]{1,0:T(8,128)(2,1)S(1)} %collective-permute-done.6.refs_0_, bf16[32,3456]{1,0:T(8,128)(2,1)S(1)} %collective-permute-done.7.refs_1_, bf16[32,3456]{1,0:T(8,128)(2,1)S(1)} %collective-permute-done.8.refs_2_, ...), custom_call_target="tpu_custom_call" | custom-call | flops 1 | bytes 1 | tf_op jit(solution)/shard_map/prepare_own/pallas_call | solution.py:96
  48.9 0.0 collective-permute-done.9.refs_1_
  49.0 0.2 collective-permute-done.15.refs_5_
  49.1 1.7 %collective-permute-done.11.refs_3_ = bf16[2,32,9216]{2,1,0:T(8,128)(2,1)S(1)} collective-permute-done((bf16[2,32,9216]{2,1,0:T(8,128)(2,1)S(1)}, bf16[2,32,9216]{2,1,0:T(8,128)(2,1)S(1)}, u32[]{:S(2)}, u32[]{:S(2)}) %collective-permute-start.11) | collective-permute-done | bytes 1179680 | tf_op jit(solution)/shard_map/ppermute | solution.py:262
  50.8 10.6 %products.3 = (f32[4,64,256]{2,1,0:T(8,128)S(1)}, bf16[4,64,256]{2,1,0:T(8,128)(2,1)S(1)}, bf16[4,64,256]{2,1,0:T(8,128)(2,1)S(1)}, bf16[4,64,256]{2,1,0:T(8,128)(2,1)S(1)}) custom-call(bf16[9,16,9216]{2,1,0:T(8,128)(2,1)S(1)} %band_matrices.1.x_ref, bf16[2,32,9216]{2,1,0:T(8,128)(2,1)S(1)} %prepare_own.4._.refs_0_, ...), custom_call_target="tpu_custom_call" | custom-call | flops 9663676416 | bytes 9437184 | tf_op jit(solution)/shard_map/products/pallas_call | solution.py:149
  61.4 2.1 %collective-permute-start.18 = (bf16[4,64,256]{2,1,0:T(8,128)(2,1)S(1)}, bf16[4,64,256]{2,1,0:T(8,128)(2,1)S(1)}, u32[]{:S(2)}, u32[]{:S(2)}) collective-permute-start(bf16[4,64,256]{2,1,0:T(8,128)(2,1)S(1)} %get-tuple-element.75), channel_id=1, source_target_pairs={{0,2},{1,3},{2,4},{3,5},{4,6},{5,7},{6,0},{7,1},{8,10},{9,11},{10,... | collective-permute-start | bytes 393224 | tf_op jit(solution)/shard_map/ppermute | solution.py:262
  63.6 3.4 %collective-permute-start.19 = (bf16[4,64,256]{2,1,0:T(8,128)(2,1)S(1)}, bf16[4,64,256]{2,1,0:T(8,128)(2,1)S(1)}, u32[]{:S(2)}, u32[]{:S(2)}) collective-permute-start(bf16[4,64,256]{2,1,0:T(8,128)(2,1)S(1)} %get-tuple-element.76), channel_id=1, source_target_pairs={{0,4},{1,5},{2,6},{3,7},{4,0},{5,1},{6,2},{7,3},{8,12},{9,13},{10,... | collective-permute-start | bytes 393224 | tf_op jit(solution)/shard_map/ppermute | solution.py:262
  66.9 0.0 collective-permute-start.20
  66.9 10.4 %products.4 = (f32[4,64,256]{2,1,0:T(8,128)S(1)}, bf16[4,64,256]{2,1,0:T(8,128)(2,1)S(1)}, bf16[4,64,256]{2,1,0:T(8,128)(2,1)S(1)}, bf16[4,64,256]{2,1,0:T(8,128)(2,1)S(1)}) custom-call(bf16[9,16,9216]{2,1,0:T(8,128)(2,1)S(1)} %band_matrices.1.x_ref, bf16[2,32,9216]{2,1,0:T(8,128)(2,1)S(1)} %prepare_own.4._.refs_0_, ...), custom_call_target="tpu_custom_call" | custom-call | flops 9663676416 | bytes 9437184 | tf_op jit(solution)/shard_map/products/pallas_call | solution.py:149
  77.3 2.1 %collective-permute-start.21 = (bf16[4,64,256]{2,1,0:T(8,128)(2,1)S(1)}, bf16[4,64,256]{2,1,0:T(8,128)(2,1)S(1)}, u32[]{:S(2)}, u32[]{:S(2)}) collective-permute-start(bf16[4,64,256]{2,1,0:T(8,128)(2,1)S(1)} %get-tuple-element.90), channel_id=1, source_target_pairs={{0,2},{1,3},{2,4},{3,5},{4,6},{5,7},{6,0},{7,1},{8,10},{9,11},{10,... | collective-permute-start | bytes 393224 | tf_op jit(solution)/shard_map/ppermute | solution.py:262
  79.4 0.0 collective-permute-start.22
  79.4 0.0 collective-permute-done.18
  79.4 2.4 %collective-permute-start.23 = (bf16[4,64,256]{2,1,0:T(8,128)(2,1)S(1)}, bf16[4,64,256]{2,1,0:T(8,128)(2,1)S(1)}, u32[]{:S(2)}, u32[]{:S(2)}) collective-permute-start(bf16[4,64,256]{2,1,0:T(8,128)(2,1)S(1)} %get-tuple-element.92), channel_id=1, source_target_pairs={{0,6},{1,7},{2,0},{3,1},{4,2},{5,3},{6,4},{7,5},{8,14},{9,15},{10,... | collective-permute-start | bytes 393224 | tf_op jit(solution)/shard_map/ppermute | solution.py:262
  81.9 3.0 %products.5 = (f32[1,64,256]{2,1,0:T(8,128)S(1)}, bf16[1,64,256]{2,1,0:T(8,128)(2,1)S(1)}, bf16[1,64,256]{2,1,0:T(8,128)(2,1)S(1)}, bf16[1,64,256]{2,1,0:T(8,128)(2,1)S(1)}) custom-call(bf16[9,16,9216]{2,1,0:T(8,128)(2,1)S(1)} %band_matrices.1.x_ref, bf16[2,32,9216]{2,1,0:T(8,128)(2,1)S(1)} %prepare_own.4._.refs_0_, ...), custom_call_target="tpu_custom_call" | custom-call | flops 2415919104 | bytes 9437184 | tf_op jit(solution)/shard_map/products/pallas_call | solution.py:149
  84.9 0.1 collective-permute-start.24
  85.0 2.5 %collective-permute-start.25 = (bf16[1,64,256]{2,1,0:T(8,128)(2,1)S(1)}, bf16[1,64,256]{2,1,0:T(8,128)(2,1)S(1)}, u32[]{:S(2)}, u32[]{:S(2)}) collective-permute-start(bf16[1,64,256]{2,1,0:T(8,128)(2,1)S(1)} %get-tuple-element.99), channel_id=1, source_target_pairs={{0,4},{1,5},{2,6},{3,7},{4,0},{5,1},{6,2},{7,3},{8,12},{9,13},{10,... | collective-permute-start | bytes 98312 | tf_op jit(solution)/shard_map/ppermute | solution.py:262
  87.5 1.8 %collective-permute-start.26 = (bf16[1,64,256]{2,1,0:T(8,128)(2,1)S(1)}, bf16[1,64,256]{2,1,0:T(8,128)(2,1)S(1)}, u32[]{:S(2)}, u32[]{:S(2)}) collective-permute-start(bf16[1,64,256]{2,1,0:T(8,128)(2,1)S(1)} %get-tuple-element.100), channel_id=1, source_target_pairs={{0,6},{1,7},{2,0},{3,1},{4,2},{5,3},{6,4},{7,5},{8,14},{9,15},{10,... | collective-permute-start | bytes 98312 | tf_op jit(solution)/shard_map/ppermute | solution.py:262
  89.3 1.3 %collective-permute-done.22 = bf16[4,64,256]{2,1,0:T(8,128)(2,1)S(1)} collective-permute-done((bf16[4,64,256]{2,1,0:T(8,128)(2,1)S(1)}, bf16[4,64,256]{2,1,0:T(8,128)(2,1)S(1)}, u32[]{:S(2)}, u32[]{:S(2)}) %collective-permute-start.22) | collective-permute-done | bytes 131104 | tf_op jit(solution)/shard_map/ppermute | solution.py:262
  90.6 0.1 convert_add_fusion.1
  90.7 0.1 convert_add_fusion
  90.8 0.1 collective-permute-start.27
  90.8 0.5 collective-permute-start.28
  91.3 0.0 collective-permute-done.24
  91.4 3.4 %collective-permute-done.25 = bf16[1,64,256]{2,1,0:T(8,128)(2,1)S(1)} collective-permute-done((bf16[1,64,256]{2,1,0:T(8,128)(2,1)S(1)}, bf16[1,64,256]{2,1,0:T(8,128)(2,1)S(1)}, u32[]{:S(2)}, u32[]{:S(2)}) %collective-permute-start.25) | collective-permute-done | bytes 32800 | tf_op jit(solution)/shard_map/ppermute | solution.py:262
  94.9 0.1 collective-permute-start.29
  95.0 1.2 %collective-permute-done.29 = f32[1,32,256]{2,1,0:T(8,128)S(1)} collective-permute-done((f32[1,32,256]{2,1,0:T(8,128)S(1)}, f32[1,32,256]{2,1,0:T(8,128)S(1)}, u32[]{:S(2)}, u32[]{:S(2)}) %collective-permute-start.29) | collective-permute-done | bytes 32800 | tf_op jit(solution)/shard_map/ppermute | solution.py:262
  96.2 0.9 maximum_select_fusion
  (27 shorter events, 0.2 us)
Async XLA Ops:
  0.0 8.2 %copy-start.1 = (bf16[2,9,32,288]{3,2,1,0:T(8,128)(2,1)S(1)}, bf16[2,9,32,288]{3,2,1,0:T(8,128)(2,1)}, u32[]{:S(2)}) copy-start(bf16[2,9,32,288]{3,2,1,0:T(8,128)(2,1)} %coupling_ref.3) | copy-start | bytes 995332
  0.0 12.1 %copy-start.2 = (s32[2,288]{1,0:T(2,128)S(1)}, s32[2,288]{1,0:T(2,128)}, u32[]{:S(2)}) copy-start(s32[2,288]{1,0:T(2,128)} %kq_ref.17) | copy-start | bytes 6916
  3.0 5.2 %collective-permute-start = (bf16[9,32,288]{2,1,0:T(8,128)(2,1)}, bf16[9,32,288]{2,1,0:T(8,128)(2,1)S(1)}, u32[]{:S(2)}, u32[]{:S(2)}) collective-permute-start(bf16[9,32,288]{2,1,0:T(8,128)(2,1)} %get-tuple-element.55), channel_id=1, source_target_pairs={{0,1},{1,0},{2,3},{3,2},{4,5},{5,4},{6,7},{7,6},{8,9},{9,8},{10,11... | collective-permute-start | bytes 497672 | tf_op jit(solution)/shard_map/ppermute | solution.py:262
  3.5 10.8 %collective-permute-start.3 = (bf16[32,3456]{1,0:T(8,128)(2,1)}, bf16[32,3456]{1,0:T(8,128)(2,1)S(1)}, u32[]{:S(2)}, u32[]{:S(2)}) collective-permute-start(bf16[32,3456]{1,0:T(8,128)(2,1)} %get-tuple-element.58), channel_id=1, source_target_pairs={{0,6},{1,7},{2,0},{3,1},{4,2},{5,3},{6,4},{7,5},{8,14},{9,15},{10,... | collective-permute-start | bytes 663560 | tf_op jit(solution)/shard_map/ppermute | solution.py:262
  8.2 11.6 %collective-permute-start.6 = (bf16[32,3456]{1,0:T(8,128)(2,1)}, bf16[32,3456]{1,0:T(8,128)(2,1)S(1)}, u32[]{:S(2)}, u32[]{:S(2)}) collective-permute-start(bf16[32,3456]{1,0:T(8,128)(2,1)} %get-tuple-element.60), channel_id=1, source_target_pairs={{0,2},{1,3},{2,4},{3,5},{4,6},{5,7},{6,0},{7,1},{8,10},{9,11},{10,... | collective-permute-start | bytes 663560 | tf_op jit(solution)/shard_map/ppermute | solution.py:262
  8.2 15.5 %collective-permute-start.1 = (bf16[9,32,288]{2,1,0:T(8,128)(2,1)S(1)}, bf16[9,32,288]{2,1,0:T(8,128)(2,1)S(1)}, u32[]{:S(2)}, u32[]{:S(2)}) collective-permute-start(bf16[9,32,288]{2,1,0:T(8,128)(2,1)S(1)} %bitcast_select_fusion), channel_id=1, source_target_pairs={{0,6},{1,7},{2,0},{3,1},{4,2},{5,3},{6,4},{7,5},{8,14},{9,15},{10,... | collective-permute-start | bytes 497672 | tf_op jit(solution)/shard_map/ppermute | solution.py:262
  12.1 1.2 %copy-start = (bf16[32,13824]{1,0:T(8,128)(2,1)S(1)}, bf16[32,13824]{1,0:T(8,128)(2,1)}, u32[]{:S(2)}) copy-start(bf16[32,13824]{1,0:T(8,128)(2,1)} %get-tuple-element.54.refs_0_) | copy-start | bytes 2654212
  14.3 7.1 %copy-start.3 = (bf16[32,3456]{1,0:T(8,128)(2,1)S(1)}, bf16[32,3456]{1,0:T(8,128)(2,1)}, u32[]{:S(2)}) copy-start(bf16[32,3456]{1,0:T(8,128)(2,1)} %get-tuple-element.57) | copy-start | bytes 663556
  14.3 10.9 %collective-permute-start.4 = (bf16[32,3456]{1,0:T(8,128)(2,1)S(1)}, bf16[32,3456]{1,0:T(8,128)(2,1)S(1)}, u32[]{:S(2)}, u32[]{:S(2)}) collective-permute-start(bf16[32,3456]{1,0:T(8,128)(2,1)S(1)} %collective-permute-done.3.refs_0_), channel_id=1, source_target_pairs={{0,8},{1,17},{2,10},{3,19},{4,12},{5,21},{6,14},{7,23},{8,0},{9,25... | collective-permute-start | bytes 663560 | tf_op jit(solution)/shard_map/ppermute | solution.py:262
  19.8 8.2 %collective-permute-start.7 = (bf16[32,3456]{1,0:T(8,128)(2,1)S(1)}, bf16[32,3456]{1,0:T(8,128)(2,1)S(1)}, u32[]{:S(2)}, u32[]{:S(2)}) collective-permute-start(bf16[32,3456]{1,0:T(8,128)(2,1)S(1)} %collective-permute-done.6.refs_0_), channel_id=1, source_target_pairs={{0,8},{1,17},{2,10},{3,19},{4,12},{5,21},{6,14},{7,23},{8,0},{9,25... | collective-permute-start | bytes 663560 | tf_op jit(solution)/shard_map/ppermute | solution.py:262
  21.3 11.9 %collective-permute-start.2 = (bf16[32,3456]{1,0:T(8,128)(2,1)S(1)}, bf16[32,3456]{1,0:T(8,128)(2,1)S(1)}, u32[]{:S(2)}, u32[]{:S(2)}) collective-permute-start(bf16[32,3456]{1,0:T(8,128)(2,1)S(1)} %copy-done.3), channel_id=1, source_target_pairs={{0,4},{1,5},{2,6},{3,7},{4,0},{5,1},{6,2},{7,3},{8,12},{9,13},{10,... | collective-permute-start | bytes 663560 | tf_op jit(solution)/shard_map/ppermute | solution.py:262
  21.6 11.7 %collective-permute-start.5 = (bf16[32,3456]{1,0:T(8,128)(2,1)S(1)}, bf16[32,3456]{1,0:T(8,128)(2,1)S(1)}, u32[]{:S(2)}, u32[]{:S(2)}) collective-permute-start(bf16[32,3456]{1,0:T(8,128)(2,1)S(1)} %collective-permute-done.3.refs_0_), channel_id=1, source_target_pairs={{0,16},{1,9},{2,18},{3,11},{4,20},{5,13},{6,22},{7,15},{8,24},{9,1... | collective-permute-start | bytes 663560 | tf_op jit(solution)/shard_map/ppermute | solution.py:262
  23.7 9.6 %collective-permute-start.8 = (bf16[32,3456]{1,0:T(8,128)(2,1)S(1)}, bf16[32,3456]{1,0:T(8,128)(2,1)S(1)}, u32[]{:S(2)}, u32[]{:S(2)}) collective-permute-start(bf16[32,3456]{1,0:T(8,128)(2,1)S(1)} %collective-permute-done.6.refs_0_), channel_id=1, source_target_pairs={{0,16},{1,9},{2,18},{3,11},{4,20},{5,13},{6,22},{7,15},{8,24},{9,1... | collective-permute-start | bytes 663560 | tf_op jit(solution)/shard_map/ppermute | solution.py:262
  25.2 15.4 %collective-permute-start.10 = (bf16[32,3456]{1,0:T(8,128)(2,1)S(1)}, bf16[32,3456]{1,0:T(8,128)(2,1)S(1)}, u32[]{:S(2)}, u32[]{:S(2)}) collective-permute-start(bf16[32,3456]{1,0:T(8,128)(2,1)S(1)} %collective-permute-done.4.refs_1_), channel_id=1, source_target_pairs={{0,16},{1,9},{2,18},{3,11},{4,20},{5,13},{6,22},{7,15},{8,24},{9,1... | collective-permute-start | bytes 663560 | tf_op jit(solution)/shard_map/ppermute | solution.py:262
  28.1 14.8 %collective-permute-start.16 = (bf16[32,3456]{1,0:T(8,128)(2,1)S(1)}, bf16[32,3456]{1,0:T(8,128)(2,1)S(1)}, u32[]{:S(2)}, u32[]{:S(2)}) collective-permute-start(bf16[32,3456]{1,0:T(8,128)(2,1)S(1)} %collective-permute-done.7.refs_1_), channel_id=1, source_target_pairs={{0,16},{1,9},{2,18},{3,11},{4,20},{5,13},{6,22},{7,15},{8,24},{9,1... | collective-permute-start | bytes 663560 | tf_op jit(solution)/shard_map/ppermute | solution.py:262
  33.3 11.2 %collective-permute-start.14 = (bf16[32,3456]{1,0:T(8,128)(2,1)S(1)}, bf16[32,3456]{1,0:T(8,128)(2,1)S(1)}, u32[]{:S(2)}, u32[]{:S(2)}) collective-permute-start(bf16[32,3456]{1,0:T(8,128)(2,1)S(1)} %collective-permute-done.2.refs_0_), channel_id=1, source_target_pairs={{0,24},{1,25},{2,26},{3,27},{4,28},{5,29},{6,30},{7,31},{8,16},{9,... | collective-permute-start | bytes 663560 | tf_op jit(solution)/shard_map/ppermute | solution.py:262
  35.0 10.2 %collective-permute-start.13 = (bf16[32,3456]{1,0:T(8,128)(2,1)S(1)}, bf16[32,3456]{1,0:T(8,128)(2,1)S(1)}, u32[]{:S(2)}, u32[]{:S(2)}) collective-permute-start(bf16[32,3456]{1,0:T(8,128)(2,1)S(1)} %collective-permute-done.2.refs_0_), channel_id=1, source_target_pairs={{0,16},{1,17},{2,18},{3,19},{4,20},{5,21},{6,22},{7,23},{8,24},{9,... | collective-permute-start | bytes 663560 | tf_op jit(solution)/shard_map/ppermute | solution.py:262
  36.2 9.0 %collective-permute-start.12 = (bf16[32,3456]{1,0:T(8,128)(2,1)S(1)}, bf16[32,3456]{1,0:T(8,128)(2,1)S(1)}, u32[]{:S(2)}, u32[]{:S(2)}) collective-permute-start(bf16[32,3456]{1,0:T(8,128)(2,1)S(1)} %collective-permute-done.2.refs_0_), channel_id=1, source_target_pairs={{0,8},{1,9},{2,10},{3,11},{4,12},{5,13},{6,14},{7,15},{8,0},{9,1},... | collective-permute-start | bytes 663560 | tf_op jit(solution)/shard_map/ppermute | solution.py:262
  40.6 8.3 %collective-permute-start.9 = (bf16[2,32,9216]{2,1,0:T(8,128)(2,1)S(1)}, bf16[2,32,9216]{2,1,0:T(8,128)(2,1)S(1)}, u32[]{:S(2)}, u32[]{:S(2)}) collective-permute-start(bf16[2,32,9216]{2,1,0:T(8,128)(2,1)S(1)} %prepare_other.4), channel_id=1, source_target_pairs={{0,1},{1,0},{2,3},{3,2},{4,5},{5,4},{6,7},{7,6},{8,9},{9,8},{10,11... | collective-permute-start | bytes 3538952 | tf_op jit(solution)/shard_map/ppermute | solution.py:262
  43.9 5.0 %collective-permute-start.17 = (bf16[2,32,9216]{2,1,0:T(8,128)(2,1)S(1)}, bf16[2,32,9216]{2,1,0:T(8,128)(2,1)S(1)}, u32[]{:S(2)}, u32[]{:S(2)}) collective-permute-start(bf16[2,32,9216]{2,1,0:T(8,128)(2,1)S(1)} %prepare_other.7), channel_id=1, source_target_pairs={{0,1},{1,0},{2,3},{3,2},{4,5},{5,4},{6,7},{7,6},{8,9},{9,8},{10,11... | collective-permute-start | bytes 3538952 | tf_op jit(solution)/shard_map/ppermute | solution.py:262
  46.2 2.9 %collective-permute-start.15 = (bf16[2,32,9216]{2,1,0:T(8,128)(2,1)S(1)}, bf16[2,32,9216]{2,1,0:T(8,128)(2,1)S(1)}, u32[]{:S(2)}, u32[]{:S(2)}) collective-permute-start(bf16[2,32,9216]{2,1,0:T(8,128)(2,1)S(1)} %prepare_other.6), channel_id=1, source_target_pairs={{0,1},{1,0},{2,3},{3,2},{4,5},{5,4},{6,7},{7,6},{8,9},{9,8},{10,11... | collective-permute-start | bytes 3538952 | tf_op jit(solution)/shard_map/ppermute | solution.py:262
  46.3 4.5 %collective-permute-start.11 = (bf16[2,32,9216]{2,1,0:T(8,128)(2,1)S(1)}, bf16[2,32,9216]{2,1,0:T(8,128)(2,1)S(1)}, u32[]{:S(2)}, u32[]{:S(2)}) collective-permute-start(bf16[2,32,9216]{2,1,0:T(8,128)(2,1)S(1)} %prepare_other.5), channel_id=1, source_target_pairs={{0,1},{1,0},{2,3},{3,2},{4,5},{5,4},{6,7},{7,6},{8,9},{9,8},{10,11... | collective-permute-start | bytes 3538952 | tf_op jit(solution)/shard_map/ppermute | solution.py:262
  61.4 18.0 %collective-permute-start.18 = (bf16[4,64,256]{2,1,0:T(8,128)(2,1)S(1)}, bf16[4,64,256]{2,1,0:T(8,128)(2,1)S(1)}, u32[]{:S(2)}, u32[]{:S(2)}) collective-permute-start(bf16[4,64,256]{2,1,0:T(8,128)(2,1)S(1)} %get-tuple-element.75), channel_id=1, source_target_pairs={{0,2},{1,3},{2,4},{3,5},{4,6},{5,7},{6,0},{7,1},{8,10},{9,11},{10,... | collective-permute-start | bytes 393224 | tf_op jit(solution)/shard_map/ppermute | solution.py:262
  63.6 18.3 %collective-permute-start.19 = (bf16[4,64,256]{2,1,0:T(8,128)(2,1)S(1)}, bf16[4,64,256]{2,1,0:T(8,128)(2,1)S(1)}, u32[]{:S(2)}, u32[]{:S(2)}) collective-permute-start(bf16[4,64,256]{2,1,0:T(8,128)(2,1)S(1)} %get-tuple-element.76), channel_id=1, source_target_pairs={{0,4},{1,5},{2,6},{3,7},{4,0},{5,1},{6,2},{7,3},{8,12},{9,13},{10,... | collective-permute-start | bytes 393224 | tf_op jit(solution)/shard_map/ppermute | solution.py:262
  66.9 14.9 %collective-permute-start.20 = (bf16[4,64,256]{2,1,0:T(8,128)(2,1)S(1)}, bf16[4,64,256]{2,1,0:T(8,128)(2,1)S(1)}, u32[]{:S(2)}, u32[]{:S(2)}) collective-permute-start(bf16[4,64,256]{2,1,0:T(8,128)(2,1)S(1)} %get-tuple-element.77), channel_id=1, source_target_pairs={{0,6},{1,7},{2,0},{3,1},{4,2},{5,3},{6,4},{7,5},{8,14},{9,15},{10,... | collective-permute-start | bytes 393224 | tf_op jit(solution)/shard_map/ppermute | solution.py:262
  77.3 10.2 %collective-permute-start.21 = (bf16[4,64,256]{2,1,0:T(8,128)(2,1)S(1)}, bf16[4,64,256]{2,1,0:T(8,128)(2,1)S(1)}, u32[]{:S(2)}, u32[]{:S(2)}) collective-permute-start(bf16[4,64,256]{2,1,0:T(8,128)(2,1)S(1)} %get-tuple-element.90), channel_id=1, source_target_pairs={{0,2},{1,3},{2,4},{3,5},{4,6},{5,7},{6,0},{7,1},{8,10},{9,11},{10,... | collective-permute-start | bytes 393224 | tf_op jit(solution)/shard_map/ppermute | solution.py:262
  79.4 11.2 %collective-permute-start.22 = (bf16[4,64,256]{2,1,0:T(8,128)(2,1)S(1)}, bf16[4,64,256]{2,1,0:T(8,128)(2,1)S(1)}, u32[]{:S(2)}, u32[]{:S(2)}) collective-permute-start(bf16[4,64,256]{2,1,0:T(8,128)(2,1)S(1)} %get-tuple-element.91), channel_id=1, source_target_pairs={{0,4},{1,5},{2,6},{3,7},{4,0},{5,1},{6,2},{7,3},{8,12},{9,13},{10,... | collective-permute-start | bytes 393224 | tf_op jit(solution)/shard_map/ppermute | solution.py:262
  79.4 11.2 %collective-permute-start.23 = (bf16[4,64,256]{2,1,0:T(8,128)(2,1)S(1)}, bf16[4,64,256]{2,1,0:T(8,128)(2,1)S(1)}, u32[]{:S(2)}, u32[]{:S(2)}) collective-permute-start(bf16[4,64,256]{2,1,0:T(8,128)(2,1)S(1)} %get-tuple-element.92), channel_id=1, source_target_pairs={{0,6},{1,7},{2,0},{3,1},{4,2},{5,3},{6,4},{7,5},{8,14},{9,15},{10,... | collective-permute-start | bytes 393224 | tf_op jit(solution)/shard_map/ppermute | solution.py:262
  84.9 6.4 %collective-permute-start.24 = (bf16[1,64,256]{2,1,0:T(8,128)(2,1)S(1)}, bf16[1,64,256]{2,1,0:T(8,128)(2,1)S(1)}, u32[]{:S(2)}, u32[]{:S(2)}) collective-permute-start(bf16[1,64,256]{2,1,0:T(8,128)(2,1)S(1)} %get-tuple-element.98), channel_id=1, source_target_pairs={{0,2},{1,3},{2,4},{3,5},{4,6},{5,7},{6,0},{7,1},{8,10},{9,11},{10,... | collective-permute-start | bytes 98312 | tf_op jit(solution)/shard_map/ppermute | solution.py:262
  85.0 9.8 %collective-permute-start.25 = (bf16[1,64,256]{2,1,0:T(8,128)(2,1)S(1)}, bf16[1,64,256]{2,1,0:T(8,128)(2,1)S(1)}, u32[]{:S(2)}, u32[]{:S(2)}) collective-permute-start(bf16[1,64,256]{2,1,0:T(8,128)(2,1)S(1)} %get-tuple-element.99), channel_id=1, source_target_pairs={{0,4},{1,5},{2,6},{3,7},{4,0},{5,1},{6,2},{7,3},{8,12},{9,13},{10,... | collective-permute-start | bytes 98312 | tf_op jit(solution)/shard_map/ppermute | solution.py:262
  87.5 7.3 %collective-permute-start.26 = (bf16[1,64,256]{2,1,0:T(8,128)(2,1)S(1)}, bf16[1,64,256]{2,1,0:T(8,128)(2,1)S(1)}, u32[]{:S(2)}, u32[]{:S(2)}) collective-permute-start(bf16[1,64,256]{2,1,0:T(8,128)(2,1)S(1)} %get-tuple-element.100), channel_id=1, source_target_pairs={{0,6},{1,7},{2,0},{3,1},{4,2},{5,3},{6,4},{7,5},{8,14},{9,15},{10,... | collective-permute-start | bytes 98312 | tf_op jit(solution)/shard_map/ppermute | solution.py:262
  90.8 5.4 %collective-permute-start.27 = (f32[4,32,256]{2,1,0:T(8,128)S(1)}, f32[4,32,256]{2,1,0:T(8,128)S(1)}, u32[]{:S(2)}, u32[]{:S(2)}) collective-permute-start(f32[4,32,256]{2,1,0:T(8,128)S(1)} %get-tuple-element.102), channel_id=1, source_target_pairs={{0,1},{1,0},{2,3},{3,2},{4,5},{5,4},{6,7},{7,6},{8,9},{9,8},{10,11... | collective-permute-start | bytes 393224 | tf_op jit(solution)/shard_map/ppermute | solution.py:262
  90.8 5.3 %collective-permute-start.28 = (f32[4,32,256]{2,1,0:T(8,128)S(1)}, f32[4,32,256]{2,1,0:T(8,128)S(1)}, u32[]{:S(2)}, u32[]{:S(2)}) collective-permute-start(f32[4,32,256]{2,1,0:T(8,128)S(1)} %get-tuple-element.107), channel_id=1, source_target_pairs={{0,1},{1,0},{2,3},{3,2},{4,5},{5,4},{6,7},{7,6},{8,9},{9,8},{10,11... | collective-permute-start | bytes 393224 | tf_op jit(solution)/shard_map/ppermute | solution.py:262
  94.9 1.3 %collective-permute-start.29 = (f32[1,32,256]{2,1,0:T(8,128)S(1)}, f32[1,32,256]{2,1,0:T(8,128)S(1)}, u32[]{:S(2)}, u32[]{:S(2)}) collective-permute-start(f32[1,32,256]{2,1,0:T(8,128)S(1)} %get-tuple-element.106), channel_id=1, source_target_pairs={{0,1},{1,0},{2,3},{3,2},{4,5},{5,4},{6,7},{7,6},{8,9},{9,8},{10,11... | collective-permute-start | bytes 98312 | tf_op jit(solution)/shard_map/ppermute | solution.py:262

commit v10 on v9

--- a/solution.py
+++ b/solution.py
@@ -34,9 +34,8 @@
     return base, base + step, lax.rem(LINE - lax.rem(origin, KY) * BANDS, LINE)
 
 
-def cut_kernel(block, env_ref, coupling_ref, *refs):
-    pieces, (window, give, sems) = refs[:-3], refs[-3:]
-    n_z = len(pieces) + 1
+def cut_kernel(block, n_z, sources, env_ref, coupling_ref, *refs):
+    outs, sems = refs[:-1], refs[-1]
     pb, z, core = place()
     part = block // 4
 
@@ -44,13 +43,15 @@
         return pl.ds(pl.multiple_of(lax.rem(8 * chip + index, 8 * n_z) * part, 128), part)
 
     jobs = []
-    for e in range(1, n_z):
+    for e, out in zip(sources, outs):
         to = lax.rem(z - e + n_z, n_z)
         for i in range(3):
-            jobs.append((env_ref.at[:, lanes(to, 3 * pb + i)], pieces[e - 1].at[:, i * part : (i + 1) * part]))
-    for i in range(12):
-        jobs.append((env_ref.at[:, lanes(z, i)], window.at[:, i * part : (i + 1) * part]))
-    jobs.append((coupling_ref.at[1 - core], give))
+            jobs.append((env_ref.at[:, lanes(to, 3 * pb + i)], out.at[:, i * part : (i + 1) * part]))
+    if len(outs) > len(sources):
+        window, give = outs[-2:]
+        for i in range(12):
+            jobs.append((env_ref.at[:, lanes(z, i)], window.at[:, i * part : (i + 1) * part]))
+        jobs.append((coupling_ref.at[1 - core], give))
     copies = [pltpu.make_async_copy(src, dst, sems.at[i]) for i, (src, dst) in enumerate(jobs)]
     for copy in copies:
         copy.start()
@@ -58,18 +59,20 @@
         copy.wait()
 
 
-def cut(envelopes, coupling, n_z, block):
+def cut(envelopes, coupling, n_z, block, sources, own):
     rows = envelopes.shape[0]
     shape = functools.partial(jax.ShapeDtypeStruct, dtype=BF16)
-    outs = [shape((rows, 3 * block // 4))] * (n_z - 1) + [shape((rows, 3 * block)), shape(coupling.shape[1:])]
-    return pl.pallas_call(
-        functools.partial(cut_kernel, block),
+    outs = [shape((rows, 3 * block // 4))] * len(sources)
+    if own:
+        outs += [shape((rows, 3 * block)), shape(coupling.shape[1:])]
+    return pl.pallas_call(
+        functools.partial(cut_kernel, block, n_z, sources),
         in_specs=[pl.BlockSpec(memory_space=pl.ANY)] * 2,
         out_specs=[pl.BlockSpec(memory_space=pltpu.VMEM)] * len(outs),
         out_shape=outs,
-        scratch_shapes=[pltpu.SemaphoreType.DMA((3 * n_z + 10,))],
+        scratch_shapes=[pltpu.SemaphoreType.DMA((3 * len(sources) + 13,))],
         cost_estimate=SMALL,
-        name="cut",
+        name="cut_own" if own else "cut",
     )(envelopes, coupling)
 
 
@@ -278,12 +281,14 @@
 
     near = sorted({1, n_z - 1})
     far = [e for e in range(2, n_z - 1)]
-    *pieces, window, give = cut(envelopes, coupling, n_z, block)
-    arrived = {e: passed_down(pieces[e - 1], e) for e in near}
+    first = cut(envelopes, coupling, n_z, block, near, False)
+    arrived = {e: passed_down(piece, e) for e, piece in zip(near, first)}
+    *later, window, give = cut(after(envelopes, first[0]), coupling, n_z, block, far, True)
+    pieces = dict(zip(far, later))
     pass_on = prepared([window], True)
     keep = prepared([after(window, pass_on)], False)
     for e in far:
-        arrived[e] = passed_down(after(pieces[e - 1], keep), e)
+        arrived[e] = passed_down(after(pieces[e], keep), e)
     spread = spread_matrices(min(coupling.shape[3], 64), keep)
     amps = {0: (keep, sibling(pass_on))}
 
@@ -299,15 +304,15 @@
         if e == 1:
             one = after(one, next_table)
         three = permute(one, lambda p, zz, c: (p ^ (2 - c), zz, c))
-        first_steps += [one, two]
+        first_steps += [one, two, three] if e == 1 else [one, two]
         parts[e] = [piece, one, two, three]
+    x = band_matrices(kq_map, spread, coupling, other_table, next_table, lines_all)
     for e in far:
-        piece = after(arrived[e], next_table, *first_steps)
+        piece = after(arrived[e], x, *first_steps)
         parts[e] = [piece] + [permute(piece, lambda p, zz, c: (p ^ i, zz, c)) for i in (1, 2, 3)]
-    x = band_matrices(kq_map, spread, coupling, other_table, after(next_table, *[parts[e][0] for e in far]), lines_all)
     for e in near + far:
         piece, *others = parts[e]
-        done = [x] if e in near else [x, amps[1][0]]
+        done = [parts[far[0]][0]] if e in near else [amps[1][0]]
         pass_on = prepared([after(piece, *done)] + others, True, e in far)
         keep = prepared([after(piece, pass_on)] + others, False, e in far)
         amps[e] = (keep, sibling(pass_on))
@@ -324,10 +329,13 @@
         if received:
             own, received[-1] = lax.optimization_barrier((own, received[-1]))
         received.append([own] + [permute(p, lambda p, zz, c: (p, zz + e, c)) for e, p in enumerate(sends, 1)])
+    totals = []
     for parts in received:
         total = parts[0]
         for part in parts[1:]:
             total = total + part.astype(F32)
+        totals.append(total)
+    for total in totals[:-2] + [jnp.concatenate(totals[-2:], axis=0)]:
         mine.append(total[:, :rows])
         other.append(sibling(total[:, rows:]))
     mine, other = jnp.concatenate(mine, axis=0), jnp.concatenate(other, axis=0)

time: 97.2 us -> 97.4 us (level)
  starting transfers between devices: 36.9 us -> 34.5 us
  Pallas kernels: 39.2 us -> 40.8 us
    ppermute x30 -> x29, starting transfers between devices: 36.9 us -> 34.5 us  [permute(): return lax.ppermute(x, ('pb', 'ka'), pairs)]
    pallas_call x1 -> x2, Pallas kernels: 2.97 us -> 4.58 us  [cut(): pl.pallas_call(functools.partial(cut_kernel, block, n_z, sources), in_spe...]
    ppermute x30 -> x29, waiting for transfers between devices: 18.4 us -> 19.3 us  [permute(): return lax.ppermute(x, ('pb', 'ka'), pairs)]
  transfers between devices with their start and end apart: 30 -> 29, of which waited for: 10 -> 11; matrix products, arithmetic and copies ran while one was open for 0% -> 0% of each run, Pallas kernels for 26% -> 29%
where the time goes in v10:
time: 97.4 us; the launch traced here: 97.2 us
  Pallas kernels  40.8 us (42%)
  starting transfers between devices  34.5 us (35%)
  waiting for transfers between devices  19.3 us (20%)
  local copies, waits for them, and re-layouts  1.21 us (1%)
  other arithmetic  1.09 us (1%)
    ppermute x29, starting transfers between devices, permute(): return lax.ppermute(x, ('pb', 'ka'), pairs)  34.5 us
    pallas_call x3, Pallas kernels, products(): pl.pallas_call(functools.partial(main_kernel, sources, first, branches, f...  24 us
    ppermute x29, waiting for transfers between devices, permute(): return lax.ppermute(x, ('pb', 'ka'), pairs)  19.3 us
    pallas_call x8, Pallas kernels, prepare(): pl.pallas_call(functools.partial(prep_kernel, block // LINE, lines_all, f...  8.31 us
    pallas_call x2, Pallas kernels, cut(): pl.pallas_call(functools.partial(cut_kernel, block, n_z, sources), in_spe...  4.58 us
    pallas_call x1, Pallas kernels, band_matrices(): pl.pallas_call(functools.partial(band_kernel, count // KY, lines_all), in...  3.72 us
  transfers between devices with their start and end apart: 29, of which 11 were waited for; matrix products, arithmetic and copies ran while one was open for 0% of the time, Pallas kernels for 29%

profile of v10, /device:TPU:0, one launch (start us, length us, event | category | flops | bytes accessed | tf_op | source)
XLA Modules:
  0.0 97.2 jit_solution(12806688923750662243)
XLA Ops:
  0.0 2.0 %cut.1 = (bf16[32,3456]{1,0:T(8,128)(2,1)}, bf16[32,3456]{1,0:T(8,128)(2,1)}) custom-call(bf16[32,36864]{1,0:T(8,128)(2,1)} %env_ref.2, bf16[2,9,32,288]{3,2,1,0:T(8,128)(2,1)} %coupling_ref.5), custom_call_target="tpu_custom_call" | custom-call | flops 1 | bytes 1 | tf_op jit(solution)/shard_map/cut/pallas_call | solution.py:68
  2.0 0.0 copy-start
  2.0 0.0 copy-start.2
  2.0 5.1 %collective-permute-start.3 = (bf16[32,3456]{1,0:T(8,128)(2,1)}, bf16[32,3456]{1,0:T(8,128)(2,1)S(1)}, u32[]{:S(2)}, u32[]{:S(2)}) collective-permute-start(bf16[32,3456]{1,0:T(8,128)(2,1)} %get-tuple-element.53), channel_id=1, source_target_pairs={{0,6},{1,7},{2,0},{3,1},{4,2},{5,3},{6,4},{7,5},{8,14},{9,15},{10,... | collective-permute-start | bytes 663560 | tf_op jit(solution)/shard_map/ppermute | solution.py:265
  7.1 2.6 %cut_own.1 = (bf16[32,3456]{1,0:T(8,128)(2,1)}, bf16[32,13824]{1,0:T(8,128)(2,1)}, bf16[9,32,288]{2,1,0:T(8,128)(2,1)}) custom-call(bf16[32,36864]{1,0:T(8,128)(2,1)} %env_ref.2, bf16[2,9,32,288]{3,2,1,0:T(8,128)(2,1)} %coupling_ref.5), custom_call_target="tpu_custom_call" | custom-call | flops 1 | bytes 1 | tf_op jit(solution)/shard_map/cut_own/pallas_call | solution.py:68
  9.7 0.1 collective-permute-start
  9.8 0.1 collective-permute-start.8
  9.9 3.4 %collective-permute-done.3.refs_0_ = bf16[32,3456]{1,0:T(8,128)(2,1)S(1)} collective-permute-done((bf16[32,3456]{1,0:T(8,128)(2,1)}, bf16[32,3456]{1,0:T(8,128)(2,1)S(1)}, u32[]{:S(2)}, u32[]{:S(2)}) %collective-permute-start.3) | collective-permute-done | bytes 221216 | tf_op jit(solution)/shard_map/ppermute | solution.py:265
  13.3 1.5 %collective-permute-start.5 = (bf16[32,3456]{1,0:T(8,128)(2,1)S(1)}, bf16[32,3456]{1,0:T(8,128)(2,1)S(1)}, u32[]{:S(2)}, u32[]{:S(2)}) collective-permute-start(bf16[32,3456]{1,0:T(8,128)(2,1)S(1)} %collective-permute-done.3.refs_0_), channel_id=1, source_target_pairs={{0,8},{1,17},{2,10},{3,19},{4,12},{5,21},{6,14},{7,23},{8,0},{9,25... | collective-permute-start | bytes 663560 | tf_op jit(solution)/shard_map/ppermute | solution.py:265
  14.8 0.0 collective-permute-done.other_ref
  14.9 4.2 %collective-permute-start.1 = (bf16[9,32,288]{2,1,0:T(8,128)(2,1)S(1)}, bf16[9,32,288]{2,1,0:T(8,128)(2,1)S(1)}, u32[]{:S(2)}, u32[]{:S(2)}) collective-permute-start(bf16[9,32,288]{2,1,0:T(8,128)(2,1)S(1)} %bitcast_select_fusion), channel_id=1, source_target_pairs={{0,6},{1,7},{2,0},{3,1},{4,2},{5,3},{6,4},{7,5},{8,14},{9,15},{10,... | collective-permute-start | bytes 497672 | tf_op jit(solution)/shard_map/ppermute | solution.py:265
  19.1 1.2 %copy-done.1 = bf16[32,13824]{1,0:T(8,128)(2,1)S(1)} copy-done((bf16[32,13824]{1,0:T(8,128)(2,1)S(1)}, bf16[32,13824]{1,0:T(8,128)(2,1)}, u32[]{:S(2)}) %copy-start.1) | copy-done | bytes 884760
  20.3 1.0 %prepare_other.4 = bf16[2,32,9216]{2,1,0:T(8,128)(2,1)S(1)} custom-call(s32[2,288]{1,0:T(2,128)S(1)} %copy-done.2, bf16[32,13824]{1,0:T(8,128)(2,1)S(1)} %copy-done.1), custom_call_target="tpu_custom_call" | custom-call | flops 1 | bytes 1 | tf_op jit(solution)/shard_map/prepare_other/pallas_call | solution.py:99
  21.3 0.0 copy-start.3
  21.3 1.0 %prepare_own.4._.refs_0_ = bf16[2,32,9216]{2,1,0:T(8,128)(2,1)S(1)} custom-call(s32[2,288]{1,0:T(2,128)S(1)} %copy-done.2, bf16[32,13824]{1,0:T(8,128)(2,1)S(1)} %copy-done.1), custom_call_target="tpu_custom_call" | custom-call | flops 1 | bytes 1 | tf_op jit(solution)/shard_map/prepare_own/pallas_call | solution.py:99
  22.3 0.1 collective-permute-start.4
  22.4 1.6 %collective-permute-start.10 = (bf16[32,3456]{1,0:T(8,128)(2,1)S(1)}, bf16[32,3456]{1,0:T(8,128)(2,1)S(1)}, u32[]{:S(2)}, u32[]{:S(2)}) collective-permute-start(bf16[32,3456]{1,0:T(8,128)(2,1)S(1)} %collective-permute-done.8.refs_0_), channel_id=1, source_target_pairs={{0,16},{1,9},{2,18},{3,11},{4,20},{5,13},{6,22},{7,15},{8,24},{9,1... | collective-permute-start | bytes 663560 | tf_op jit(solution)/shard_map/ppermute | solution.py:265
  24.0 0.5 collective-permute-start.9
  24.5 0.3 collective-permute-done.1.next_ref
  24.8 1.3 %collective-permute-start.6 = (bf16[32,3456]{1,0:T(8,128)(2,1)S(1)}, bf16[32,3456]{1,0:T(8,128)(2,1)S(1)}, u32[]{:S(2)}, u32[]{:S(2)}) collective-permute-start(bf16[32,3456]{1,0:T(8,128)(2,1)S(1)} %collective-permute-done.3.refs_0_), channel_id=1, source_target_pairs={{0,16},{1,9},{2,18},{3,11},{4,20},{5,13},{6,22},{7,15},{8,24},{9,1... | collective-permute-start | bytes 663560 | tf_op jit(solution)/shard_map/ppermute | solution.py:265
  26.1 0.8 collective-permute-start.7
  26.9 0.1 spread.1
  27.0 3.7 %band_matrices.1.x_ref = bf16[9,16,9216]{2,1,0:T(8,128)(2,1)S(1)} custom-call(s32[2,288]{1,0:T(2,128)S(1)} %copy-done.2, bf16[2,256,1024]{2,1,0:T(8,128)(2,1)S(1)} %spread.1, bf16[2,9,32,288]{3,2,1,0:T(8,128)(2,1)S(1)} %copy-done, bf16[9,32,288]{2,1,0:T(8,128)(2,1)S(1)} %collective-permute-done.other_ref, bf16[9,32,288]{2,1,0:T(8,128)(2,1)S(1)} %collective-permute-done.1.next_ref), custom_call_target="tpu_custom_call" | custom-call | flops 1 | bytes 1 | tf_op jit(solution)/shard_map/band_matrices/pallas_call | solution.py:238
  30.7 1.5 %collective-permute-done.9.refs_1_ = bf16[32,3456]{1,0:T(8,128)(2,1)S(1)} collective-permute-done((bf16[32,3456]{1,0:T(8,128)(2,1)S(1)}, bf16[32,3456]{1,0:T(8,128)(2,1)S(1)}, u32[]{:S(2)}, u32[]{:S(2)}) %collective-permute-start.9) | collective-permute-done | bytes 221216 | tf_op jit(solution)/shard_map/ppermute | solution.py:265
  32.2 0.5 collective-permute-start.16
  32.8 0.9 collective-permute-done.4.refs_0_
  33.7 0.0 collective-permute-done.6.refs_2_
  33.7 0.0 collective-permute-done.7.refs_3_
  33.7 1.9 %collective-permute-start.14 = (bf16[32,3456]{1,0:T(8,128)(2,1)S(1)}, bf16[32,3456]{1,0:T(8,128)(2,1)S(1)}, u32[]{:S(2)}, u32[]{:S(2)}) collective-permute-start(bf16[32,3456]{1,0:T(8,128)(2,1)S(1)} %collective-permute-done.4.refs_0_), channel_id=1, source_target_pairs={{0,24},{1,25},{2,26},{3,27},{4,28},{5,29},{6,30},{7,31},{8,16},{9,... | collective-permute-start | bytes 663560 | tf_op jit(solution)/shard_map/ppermute | solution.py:265
  35.6 1.1 %collective-permute-start.13 = (bf16[32,3456]{1,0:T(8,128)(2,1)S(1)}, bf16[32,3456]{1,0:T(8,128)(2,1)S(1)}, u32[]{:S(2)}, u32[]{:S(2)}) collective-permute-start(bf16[32,3456]{1,0:T(8,128)(2,1)S(1)} %collective-permute-done.4.refs_0_), channel_id=1, source_target_pairs={{0,16},{1,17},{2,18},{3,19},{4,20},{5,21},{6,22},{7,23},{8,24},{9,... | collective-permute-start | bytes 663560 | tf_op jit(solution)/shard_map/ppermute | solution.py:265
  36.7 0.5 collective-permute-start.12
  37.2 0.0 collective-permute-start.2
  37.2 1.1 %prepare_other.5 = bf16[2,32,9216]{2,1,0:T(8,128)(2,1)S(1)} custom-call(s32[2,288]{1,0:T(2,128)S(1)} %copy-done.2, bf16[32,3456]{1,0:T(8,128)(2,1)S(1)} %collective-permute-done.3.refs_0_, bf16[32,3456]{1,0:T(8,128)(2,1)S(1)} %collective-permute-done.5.refs_1_, bf16[32,3456]{1,0:T(8,128)(2,1)S(1)} %collective-permute-done.6.refs_2_, ...), custom_call_target="tpu_custom_call" | custom-call | flops 1 | bytes 1 | tf_op jit(solution)/shard_map/prepare_other/pallas_call | solution.py:99
  38.3 1.1 %prepare_own.5.refs_2_ = bf16[2,32,9216]{2,1,0:T(8,128)(2,1)S(1)} custom-call(s32[2,288]{1,0:T(2,128)S(1)} %copy-done.2, bf16[32,3456]{1,0:T(8,128)(2,1)S(1)} %collective-permute-done.3.refs_0_, bf16[32,3456]{1,0:T(8,128)(2,1)S(1)} %collective-permute-done.5.refs_1_, bf16[32,3456]{1,0:T(8,128)(2,1)S(1)} %collective-permute-done.6.refs_2_, ...), custom_call_target="tpu_custom_call" | custom-call | flops 1 | bytes 1 | tf_op jit(solution)/shard_map/prepare_own/pallas_call | solution.py:99
  39.4 4.3 %collective-permute-done.16.refs_3_ = bf16[32,3456]{1,0:T(8,128)(2,1)S(1)} collective-permute-done((bf16[32,3456]{1,0:T(8,128)(2,1)S(1)}, bf16[32,3456]{1,0:T(8,128)(2,1)S(1)}, u32[]{:S(2)}, u32[]{:S(2)}) %collective-permute-start.16) | collective-permute-done | bytes 221216 | tf_op jit(solution)/shard_map/ppermute | solution.py:265
  43.6 1.1 %prepare_other.7 = bf16[2,32,9216]{2,1,0:T(8,128)(2,1)S(1)} custom-call(s32[2,288]{1,0:T(2,128)S(1)} %copy-done.2, bf16[32,3456]{1,0:T(8,128)(2,1)S(1)} %collective-permute-done.8.refs_0_, bf16[32,3456]{1,0:T(8,128)(2,1)S(1)} %collective-permute-done.9.refs_1_, bf16[32,3456]{1,0:T(8,128)(2,1)S(1)} %collective-permute-done.10.refs_2_, ...), custom_call_target="tpu_custom_call" | custom-call | flops 1 | bytes 1 | tf_op jit(solution)/shard_map/prepare_other/pallas_call | solution.py:99
  44.7 0.6 collective-permute-start.17
  45.3 2.4 %collective-permute-done.13.refs_2_ = bf16[32,3456]{1,0:T(8,128)(2,1)S(1)} collective-permute-done((bf16[32,3456]{1,0:T(8,128)(2,1)S(1)}, bf16[32,3456]{1,0:T(8,128)(2,1)S(1)}, u32[]{:S(2)}, u32[]{:S(2)}) %collective-permute-start.13) | collective-permute-done | bytes 221216 | tf_op jit(solution)/shard_map/ppermute | solution.py:265
  47.7 1.0 %prepare_other.6 = bf16[2,32,9216]{2,1,0:T(8,128)(2,1)S(1)} custom-call(s32[2,288]{1,0:T(2,128)S(1)} %copy-done.2, bf16[32,3456]{1,0:T(8,128)(2,1)S(1)} %collective-permute-done.4.refs_0_, bf16[32,3456]{1,0:T(8,128)(2,1)S(1)} %collective-permute-done.12.refs_1_, bf16[32,3456]{1,0:T(8,128)(2,1)S(1)} %collective-permute-done.13.refs_2_, ...), custom_call_target="tpu_custom_call" | custom-call | flops 1 | bytes 1 | tf_op jit(solution)/shard_map/prepare_other/pallas_call | solution.py:99
  48.7 0.1 collective-permute-start.15
  48.8 1.1 %prepare_own.7.refs_6_ = bf16[2,32,9216]{2,1,0:T(8,128)(2,1)S(1)} custom-call(s32[2,288]{1,0:T(2,128)S(1)} %copy-done.2, bf16[32,3456]{1,0:T(8,128)(2,1)S(1)} %collective-permute-done.8.refs_0_, bf16[32,3456]{1,0:T(8,128)(2,1)S(1)} %collective-permute-done.9.refs_1_, bf16[32,3456]{1,0:T(8,128)(2,1)S(1)} %collective-permute-done.10.refs_2_, ...), custom_call_target="tpu_custom_call" | custom-call | flops 1 | bytes 1 | tf_op jit(solution)/shard_map/prepare_own/pallas_call | solution.py:99
  49.9 1.1 %prepare_own.6.refs_4_ = bf16[2,32,9216]{2,1,0:T(8,128)(2,1)S(1)} custom-call(s32[2,288]{1,0:T(2,128)S(1)} %copy-done.2, bf16[32,3456]{1,0:T(8,128)(2,1)S(1)} %collective-permute-done.4.refs_0_, bf16[32,3456]{1,0:T(8,128)(2,1)S(1)} %collective-permute-done.12.refs_1_, bf16[32,3456]{1,0:T(8,128)(2,1)S(1)} %collective-permute-done.13.refs_2_, ...), custom_call_target="tpu_custom_call" | custom-call | flops 1 | bytes 1 | tf_op jit(solution)/shard_map/prepare_own/pallas_call | solution.py:99
  50.9 0.7 collective-permute-done.15.refs_5_
  51.6 10.6 %products.3 = (f32[4,64,256]{2,1,0:T(8,128)S(1)}, bf16[4,64,256]{2,1,0:T(8,128)(2,1)S(1)}, bf16[4,64,256]{2,1,0:T(8,128)(2,1)S(1)}, bf16[4,64,256]{2,1,0:T(8,128)(2,1)S(1)}) custom-call(bf16[9,16,9216]{2,1,0:T(8,128)(2,1)S(1)} %band_matrices.1.x_ref, bf16[2,32,9216]{2,1,0:T(8,128)(2,1)S(1)} %prepare_own.4._.refs_0_, ...), custom_call_target="tpu_custom_call" | custom-call | flops 9663676416 | bytes 9437184 | tf_op jit(solution)/shard_map/products/pallas_call | solution.py:152
  62.2 2.7 %collective-permute-start.18 = (bf16[4,64,256]{2,1,0:T(8,128)(2,1)S(1)}, bf16[4,64,256]{2,1,0:T(8,128)(2,1)S(1)}, u32[]{:S(2)}, u32[]{:S(2)}) collective-permute-start(bf16[4,64,256]{2,1,0:T(8,128)(2,1)S(1)} %get-tuple-element.75), channel_id=1, source_target_pairs={{0,2},{1,3},{2,4},{3,5},{4,6},{5,7},{6,0},{7,1},{8,10},{9,11},{10,... | collective-permute-start | bytes 393224 | tf_op jit(solution)/shard_map/ppermute | solution.py:265
  64.9 0.9 collective-permute-start.19
  65.7 1.6 %collective-permute-start.20 = (bf16[4,64,256]{2,1,0:T(8,128)(2,1)S(1)}, bf16[4,64,256]{2,1,0:T(8,128)(2,1)S(1)}, u32[]{:S(2)}, u32[]{:S(2)}) collective-permute-start(bf16[4,64,256]{2,1,0:T(8,128)(2,1)S(1)} %get-tuple-element.77), channel_id=1, source_target_pairs={{0,6},{1,7},{2,0},{3,1},{4,2},{5,3},{6,4},{7,5},{8,14},{9,15},{10,... | collective-permute-start | bytes 393224 | tf_op jit(solution)/shard_map/ppermute | solution.py:265
  67.3 10.4 %products.4 = (f32[4,64,256]{2,1,0:T(8,128)S(1)}, bf16[4,64,256]{2,1,0:T(8,128)(2,1)S(1)}, bf16[4,64,256]{2,1,0:T(8,128)(2,1)S(1)}, bf16[4,64,256]{2,1,0:T(8,128)(2,1)S(1)}) custom-call(bf16[9,16,9216]{2,1,0:T(8,128)(2,1)S(1)} %band_matrices.1.x_ref, bf16[2,32,9216]{2,1,0:T(8,128)(2,1)S(1)} %prepare_own.4._.refs_0_, ...), custom_call_target="tpu_custom_call" | custom-call | flops 9663676416 | bytes 9437184 | tf_op jit(solution)/shard_map/products/pallas_call | solution.py:152
  77.7 0.5 collective-permute-start.21
  78.2 2.1 %collective-permute-start.22 = (bf16[4,64,256]{2,1,0:T(8,128)(2,1)S(1)}, bf16[4,64,256]{2,1,0:T(8,128)(2,1)S(1)}, u32[]{:S(2)}, u32[]{:S(2)}) collective-permute-start(bf16[4,64,256]{2,1,0:T(8,128)(2,1)S(1)} %get-tuple-element.91), channel_id=1, source_target_pairs={{0,4},{1,5},{2,6},{3,7},{4,0},{5,1},{6,2},{7,3},{8,12},{9,13},{10,... | collective-permute-start | bytes 393224 | tf_op jit(solution)/shard_map/ppermute | solution.py:265
  80.3 1.3 %collective-permute-start.23 = (bf16[4,64,256]{2,1,0:T(8,128)(2,1)S(1)}, bf16[4,64,256]{2,1,0:T(8,128)(2,1)S(1)}, u32[]{:S(2)}, u32[]{:S(2)}) collective-permute-start(bf16[4,64,256]{2,1,0:T(8,128)(2,1)S(1)} %get-tuple-element.92), channel_id=1, source_target_pairs={{0,6},{1,7},{2,0},{3,1},{4,2},{5,3},{6,4},{7,5},{8,14},{9,15},{10,... | collective-permute-start | bytes 393224 | tf_op jit(solution)/shard_map/ppermute | solution.py:265
  81.6 3.0 %products.5 = (f32[1,64,256]{2,1,0:T(8,128)S(1)}, bf16[1,64,256]{2,1,0:T(8,128)(2,1)S(1)}, bf16[1,64,256]{2,1,0:T(8,128)(2,1)S(1)}, bf16[1,64,256]{2,1,0:T(8,128)(2,1)S(1)}) custom-call(bf16[9,16,9216]{2,1,0:T(8,128)(2,1)S(1)} %band_matrices.1.x_ref, bf16[2,32,9216]{2,1,0:T(8,128)(2,1)S(1)} %prepare_own.4._.refs_0_, ...), custom_call_target="tpu_custom_call" | custom-call | flops 2415919104 | bytes 9437184 | tf_op jit(solution)/shard_map/products/pallas_call | solution.py:152
  84.6 0.8 collective-permute-start.24
  85.4 1.4 %collective-permute-start.25 = (bf16[1,64,256]{2,1,0:T(8,128)(2,1)S(1)}, bf16[1,64,256]{2,1,0:T(8,128)(2,1)S(1)}, u32[]{:S(2)}, u32[]{:S(2)}) collective-permute-start(bf16[1,64,256]{2,1,0:T(8,128)(2,1)S(1)} %get-tuple-element.99), channel_id=1, source_target_pairs={{0,4},{1,5},{2,6},{3,7},{4,0},{5,1},{6,2},{7,3},{8,12},{9,13},{10,... | collective-permute-start | bytes 98312 | tf_op jit(solution)/shard_map/ppermute | solution.py:265
  86.8 2.8 %collective-permute-start.26 = (bf16[1,64,256]{2,1,0:T(8,128)(2,1)S(1)}, bf16[1,64,256]{2,1,0:T(8,128)(2,1)S(1)}, u32[]{:S(2)}, u32[]{:S(2)}) collective-permute-start(bf16[1,64,256]{2,1,0:T(8,128)(2,1)S(1)} %get-tuple-element.100), channel_id=1, source_target_pairs={{0,6},{1,7},{2,0},{3,1},{4,2},{5,3},{6,4},{7,5},{8,14},{9,15},{10,... | collective-permute-start | bytes 98312 | tf_op jit(solution)/shard_map/ppermute | solution.py:265
  89.6 1.4 %collective-permute-done.22 = bf16[4,64,256]{2,1,0:T(8,128)(2,1)S(1)} collective-permute-done((bf16[4,64,256]{2,1,0:T(8,128)(2,1)S(1)}, bf16[4,64,256]{2,1,0:T(8,128)(2,1)S(1)}, u32[]{:S(2)}, u32[]{:S(2)}) %collective-permute-start.22) | collective-permute-done | bytes 131104 | tf_op jit(solution)/shard_map/ppermute | solution.py:265
  91.0 0.1 convert_add_fusion.1
  91.1 0.1 convert_add_fusion
  91.2 0.6 collective-permute-done.24
  91.7 2.9 %collective-permute-done.25 = bf16[1,64,256]{2,1,0:T(8,128)(2,1)S(1)} collective-permute-done((bf16[1,64,256]{2,1,0:T(8,128)(2,1)S(1)}, bf16[1,64,256]{2,1,0:T(8,128)(2,1)S(1)}, u32[]{:S(2)}, u32[]{:S(2)}) %collective-permute-start.25) | collective-permute-done | bytes 32800 | tf_op jit(solution)/shard_map/ppermute | solution.py:265
  94.7 0.1 collective-permute-start.28
  94.8 0.6 collective-permute-start.27
  95.4 1.0 collective-permute-done.27
  96.3 0.9 maximum_select_fusion
  (28 shorter events, 0.2 us)
Async XLA Ops:
  2.0 7.8 %copy-start.4 = (bf16[32,3456]{1,0:T(8,128)(2,1)S(1)}, bf16[32,3456]{1,0:T(8,128)(2,1)}, u32[]{:S(2)}) copy-start(bf16[32,3456]{1,0:T(8,128)(2,1)} %get-tuple-element.61) | copy-start | bytes 663556
  2.0 12.8 %copy-start = (bf16[2,9,32,288]{3,2,1,0:T(8,128)(2,1)S(1)}, bf16[2,9,32,288]{3,2,1,0:T(8,128)(2,1)}, u32[]{:S(2)}) copy-start(bf16[2,9,32,288]{3,2,1,0:T(8,128)(2,1)} %coupling_ref.5) | copy-start | bytes 995332
  2.0 17.1 %copy-start.2 = (s32[2,288]{1,0:T(2,128)S(1)}, s32[2,288]{1,0:T(2,128)}, u32[]{:S(2)}) copy-start(s32[2,288]{1,0:T(2,128)} %kq_ref.17) | copy-start | bytes 6916
  2.0 11.3 %collective-permute-start.3 = (bf16[32,3456]{1,0:T(8,128)(2,1)}, bf16[32,3456]{1,0:T(8,128)(2,1)S(1)}, u32[]{:S(2)}, u32[]{:S(2)}) collective-permute-start(bf16[32,3456]{1,0:T(8,128)(2,1)} %get-tuple-element.53), channel_id=1, source_target_pairs={{0,6},{1,7},{2,0},{3,1},{4,2},{5,3},{6,4},{7,5},{8,14},{9,15},{10,... | collective-permute-start | bytes 663560 | tf_op jit(solution)/shard_map/ppermute | solution.py:265
  9.7 5.1 %collective-permute-start = (bf16[9,32,288]{2,1,0:T(8,128)(2,1)}, bf16[9,32,288]{2,1,0:T(8,128)(2,1)S(1)}, u32[]{:S(2)}, u32[]{:S(2)}) collective-permute-start(bf16[9,32,288]{2,1,0:T(8,128)(2,1)} %get-tuple-element.57), channel_id=1, source_target_pairs={{0,1},{1,0},{2,3},{3,2},{4,5},{5,4},{6,7},{7,6},{8,9},{9,8},{10,11... | collective-permute-start | bytes 497672 | tf_op jit(solution)/shard_map/ppermute | solution.py:265
  9.8 12.6 %collective-permute-start.8 = (bf16[32,3456]{1,0:T(8,128)(2,1)S(1)}, bf16[32,3456]{1,0:T(8,128)(2,1)S(1)}, u32[]{:S(2)}, u32[]{:S(2)}) collective-permute-start(bf16[32,3456]{1,0:T(8,128)(2,1)S(1)} %copy-done.4), channel_id=1, source_target_pairs={{0,2},{1,3},{2,4},{3,5},{4,6},{5,7},{6,0},{7,1},{8,10},{9,11},{10,... | collective-permute-start | bytes 663560 | tf_op jit(solution)/shard_map/ppermute | solution.py:265
  13.3 12.7 %collective-permute-start.5 = (bf16[32,3456]{1,0:T(8,128)(2,1)S(1)}, bf16[32,3456]{1,0:T(8,128)(2,1)S(1)}, u32[]{:S(2)}, u32[]{:S(2)}) collective-permute-start(bf16[32,3456]{1,0:T(8,128)(2,1)S(1)} %collective-permute-done.3.refs_0_), channel_id=1, source_target_pairs={{0,8},{1,17},{2,10},{3,19},{4,12},{5,21},{6,14},{7,23},{8,0},{9,25... | collective-permute-start | bytes 663560 | tf_op jit(solution)/shard_map/ppermute | solution.py:265
  14.9 10.0 %collective-permute-start.1 = (bf16[9,32,288]{2,1,0:T(8,128)(2,1)S(1)}, bf16[9,32,288]{2,1,0:T(8,128)(2,1)S(1)}, u32[]{:S(2)}, u32[]{:S(2)}) collective-permute-start(bf16[9,32,288]{2,1,0:T(8,128)(2,1)S(1)} %bitcast_select_fusion), channel_id=1, source_target_pairs={{0,6},{1,7},{2,0},{3,1},{4,2},{5,3},{6,4},{7,5},{8,14},{9,15},{10,... | collective-permute-start | bytes 497672 | tf_op jit(solution)/shard_map/ppermute | solution.py:265
  19.1 1.2 %copy-start.1 = (bf16[32,13824]{1,0:T(8,128)(2,1)S(1)}, bf16[32,13824]{1,0:T(8,128)(2,1)}, u32[]{:S(2)}) copy-start(bf16[32,13824]{1,0:T(8,128)(2,1)} %get-tuple-element.56.refs_0_) | copy-start | bytes 2654212
  21.3 1.0 %copy-start.3 = (bf16[32,3456]{1,0:T(8,128)(2,1)S(1)}, bf16[32,3456]{1,0:T(8,128)(2,1)}, u32[]{:S(2)}) copy-start(bf16[32,3456]{1,0:T(8,128)(2,1)} %get-tuple-element.59) | copy-start | bytes 663556
  22.3 11.4 %collective-permute-start.4 = (bf16[32,3456]{1,0:T(8,128)(2,1)S(1)}, bf16[32,3456]{1,0:T(8,128)(2,1)S(1)}, u32[]{:S(2)}, u32[]{:S(2)}) collective-permute-start(bf16[32,3456]{1,0:T(8,128)(2,1)S(1)} %copy-done.3), channel_id=1, source_target_pairs={{0,4},{1,5},{2,6},{3,7},{4,0},{5,1},{6,2},{7,3},{8,12},{9,13},{10,... | collective-permute-start | bytes 663560 | tf_op jit(solution)/shard_map/ppermute | solution.py:265
  22.4 11.3 %collective-permute-start.10 = (bf16[32,3456]{1,0:T(8,128)(2,1)S(1)}, bf16[32,3456]{1,0:T(8,128)(2,1)S(1)}, u32[]{:S(2)}, u32[]{:S(2)}) collective-permute-start(bf16[32,3456]{1,0:T(8,128)(2,1)S(1)} %collective-permute-done.8.refs_0_), channel_id=1, source_target_pairs={{0,16},{1,9},{2,18},{3,11},{4,20},{5,13},{6,22},{7,15},{8,24},{9,1... | collective-permute-start | bytes 663560 | tf_op jit(solution)/shard_map/ppermute | solution.py:265
  24.0 8.3 %collective-permute-start.9 = (bf16[32,3456]{1,0:T(8,128)(2,1)S(1)}, bf16[32,3456]{1,0:T(8,128)(2,1)S(1)}, u32[]{:S(2)}, u32[]{:S(2)}) collective-permute-start(bf16[32,3456]{1,0:T(8,128)(2,1)S(1)} %collective-permute-done.8.refs_0_), channel_id=1, source_target_pairs={{0,8},{1,17},{2,10},{3,19},{4,12},{5,21},{6,14},{7,23},{8,0},{9,25... | collective-permute-start | bytes 663560 | tf_op jit(solution)/shard_map/ppermute | solution.py:265
  24.8 8.8 %collective-permute-start.6 = (bf16[32,3456]{1,0:T(8,128)(2,1)S(1)}, bf16[32,3456]{1,0:T(8,128)(2,1)S(1)}, u32[]{:S(2)}, u32[]{:S(2)}) collective-permute-start(bf16[32,3456]{1,0:T(8,128)(2,1)S(1)} %collective-permute-done.3.refs_0_), channel_id=1, source_target_pairs={{0,16},{1,9},{2,18},{3,11},{4,20},{5,13},{6,22},{7,15},{8,24},{9,1... | collective-permute-start | bytes 663560 | tf_op jit(solution)/shard_map/ppermute | solution.py:265
  26.1 7.6 %collective-permute-start.7 = (bf16[32,3456]{1,0:T(8,128)(2,1)S(1)}, bf16[32,3456]{1,0:T(8,128)(2,1)S(1)}, u32[]{:S(2)}, u32[]{:S(2)}) collective-permute-start(bf16[32,3456]{1,0:T(8,128)(2,1)S(1)} %collective-permute-done.5.refs_1_), channel_id=1, source_target_pairs={{0,16},{1,9},{2,18},{3,11},{4,20},{5,13},{6,22},{7,15},{8,24},{9,1... | collective-permute-start | bytes 663560 | tf_op jit(solution)/shard_map/ppermute | solution.py:265
  32.2 11.4 %collective-permute-start.16 = (bf16[32,3456]{1,0:T(8,128)(2,1)S(1)}, bf16[32,3456]{1,0:T(8,128)(2,1)S(1)}, u32[]{:S(2)}, u32[]{:S(2)}) collective-permute-start(bf16[32,3456]{1,0:T(8,128)(2,1)S(1)} %collective-permute-done.9.refs_1_), channel_id=1, source_target_pairs={{0,16},{1,9},{2,18},{3,11},{4,20},{5,13},{6,22},{7,15},{8,24},{9,1... | collective-permute-start | bytes 663560 | tf_op jit(solution)/shard_map/ppermute | solution.py:265
  33.7 11.0 %collective-permute-start.14 = (bf16[32,3456]{1,0:T(8,128)(2,1)S(1)}, bf16[32,3456]{1,0:T(8,128)(2,1)S(1)}, u32[]{:S(2)}, u32[]{:S(2)}) collective-permute-start(bf16[32,3456]{1,0:T(8,128)(2,1)S(1)} %collective-permute-done.4.refs_0_), channel_id=1, source_target_pairs={{0,24},{1,25},{2,26},{3,27},{4,28},{5,29},{6,30},{7,31},{8,16},{9,... | collective-permute-start | bytes 663560 | tf_op jit(solution)/shard_map/ppermute | solution.py:265
  35.6 12.1 %collective-permute-start.13 = (bf16[32,3456]{1,0:T(8,128)(2,1)S(1)}, bf16[32,3456]{1,0:T(8,128)(2,1)S(1)}, u32[]{:S(2)}, u32[]{:S(2)}) collective-permute-start(bf16[32,3456]{1,0:T(8,128)(2,1)S(1)} %collective-permute-done.4.refs_0_), channel_id=1, source_target_pairs={{0,16},{1,17},{2,18},{3,19},{4,20},{5,21},{6,22},{7,23},{8,24},{9,... | collective-permute-start | bytes 663560 | tf_op jit(solution)/shard_map/ppermute | solution.py:265
  36.7 11.0 %collective-permute-start.12 = (bf16[32,3456]{1,0:T(8,128)(2,1)S(1)}, bf16[32,3456]{1,0:T(8,128)(2,1)S(1)}, u32[]{:S(2)}, u32[]{:S(2)}) collective-permute-start(bf16[32,3456]{1,0:T(8,128)(2,1)S(1)} %collective-permute-done.4.refs_0_), channel_id=1, source_target_pairs={{0,8},{1,9},{2,10},{3,11},{4,12},{5,13},{6,14},{7,15},{8,0},{9,1},... | collective-permute-start | bytes 663560 | tf_op jit(solution)/shard_map/ppermute | solution.py:265
  37.2 13.7 %collective-permute-start.2 = (bf16[2,32,9216]{2,1,0:T(8,128)(2,1)S(1)}, bf16[2,32,9216]{2,1,0:T(8,128)(2,1)S(1)}, u32[]{:S(2)}, u32[]{:S(2)}) collective-permute-start(bf16[2,32,9216]{2,1,0:T(8,128)(2,1)S(1)} %prepare_other.4), channel_id=1, source_target_pairs={{0,1},{1,0},{2,3},{3,2},{4,5},{5,4},{6,7},{7,6},{8,9},{9,8},{10,11... | collective-permute-start | bytes 3538952 | tf_op jit(solution)/shard_map/ppermute | solution.py:265
  43.6 7.3 %collective-permute-start.11 = (bf16[2,32,9216]{2,1,0:T(8,128)(2,1)S(1)}, bf16[2,32,9216]{2,1,0:T(8,128)(2,1)S(1)}, u32[]{:S(2)}, u32[]{:S(2)}) collective-permute-start(bf16[2,32,9216]{2,1,0:T(8,128)(2,1)S(1)} %prepare_other.5), channel_id=1, source_target_pairs={{0,1},{1,0},{2,3},{3,2},{4,5},{5,4},{6,7},{7,6},{8,9},{9,8},{10,11... | collective-permute-start | bytes 3538952 | tf_op jit(solution)/shard_map/ppermute | solution.py:265
  44.7 6.2 %collective-permute-start.17 = (bf16[2,32,9216]{2,1,0:T(8,128)(2,1)S(1)}, bf16[2,32,9216]{2,1,0:T(8,128)(2,1)S(1)}, u32[]{:S(2)}, u32[]{:S(2)}) collective-permute-start(bf16[2,32,9216]{2,1,0:T(8,128)(2,1)S(1)} %prepare_other.7), channel_id=1, source_target_pairs={{0,1},{1,0},{2,3},{3,2},{4,5},{5,4},{6,7},{7,6},{8,9},{9,8},{10,11... | collective-permute-start | bytes 3538952 | tf_op jit(solution)/shard_map/ppermute | solution.py:265
  48.7 2.9 %collective-permute-start.15 = (bf16[2,32,9216]{2,1,0:T(8,128)(2,1)S(1)}, bf16[2,32,9216]{2,1,0:T(8,128)(2,1)S(1)}, u32[]{:S(2)}, u32[]{:S(2)}) collective-permute-start(bf16[2,32,9216]{2,1,0:T(8,128)(2,1)S(1)} %prepare_other.6), channel_id=1, source_target_pairs={{0,1},{1,0},{2,3},{3,2},{4,5},{5,4},{6,7},{7,6},{8,9},{9,8},{10,11... | collective-permute-start | bytes 3538952 | tf_op jit(solution)/shard_map/ppermute | solution.py:265
  62.2 18.1 %collective-permute-start.18 = (bf16[4,64,256]{2,1,0:T(8,128)(2,1)S(1)}, bf16[4,64,256]{2,1,0:T(8,128)(2,1)S(1)}, u32[]{:S(2)}, u32[]{:S(2)}) collective-permute-start(bf16[4,64,256]{2,1,0:T(8,128)(2,1)S(1)} %get-tuple-element.75), channel_id=1, source_target_pairs={{0,2},{1,3},{2,4},{3,5},{4,6},{5,7},{6,0},{7,1},{8,10},{9,11},{10,... | collective-permute-start | bytes 393224 | tf_op jit(solution)/shard_map/ppermute | solution.py:265
  64.9 16.7 %collective-permute-start.19 = (bf16[4,64,256]{2,1,0:T(8,128)(2,1)S(1)}, bf16[4,64,256]{2,1,0:T(8,128)(2,1)S(1)}, u32[]{:S(2)}, u32[]{:S(2)}) collective-permute-start(bf16[4,64,256]{2,1,0:T(8,128)(2,1)S(1)} %get-tuple-element.76), channel_id=1, source_target_pairs={{0,4},{1,5},{2,6},{3,7},{4,0},{5,1},{6,2},{7,3},{8,12},{9,13},{10,... | collective-permute-start | bytes 393224 | tf_op jit(solution)/shard_map/ppermute | solution.py:265
  65.7 15.9 %collective-permute-start.20 = (bf16[4,64,256]{2,1,0:T(8,128)(2,1)S(1)}, bf16[4,64,256]{2,1,0:T(8,128)(2,1)S(1)}, u32[]{:S(2)}, u32[]{:S(2)}) collective-permute-start(bf16[4,64,256]{2,1,0:T(8,128)(2,1)S(1)} %get-tuple-element.77), channel_id=1, source_target_pairs={{0,6},{1,7},{2,0},{3,1},{4,2},{5,3},{6,4},{7,5},{8,14},{9,15},{10,... | collective-permute-start | bytes 393224 | tf_op jit(solution)/shard_map/ppermute | solution.py:265
  77.7 9.1 %collective-permute-start.21 = (bf16[4,64,256]{2,1,0:T(8,128)(2,1)S(1)}, bf16[4,64,256]{2,1,0:T(8,128)(2,1)S(1)}, u32[]{:S(2)}, u32[]{:S(2)}) collective-permute-start(bf16[4,64,256]{2,1,0:T(8,128)(2,1)S(1)} %get-tuple-element.90), channel_id=1, source_target_pairs={{0,2},{1,3},{2,4},{3,5},{4,6},{5,7},{6,0},{7,1},{8,10},{9,11},{10,... | collective-permute-start | bytes 393224 | tf_op jit(solution)/shard_map/ppermute | solution.py:265
  78.2 12.8 %collective-permute-start.22 = (bf16[4,64,256]{2,1,0:T(8,128)(2,1)S(1)}, bf16[4,64,256]{2,1,0:T(8,128)(2,1)S(1)}, u32[]{:S(2)}, u32[]{:S(2)}) collective-permute-start(bf16[4,64,256]{2,1,0:T(8,128)(2,1)S(1)} %get-tuple-element.91), channel_id=1, source_target_pairs={{0,4},{1,5},{2,6},{3,7},{4,0},{5,1},{6,2},{7,3},{8,12},{9,13},{10,... | collective-permute-start | bytes 393224 | tf_op jit(solution)/shard_map/ppermute | solution.py:265
  80.3 10.8 %collective-permute-start.23 = (bf16[4,64,256]{2,1,0:T(8,128)(2,1)S(1)}, bf16[4,64,256]{2,1,0:T(8,128)(2,1)S(1)}, u32[]{:S(2)}, u32[]{:S(2)}) collective-permute-start(bf16[4,64,256]{2,1,0:T(8,128)(2,1)S(1)} %get-tuple-element.92), channel_id=1, source_target_pairs={{0,6},{1,7},{2,0},{3,1},{4,2},{5,3},{6,4},{7,5},{8,14},{9,15},{10,... | collective-permute-start | bytes 393224 | tf_op jit(solution)/shard_map/ppermute | solution.py:265
  84.6 7.1 %collective-permute-start.24 = (bf16[1,64,256]{2,1,0:T(8,128)(2,1)S(1)}, bf16[1,64,256]{2,1,0:T(8,128)(2,1)S(1)}, u32[]{:S(2)}, u32[]{:S(2)}) collective-permute-start(bf16[1,64,256]{2,1,0:T(8,128)(2,1)S(1)} %get-tuple-element.98), channel_id=1, source_target_pairs={{0,2},{1,3},{2,4},{3,5},{4,6},{5,7},{6,0},{7,1},{8,10},{9,11},{10,... | collective-permute-start | bytes 98312 | tf_op jit(solution)/shard_map/ppermute | solution.py:265
  85.4 9.2 %collective-permute-start.25 = (bf16[1,64,256]{2,1,0:T(8,128)(2,1)S(1)}, bf16[1,64,256]{2,1,0:T(8,128)(2,1)S(1)}, u32[]{:S(2)}, u32[]{:S(2)}) collective-permute-start(bf16[1,64,256]{2,1,0:T(8,128)(2,1)S(1)} %get-tuple-element.99), channel_id=1, source_target_pairs={{0,4},{1,5},{2,6},{3,7},{4,0},{5,1},{6,2},{7,3},{8,12},{9,13},{10,... | collective-permute-start | bytes 98312 | tf_op jit(solution)/shard_map/ppermute | solution.py:265
  86.8 7.8 %collective-permute-start.26 = (bf16[1,64,256]{2,1,0:T(8,128)(2,1)S(1)}, bf16[1,64,256]{2,1,0:T(8,128)(2,1)S(1)}, u32[]{:S(2)}, u32[]{:S(2)}) collective-permute-start(bf16[1,64,256]{2,1,0:T(8,128)(2,1)S(1)} %get-tuple-element.100), channel_id=1, source_target_pairs={{0,6},{1,7},{2,0},{3,1},{4,2},{5,3},{6,4},{7,5},{8,14},{9,15},{10,... | collective-permute-start | bytes 98312 | tf_op jit(solution)/shard_map/ppermute | solution.py:265
  94.7 1.7 %collective-permute-start.28 = (f32[5,32,256]{2,1,0:T(8,128)S(1)}, f32[5,32,256]{2,1,0:T(8,128)S(1)}, u32[]{:S(2)}, u32[]{:S(2)}) collective-permute-start(f32[5,32,256]{2,1,0:T(8,128)S(1)} %get-tuple-element.102), channel_id=1, source_target_pairs={{0,1},{1,0},{2,3},{3,2},{4,5},{5,4},{6,7},{7,6},{8,9},{9,8},{10,11... | collective-permute-start | bytes 491528 | tf_op jit(solution)/shard_map/ppermute | solution.py:265
  94.8 1.5 %collective-permute-start.27 = (f32[4,32,256]{2,1,0:T(8,128)S(1)}, f32[4,32,256]{2,1,0:T(8,128)S(1)}, u32[]{:S(2)}, u32[]{:S(2)}) collective-permute-start(f32[4,32,256]{2,1,0:T(8,128)S(1)} %get-tuple-element.104), channel_id=1, source_target_pairs={{0,1},{1,0},{2,3},{3,2},{4,5},{5,4},{6,7},{7,6},{8,9},{9,8},{10,11... | collective-permute-start | bytes 393224 | tf_op jit(solution)/shard_map/ppermute | solution.py:265
